TPU v7x, 32 devices: a whole 2x2x4 slice. The times are simulated.
32 devices in a mesh: seq: 8 (over z, x), rows: 4 (over y, core).
Axes of the slice: x: 2, y: 2, z: 4, core: 2. Of those that a mesh axis runs over, the one named last changes fastest.
Arguments:
- frames: bfloat16 [64, 64, 4096], P('seq', 'rows'), may hold values from -12 to 12
- cotangent: bfloat16 [64, 64, 4096], P('seq', 'rows'), may hold values from -12 to 12
- actions: int32 [64], P('seq'), may hold values from 0 to 17
- noise_ids: int32 [64], P('seq'), may hold values from 0 to 31
- valid: int32 [64], P('seq'), may hold values 0 or 1
- act_table: bfloat16 [18, 256], P(None, 'seq'), may hold values from -5 to 5
- noise_table: bfloat16 [32, 256], P(None, 'seq'), may hold values from -5 to 5
- ada_one: bfloat16 [256, 128], P('seq'), may hold values from -0.1875 to 0.1875
- ada_two: bfloat16 [256, 128], P('seq'), may hold values from -0.1875 to 0.1875
- conv_one: bfloat16 [576, 64], P('seq'), may hold values from -0.25 to 0.25
- conv_two: bfloat16 [576, 64], P('seq'), may hold values from -0.25 to 0.25
- down_kernel: bfloat16 [576, 64], P('seq'), may hold values from -0.25 to 0.25
- up_kernel: bfloat16 [1152, 64], P('seq'), may hold values from -0.1875 to 0.1875
- bias_one: bfloat16 [64], P('seq'), may hold values from -3 to 3
- bias_two: bfloat16 [64], P('seq'), may hold values from -3 to 3
- bias_down: bfloat16 [64], P('seq'), may hold values from -3 to 3
- bias_up: bfloat16 [64], P('seq'), may hold values from -3 to 3
Outputs:
- output: bfloat16 [64, 64, 4096], P('seq', 'rows')
- frames_grad: float32 [64, 64, 4096], P('seq', 'rows')
- act_table_grad: float32 [18, 256], P(None, 'seq')
- noise_table_grad: float32 [32, 256], P(None, 'seq')
- ada_one_grad: float32 [256, 128], P('seq')
- ada_two_grad: float32 [256, 128], P('seq')
- conv_one_grad: float32 [576, 64], P('seq')
- conv_two_grad: float32 [576, 64], P('seq')
- down_grad: float32 [576, 64], P('seq')
- up_grad: float32 [1152, 64], P('seq')
- bias_one_grad: float32 [64], P('seq')
- bias_two_grad: float32 [64], P('seq')
- bias_down_grad: float32 [64], P('seq')
- bias_up_grad: float32 [64], P('seq')
All inputs are finite; a program needn't handle non-finite values. No bound on the sum of `valid` on one device may be relied on, other than what follows from the above.
Results may differ from a plain program's by a relative error of at most 0.0066.
Values may be sent and summed in bfloat16 or wider, within the bound.
No kernel may reach another device: no remote copies, remote signals or barrier semaphores. Data moves between devices by JAX's collectives and lax.ppermute only.
A program may use at most 192 MiB of HBM per device.

v0:
```python
import jax
import jax.numpy as jnp
from jax import lax
from jax.experimental import pallas as pl
from jax.experimental.pallas import tpu as pltpu
from jax.sharding import PartitionSpec as P

C = 64
NACT = 18
GROUPS = 32
NLEV = 32
H = 64
W = 64
PAIRS = W // 2
HALF = H // 2
LANES = 2 * C
BLOCK = PAIRS * HALF
MEMBERS = float(H * W * (C // GROUPS))
EPS = 1e-05

precise = lax.Precision.HIGHEST
f32 = jnp.float32
bf16 = jnp.bfloat16
VMEM_LIMIT = 60 * 2**20


def lane_ids(shape):
    return lax.broadcasted_iota(jnp.int32, shape, len(shape) - 1)


def swap_halves(x):
    return pltpu.roll(x, C, axis=x.ndim - 1)


def row_before(x):
    rows = lax.broadcasted_iota(jnp.int32, x.shape, 0)
    return jnp.where(rows == 0, 0.0, pltpu.roll(x, 1, axis=0))


def row_after(x):
    rows = lax.broadcasted_iota(jnp.int32, x.shape, 0)
    return jnp.where(rows == x.shape[0] - 1, 0.0, pltpu.roll(x, x.shape[0] - 1, axis=0))


def both_parities(x):
    x = jnp.broadcast_to(x, (8, LANES))
    return x + swap_halves(x)


def group_sum(x):
    even = lane_ids(x.shape) % 2 == 0
    return x + jnp.where(even, pltpu.roll(x, LANES - 1, axis=1), pltpu.roll(x, 1, axis=1))


def total(x):
    return jnp.sum(x, axis=0, keepdims=True)


def build_windows(windows, tile):
    low_lanes = lane_ids((HALF, LANES)) < C
    zero = jnp.zeros((HALF, LANES), f32)

    def write(j, even, odd):
        windows[0, j] = row_before(odd).astype(bf16)
        windows[1, j] = even.astype(bf16)
        windows[2, j] = odd.astype(bf16)
        windows[3, j] = row_after(even).astype(bf16)

    def body(j, carry):
        even_past, odd_past = carry
        even = swap_halves(tile(0, j))
        odd = swap_halves(tile(1, j))
        write(j, jnp.where(low_lanes, even_past, even), jnp.where(low_lanes, odd_past, odd))
        return even, odd

    even, odd = lax.fori_loop(0, PAIRS, body, (zero, zero), unroll=4)
    write(PAIRS, jnp.where(low_lanes, even, 0.0), jnp.where(low_lanes, odd, 0.0))


def window_operand(windows, slots):
    parts = []
    for slot in slots:
        for shift in (0, 1):
            parts.append(windows[slot, shift : shift + PAIRS].reshape(BLOCK, LANES))
    return jnp.concatenate(parts, axis=1)


def matmul(left, right):
    return jnp.dot(left, right, preferred_element_type=f32)


def tiles_of(y):
    return y.reshape(PAIRS, HALF, LANES)


def norm_stats(sums, squares):
    average = group_sum(both_parities(sums)) / MEMBERS
    variance = group_sum(both_parities(squares)) / MEMBERS - average * average
    return average, lax.rsqrt(variance + EPS)


def strip_start(member, offset, strip):
    return pl.multiple_of((member ^ offset) * strip, strip)


def load_strips(member, strips, image):
    for offset, strip in enumerate(strips):
        rows = strip.shape[1]
        start = strip_start(member, offset, rows)
        for j in range(PAIRS):
            image[j, pl.ds(start, rows), :] = strip[0, :, j * LANES : (j + 1) * LANES].astype(f32)


def store_strips(member, image, strips):
    for offset in range(strips.shape[0]):
        rows = strips.shape[2]
        start = strip_start(member, offset, rows)
        for j in range(PAIRS):
            strips[offset, 0, :, j * LANES : (j + 1) * LANES] = image[j, pl.ds(start, rows), :].astype(strips.dtype)


def parity_rows(image, parity, j):
    return image[j, pl.ds(parity, HALF, stride=2), :]


def forward_kernel(count, *refs):
    member_ref = refs[0]
    strips = refs[1 : 1 + count]
    styles, biases, w_one, w_two, w_down, w_up = refs[1 + count : 7 + count]
    out, win_one, win_two, win_level, win_coarse, middle, down, stats = refs[7 + count : 15 + count]
    image, level = refs[15 + count :]
    member = member_ref[0]
    win_one, win_two, win_level, win_coarse = (ref.at[0] for ref in (win_one, win_two, win_level, win_coarse))
    middle, down = middle.at[0], down.at[0]

    load_strips(member, strips, image)

    def add_stats(j, carry):
        x = image[j]
        s, q = carry
        return s + x, q + x * x

    zero = jnp.zeros((H, LANES), f32)
    s, q = lax.fori_loop(0, PAIRS, add_stats, (zero, zero), unroll=4)
    average_one, inverse_one = norm_stats(total(s), total(q))
    gain_one = inverse_one * styles[0, 0:1, :]
    half_gain = 0.5 * gain_one[0:1]
    half_shift = 0.5 * (styles[0, 1:2, :] - average_one[0:1] * gain_one[0:1])

    def act_one(parity, j):
        h = parity_rows(image, parity, j) * half_gain + half_shift
        return h * jnp.tanh(h) + h

    build_windows(win_one, act_one)
    y = matmul(window_operand(win_one, range(4)), w_one[...])
    sums = jnp.zeros((1, LANES), f32)
    squares = jnp.zeros((1, LANES), f32)
    for a in range(2):
        v = y[:, a * LANES : (a + 1) * LANES] + biases[0:1, :]
        sums = sums + total(v)
        squares = squares + total(v * v)
        middle[a] = tiles_of(v)
    average_two, inverse_two = norm_stats(sums, squares)
    stats[0, 0:1, :] = average_one[0:1]
    stats[0, 1:2, :] = inverse_one[0:1]
    stats[0, 2:3, :] = average_two[0:1]
    stats[0, 3:4, :] = inverse_two[0:1]
    stats[0, 4:8, :] = jnp.zeros((4, LANES), f32)
    gain_two = inverse_two * styles[0, 2:3, :]
    half_gain_two = 0.5 * gain_two[0:1]
    half_shift_two = 0.5 * (styles[0, 3:4, :] - average_two[0:1] * gain_two[0:1])

    def act_two(parity, j):
        h = middle[parity, j] * half_gain_two + half_shift_two
        return h * jnp.tanh(h) + h

    build_windows(win_two, act_two)
    y = matmul(window_operand(win_two, range(4)), w_two[...])
    for a in range(2):
        v = y[:, a * LANES : (a + 1) * LANES] + biases[1:2, :]
        level[a] = tiles_of(v) + image[:, pl.ds(a, HALF, stride=2), :]

    build_windows(win_level, lambda parity, j: level[parity, j])
    operand = window_operand(win_level, range(4))
    y = matmul(operand[:, : 6 * LANES], w_down[...]) + biases[2:3, :]
    down[...] = tiles_of(y)

    low_lanes = lane_ids((HALF, LANES)) < C

    def write_coarse(j, cells):
        win_coarse[0, j] = row_before(cells).astype(bf16)
        win_coarse[1, j] = cells.astype(bf16)
        win_coarse[2, j] = row_after(cells).astype(bf16)

    def coarse_body(j, past):
        h = down[j] * 0.5
        coarse = h * jnp.tanh(h) + h
        write_coarse(j, jnp.where(low_lanes, past, coarse))
        return coarse

    past = lax.fori_loop(0, PAIRS, coarse_body, jnp.zeros((HALF, LANES), f32), unroll=4)
    write_coarse(PAIRS, jnp.where(low_lanes, past, 0.0))

    operand = window_operand(win_level, range(4))
    coarse_operand = window_operand(win_coarse, (0, 1, 1, 2))
    y = matmul(operand, w_up[: 16 * C, :]) + matmul(coarse_operand, w_up[16 * C :, :])
    for a in range(2):
        v = y[:, a * LANES : (a + 1) * LANES] + biases[3:4, :]
        image[:, pl.ds(a, HALF, stride=2), :] = tiles_of(v) + level[a]
    store_strips(member, image, out)


def slope_twice(h):
    t = jnp.tanh(h)
    return (1.0 + t) + h * (1.0 - t * t)


def backward_kernel(count, *refs):
    member_ref = refs[0]
    cot_strips = refs[1 : 1 + count]
    frame_strips = refs[1 + count : 1 + 2 * count]
    styles, stats, middle, down, w_up, w_down, w_two, w_one = refs[1 + 2 * count : 9 + 2 * count]
    out, tile_out, tile_level, tile_mid, coarse_pairs, pieces, bias_sums = refs[9 + 2 * count : 16 + 2 * count]
    image, level_grad, pre_grad, windows, coarse_below, row_sums = refs[16 + 2 * count :]
    member = member_ref[0]
    tile_out, tile_level, tile_mid, coarse_pairs = (ref.at[0] for ref in (tile_out, tile_level, tile_mid, coarse_pairs))
    middle, down = middle.at[0], down.at[0]
    low_lanes = lane_ids((HALF, LANES)) < C

    load_strips(member, cot_strips, image)

    def add_rows(j, s):
        return s + image[j]

    sums = lax.fori_loop(0, PAIRS, add_rows, jnp.zeros((H, LANES), f32), unroll=4)
    bias_up_sum = both_parities(total(sums))

    def out_tile(parity, j):
        x = parity_rows(image, parity, j)
        tile_out[parity, j] = x.astype(bf16)
        return x

    build_windows(windows, out_tile)
    y = matmul(window_operand(windows, range(4)), w_up[...])
    for a in range(2):
        level_grad[a] = tiles_of(y[:, (2 + a) * LANES : (3 + a) * LANES]) + image[:, pl.ds(a, HALF, stride=2), :]
    coarse = y[:, :LANES] + y[:, LANES : 2 * LANES]
    pre_grad[0] = tiles_of(coarse)

    def coarse_body(t, carry):
        after, sums = carry
        j = PAIRS - 1 - t
        g = pre_grad[0, j]
        g = g + swap_halves(g)
        h = down[j] * 0.5
        d = 0.5 * g * slope_twice(h)
        pair = jnp.where(low_lanes, d, after)
        coarse_pairs[j] = pair.astype(bf16)
        coarse_below[j] = row_after(pair).astype(bf16)
        return d, sums + d

    zero = jnp.zeros((HALF, LANES), f32)
    _, sums = lax.fori_loop(0, PAIRS, coarse_body, (zero, zero), unroll=4)
    bias_down_sum = jnp.broadcast_to(total(sums), (8, LANES))

    operand = jnp.concatenate(
        [coarse_pairs[...].reshape(BLOCK, LANES), coarse_below[...].reshape(BLOCK, LANES)], axis=1
    )
    y = matmul(operand, w_down[...])
    sums = jnp.zeros((1, LANES), f32)
    for a in range(2):
        v = y[:, a * LANES : (a + 1) * LANES] + level_grad[a].reshape(BLOCK, LANES)
        sums = sums + total(v)
        level_grad[a] = tiles_of(v)
    bias_two_sum = both_parities(sums)

    def level_tile(parity, j):
        x = level_grad[parity, j]
        tile_level[parity, j] = x.astype(bf16)
        return x

    build_windows(windows, level_tile)

    def norm_slopes(y, value, k):
        average, inverse = stats[0, 2 * k : 2 * k + 1, :], stats[0, 2 * k + 1 : 2 * k + 2, :]
        gain = inverse * styles[0, 2 * k : 2 * k + 1, :]
        half_gain = 0.5 * gain
        half_shift = 0.5 * (styles[0, 2 * k + 1 : 2 * k + 2, :] - average * gain)
        scale_sum = jnp.zeros((1, LANES), f32)
        shift_sum = jnp.zeros((1, LANES), f32)
        for a in range(2):
            v = value(a)
            g = 0.5 * y[:, a * LANES : (a + 1) * LANES] * slope_twice(v * half_gain + half_shift)
            pre_grad[a] = tiles_of(g)
            shift_sum = shift_sum + total(g)
            scale_sum = scale_sum + total(g * ((v - average) * inverse))
        scale_sum, shift_sum = both_parities(scale_sum), both_parities(shift_sum)
        factor = styles[0, 2 * k : 2 * k + 1, :]
        center = group_sum(factor * shift_sum) / MEMBERS
        tilt = group_sum(factor * scale_sum) / MEMBERS
        return scale_sum, shift_sum, gain, (inverse * center)[0:1], (inverse * tilt)[0:1], average, inverse

    y = matmul(window_operand(windows, range(4)), w_two[...])
    scale_two, shift_two, gain, center, tilt, average, inverse = norm_slopes(
        y, lambda a: middle[a].reshape(BLOCK, LANES), 1
    )
    tilt_slope = tilt * inverse
    constant = tilt_slope * average - center

    def mid_tile(parity, j):
        x = pre_grad[parity, j] * gain + (constant - middle[parity, j] * tilt_slope)
        tile_mid[parity, j] = x.astype(bf16)
        row_sums[...] += x
        return x

    row_sums[...] = jnp.zeros_like(row_sums)
    build_windows(windows, mid_tile)
    bias_one_sum = both_parities(total(row_sums[...]))

    load_strips(member, frame_strips, image)
    y = matmul(window_operand(windows, range(4)), w_one[...])
    scale_one, shift_one, gain_one, center_one, tilt_one, average_one, inverse_one = norm_slopes(
        y, lambda a: image[:, pl.ds(a, HALF, stride=2), :].reshape(BLOCK, LANES), 0
    )
    slope_one = tilt_one * inverse_one
    constant_one = slope_one * average_one - center_one

    def frame_body(j, carry):
        for parity in range(2):
            x = parity_rows(image, parity, j)
            g = pre_grad[parity, j] * gain_one + (constant_one - x * slope_one) + level_grad[parity, j]
            image[j, pl.ds(parity, HALF, stride=2), :] = g
        return carry

    lax.fori_loop(0, PAIRS, frame_body, 0, unroll=4)
    store_strips(member, image, out)
    for k, value in enumerate((scale_one, shift_one, scale_two, shift_two)):
        pieces[0, k : k + 1, :] = value[0:1]
    pieces[0, 4:8, :] = jnp.zeros((4, LANES), f32)
    for k, value in enumerate((bias_one_sum, bias_two_sum, bias_down_sum, bias_up_sum)):
        bias_sums[0, k : k + 1, :] = value[0:1]
    bias_sums[0, 4:8, :] = jnp.zeros((4, LANES), f32)


def outer(left, right):
    return lax.dot_general(left, right, (((0,), (0,)), ((), ())), preferred_element_type=f32)


def weight_kernel(
    win_one, win_two, win_level, win_coarse, tile_out, tile_level, tile_mid, coarse_pairs,
    g_one, g_two, g_down, g_up,
    sum_one, sum_two, sum_down, sum_up,
):
    step = pl.program_id(0)

    @pl.when(step == 0)
    def _():
        for ref in (sum_one, sum_two, sum_down, sum_up):
            ref[...] = jnp.zeros_like(ref)

    def blocks(tiles):
        return jnp.concatenate([tiles[0, a].reshape(BLOCK, LANES) for a in range(2)], axis=1)

    level_operand = window_operand(win_level.at[0], range(4))
    out_blocks = blocks(tile_out)
    sum_up[16 * C :, :] += outer(window_operand(win_coarse.at[0], (0, 1, 1, 2)), out_blocks)
    sum_up[: 16 * C, :] += outer(level_operand, out_blocks)
    sum_down[...] += outer(level_operand[:, : 6 * LANES], coarse_pairs[0].reshape(BLOCK, LANES))
    sum_two[...] += outer(window_operand(win_two.at[0], range(4)), blocks(tile_level))
    sum_one[...] += outer(window_operand(win_one.at[0], range(4)), blocks(tile_mid))

    @pl.when(step == pl.num_programs(0) - 1)
    def _():
        def fold(sums, base, p, q):
            halves = []
            for b in range(2):
                rows = [base + ((a + p) * 4 + b + q) * C for a in range(2)]
                halves.append(sums[rows[0] : rows[0] + C, :LANES] + sums[rows[1] : rows[1] + C, LANES:])
            return halves[0] + swap_halves(halves[1])

        for p in range(3):
            for q in range(3):
                at = (3 * p + q) * C
                g_one[at : at + C, :] = fold(sum_one, 0, p, q)[:, :C]
                g_two[at : at + C, :] = fold(sum_two, 0, p, q)[:, :C]
                g_up[2 * at : 2 * at + C, :] = fold(sum_up, 16 * C, p, q)[:, :C]
                g_up[2 * at + C : 2 * at + 2 * C, :] = fold(sum_up, 0, p, q)[:, :C]
                place = (p * 4 + q) * C
                g_down[at : at + C, :] = sum_down[place : place + C, :C]


def expand_kernel(conv_one, conv_two, down_kernel, up_kernel, f_one, f_two, f_down, f_up, b_one, b_two, b_down, b_up):
    low_lanes = lane_ids((C, LANES)) < C
    zero = jnp.zeros((C, LANES), f32)

    def taps(ref, base, step):
        plain, turned = {}, {}
        for p in range(3):
            for q in range(3):
                at = (3 * p + q) * step + base
                k = ref[at : at + C, :].astype(f32)
                plain[p, q] = jnp.concatenate([k, k], axis=1)
                turned[p, q] = jnp.concatenate([k, k], axis=0).T
        return plain, turned

    def write_forward(ref, base, plain):
        for w in range(4):
            for p in range(3):
                tile = jnp.where(low_lanes, plain.get((p, w), zero), plain.get((p, w - 1), zero)).astype(bf16)
                for a in range(2):
                    at = base + ((a + p) * 4 + w) * C
                    ref[at : at + C, a * LANES : (a + 1) * LANES] = tile
            for a in range(2):
                for r in range(4):
                    if not 0 <= r - a < 3:
                        at = base + (r * 4 + w) * C
                        ref[at : at + C, a * LANES : (a + 1) * LANES] = zero.astype(bf16)

    def write_backward(ref, lane, turned):
        for w in range(4):
            for p in range(3):
                tile = jnp.where(low_lanes, turned.get((p, 2 - w), zero), turned.get((p, 3 - w), zero)).astype(bf16)
                for a in range(2):
                    at = ((a + 2 - p) * 4 + w) * C
                    ref[at : at + C, lane + a * LANES : lane + (a + 1) * LANES] = tile
            for a in range(2):
                for r in range(4):
                    if not 0 <= a + 2 - r < 3:
                        at = (r * 4 + w) * C
                        ref[at : at + C, lane + a * LANES : lane + (a + 1) * LANES] = zero.astype(bf16)

    for ref, forward, backward in ((conv_one, f_one, b_one), (conv_two, f_two, b_two)):
        plain, turned = taps(ref, 0, C)
        write_forward(forward, 0, plain)
        write_backward(backward, 0, turned)
    plain, turned = taps(up_kernel, 0, 2 * C)
    write_forward(f_up, 16 * C, plain)
    write_backward(b_up, 0, turned)
    plain, turned = taps(up_kernel, C, 2 * C)
    write_forward(f_up, 0, plain)
    write_backward(b_up, 2 * LANES, turned)
    plain, turned = taps(down_kernel, 0, C)
    for p in range(3):
        for w in range(4):
            at = (p * 4 + w) * C
            f_down[at : at + C, :] = plain.get((p, w), zero).astype(bf16)
    for below in range(2):
        for right in range(2):
            at = (below * 2 + right) * C
            for a in range(2):
                p = {(0, 0): 1, (0, 1): 2, (1, 1): 0}.get((below, a))
                first, second = zero, zero
                if p is not None:
                    first = turned[p, 1] if right == 0 else zero
                    second = turned[p, 2] if right == 0 else turned[p, 0]
                b_down[at : at + C, a * LANES : (a + 1) * LANES] = jnp.where(low_lanes, first, second).astype(bf16)


def shape(dims, kind):
    return jax.ShapeDtypeStruct(dims, kind)


def whole(dims):
    return pl.BlockSpec(dims, lambda f: (0,) * len(dims))


def per_frame(dims):
    return pl.BlockSpec((1,) + dims, lambda f: (f,) + (0,) * len(dims))


def strip_specs(count, strip):
    return [pl.BlockSpec((1, strip, W * C), lambda f: (f, 0, 0))] * count


def out_strips(count, strip):
    return pl.BlockSpec((count, 1, strip, W * C), lambda f: (0, f, 0, 0))


SMALL = (8, LANES)
WINDOWS = (4, PAIRS + 1, HALF, LANES)
COARSE_WINDOWS = (3, PAIRS + 1, HALF, LANES)
TILES = (2, PAIRS, HALF, LANES)
COARSE = (PAIRS, HALF, LANES)
IMAGE = (PAIRS, H, LANES)
KEYS = 16 * C


def params():
    return pltpu.CompilerParams(vmem_limit_bytes=VMEM_LIMIT)


def expand(conv_one, conv_two, down_kernel, up_kernel):
    vmem = pl.BlockSpec(memory_space=pltpu.VMEM)
    return pl.pallas_call(
        expand_kernel,
        in_specs=[vmem] * 4,
        out_specs=[vmem] * 8,
        out_shape=[
            shape((KEYS, 2 * LANES), bf16),
            shape((KEYS, 2 * LANES), bf16),
            shape((6 * LANES, LANES), bf16),
            shape((2 * KEYS, 2 * LANES), bf16),
            shape((KEYS, 2 * LANES), bf16),
            shape((KEYS, 2 * LANES), bf16),
            shape((2 * LANES, 2 * LANES), bf16),
            shape((KEYS, 4 * LANES), bf16),
        ],
        compiler_params=params(),
        name="expand",
    )(conv_one, conv_two, down_kernel, up_kernel)


def forward(member, strips, styles, biases, w_one, w_two, w_down, w_up):
    count = len(strips)
    frames, strip, _ = strips[0].shape
    return pl.pallas_call(
        lambda *refs: forward_kernel(count, *refs),
        grid=(frames,),
        in_specs=[pl.BlockSpec(memory_space=pltpu.SMEM)]
        + strip_specs(count, strip)
        + [per_frame(SMALL), whole(SMALL)]
        + [whole(w.shape) for w in (w_one, w_two, w_down, w_up)],
        out_specs=[out_strips(count, strip)]
        + [per_frame(d) for d in (WINDOWS, WINDOWS, WINDOWS, COARSE_WINDOWS, TILES, COARSE, SMALL)],
        out_shape=[
            shape((count, frames, strip, W * C), bf16),
            shape((frames,) + WINDOWS, bf16),
            shape((frames,) + WINDOWS, bf16),
            shape((frames,) + WINDOWS, bf16),
            shape((frames,) + COARSE_WINDOWS, bf16),
            shape((frames,) + TILES, f32),
            shape((frames,) + COARSE, f32),
            shape((frames,) + SMALL, f32),
        ],
        scratch_shapes=[pltpu.VMEM(IMAGE, f32), pltpu.VMEM(TILES, f32)],
        compiler_params=params(),
        name="forward",
    )(member, *strips, styles, biases, w_one, w_two, w_down, w_up)


def backward(member, cot_strips, frame_strips, styles, stats, middle, down, w_up, w_down, w_two, w_one):
    count = len(cot_strips)
    frames, strip, _ = cot_strips[0].shape
    return pl.pallas_call(
        lambda *refs: backward_kernel(count, *refs),
        grid=(frames,),
        in_specs=[pl.BlockSpec(memory_space=pltpu.SMEM)]
        + strip_specs(2 * count, strip)
        + [per_frame(d) for d in (SMALL, SMALL, TILES, COARSE)]
        + [whole(w.shape) for w in (w_up, w_down, w_two, w_one)],
        out_specs=[out_strips(count, strip)]
        + [per_frame(d) for d in (TILES, TILES, TILES, COARSE, SMALL, SMALL)],
        out_shape=[
            shape((count, frames, strip, W * C), bf16),
            shape((frames,) + TILES, bf16),
            shape((frames,) + TILES, bf16),
            shape((frames,) + TILES, bf16),
            shape((frames,) + COARSE, bf16),
            shape((frames,) + SMALL, f32),
            shape((frames,) + SMALL, f32),
        ],
        scratch_shapes=[
            pltpu.VMEM(IMAGE, f32),
            pltpu.VMEM(TILES, f32),
            pltpu.VMEM(TILES, f32),
            pltpu.VMEM(WINDOWS, bf16),
            pltpu.VMEM(COARSE, bf16),
            pltpu.VMEM((HALF, LANES), f32),
        ],
        compiler_params=params(),
        name="backward",
    )(member, *cot_strips, *frame_strips, styles, stats, middle, down, w_up, w_down, w_two, w_one)


def weight_grads(win_one, win_two, win_level, win_coarse, tile_out, tile_level, tile_mid, coarse_pairs):
    frames = win_one.shape[0]
    return pl.pallas_call(
        weight_kernel,
        grid=(frames,),
        in_specs=[
            per_frame(d) for d in (WINDOWS, WINDOWS, WINDOWS, COARSE_WINDOWS, TILES, TILES, TILES, COARSE)
        ],
        out_specs=[whole((9 * C, C)), whole((9 * C, C)), whole((9 * C, C)), whole((18 * C, C))],
        out_shape=[shape((9 * C, C), f32)] * 3 + [shape((18 * C, C), f32)],
        scratch_shapes=[
            pltpu.VMEM((KEYS, 2 * LANES), f32),
            pltpu.VMEM((KEYS, 2 * LANES), f32),
            pltpu.VMEM((6 * LANES, LANES), f32),
            pltpu.VMEM((2 * KEYS, 2 * LANES), f32),
        ],
        compiler_params=params(),
        name="weights",
    )(win_one, win_two, win_level, win_coarse, tile_out, tile_level, tile_mid, coarse_pairs)


def twice(values):
    return jnp.concatenate([values, values], axis=-1)


def pad_small(rows):
    stacked = jnp.stack(rows, axis=-2)
    gaps = [(0, 0)] * (stacked.ndim - 2) + [(0, 8 - len(rows)), (0, 0)]
    return jnp.pad(stacked, gaps)


def trade(value, offset):
    if offset == 0:
        return value
    count = lax.axis_size("rows")
    return lax.ppermute(value, "rows", [(i, i ^ offset) for i in range(count)])


def spread_strips(array, member):
    count = lax.axis_size("rows")
    share = array.shape[0] // count
    return [
        trade(lax.dynamic_slice_in_dim(array, (member ^ offset) * share, share, axis=0), offset)
        for offset in range(count)
    ]


def collect_strips(strips, member, kind):
    count, share = strips.shape[:2]
    result = jnp.zeros((count * share,) + strips.shape[2:], kind)
    for offset in range(count):
        part = trade(strips[offset], offset).astype(kind)
        result = lax.dynamic_update_slice_in_dim(result, part, (member ^ offset) * share, axis=0)
    return result


def local(
    frames,
    cotangent,
    actions,
    noise_ids,
    valid,
    act_table,
    noise_table,
    ada_one,
    ada_two,
    conv_one,
    conv_two,
    down_kernel,
    up_kernel,
    bias_one,
    bias_two,
    bias_down,
    bias_up,
):
    member = lax.axis_index("rows")
    count = lax.axis_size("rows")
    share = frames.shape[0] // count
    member_box = member.astype(jnp.int32).reshape(1)

    def gathered(value, axis):
        return lax.all_gather(value, "seq", axis=axis, tiled=True)

    frame_strips = spread_strips(frames, member)
    cot_strips = spread_strips(cotangent, member)
    act_full = gathered(act_table, 1)
    noise_full = gathered(noise_table, 1)
    ada_full = gathered(jnp.concatenate([ada_one, ada_two], axis=1), 0).astype(f32)
    biases = gathered(jnp.stack([bias_one, bias_two, bias_down, bias_up]), 1).astype(f32)
    expanded = expand(gathered(conv_one, 0), gathered(conv_two, 0), gathered(down_kernel, 0), gathered(up_kernel, 0))
    f_one, f_two, f_down, f_up, b_one, b_two, b_down, b_up = expanded

    own = lambda ids: lax.dynamic_slice_in_dim(ids, member * share, share)
    own_actions, own_noise, own_valid = own(actions), own(noise_ids), own(valid)
    action_hot = (own_actions[:, None] == jnp.arange(NACT, dtype=jnp.int32)[None, :]).astype(f32) * own_valid[
        :, None
    ].astype(f32)
    noise_hot = (own_noise[:, None] == jnp.arange(NLEV, dtype=jnp.int32)[None, :]).astype(f32)
    embed = jnp.dot(action_hot, act_full.astype(f32), precision=precise) + jnp.dot(
        noise_hot, noise_full.astype(f32), precision=precise
    )
    style = jnp.dot(embed, ada_full, precision=precise)
    styles = pad_small(
        [
            twice(1.0 + style[:, :C]),
            twice(style[:, C : 2 * C]),
            twice(1.0 + style[:, 2 * C : 3 * C]),
            twice(style[:, 3 * C :]),
        ]
    )
    bias_rows = pad_small([twice(biases[k]) for k in range(4)])

    out, win_one, win_two, win_level, win_coarse, middle, down, stats = forward(
        member_box, frame_strips, styles, bias_rows, f_one, f_two, f_down, f_up
    )
    result = collect_strips(out, member, bf16)
    grad_strips, tile_out, tile_level, tile_mid, coarse_pairs, pieces, bias_sums = backward(
        member_box, cot_strips, frame_strips, styles, stats, middle, down, b_up, b_down, b_two, b_one
    )
    frames_grad = collect_strips(grad_strips, member, f32)
    g_one, g_two, g_down, g_up = weight_grads(
        win_one, win_two, win_level, win_coarse, tile_out, tile_level, tile_mid, coarse_pairs
    )

    pieces_one = jnp.concatenate([pieces[:, 0, :C], pieces[:, 1, :C]], axis=1)
    pieces_two = jnp.concatenate([pieces[:, 2, :C], pieces[:, 3, :C]], axis=1)
    ada_one_grad = jnp.dot(embed.T, pieces_one, precision=precise)
    ada_two_grad = jnp.dot(embed.T, pieces_two, precision=precise)
    embed_grad = jnp.dot(jnp.concatenate([pieces_one, pieces_two], axis=1), ada_full.T, precision=precise)
    act_table_grad = jnp.dot(action_hot.T, embed_grad, precision=precise)
    noise_table_grad = jnp.dot(noise_hot.T, embed_grad, precision=precise)
    bias_total = jnp.sum(bias_sums, axis=0)[:4, :C]

    def shard(value, axis):
        return lax.psum_scatter(value, "seq", scatter_dimension=axis, tiled=True)

    shards = (
        shard(act_table_grad, 1),
        shard(noise_table_grad, 1),
        shard(ada_one_grad, 0),
        shard(ada_two_grad, 0),
        shard(g_one, 0),
        shard(g_two, 0),
        shard(g_down, 0),
        shard(g_up, 0),
        shard(bias_total[0], 0),
        shard(bias_total[1], 0),
        shard(bias_total[2], 0),
        shard(bias_total[3], 0),
    )
    return (result, frames_grad) + lax.psum(shards, "rows")


def solution(mesh):
    in_specs = (
        P("seq", "rows", None),
        P("seq", "rows", None),
        P("seq"),
        P("seq"),
        P("seq"),
        P(None, "seq"),
        P(None, "seq"),
        P("seq", None),
        P("seq", None),
        P("seq", None),
        P("seq", None),
        P("seq", None),
        P("seq", None),
        P("seq"),
        P("seq"),
        P("seq"),
        P("seq"),
    )
    out_specs = (
        P("seq", "rows", None),
        P("seq", "rows", None),
        P(None, "seq"),
        P(None, "seq"),
        P("seq", None),
        P("seq", None),
        P("seq", None),
        P("seq", None),
        P("seq", None),
        P("seq", None),
        P("seq"),
        P("seq"),
        P("seq"),
        P("seq"),
    )
    return jax.shard_map(local, mesh=mesh, in_specs=in_specs, out_specs=out_specs, check_vma=False)
```

profile of v0, /device:TPU:0, one launch (start us, length us, event | category | flops | bytes accessed | tf_op | source)
XLA Modules:
  0.0 861.4 jit_solution(15938323746184363547)
XLA Ops:
  7.4 2.2 constant_dynamic-slice_fusion.4
  10.0 2.6 collective-permute-start.1
  12.7 0.8 constant_dynamic-slice_fusion
  13.6 1.9 collective-permute-start.7
  15.7 30.8 %all_gather.25 = bf16[32,256]{0,1:T(8,128)(2,1)S(1)} all-gather(bf16[32,32]{0,1:T(8,128)(2,1)S(1)} %copy.64), channel_id=1, replica_groups=mesh['seq'=8,'rows'=4] {'seq'}, dimensions={1}, use_global_device_ids=true | all-gather | bytes 18432 | tf_op jit(solution)/shard_map/all_gather | solution.py:656
  46.7 30.7 %all-gather = bf16[8,32,18]{1,2,0:T(8,128)(2,1)S(1)} all-gather(bf16[1,32,18]{1,2,0:T(8,128)(2,1)S(1)} %bitcast.111), channel_id=1, replica_groups=mesh['seq'=8,'rows'=4] {'seq'}, dimensions={0}, use_global_device_ids=true | all-gather | bytes 10368 | tf_op jit(solution)/shard_map/all_gather | solution.py:656
  77.5 30.5 %all_gather.26 = bf16[256,256]{1,0:T(8,128)(2,1)S(1)} all-gather(bf16[32,256]{1,0:T(8,128)(2,1)S(1)} %pad_maximum_fusion), channel_id=1, replica_groups=mesh['seq'=8,'rows'=4] {'seq'}, dimensions={0}, use_global_device_ids=true | all-gather | bytes 147456 | tf_op jit(solution)/shard_map/all_gather | solution.py:656
  108.7 20.4 %all-gather.1 = bf16[8,8,4]{1,2,0:T(4,128)(2,1)S(1)} all-gather(bf16[1,8,4]{1,2,0:T(4,128)(2,1)S(1)} %maximum_bitcast_fusion), channel_id=1, replica_groups=mesh['seq'=8,'rows'=4] {'seq'}, dimensions={0}, use_global_device_ids=true | all-gather | bytes 576 | tf_op jit(solution)/shard_map/all_gather | solution.py:656
  129.3 30.7 %all-gather.5 = bf16[8,144,64]{1,2,0:T(8,128)(2,1)S(1)} all-gather(bf16[1,144,64]{1,2,0:T(8,128)(2,1)S(1)} %bitcast.96), channel_id=1, replica_groups=mesh['seq'=8,'rows'=4] {'seq'}, dimensions={0}, use_global_device_ids=true | all-gather | bytes 165888 | tf_op jit(solution)/shard_map/all_gather | solution.py:656
  160.0 30.5 %all-gather.2 = bf16[8,72,64]{1,2,0:T(8,128)(2,1)S(1)} all-gather(bf16[1,72,64]{1,2,0:T(8,128)(2,1)S(1)} %bitcast.97), channel_id=1, replica_groups=mesh['seq'=8,'rows'=4] {'seq'}, dimensions={0}, use_global_device_ids=true | all-gather | bytes 82944 | tf_op jit(solution)/shard_map/all_gather | solution.py:656
  190.8 30.6 %all-gather.3 = bf16[8,72,64]{1,2,0:T(8,128)(2,1)S(1)} all-gather(bf16[1,72,64]{1,2,0:T(8,128)(2,1)S(1)} %bitcast.98), channel_id=1, replica_groups=mesh['seq'=8,'rows'=4] {'seq'}, dimensions={0}, use_global_device_ids=true | all-gather | bytes 82944 | tf_op jit(solution)/shard_map/all_gather | solution.py:656
  221.4 0.9 copy.70
  222.2 0.8 copy.67
  223.0 0.8 copy.68
  223.8 30.5 %all-gather.4 = bf16[8,72,64]{1,2,0:T(8,128)(2,1)S(1)} all-gather(bf16[1,72,64]{1,2,0:T(8,128)(2,1)S(1)} %bitcast.99), channel_id=1, replica_groups=mesh['seq'=8,'rows'=4] {'seq'}, dimensions={0}, use_global_device_ids=true | all-gather | bytes 82944 | tf_op jit(solution)/shard_map/all_gather | solution.py:656
  254.3 0.8 copy.69
  255.1 4.0 expand.1
  259.1 0.6 select_maximum_fusion.3.refs_6_
  259.7 0.6 select_maximum_fusion.refs_5_.refs_9_
  260.3 0.7 copy-done.7
  261.1 22.2 %forward.1 = (bf16[4,2,16,4096]{3,2,1,0:T(8,128)(2,1)}, bf16[2,4,33,32,128]{4,3,2,1,0:T(8,128)(2,1)}, bf16[2,4,33,32,128]{4,3,2,1,0:T(8,128)(2,1)}, bf16[2,4,33,...) custom-call(s32[1]{0:T(128)} %bitcast.refs_0_, ...), custom_call_target="tpu_custom_call" | custom-call | tf_op jit(solution)/shard_map/forward/pallas_call | solution.py:516
  283.4 0.7 copy-done.9
  284.1 21.5 %backward.1 = (bf16[4,2,16,4096]{3,2,1,0:T(8,128)(2,1)}, bf16[2,2,32,32,128]{4,3,2,1,0:T(8,128)(2,1)}, bf16[2,2,32,32,128]{4,3,2,1,0:T(8,128)(2,1)}, bf16[2,2,32...) custom-call(s32[1]{0:T(128)} %bitcast.refs_0_, ...), custom_call_target="tpu_custom_call" | custom-call | tf_op jit(solution)/shard_map/backward/pallas_call | solution.py:544
  305.6 0.9 fusion.30
  306.7 1.1 convolution_bitcast_fusion
  307.9 1.0 convolution_bitcast_fusion.1
  309.0 1.1 fusion.12
  311.5 1.1 fusion.8
  312.7 2.0 slice_bitcast_fusion
  314.6 10.1 %weights.1 = (f32[576,64]{1,0:T(8,128)}, f32[576,64]{1,0:T(8,128)}, f32[576,64]{1,0:T(8,128)}, f32[1152,64]{1,0:T(8,128)}) custom-call(bf16[2,4,33,32,128]{4,3,2,1,0:T(8,128)(2,1)} %get-tuple-element.55.win_one, bf16[2,4,33,32,128]{4,3,2,1,0:T(8,128)(2,1)} %get-tuple-element.56.win_two, bf16[2,4,33,32,128]{4,3,2,1,0:T(8,128)(2,1)} %get-tuple-element.57.win_level, ...), custom_call_target="tpu_custom_call" | custom-call | tf_op jit(solution)/shard_map/weights/pallas_call | solution.py:577
  325.0 1.0 convert_dynamic-update-slice_fusion
  326.1 17.2 %all-reduce.9 = (f32[64]{0:T(128)S(1)}, f32[64]{0:T(128)S(1)}, f32[64]{0:T(128)S(1)}, f32[64]{0:T(128)S(1)}) all-reduce(f32[64]{0:T(128)S(1)} %get-tuple-element.161, f32[64]{0:T(128)S(1)} %get-tuple-element.160, f32[64]{0:T(128)S(1)} %get-tuple-element.159, ...), channel_id=10, replica_groups=mesh['seq'=8,'rows'=4] {'seq'}, use_global_device_ids=true, to_apply=%region_17.18.clone | all-reduce | flops 256 | bytes 2048
  343.3 0.6 dynamic-slice.11
  346.2 1.3 collective-permute-start.11
  347.6 0.9 slice_bitcast_fusion.3
  349.0 1.0 copy-done.3
  350.6 14.6 %reduce-scatter.25.cloned.1.call-done = f32[32,18]{1,0:T(8,128)} async-done(((f32[256,18]{1,0:T(8,128)}), f32[32,18]{1,0:T(8,128)}) %reduce-scatter.25.cloned.1.call-update) | async-done | bytes 2320
  365.2 1.4 copy.76
  366.6 61.9 %reduce-scatter.27.cloned.1.call-done = f32[32,32]{1,0:T(8,128)} async-done(((f32[256,32]{1,0:T(8,128)}), f32[32,32]{1,0:T(8,128)}) %reduce-scatter.27.cloned.1.call-update) | async-done | bytes 4112
  428.4 1.4 copy.78
  429.8 1.0 convert_dynamic-update-slice_fusion.3
  430.8 1.0 convert_dynamic-update-slice_fusion.2
  431.8 1.0 convert_dynamic-update-slice_fusion.1
  432.9 1.2 constant_dynamic-update-slice_fusion.2
  434.1 1.0 constant_dynamic-update-slice_fusion.1
  435.0 56.6 %reduce-scatter.21.cloned.1.call-done = f32[32,128]{1,0:T(8,128)} async-done(((f32[256,128]{1,0:T(8,128)}), f32[32,128]{1,0:T(8,128)}) %reduce-scatter.21.cloned.1.call-update) | async-done | bytes 16400 | tf_op jit(solution)/shard_map/reduce_scatter | solution.py:709
  491.7 63.1 %reduce-scatter.19.cloned.1.call-done = f32[32,128]{1,0:T(8,128)} async-done(((f32[256,128]{1,0:T(8,128)}), f32[32,128]{1,0:T(8,128)}) %reduce-scatter.19.cloned.1.call-update) | async-done | bytes 16400 | tf_op jit(solution)/shard_map/reduce_scatter | solution.py:709
  554.8 61.0 %reduce-scatter.29.cloned.1.call-done = f32[72,64]{1,0:T(8,128)} async-done(((f32[576,64]{1,0:T(8,128)}), f32[72,64]{1,0:T(8,128)}) %reduce-scatter.29.cloned.1.call-update) | async-done | bytes 18448
  615.7 60.9 %reduce-scatter.31.cloned.1.call-done = f32[72,64]{1,0:T(8,128)} async-done(((f32[576,64]{1,0:T(8,128)}), f32[72,64]{1,0:T(8,128)}) %reduce-scatter.31.cloned.1.call-update) | async-done | bytes 18448
  676.6 61.0 %reduce-scatter.33.cloned.1.call-done = f32[72,64]{1,0:T(8,128)} async-done(((f32[576,64]{1,0:T(8,128)}), f32[72,64]{1,0:T(8,128)}) %reduce-scatter.33.cloned.1.call-update) | async-done | bytes 18448
  737.6 64.5 %reduce-scatter.23.cloned.1.call-done = f32[144,64]{1,0:T(8,128)} async-done(((f32[1152,64]{1,0:T(8,128)}), f32[144,64]{1,0:T(8,128)}) %reduce-scatter.23.cloned.1.call-update) | async-done | bytes 36880 | tf_op jit(solution)/shard_map/reduce_scatter | solution.py:709
  802.1 36.9 %all-reduce.13.cloned.1.call-done = (f32[18,32]{1,0:T(8,128)}, f32[32,32]{1,0:T(8,128)}, f32[32,128]{1,0:T(8,128)}, f32[32,128]{1,0:T(8,128)}, f32[72,64]{1,0:T(...) async-done(((f32[18,32]{1,0:T(8,128)}, f32[32,32]{1,0:T(8,128)}, ...) | async-done | bytes 131472 | tf_op jit(solution)/shard_map/psum | solution.py:725
  839.0 1.6 copy.74
  840.6 1.5 copy.71
  842.0 1.5 copy.72
  843.5 1.5 copy.73
  845.0 1.3 copy.100
  846.3 1.3 copy.101
  847.6 1.3 copy.102
  848.9 1.3 copy.103
  850.3 1.1 copy.104
  851.4 1.2 copy.105
  852.6 1.2 copy.106
  853.7 1.1 copy.107
  (122 shorter events, 7.5 us)
Async XLA Ops:
  7.2 5.5 copy-start.1
  7.2 358.0 %reduce-scatter.25.cloned.1.call-start = ((), (), s32[]{:S(2)}) async-start(), calls=%async_computation.11 | async-start | bytes 147456
  7.3 8.2 copy-start.24
  7.3 8.3 copy-start.15
  7.3 39.2 %copy-start.25 = (s32[8]{0:T(128)S(1)}, s32[8]{0:T(128)}, u32[]{:S(2)}) copy-start(s32[8]{0:T(128)} %param.21) | copy-start | bytes 100
  7.3 39.3 %copy-start.26 = (s32[8]{0:T(128)S(1)}, s32[8]{0:T(128)}, u32[]{:S(2)}) copy-start(s32[8]{0:T(128)} %param.19) | copy-start | bytes 100
  7.3 39.4 %copy-start.19 = (bf16[18,32]{1,0:T(8,128)(2,1)S(1)}, bf16[18,32]{1,0:T(8,128)(2,1)}, u32[]{:S(2)}) copy-start(bf16[18,32]{1,0:T(8,128)(2,1)} %param.22) | copy-start | bytes 3460
  7.3 70.1 %copy-start.17 = (bf16[32,128]{1,0:T(8,128)(2,1)S(1)}, bf16[32,128]{1,0:T(8,128)(2,1)}, u32[]{:S(2)}) copy-start(bf16[32,128]{1,0:T(8,128)(2,1)} %param.25) | copy-start | bytes 24580
  7.3 70.1 %copy-start.18 = (bf16[32,128]{1,0:T(8,128)(2,1)S(1)}, bf16[32,128]{1,0:T(8,128)(2,1)}, u32[]{:S(2)}) copy-start(bf16[32,128]{1,0:T(8,128)(2,1)} %param.24) | copy-start | bytes 24580
  7.3 101.3 %copy-start.20 = (bf16[8]{0:T(256)(128)(2,1)S(1)}, bf16[8]{0:T(256)(128)(2,1)}, u32[]{:S(2)}) copy-start(bf16[8]{0:T(256)(128)(2,1)} %param.33) | copy-start | bytes 52
  7.3 101.3 %copy-start.21 = (bf16[8]{0:T(256)(128)(2,1)S(1)}, bf16[8]{0:T(256)(128)(2,1)}, u32[]{:S(2)}) copy-start(bf16[8]{0:T(256)(128)(2,1)} %param.32) | copy-start | bytes 52
  7.4 101.3 %copy-start.22 = (bf16[8]{0:T(256)(128)(2,1)S(1)}, bf16[8]{0:T(256)(128)(2,1)}, u32[]{:S(2)}) copy-start(bf16[8]{0:T(256)(128)(2,1)} %param.31) | copy-start | bytes 52
  7.4 101.3 %copy-start.23 = (bf16[8]{0:T(256)(128)(2,1)S(1)}, bf16[8]{0:T(256)(128)(2,1)}, u32[]{:S(2)}) copy-start(bf16[8]{0:T(256)(128)(2,1)} %param.30) | copy-start | bytes 52
  7.4 121.9 %copy-start.11 = (bf16[144,64]{0,1:T(8,128)(2,1)S(1)}, bf16[144,64]{0,1:T(8,128)(2,1)}, u32[]{:S(2)}) copy-start(bf16[144,64]{0,1:T(8,128)(2,1)} %param.29) | copy-start | bytes 55300
  9.5 150.5 %copy-start.12 = (bf16[72,64]{0,1:T(8,128)(2,1)S(1)}, bf16[72,64]{0,1:T(8,128)(2,1)}, u32[]{:S(2)}) copy-start(bf16[72,64]{0,1:T(8,128)(2,1)} %param.26) | copy-start | bytes 27652
  9.5 181.2 %copy-start.13 = (bf16[72,64]{0,1:T(8,128)(2,1)S(1)}, bf16[72,64]{0,1:T(8,128)(2,1)}, u32[]{:S(2)}) copy-start(bf16[72,64]{0,1:T(8,128)(2,1)} %param.27) | copy-start | bytes 27652
  9.5 181.2 %collective-permute-start = (bf16[2,16,4096]{2,1,0:T(8,128)(2,1)}, bf16[2,16,4096]{2,1,0:T(8,128)(2,1)S(1)}, u32[]{:S(2)}, u32[]{:S(2)}) collective-permute-start(bf16[2,16,4096]{2,1,0:T(8,128)(2,1)} %get-tuple-element.151), channel_id=1, source_target_pairs={{0,1},{1,0},{2,3},{3,2},{4,5},{5,4},{6,7},{7,6},{8,9},{9,8},{10,11... | collective-permute-start | bytes 786440 | tf_op jit(solution)/shard_map/ppermute | solution.py:610
  10.0 250.3 %collective-permute-start.1 = (bf16[2,16,4096]{2,1,0:T(8,128)(2,1)S(1)}, bf16[2,16,4096]{2,1,0:T(8,128)(2,1)S(1)}, u32[]{:S(2)}, u32[]{:S(2)}) collective-permute-start(bf16[2,16,4096]{2,1,0:T(8,128)(2,1)S(1)} %get-tuple-element.153), channel_id=1, source_target_pairs={{0,2},{1,3},{2,0},{3,1},{4,6},{5,7},{6,4},{7,5},{8,10},{9,11},{10,... | collective-permute-start | bytes 786440 | tf_op jit(solution)/shard_map/ppermute | solution.py:610
  12.6 211.2 %copy-start.14 = (bf16[72,64]{0,1:T(8,128)(2,1)S(1)}, bf16[72,64]{0,1:T(8,128)(2,1)}, u32[]{:S(2)}) copy-start(bf16[72,64]{0,1:T(8,128)(2,1)} %param.28) | copy-start | bytes 27652
  12.6 247.7 %collective-permute-start.2 = (bf16[2,16,4096]{2,1,0:T(8,128)(2,1)S(1)}, bf16[2,16,4096]{2,1,0:T(8,128)(2,1)S(1)}, u32[]{:S(2)}, u32[]{:S(2)}) collective-permute-start(bf16[2,16,4096]{2,1,0:T(8,128)(2,1)S(1)} %get-tuple-element.150), channel_id=1, source_target_pairs={{0,3},{1,2},{2,1},{3,0},{4,7},{5,6},{6,5},{7,4},{8,11},{9,10},{10,... | collective-permute-start | bytes 786440 | tf_op jit(solution)/shard_map/ppermute | solution.py:610
  13.4 269.9 %collective-permute-start.6 = (bf16[2,16,4096]{2,1,0:T(8,128)(2,1)S(1)}, bf16[2,16,4096]{2,1,0:T(8,128)(2,1)S(1)}, u32[]{:S(2)}, u32[]{:S(2)}) collective-permute-start(bf16[2,16,4096]{2,1,0:T(8,128)(2,1)S(1)} %get-tuple-element.144), channel_id=1, source_target_pairs={{0,1},{1,0},{2,3},{3,2},{4,5},{5,4},{6,7},{7,6},{8,9},{9,8},{10,11... | collective-permute-start | bytes 786440 | tf_op jit(solution)/shard_map/ppermute | solution.py:610
  13.6 269.7 %collective-permute-start.7 = (bf16[2,16,4096]{2,1,0:T(8,128)(2,1)S(1)}, bf16[2,16,4096]{2,1,0:T(8,128)(2,1)S(1)}, u32[]{:S(2)}, u32[]{:S(2)}) collective-permute-start(bf16[2,16,4096]{2,1,0:T(8,128)(2,1)S(1)} %get-tuple-element.146), channel_id=1, source_target_pairs={{0,2},{1,3},{2,0},{3,1},{4,6},{5,7},{6,4},{7,5},{8,10},{9,11},{10,... | collective-permute-start | bytes 786440 | tf_op jit(solution)/shard_map/ppermute | solution.py:610
  190.7 69.6 %copy-start.6 = (bf16[2,16,4096]{2,1,0:T(8,128)(2,1)}, bf16[2,16,4096]{2,1,0:T(8,128)(2,1)S(1)}, u32[]{:S(2)}) copy-start(bf16[2,16,4096]{2,1,0:T(8,128)(2,1)S(1)} %collective-permute-done.refs_2_.refs_6_) | copy-start | bytes 786436
  190.7 92.6 %collective-permute-start.8 = (bf16[2,16,4096]{2,1,0:T(8,128)(2,1)S(1)}, bf16[2,16,4096]{2,1,0:T(8,128)(2,1)}, u32[]{:S(2)}, u32[]{:S(2)}) collective-permute-start(bf16[2,16,4096]{2,1,0:T(8,128)(2,1)S(1)} %get-tuple-element.143), channel_id=1, source_target_pairs={{0,3},{1,2},{2,1},{3,0},{4,7},{5,6},{6,5},{7,4},{8,11},{9,10},{10,... | collective-permute-start | bytes 786440 | tf_op jit(solution)/shard_map/ppermute | solution.py:610
  260.3 0.7 copy-start.7
  260.3 0.8 copy-start.8
  283.3 0.7 copy-start.9
  283.3 0.8 copy-start.10
  284.1 26.2 %copy-start.27 = (u32[32]{0:T(128)S(1)}, u32[32]{0:T(128)}, u32[]{:S(2)}) copy-start(u32[32]{0:T(128)} %constant.29) | copy-start | bytes 388
  307.9 120.6 %reduce-scatter.27.cloned.1.call-start = ((), (), s32[]{:S(2)}) async-start(), calls=%async_computation.12 | async-start | bytes 147456
  308.9 182.8 %reduce-scatter.21.cloned.1.call-start = ((), (), s32[]{:S(2)}) async-start(), calls=%async_computation.9 | async-start | bytes 147456 | tf_op jit(solution)/shard_map/reduce_scatter | solution.py:709
  310.1 244.7 %reduce-scatter.19.cloned.1.call-start = ((), (), s32[]{:S(2)}) async-start(), calls=%async_computation.8 | async-start | bytes 147456 | tf_op jit(solution)/shard_map/reduce_scatter | solution.py:709
  312.6 303.1 %reduce-scatter.29.cloned.1.call-start = ((), (), s32[]{:S(2)}) async-start(), calls=%async_computation.13 | async-start | bytes 331776
  324.8 1.3 copy-start.16
  324.8 22.8 %copy-start.2 = (bf16[4,2,16,4096]{3,2,1,0:T(8,128)(2,1)S(1)}, bf16[4,2,16,4096]{3,2,1,0:T(8,128)(2,1)}, u32[]{:S(2)}) copy-start(bf16[4,2,16,4096]{3,2,1,0:T(8,128)(2,1)} %get-tuple-element.45) | copy-start | bytes 3145732
  324.8 351.8 %reduce-scatter.31.cloned.1.call-start = ((), (), s32[]{:S(2)}) async-start(), calls=%async_computation.14 | async-start | bytes 331776
  345.6 84.2 %collective-permute-start.9 = (bf16[2,16,4096]{2,1,0:T(8,128)(2,1)S(1)}, bf16[2,16,4096]{2,1,0:T(8,128)(2,1)}, u32[]{:S(2)}, u32[]{:S(2)}) collective-permute-start(bf16[2,16,4096]{2,1,0:T(8,128)(2,1)S(1)} %get-tuple-element.142), channel_id=1, source_target_pairs={{0,1},{1,0},{2,3},{3,2},{4,5},{5,4},{6,7},{7,6},{8,9},{9,8},{10,11... | collective-permute-start | bytes 786440 | tf_op jit(solution)/shard_map/ppermute | solution.py:610
  345.6 85.2 %collective-permute-start.10 = (bf16[2,16,4096]{2,1,0:T(8,128)(2,1)}, bf16[2,16,4096]{2,1,0:T(8,128)(2,1)}, u32[]{:S(2)}, u32[]{:S(2)}) collective-permute-start(bf16[2,16,4096]{2,1,0:T(8,128)(2,1)} %get-tuple-element.141), channel_id=1, source_target_pairs={{0,2},{1,3},{2,0},{3,1},{4,6},{5,7},{6,4},{7,5},{8,10},{9,11},{10,... | collective-permute-start | bytes 786440 | tf_op jit(solution)/shard_map/ppermute | solution.py:610
  346.2 85.7 %collective-permute-start.11 = (bf16[2,16,4096]{2,1,0:T(8,128)(2,1)}, bf16[2,16,4096]{2,1,0:T(8,128)(2,1)}, u32[]{:S(2)}, u32[]{:S(2)}) collective-permute-start(bf16[2,16,4096]{2,1,0:T(8,128)(2,1)} %get-tuple-element.140), channel_id=1, source_target_pairs={{0,3},{1,2},{2,1},{3,0},{4,7},{5,6},{6,5},{7,4},{8,11},{9,10},{10,... | collective-permute-start | bytes 786440 | tf_op jit(solution)/shard_map/ppermute | solution.py:610
  347.5 390.1 %reduce-scatter.33.cloned.1.call-start = ((), (), s32[]{:S(2)}) async-start(), calls=%async_computation.15 | async-start | bytes 331776
  348.5 84.4 %collective-permute-start.3 = (bf16[2,16,4096]{2,1,0:T(8,128)(2,1)}, bf16[2,16,4096]{2,1,0:T(8,128)(2,1)}, u32[]{:S(2)}, u32[]{:S(2)}) collective-permute-start(bf16[2,16,4096]{2,1,0:T(8,128)(2,1)} %get-tuple-element.149), channel_id=1, source_target_pairs={{0,1},{1,0},{2,3},{3,2},{4,5},{5,4},{6,7},{7,6},{8,9},{9,8},{10,11... | collective-permute-start | bytes 786440 | tf_op jit(solution)/shard_map/ppermute | solution.py:610
  348.8 453.2 %reduce-scatter.23.cloned.1.call-start = ((), (), s32[]{:S(2)}) async-start(), calls=%async_computation.10 | async-start | bytes 663552 | tf_op jit(solution)/shard_map/reduce_scatter | solution.py:709
  349.0 1.0 copy-start.3
  349.9 82.9 %copy-start.4 = (bf16[8,16,4096]{2,1,0:T(8,128)(2,1)S(1)}, bf16[8,16,4096]{2,1,0:T(8,128)(2,1)}, u32[]{:S(2)}) copy-start(bf16[8,16,4096]{2,1,0:T(8,128)(2,1)} %copy-done.3) | copy-start | bytes 3145732
  349.9 84.1 %collective-permute-start.4 = (bf16[2,16,4096]{2,1,0:T(8,128)(2,1)}, bf16[2,16,4096]{2,1,0:T(8,128)(2,1)}, u32[]{:S(2)}, u32[]{:S(2)}) collective-permute-start(bf16[2,16,4096]{2,1,0:T(8,128)(2,1)} %get-tuple-element.148), channel_id=1, source_target_pairs={{0,2},{1,3},{2,0},{3,1},{4,6},{5,7},{6,4},{7,5},{8,10},{9,11},{10,... | collective-permute-start | bytes 786440 | tf_op jit(solution)/shard_map/ppermute | solution.py:610
  350.5 488.5 %all-reduce.13.cloned.1.call-start = ((), (), s32[]{:S(2)}) async-start(), calls=%async_computation.16 | async-start | bytes 495616 | tf_op jit(solution)/shard_map/psum | solution.py:725
  429.8 372.2 %collective-permute-start.5 = (bf16[2,16,4096]{2,1,0:T(8,128)(2,1)}, bf16[2,16,4096]{2,1,0:T(8,128)(2,1)S(1)}, u32[]{:S(2)}, u32[]{:S(2)}) collective-permute-start(bf16[2,16,4096]{2,1,0:T(8,128)(2,1)} %get-tuple-element.147), channel_id=1, source_target_pairs={{0,3},{1,2},{2,1},{3,0},{4,7},{5,6},{6,5},{7,4},{8,11},{9,10},{10,... | collective-permute-start | bytes 786440 | tf_op jit(solution)/shard_map/ppermute | solution.py:610
  432.8 422.0 %copy-start = (f32[8,16,4096]{2,1,0:T(8,128)}, f32[8,16,4096]{2,1,0:T(8,128)S(1)}, u32[]{:S(2)}) copy-start(f32[8,16,4096]{2,1,0:T(8,128)S(1)} %convert_dynamic-update-slice_fusion.1) | copy-start | bytes 6291460
  802.1 52.8 %copy-start.5 = (bf16[8,16,4096]{2,1,0:T(8,128)(2,1)}, bf16[8,16,4096]{2,1,0:T(8,128)(2,1)S(1)}, u32[]{:S(2)}) copy-start(bf16[8,16,4096]{2,1,0:T(8,128)(2,1)S(1)} %constant_dynamic-update-slice_fusion) | copy-start | bytes 3145732
Sparse Core Ops, SparseCore 0:
  308.0 57.1 reduce-scatter.24
  368.5 59.9 reduce-scatter.26
  431.8 59.8 reduce-scatter.20
  494.8 59.8 reduce-scatter.18
  557.9 57.7 reduce-scatter.28
  618.9 57.6 reduce-scatter.30
  679.9 57.6 reduce-scatter.32
  740.9 61.1 reduce-scatter.22
  806.8 32.1 all-reduce.12
where the time goes:
time: 863 us; the launch traced here: 861 us
  waiting for transfers between devices  481 us (56%)
  blocking collectives  252 us (29%)
  Pallas kernels  57.8 us (7%)
  local copies, waits for them, and re-layouts  37 us (4%)
  between operations  15 us (2%)
    unnamed x14, waiting for transfers between devices  259 us
    all_gather x8, blocking collectives, gathered(): return lax.all_gather(value, 'seq', axis=axis, tiled=True)  235 us
    reduce_scatter x3, waiting for transfers between devices, shard(): return lax.psum_scatter(value, 'seq', scatter_dimension=axis, tiled=True)  184 us
    psum x1, waiting for transfers between devices, local(): return (result, frames_grad) + lax.psum(shards, 'rows')  36.9 us
    unnamed x77, local copies, waits for them, and re-layouts  24.4 us
    pallas_call x1, Pallas kernels, forward(): pl.pallas_call(lambda *refs: forward_kernel(count, *refs), grid=(frames,)...  22.2 us
    pallas_call x1, Pallas kernels, backward(): pl.pallas_call(lambda *refs: backward_kernel(count, *refs), grid=(frames,...  21.5 us
  transfers between devices with their start and end apart: 21, of which 9 were waited for; matrix products, arithmetic and copies ran while one was open for 3% of the time, Pallas kernels for 4%

commit v1 on v0

--- a/solution.py
+++ b/solution.py
@@ -346,16 +346,14 @@
     return lax.dot_general(left, right, (((0,), (0,)), ((), ())), preferred_element_type=f32)
 
 
-def weight_kernel(
-    win_one, win_two, win_level, win_coarse, tile_out, tile_level, tile_mid, coarse_pairs,
-    g_one, g_two, g_down, g_up,
-    sum_one, sum_two, sum_down, sum_up,
-):
-    step = pl.program_id(0)
-
-    @pl.when(step == 0)
+def accumulate(wins, tiles, sums):
+    win_one, win_two, win_level, win_coarse = wins
+    tile_out, tile_level, tile_mid, coarse_pairs = tiles
+    sum_one, sum_two, sum_down, sum_up = sums
+
+    @pl.when(pl.program_id(0) == 0)
     def _():
-        for ref in (sum_one, sum_two, sum_down, sum_up):
+        for ref in sums:
             ref[...] = jnp.zeros_like(ref)
 
     def blocks(tiles):
@@ -369,15 +367,23 @@
     sum_two[...] += outer(window_operand(win_two.at[0], range(4)), blocks(tile_level))
     sum_one[...] += outer(window_operand(win_one.at[0], range(4)), blocks(tile_mid))
 
-    @pl.when(step == pl.num_programs(0) - 1)
+
+def fold(sums, base, p, q):
+    halves = []
+    for b in range(2):
+        rows = [base + ((a + p) * 4 + b + q) * C for a in range(2)]
+        halves.append(sums[rows[0] : rows[0] + C, :LANES] + sums[rows[1] : rows[1] + C, LANES:])
+    return halves[0] + swap_halves(halves[1])
+
+
+def weight_kernel(*refs):
+    wins, tiles, grads, sums = refs[:4], refs[4:8], refs[8:12], refs[12:]
+    g_one, g_two, g_down, g_up = grads
+    sum_one, sum_two, sum_down, sum_up = sums
+    accumulate(wins, tiles, sums)
+
+    @pl.when(pl.program_id(0) == pl.num_programs(0) - 1)
     def _():
-        def fold(sums, base, p, q):
-            halves = []
-            for b in range(2):
-                rows = [base + ((a + p) * 4 + b + q) * C for a in range(2)]
-                halves.append(sums[rows[0] : rows[0] + C, :LANES] + sums[rows[1] : rows[1] + C, LANES:])
-            return halves[0] + swap_halves(halves[1])
-
         for p in range(3):
             for q in range(3):
                 at = (3 * p + q) * C
@@ -389,18 +395,158 @@
                 g_down[at : at + C, :] = sum_down[place : place + C, :C]
 
 
-def expand_kernel(conv_one, conv_two, down_kernel, up_kernel, f_one, f_two, f_down, f_up, b_one, b_two, b_down, b_up):
+PARTS = 16
+
+
+def message_kernel(count, rows, *refs):
+    where_ref, wins, tiles = refs[0], refs[1:5], refs[5:9]
+    pieces, bias_sums, own, messages = refs[9:13]
+    sums = refs[13:17]
+    g_pair, g_up, g_down, small = refs[17:]
+    sum_one, sum_two, sum_down, sum_up = sums
+    accumulate(wins, tiles, sums)
+
+    @pl.when(pl.program_id(0) == pl.num_programs(0) - 1)
+    def _():
+        low_lanes = lane_ids((C, LANES)) < C
+        for p in range(3):
+            for q in range(3):
+                at = (3 * p + q) * C
+                g_pair[at : at + C, :] = jnp.where(
+                    low_lanes, fold(sum_one, 0, p, q), swap_halves(fold(sum_two, 0, p, q))
+                )
+                g_up[2 * at : 2 * at + C, :] = fold(sum_up, 16 * C, p, q)
+                g_up[2 * at + C : 2 * at + 2 * C, :] = fold(sum_up, 0, p, q)
+                place = (p * 4 + q) * C
+                g_down[at : at + C, :] = sum_down[place : place + C, :]
+        frames = pieces.shape[0]
+        small[...] = jnp.zeros_like(small)
+        total_bias = bias_sums[0, 0:4, :]
+        for f in range(frames):
+            small[4 * f : 4 * f + 4, :] = pieces[f, 0:4, :]
+            if f > 0:
+                total_bias = total_bias + bias_sums[f, 0:4, :]
+        small[4 * frames : 4 * frames + 4, :] = total_bias
+        exact = small[...]
+        high = exact.astype(bf16).astype(f32)
+        rest = exact - high
+        mid = rest.astype(bf16).astype(f32)
+        parts = (high, mid, rest - mid)
+        low_lanes = lane_ids((rows, LANES)) < C
+        nothing = jnp.zeros((rows - 3 * PARTS, LANES), f32)
+        sent = jnp.concatenate([*parts, nothing], axis=0)
+        kept = jnp.concatenate([exact, jnp.zeros((2 * PARTS, LANES), f32), nothing], axis=0)
+        for offset in range(count):
+            start = pl.multiple_of(seq_owner(where_ref[0], offset) * rows, 8)
+            block = jnp.concatenate(
+                [
+                    g_pair[pl.ds(start, rows), :],
+                    jnp.where(
+                        low_lanes,
+                        g_up[pl.ds(pl.multiple_of(2 * start, 8), rows), :],
+                        swap_halves(g_up[pl.ds(pl.multiple_of(2 * start + rows, 8), rows), :]),
+                    ),
+                    jnp.where(low_lanes, g_down[pl.ds(start, rows), :], kept if offset == 0 else sent),
+                ],
+                axis=0,
+            )
+            if offset == 0:
+                own[...] = block
+            else:
+                messages[offset - 1] = block.astype(bf16)
+
+
+def reduce_kernel(count, rows, cells, frames, *refs):
+    where_ref, own = refs[:2]
+    messages = refs[2 : 1 + count]
+    packs = refs[1 + count : 1 + 2 * count]
+    act_table, noise_table, ada_one, ada_two, out, pieces_one, pieces_two, table = refs[1 + 2 * count :]
+    place, member = where_ref[0], where_ref[1]
+    taken = 4 * frames
+    bias = jnp.zeros((4, LANES), f32)
+    sums = own[...]
+    lanes = lane_ids((1, LANES))
+    low_lanes = lanes < C
+    hot = []
+    for offset in range(count):
+        if offset == 0:
+            small = sums[2 * rows : 2 * rows + PARTS]
+        else:
+            message = messages[offset - 1][...].astype(f32)
+            sums = sums + message
+            first = 2 * rows
+            small = (
+                message[first : first + PARTS]
+                + message[first + PARTS : first + 2 * PARTS]
+                + message[first + 2 * PARTS : first + 3 * PARTS]
+            )
+        turned = swap_halves(small)
+        bias = bias + small[taken : taken + 4]
+        ids = packs[offset][2 * rows + ID_ROW : 2 * rows + ID_ROW + 8, :].astype(f32)
+        for f in range(frames):
+            at = offset * frames + f
+            for k, ref in ((0, pieces_one), (2, pieces_two)):
+                ref[at : at + 1, :] = jnp.where(low_lanes, turned[4 * f + k : 4 * f + k + 1], small[4 * f + k + 1 : 4 * f + k + 2])
+            mine = jnp.where(lane_ids(ids.shape) == C + member * frames + f, ids, 0.0)
+            mine = jnp.sum(mine, axis=1, keepdims=True)
+            action, noise, valid = mine[0:1], mine[1:2], mine[2:3]
+            place_at = lanes.astype(f32)
+            hot.append(jnp.where(place_at == action + ACT_ROW, valid, 0.0) + jnp.where(place_at == noise + NOISE_ROW, 1.0, 0.0))
+    hot = jnp.concatenate(hot, axis=0)[:, :TABLE_ROWS]
+    table[...] = jnp.zeros_like(table)
+    table[ACT_ROW : ACT_ROW + NACT, :] = act_table[...].astype(f32)
+    table[NOISE_ROW : NOISE_ROW + NLEV, :] = noise_table[...].astype(f32)
+    embed = matmul(hot.astype(bf16), table[...].astype(bf16))
+
+    def exact(left, right, dims):
+        return lax.dot_general(left, right, (dims, ((), ())), precision=precise, preferred_element_type=f32)
+
+    one, two = pieces_one[...], pieces_two[...]
+    at = 3 * rows
+    out[:at, :] = sums
+    out[at : at + cells, :] = exact(embed, one, ((0,), (0,)))
+    out[at + cells : at + 2 * cells, :] = exact(embed, two, ((0,), (0,)))
+    embed_grad = exact(one, ada_one[...].astype(f32), ((1,), (1,))) + exact(two, ada_two[...].astype(f32), ((1,), (1,)))
+    at = at + 2 * cells
+    out[at : at + TABLE_ROWS, :] = jnp.zeros((TABLE_ROWS, LANES), f32)
+    out[at : at + TABLE_ROWS, :cells] = exact(hot, embed_grad, ((0,), (0,)))
+    at = at + TABLE_ROWS
+    bias = jnp.concatenate([bias, jnp.zeros((4, LANES), f32)], axis=0)
+    width = C // count
+    out[at : at + 8, :] = pltpu.roll(bias, (C - place * width) % LANES, axis=1)
+
+
+def finish_kernel(rows, cells, width, first, second, *outs):
+    act_grad, noise_grad, ada_one, ada_two, g_one, g_two, g_down, g_up = outs[:8]
+    bias_grads = outs[8]
+    sums = first[...] + second[...]
+    pair, halves, down = (sums[k * rows : (k + 1) * rows] for k in range(3))
+    g_one[...] = pair[:, :C]
+    g_two[...] = swap_halves(pair)[:, :C]
+    g_up[:rows, :] = halves[:, :C]
+    g_up[rows:, :] = swap_halves(halves)[:, :C]
+    g_down[...] = down[:, :C]
+    at = 3 * rows
+    ada_one[...] = sums[at : at + cells]
+    ada_two[...] = sums[at + cells : at + 2 * cells]
+    at = at + 2 * cells
+    act_grad[...] = sums[at + ACT_ROW : at + ACT_ROW + NACT, :cells]
+    noise_grad[...] = sums[at + NOISE_ROW : at + NOISE_ROW + NLEV, :cells]
+    at = at + TABLE_ROWS
+    bias_grads[...] = sums[at : at + 4, :width]
+
+
+def write_operands(block, f_one, f_two, f_down, f_up, b_one, b_two, b_down, b_up):
     low_lanes = lane_ids((C, LANES)) < C
     zero = jnp.zeros((C, LANES), f32)
 
-    def taps(ref, base, step):
+    def taps(name, base, step):
         plain, turned = {}, {}
         for p in range(3):
             for q in range(3):
-                at = (3 * p + q) * step + base
-                k = ref[at : at + C, :].astype(f32)
-                plain[p, q] = jnp.concatenate([k, k], axis=1)
-                turned[p, q] = jnp.concatenate([k, k], axis=0).T
+                k = block(name, (3 * p + q) * step + base)
+                plain[p, q] = k
+                turned[p, q] = jnp.concatenate([k, k], axis=0).T[:C]
         return plain, turned
 
     def write_forward(ref, base, plain):
@@ -429,17 +575,17 @@
                         at = (r * 4 + w) * C
                         ref[at : at + C, lane + a * LANES : lane + (a + 1) * LANES] = zero.astype(bf16)
 
-    for ref, forward, backward in ((conv_one, f_one, b_one), (conv_two, f_two, b_two)):
-        plain, turned = taps(ref, 0, C)
-        write_forward(forward, 0, plain)
-        write_backward(backward, 0, turned)
-    plain, turned = taps(up_kernel, 0, 2 * C)
+    for name, forward_ref, backward_ref in (("one", f_one, b_one), ("two", f_two, b_two)):
+        plain, turned = taps(name, 0, C)
+        write_forward(forward_ref, 0, plain)
+        write_backward(backward_ref, 0, turned)
+    plain, turned = taps("up", 0, 2 * C)
     write_forward(f_up, 16 * C, plain)
     write_backward(b_up, 0, turned)
-    plain, turned = taps(up_kernel, C, 2 * C)
+    plain, turned = taps("up", C, 2 * C)
     write_forward(f_up, 0, plain)
     write_backward(b_up, 2 * LANES, turned)
-    plain, turned = taps(down_kernel, 0, C)
+    plain, turned = taps("down", 0, C)
     for p in range(3):
         for w in range(4):
             at = (p * 4 + w) * C
@@ -454,6 +600,112 @@
                     first = turned[p, 1] if right == 0 else zero
                     second = turned[p, 2] if right == 0 else turned[p, 0]
                 b_down[at : at + C, a * LANES : (a + 1) * LANES] = jnp.where(low_lanes, first, second).astype(bf16)
+
+
+def expand_kernel(conv_one, conv_two, down_kernel, up_kernel, *outs):
+    kernels = {"one": conv_one, "two": conv_two, "down": down_kernel, "up": up_kernel}
+
+    def block(name, row):
+        k = kernels[name][row : row + C, :].astype(f32)
+        return jnp.concatenate([k, k], axis=1)
+
+    write_operands(block, *outs)
+
+
+ACT_ROW, NOISE_ROW, TABLE_ROWS = 0, 24, 56
+BIAS_ROW, ID_ROW = 56, 64
+
+
+def pack_sizes(rows, cells):
+    return 3 * rows, 3 * rows + 2 * cells, -(-(3 * rows + 2 * cells) // 16) * 16
+
+
+def pack_kernel(conv_one, conv_two, down_kernel, up_kernel, ada_one, ada_two, act_table, noise_table, biases, ids, out, work):
+    rows, cells = conv_one.shape[0], ada_one.shape[0]
+    style_at, end, _ = pack_sizes(rows, cells)
+    work[...] = jnp.zeros_like(work)
+    wide = lambda ref: ref[...].astype(f32)
+    work[:rows, :] = jnp.concatenate([wide(conv_one), wide(conv_two)], axis=1)
+    work[rows : 2 * rows, :] = jnp.concatenate([wide(up_kernel)[:rows], wide(up_kernel)[rows:]], axis=1)
+    work[2 * rows : 3 * rows, :C] = wide(down_kernel)
+    for at, ref in ((ACT_ROW, act_table), (NOISE_ROW, noise_table), (BIAS_ROW, biases), (ID_ROW, ids)):
+        size = ref.shape
+        work[2 * rows + at : 2 * rows + at + size[0], C : C + size[1]] = wide(ref)
+    work[style_at : style_at + cells, :] = wide(ada_one)
+    work[style_at + cells : end, :] = wide(ada_two)
+    out[...] = work[...].astype(bf16)
+
+
+def seq_owner(place, offset):
+    return place ^ offset
+
+
+def prepare_kernel(count, rows, cells, *refs):
+    where_ref, actions, noise_ids, valid = refs[:4]
+    packs = refs[4 : 4 + count]
+    outs = refs[4 + count : 12 + count]
+    styles, biases = refs[12 + count : 14 + count]
+    work_pair, work_up, work_down, work_one, work_two, work_table = refs[14 + count :]
+    place, member, frames = where_ref[0], where_ref[1], styles.shape[0]
+    style_at, _, _ = pack_sizes(rows, cells)
+    bias_rows = jnp.zeros(SMALL, f32)
+    for offset, ref in enumerate(packs):
+        pack = ref[...].astype(f32)
+        owner = seq_owner(place, offset)
+        start = pl.multiple_of(owner * rows, 8)
+        work_pair[pl.ds(start, rows), :] = pack[:rows]
+        halves = pack[rows : 2 * rows]
+        work_up[pl.ds(2 * start, rows), :] = halves
+        work_up[pl.ds(pl.multiple_of(2 * start + rows, 8), rows), :] = swap_halves(halves)
+        extra = pack[2 * rows : 3 * rows]
+        work_down[pl.ds(start, rows), :] = extra
+        work_one[offset * cells : (offset + 1) * cells, :] = pack[style_at : style_at + cells]
+        work_two[offset * cells : (offset + 1) * cells, :] = pack[style_at + cells : style_at + 2 * cells]
+        lane = (offset * cells) % LANES
+        tables = pltpu.roll(extra[:TABLE_ROWS], (lane - C) % LANES, axis=1)
+        kept = (lane_ids(tables.shape) >= lane) & (lane_ids(tables.shape) < lane + cells)
+        column = offset * cells // LANES
+        tables = jnp.where(kept, tables, 0.0)
+        if lane == 0:
+            work_table[column] = tables
+        else:
+            work_table[column] += tables
+        slots = extra[BIAS_ROW : BIAS_ROW + 8]
+        width = C // count
+        slots = jnp.where((lane_ids(SMALL) >= C) & (lane_ids(SMALL) < C + width), slots, 0.0)
+        bias_rows = bias_rows + pltpu.roll(slots, (owner * width + C) % LANES, axis=1)
+    biases[...] = bias_rows + swap_halves(bias_rows)
+
+    lanes = lane_ids((8, LANES))
+    row_at = lax.broadcasted_iota(jnp.int32, (8, LANES), 0)
+    hot = jnp.zeros((8, LANES), f32)
+    for f in range(frames):
+        at = member * frames + f
+        here = jnp.where(lanes == actions[at] + ACT_ROW, valid[at], 0) + jnp.where(lanes == noise_ids[at] + NOISE_ROW, 1, 0)
+        hot = jnp.where(row_at == f, here.astype(f32), hot)
+    hot = hot[:, :TABLE_ROWS].astype(bf16)
+    embed = jnp.concatenate([matmul(hot, work_table[k].astype(bf16)) for k in range(work_table.shape[0])], axis=1)
+    low_lanes = lanes < C
+    for k, work in enumerate((work_one, work_two)):
+        style = jnp.dot(embed, work[...], precision=precise, preferred_element_type=f32)
+        other = swap_halves(style)
+        scale = 1.0 + jnp.where(low_lanes, style, other)
+        shift = jnp.where(low_lanes, other, style)
+        for f in range(frames):
+            styles[f, 2 * k : 2 * k + 1, :] = scale[f : f + 1]
+            styles[f, 2 * k + 1 : 2 * k + 2, :] = shift[f : f + 1]
+    for f in range(frames):
+        styles[f, 4:8, :] = jnp.zeros((4, LANES), f32)
+
+    def block(name, row):
+        work = {"one": work_pair, "two": work_pair, "down": work_down, "up": work_up}[name]
+        k = work[row : row + C, :]
+        low = lane_ids(k.shape) < C
+        if name == "two":
+            return jnp.where(low, swap_halves(k), k)
+        return jnp.where(low, k, swap_halves(k))
+
+    write_operands(block, *outs)
 
 
 def shape(dims, kind):
@@ -593,6 +845,123 @@
     )(win_one, win_two, win_level, win_coarse, tile_out, tile_level, tile_mid, coarse_pairs)
 
 
+def in_vmem():
+    return pl.BlockSpec(memory_space=pltpu.VMEM)
+
+
+def in_smem():
+    return pl.BlockSpec(memory_space=pltpu.SMEM)
+
+
+def pack(conv_one, conv_two, down_kernel, up_kernel, ada_one, ada_two, act_table, noise_table, biases, ids):
+    args = (conv_one, conv_two, down_kernel, up_kernel, ada_one, ada_two, act_table, noise_table, biases, ids)
+    _, _, size = pack_sizes(conv_one.shape[0], ada_one.shape[0])
+    return pl.pallas_call(
+        pack_kernel,
+        in_specs=[in_vmem()] * len(args),
+        out_specs=in_vmem(),
+        out_shape=shape((size, LANES), bf16),
+        scratch_shapes=[pltpu.VMEM((size, LANES), f32)],
+        compiler_params=params(),
+        name="pack",
+    )(*args)
+
+
+OPERANDS = (
+    (KEYS, 2 * LANES),
+    (KEYS, 2 * LANES),
+    (6 * LANES, LANES),
+    (2 * KEYS, 2 * LANES),
+    (KEYS, 2 * LANES),
+    (KEYS, 2 * LANES),
+    (2 * LANES, 2 * LANES),
+    (KEYS, 4 * LANES),
+)
+
+
+def prepare(where, actions, noise_ids, valid, packs, rows, cells, frames):
+    count = len(packs)
+    return pl.pallas_call(
+        lambda *refs: prepare_kernel(count, rows, cells, *refs),
+        in_specs=[in_smem()] * 4 + [in_vmem()] * count,
+        out_specs=[in_vmem()] * 10,
+        out_shape=[shape(d, bf16) for d in OPERANDS] + [shape((frames,) + SMALL, f32), shape(SMALL, f32)],
+        scratch_shapes=[
+            pltpu.VMEM((9 * C, LANES), f32),
+            pltpu.VMEM((18 * C, LANES), f32),
+            pltpu.VMEM((9 * C, LANES), f32),
+            pltpu.VMEM((count * cells, LANES), f32),
+            pltpu.VMEM((count * cells, LANES), f32),
+            pltpu.VMEM((count * cells // LANES, TABLE_ROWS, LANES), f32),
+        ],
+        compiler_params=params(),
+        name="prepare",
+    )(where, actions, noise_ids, valid, *packs)
+
+
+def weight_messages(where, wins, tiles, pieces, bias_sums, count, rows):
+    frames = pieces.shape[0]
+    return pl.pallas_call(
+        lambda *refs: message_kernel(count, rows, *refs),
+        grid=(frames,),
+        in_specs=[in_smem()]
+        + [per_frame(d) for d in (WINDOWS, WINDOWS, WINDOWS, COARSE_WINDOWS, TILES, TILES, TILES, COARSE)]
+        + [whole((frames,) + SMALL)] * 2,
+        out_specs=[whole((3 * rows, LANES)), whole((count - 1, 3 * rows, LANES))],
+        out_shape=[shape((3 * rows, LANES), f32), shape((count - 1, 3 * rows, LANES), bf16)],
+        scratch_shapes=[
+            pltpu.VMEM((KEYS, 2 * LANES), f32),
+            pltpu.VMEM((KEYS, 2 * LANES), f32),
+            pltpu.VMEM((6 * LANES, LANES), f32),
+            pltpu.VMEM((2 * KEYS, 2 * LANES), f32),
+            pltpu.VMEM((9 * C, LANES), f32),
+            pltpu.VMEM((18 * C, LANES), f32),
+            pltpu.VMEM((9 * C, LANES), f32),
+            pltpu.VMEM((PARTS, LANES), f32),
+        ],
+        compiler_params=params(),
+        name="weights",
+    )(where, *wins, *tiles, pieces, bias_sums)
+
+
+def reduce_messages(where, own, messages, packs, act_table, noise_table, ada_one, ada_two, rows, cells, frames):
+    count = len(packs)
+    return pl.pallas_call(
+        lambda *refs: reduce_kernel(count, rows, cells, frames, *refs),
+        in_specs=[in_smem()] + [in_vmem()] * (2 * count + 4),
+        out_specs=in_vmem(),
+        out_shape=shape((3 * rows + 2 * cells + TABLE_ROWS + 8, LANES), f32),
+        scratch_shapes=[
+            pltpu.VMEM((count * frames, LANES), f32),
+            pltpu.VMEM((count * frames, LANES), f32),
+            pltpu.VMEM((TABLE_ROWS, cells), f32),
+        ],
+        compiler_params=params(),
+        name="reduce",
+    )(where, own, *messages, *packs, act_table, noise_table, ada_one, ada_two)
+
+
+def finish(first, second, rows, cells, width):
+    return pl.pallas_call(
+        lambda *refs: finish_kernel(rows, cells, width, *refs),
+        in_specs=[in_vmem()] * 2,
+        out_specs=[in_vmem()] * 9,
+        out_shape=[
+            shape((NACT, cells), f32),
+            shape((NLEV, cells), f32),
+            shape((cells, LANES), f32),
+            shape((cells, LANES), f32),
+            shape((rows, C), f32),
+            shape((rows, C), f32),
+            shape((rows, C), f32),
+            shape((2 * rows, C), f32),
+            shape((4, width), f32),
+        ],
+        compiler_params=params(),
+        name="finish",
+    )(first, second)
+
+
 def twice(values):
     return jnp.concatenate([values, values], axis=-1)
 
@@ -628,7 +997,28 @@
     return result
 
 
-def local(
+def seq_trade(value, offset):
+    count = lax.axis_size("seq")
+    return lax.ppermute(value, "seq", [(i, i ^ offset) for i in range(count)])
+
+
+def layers(member_box, frame_strips, cot_strips, styles, bias_rows, operands):
+    f_one, f_two, f_down, f_up, b_one, b_two, b_down, b_up = operands
+    member = member_box[0]
+    out, win_one, win_two, win_level, win_coarse, middle, down, stats = forward(
+        member_box, frame_strips, styles, bias_rows, f_one, f_two, f_down, f_up
+    )
+    result = collect_strips(out, member, bf16)
+    grad_strips, tile_out, tile_level, tile_mid, coarse_pairs, pieces, bias_sums = backward(
+        member_box, cot_strips, frame_strips, styles, stats, middle, down, b_up, b_down, b_two, b_one
+    )
+    frames_grad = collect_strips(grad_strips, member, f32)
+    wins = (win_one, win_two, win_level, win_coarse)
+    tiles = (tile_out, tile_level, tile_mid, coarse_pairs)
+    return result, frames_grad, wins, tiles, pieces, bias_sums
+
+
+def local_direct(
     frames,
     cotangent,
     actions,
@@ -647,10 +1037,56 @@
     bias_down,
     bias_up,
 ):
-    member = lax.axis_index("rows")
-    count = lax.axis_size("rows")
-    share = frames.shape[0] // count
-    member_box = member.astype(jnp.int32).reshape(1)
+    member = lax.axis_index("rows").astype(jnp.int32)
+    place = lax.axis_index("seq").astype(jnp.int32)
+    count = lax.axis_size("seq")
+    share = frames.shape[0] // lax.axis_size("rows")
+    rows, cells, width = conv_one.shape[0], ada_one.shape[0], bias_one.shape[0]
+    member_box = member.reshape(1)
+    where = jnp.stack([place, member])
+    biases = jnp.stack([bias_one, bias_two, bias_down, bias_up])
+    ids = jnp.stack([actions, noise_ids, valid])
+    packed = pack(conv_one, conv_two, down_kernel, up_kernel, ada_one, ada_two, act_table, noise_table, biases, ids)
+    packs = [packed] + [seq_trade(packed, offset) for offset in range(1, count)]
+    frame_strips = spread_strips(frames, member)
+    cot_strips = spread_strips(cotangent, member)
+    *operands, styles, bias_rows = prepare(where, actions, noise_ids, valid, packs, rows, cells, share)
+    result, frames_grad, wins, tiles, pieces, bias_sums = layers(
+        member_box, frame_strips, cot_strips, styles, bias_rows, operands
+    )
+    own, messages = weight_messages(where, wins, tiles, pieces, bias_sums, count, rows)
+    received = [seq_trade(messages[offset - 1], offset) for offset in range(1, count)]
+    sums = reduce_messages(where, own, received, packs, act_table, noise_table, ada_one, ada_two, rows, cells, share)
+    offset = 1
+    while 2 * offset < lax.axis_size("rows"):
+        sums = sums + trade(sums, offset)
+        offset *= 2
+    *grads, bias_grads = finish(sums, trade(sums, offset), rows, cells, width)
+    return (result, frames_grad, *grads, bias_grads[0], bias_grads[1], bias_grads[2], bias_grads[3])
+
+
+def local_general(
+    frames,
+    cotangent,
+    actions,
+    noise_ids,
+    valid,
+    act_table,
+    noise_table,
+    ada_one,
+    ada_two,
+    conv_one,
+    conv_two,
+    down_kernel,
+    up_kernel,
+    bias_one,
+    bias_two,
+    bias_down,
+    bias_up,
+):
+    member = lax.axis_index("rows").astype(jnp.int32)
+    share = frames.shape[0] // lax.axis_size("rows")
+    member_box = member.reshape(1)
 
     def gathered(value, axis):
         return lax.all_gather(value, "seq", axis=axis, tiled=True)
@@ -661,8 +1097,7 @@
     noise_full = gathered(noise_table, 1)
     ada_full = gathered(jnp.concatenate([ada_one, ada_two], axis=1), 0).astype(f32)
     biases = gathered(jnp.stack([bias_one, bias_two, bias_down, bias_up]), 1).astype(f32)
-    expanded = expand(gathered(conv_one, 0), gathered(conv_two, 0), gathered(down_kernel, 0), gathered(up_kernel, 0))
-    f_one, f_two, f_down, f_up, b_one, b_two, b_down, b_up = expanded
+    operands = expand(gathered(conv_one, 0), gathered(conv_two, 0), gathered(down_kernel, 0), gathered(up_kernel, 0))
 
     own = lambda ids: lax.dynamic_slice_in_dim(ids, member * share, share)
     own_actions, own_noise, own_valid = own(actions), own(noise_ids), own(valid)
@@ -683,18 +1118,10 @@
         ]
     )
     bias_rows = pad_small([twice(biases[k]) for k in range(4)])
-
-    out, win_one, win_two, win_level, win_coarse, middle, down, stats = forward(
-        member_box, frame_strips, styles, bias_rows, f_one, f_two, f_down, f_up
+    result, frames_grad, wins, tiles, pieces, bias_sums = layers(
+        member_box, frame_strips, cot_strips, styles, bias_rows, operands
     )
-    result = collect_strips(out, member, bf16)
-    grad_strips, tile_out, tile_level, tile_mid, coarse_pairs, pieces, bias_sums = backward(
-        member_box, cot_strips, frame_strips, styles, stats, middle, down, b_up, b_down, b_two, b_one
-    )
-    frames_grad = collect_strips(grad_strips, member, f32)
-    g_one, g_two, g_down, g_up = weight_grads(
-        win_one, win_two, win_level, win_coarse, tile_out, tile_level, tile_mid, coarse_pairs
-    )
+    g_one, g_two, g_down, g_up = weight_grads(*wins, *tiles)
 
     pieces_one = jnp.concatenate([pieces[:, 0, :C], pieces[:, 1, :C]], axis=1)
     pieces_two = jnp.concatenate([pieces[:, 2, :C], pieces[:, 3, :C]], axis=1)
@@ -723,6 +1150,12 @@
         shard(bias_total[3], 0),
     )
     return (result, frames_grad) + lax.psum(shards, "rows")
+
+
+def fits_direct(mesh):
+    count = mesh.shape["seq"]
+    rows, cells = 9 * C // count, 256 // count
+    return count in (2, 4, 8) and rows % 8 == 0 and rows >= ID_ROW + 8 and cells % 8 == 0 and mesh.shape["rows"] == 4
 
 
 def solution(mesh):
@@ -761,4 +1194,5 @@
         P("seq"),
         P("seq"),
     )
+    local = local_direct if fits_direct(mesh) else local_general
     return jax.shard_map(local, mesh=mesh, in_specs=in_specs, out_specs=out_specs, check_vma=False)

time: 863 us -> 151 us (0.17)
  waiting for transfers between devices: 481 us -> 15.7 us
  blocking collectives: 252 us -> 0 us
  starting transfers between devices: 8.47 us -> 34.4 us
  between operations: 15 us -> 0.99 us
  local copies, waits for them, and re-layouts: 37 us -> 26.5 us
    unnamed x14 -> x0, waiting for transfers between devices: 259 us -> none
    all_gather x8 -> x0, blocking collectives: 235 us -> none  [gathered(): return lax.all_gather(value, 'seq', axis=axis, tiled=True)]
    reduce_scatter x3 -> x0, waiting for transfers between devices: 184 us -> none  [shard(): return lax.psum_scatter(value, 'seq', scatter_dimension=axis, tiled=True)]
    psum x1 -> x0, waiting for transfers between devices: 36.9 us -> none  [local(): return (result, frames_grad) + lax.psum(shards, 'rows')]
    ppermute x0 -> x14, starting transfers between devices: none -> 23.7 us  [seq_trade(): return lax.ppermute(value, 'seq', [(i, i ^ offset) for i in range(count)])]
    unnamed x1 -> x0, blocking collectives: 17.2 us -> none
    ppermute x12 -> x14, waiting for transfers between devices: 0.03 us -> 10.3 us  [trade(): return lax.ppermute(value, 'rows', [(i, i ^ offset) for i in range(count)])]
    unnamed x77 -> x62, local copies, waits for them, and re-layouts: 24.4 us -> 15.3 us
  transfers between devices with their start and end apart: 21 -> 28, of which waited for: 9 -> 7; matrix products, arithmetic and copies ran while one was open for 3% -> 9% of each run, Pallas kernels for 4% -> 19%
where the time goes in v1:
time: 151 us; the launch traced here: 150 us
  Pallas kernels  64.7 us (43%)
  starting transfers between devices  34.4 us (23%)
  local copies, waits for them, and re-layouts  26.5 us (18%)
  waiting for transfers between devices  15.7 us (10%)
  other arithmetic  8.04 us (5%)
    ppermute x14, starting transfers between devices, seq_trade(): return lax.ppermute(value, 'seq', [(i, i ^ offset) for i in range(count)])  23.7 us
    pallas_call x1, Pallas kernels, forward(): pl.pallas_call(lambda *refs: forward_kernel(count, *refs), grid=(frames,)...  22.4 us
    pallas_call x1, Pallas kernels, backward(): pl.pallas_call(lambda *refs: backward_kernel(count, *refs), grid=(frames,...  21.5 us
    unnamed x62, local copies, waits for them, and re-layouts  15.3 us
    pallas_call x1, Pallas kernels, weight_messages(): pl.pallas_call(lambda *refs: message_kernel(count, rows, *refs), grid=(fr...  11 us
    ppermute x14, starting transfers between devices, trade(): return lax.ppermute(value, 'rows', [(i, i ^ offset) for i in range(count)])  10.6 us
    ppermute x14, waiting for transfers between devices, trade(): return lax.ppermute(value, 'rows', [(i, i ^ offset) for i in range(count)])  10.3 us
    ppermute x14, waiting for transfers between devices, seq_trade(): return lax.ppermute(value, 'seq', [(i, i ^ offset) for i in range(count)])  5.37 us
  transfers between devices with their start and end apart: 28, of which 7 were waited for; matrix products, arithmetic and copies ran while one was open for 9% of the time, Pallas kernels for 19%

profile of v1, /device:TPU:0, one launch (start us, length us, event | category | flops | bytes accessed | tf_op | source)
XLA Modules:
  0.0 150.2 jit_solution(9874323753461875107)
XLA Ops:
  0.7 1.6 %copy.34.up_kernel = bf16[144,64]{1,0:T(8,128)(2,1)} copy(bf16[144,64]{0,1:T(8,128)(2,1)} %param.29) | data formatting | bytes 36864 | tf_op args[12]
  2.2 1.4 copy.31.conv_one
  3.6 1.4 copy.32.conv_two
  5.0 1.4 copy.33.down_kernel
  6.4 1.3 pad_add_fusion.ids
  7.7 1.3 pad_maximum_fusion.biases
  9.0 1.5 %pack.1.refs_4_.refs_9_ = bf16[288,128]{1,0:T(8,128)(2,1)} custom-call(bf16[72,64]{1,0:T(8,128)(2,1)} %copy.31.conv_one, bf16[72,64]{1,0:T(8,128)(2,1)} %copy.32.conv_two, bf16[72,64]{1,0:T(8,128)(2,1)} %copy.33.down_kernel, bf16[144,64]{1,0:T(8,128)(2,1)} %copy.34.up_kernel, bf16[32,128]{1,0:T(8,128)(2,1)} %refs_19_.1, bf16[32,128]{1,0:T(8,128)(2,1)} %refs_20_.1, ...), custom_call_target="tpu_custom_call" | custom-call | tf_op jit(solution)/shard_map/pack/pallas_call | solution.py:859
  10.5 2.9 %collective-permute-start.3 = (bf16[288,128]{1,0:T(8,128)(2,1)}, bf16[288,128]{1,0:T(8,128)(2,1)S(1)}, u32[]{:S(2)}, u32[]{:S(2)}) collective-permute-start(bf16[288,128]{1,0:T(8,128)(2,1)} %pack.1.refs_4_.refs_9_), channel_id=1, source_target_pairs={{0,4},{4,0},{8,12},{12,8},{16,20},{20,16},{24,28},{28,24},{1,5},{5... | collective-permute-start | bytes 221192 | tf_op jit(solution)/shard_map/ppermute | solution.py:1002
  13.5 1.6 %collective-permute-start.4 = (bf16[288,128]{1,0:T(8,128)(2,1)}, bf16[288,128]{1,0:T(8,128)(2,1)S(1)}, u32[]{:S(2)}, u32[]{:S(2)}) collective-permute-start(bf16[288,128]{1,0:T(8,128)(2,1)} %pack.1.refs_4_.refs_9_), channel_id=1, source_target_pairs={{0,8},{4,12},{8,0},{12,4},{16,24},{20,28},{24,16},{28,20},{1,9},{5... | collective-permute-start | bytes 221192 | tf_op jit(solution)/shard_map/ppermute | solution.py:1002
  15.1 3.0 %collective-permute-start.6 = (bf16[288,128]{1,0:T(8,128)(2,1)}, bf16[288,128]{1,0:T(8,128)(2,1)S(1)}, u32[]{:S(2)}, u32[]{:S(2)}) collective-permute-start(bf16[288,128]{1,0:T(8,128)(2,1)} %pack.1.refs_4_.refs_9_), channel_id=1, source_target_pairs={{0,16},{4,20},{8,24},{12,28},{16,0},{20,4},{24,8},{28,12},{1,17},{... | collective-permute-start | bytes 221192 | tf_op jit(solution)/shard_map/ppermute | solution.py:1002
  18.1 1.3 collective-permute-start.7
  19.3 2.0 %constant_dynamic-slice_fusion.4 = (bf16[2,16,4096]{2,1,0:T(8,128)(2,1)S(1)}, bf16[2,16,4096]{2,1,0:T(8,128)(2,1)S(1)}, bf16[2,16,4096]{2,1,0:T(8,128)(2,1)}, bf16[2,16,4096]{2,1,0:T(8,128)(2,1)S(1)}) fusion(bf16[8,16,4096]{2,1,0:T(8,128)(2,1)} %param.17, s32[]{:T(128)S(6)} %select_n.11, s32[]{:T(128)S(6)} %select_n.9, s32[]{:T(128)S(6)} %select_n.8, ...), kind=kLoop, calls=%fused_computation.25 | loop fusion | bytes 2097168 | tf_op jit(solution)/shard_map/dynamic_slice | solution.py:986
  21.3 3.7 %collective-permute-start.8 = (bf16[288,128]{1,0:T(8,128)(2,1)S(1)}, bf16[288,128]{1,0:T(8,128)(2,1)S(1)}, u32[]{:S(2)}, u32[]{:S(2)}) collective-permute-start(bf16[288,128]{1,0:T(8,128)(2,1)S(1)} %copy-done.8), channel_id=1, source_target_pairs={{0,24},{4,28},{8,16},{12,20},{16,8},{20,12},{24,0},{28,4},{1,25},{... | collective-permute-start | bytes 221192 | tf_op jit(solution)/shard_map/ppermute | solution.py:1002
  25.1 1.7 %collective-permute-start.1 = (bf16[2,16,4096]{2,1,0:T(8,128)(2,1)S(1)}, bf16[2,16,4096]{2,1,0:T(8,128)(2,1)S(1)}, u32[]{:S(2)}, u32[]{:S(2)}) collective-permute-start(bf16[2,16,4096]{2,1,0:T(8,128)(2,1)S(1)} %get-tuple-element.113), channel_id=1, source_target_pairs={{0,2},{1,3},{2,0},{3,1},{4,6},{5,7},{6,4},{7,5},{8,10},{9,11},{10,... | collective-permute-start | bytes 786440 | tf_op jit(solution)/shard_map/ppermute | solution.py:979
  26.8 2.7 %collective-permute-done.7.refs_9_.refs_14_ = bf16[288,128]{1,0:T(8,128)(2,1)S(1)} collective-permute-done((bf16[288,128]{1,0:T(8,128)(2,1)}, bf16[288,128]{1,0:T(8,128)(2,1)S(1)}, u32[]{:S(2)}, u32[]{:S(2)}) %collective-permute-start.7) | collective-permute-done | bytes 73760 | tf_op jit(solution)/shard_map/ppermute | solution.py:1002
  29.5 0.9 constant_dynamic-slice_fusion
  30.4 1.6 %collective-permute-start.13 = (bf16[2,16,4096]{2,1,0:T(8,128)(2,1)}, bf16[2,16,4096]{2,1,0:T(8,128)(2,1)S(1)}, u32[]{:S(2)}, u32[]{:S(2)}) collective-permute-start(bf16[2,16,4096]{2,1,0:T(8,128)(2,1)} %get-tuple-element.104), channel_id=1, source_target_pairs={{0,1},{1,0},{2,3},{3,2},{4,5},{5,4},{6,7},{7,6},{8,9},{9,8},{10,11... | collective-permute-start | bytes 786440 | tf_op jit(solution)/shard_map/ppermute | solution.py:979
  32.1 1.5 %collective-permute-start.14 = (bf16[2,16,4096]{2,1,0:T(8,128)(2,1)S(1)}, bf16[2,16,4096]{2,1,0:T(8,128)(2,1)S(1)}, u32[]{:S(2)}, u32[]{:S(2)}) collective-permute-start(bf16[2,16,4096]{2,1,0:T(8,128)(2,1)S(1)} %get-tuple-element.106), channel_id=1, source_target_pairs={{0,2},{1,3},{2,0},{3,1},{4,6},{5,7},{6,4},{7,5},{8,10},{9,11},{10,... | collective-permute-start | bytes 786440 | tf_op jit(solution)/shard_map/ppermute | solution.py:979
  33.7 0.6 pad_add_fusion.1.refs_0_
  34.3 3.7 %prepare.1 = (bf16[1024,256]{1,0:T(8,128)(2,1)}, bf16[1024,256]{1,0:T(8,128)(2,1)}, bf16[768,128]{1,0:T(8,128)(2,1)}, bf16[2048,256]{1,0:T(8,128)(2,1)}, bf16[10...) custom-call(s32[2]{0:T(128)} %pad_add_fusion.1.refs_0_, ...), custom_call_target="tpu_custom_call" | custom-call | tf_op jit(solution)/shard_map/prepare/pallas_call | solution.py:884
  38.0 1.0 collective-permute-done.2.refs_4_.refs_8_
  39.1 0.7 copy-done.6
  39.8 22.4 %forward.1 = (bf16[4,2,16,4096]{3,2,1,0:T(8,128)(2,1)}, bf16[2,4,33,32,128]{4,3,2,1,0:T(8,128)(2,1)}, bf16[2,4,33,32,128]{4,3,2,1,0:T(8,128)(2,1)}, bf16[2,4,33,...) custom-call(s32[1]{0:T(128)} %bitcast.refs_0_, ...), custom_call_target="tpu_custom_call" | custom-call | tf_op jit(solution)/shard_map/forward/pallas_call | solution.py:768
  62.2 0.7 copy-done.16
  63.1 21.5 %backward.1 = (bf16[4,2,16,4096]{3,2,1,0:T(8,128)(2,1)}, bf16[2,2,32,32,128]{4,3,2,1,0:T(8,128)(2,1)}, bf16[2,2,32,32,128]{4,3,2,1,0:T(8,128)(2,1)}, bf16[2,2,32...) custom-call(s32[1]{0:T(128)} %bitcast.refs_0_, ...), custom_call_target="tpu_custom_call" | custom-call | tf_op jit(solution)/shard_map/backward/pallas_call | solution.py:796
  84.6 11.0 %weights.1 = (f32[216,128]{1,0:T(8,128)}, bf16[7,216,128]{2,1,0:T(8,128)(2,1)}) custom-call(s32[2]{0:T(128)} %pad_add_fusion.1.refs_0_, bf16[2,4,33,32,128]{4,3,2,1,0:T(8,128)(2,1)} %get-tuple-element.65.refs_1_, bf16[2,4,33,32,128]{4,3,2,1,0:T(8,128)(2,1)} %get-tuple-element.66.refs_2_, bf16[2,4,33,32,128]{4,3,2,1,0:T(8,128)(2,1)} %get-tuple-element.67.refs_3_, ...), custom_call_target="tpu_custom_call" | custom-call | tf_op jit(solution)/shard_map/weights/pallas_call | solution.py:904
  95.6 1.1 slice_bitcast_fusion.6
  96.7 1.7 %collective-permute-start.19 = (bf16[216,128]{1,0:T(8,128)(2,1)S(1)}, bf16[216,128]{1,0:T(8,128)(2,1)S(1)}, u32[]{:S(2)}, u32[]{:S(2)}) collective-permute-start(bf16[216,128]{1,0:T(8,128)(2,1)S(1)} %get-tuple-element.120), channel_id=1, source_target_pairs={{0,4},{4,0},{8,12},{12,8},{16,20},{20,16},{24,28},{28,24},{1,5},{5... | collective-permute-start | bytes 165896 | tf_op jit(solution)/shard_map/ppermute | solution.py:1002
  98.5 1.8 %collective-permute-start.21 = (bf16[216,128]{1,0:T(8,128)(2,1)S(1)}, bf16[216,128]{1,0:T(8,128)(2,1)S(1)}, u32[]{:S(2)}, u32[]{:S(2)}) collective-permute-start(bf16[216,128]{1,0:T(8,128)(2,1)S(1)} %get-tuple-element.118), channel_id=1, source_target_pairs={{0,12},{4,8},{8,4},{12,0},{16,28},{20,24},{24,20},{28,16},{1,13},{... | collective-permute-start | bytes 165896 | tf_op jit(solution)/shard_map/ppermute | solution.py:1002
  100.3 2.2 %collective-permute-start.22 = (bf16[216,128]{1,0:T(8,128)(2,1)S(1)}, bf16[216,128]{1,0:T(8,128)(2,1)S(1)}, u32[]{:S(2)}, u32[]{:S(2)}) collective-permute-start(bf16[216,128]{1,0:T(8,128)(2,1)S(1)} %get-tuple-element.117), channel_id=1, source_target_pairs={{0,16},{4,20},{8,24},{12,28},{16,0},{20,4},{24,8},{28,12},{1,17},{... | collective-permute-start | bytes 165896 | tf_op jit(solution)/shard_map/ppermute | solution.py:1002
  102.5 1.8 %collective-permute-start.23 = (bf16[216,128]{1,0:T(8,128)(2,1)S(1)}, bf16[216,128]{1,0:T(8,128)(2,1)S(1)}, u32[]{:S(2)}, u32[]{:S(2)}) collective-permute-start(bf16[216,128]{1,0:T(8,128)(2,1)S(1)} %get-tuple-element.116), channel_id=1, source_target_pairs={{0,20},{4,16},{8,28},{12,24},{16,4},{20,0},{24,12},{28,8},{1,21},{... | collective-permute-start | bytes 165896 | tf_op jit(solution)/shard_map/ppermute | solution.py:1002
  104.3 0.9 slice_bitcast_fusion
  105.2 0.8 slice_bitcast_fusion.3
  106.0 3.5 %collective-permute-start.24 = (bf16[216,128]{1,0:T(8,128)(2,1)S(1)}, bf16[216,128]{1,0:T(8,128)(2,1)S(1)}, u32[]{:S(2)}, u32[]{:S(2)}) collective-permute-start(bf16[216,128]{1,0:T(8,128)(2,1)S(1)} %get-tuple-element.115), channel_id=1, source_target_pairs={{0,24},{4,28},{8,16},{12,20},{16,8},{20,12},{24,0},{28,4},{1,25},{... | collective-permute-start | bytes 165896 | tf_op jit(solution)/shard_map/ppermute | solution.py:1002
  109.8 1.0 convert_dynamic-update-slice_fusion
  110.9 1.6 %collective-permute-start.17 = (bf16[2,16,4096]{2,1,0:T(8,128)(2,1)}, bf16[2,16,4096]{2,1,0:T(8,128)(2,1)}, u32[]{:S(2)}, u32[]{:S(2)}) collective-permute-start(bf16[2,16,4096]{2,1,0:T(8,128)(2,1)} %get-tuple-element.101), channel_id=1, source_target_pairs={{0,2},{1,3},{2,0},{3,1},{4,6},{5,7},{6,4},{7,5},{8,10},{9,11},{10,... | collective-permute-start | bytes 786440 | tf_op jit(solution)/shard_map/ppermute | solution.py:979
  112.6 0.2 collective-permute-start.18
  112.8 0.6 copy-done.25
  113.4 0.4 collective-permute-start.10
  113.8 2.5 %collective-permute-done.25.refs_8_ = bf16[216,128]{1,0:T(8,128)(2,1)S(1)} collective-permute-done((bf16[216,128]{1,0:T(8,128)(2,1)S(1)}, bf16[216,128]{1,0:T(8,128)(2,1)S(1)}, u32[]{:S(2)}, u32[]{:S(2)}) %collective-permute-start.25) | collective-permute-done | bytes 55328 | tf_op jit(solution)/shard_map/ppermute | solution.py:1002
  116.3 0.6 copy-done.26
  117.0 2.8 %reduce.1 = f32[344,128]{1,0:T(8,128)} custom-call(s32[2]{0:T(128)} %pad_add_fusion.1.refs_0_, f32[216,128]{1,0:T(8,128)} %get-tuple-element.75.refs_1_, bf16[216,128]{1,0:T(8,128)(2,1)} %copy-done.20, bf16[216,128]{1,0:T(8,128)(2,1)} %copy-done.21, bf16[216,128]{1,0:T(8,128)(2,1)} %copy-done.22, bf16[216,128]{1,0:T(8,128)(2,1)} %copy-done.23, ...), custom_call_target="tpu_custom_call" | custom-call | tf_op jit(solution)/shard_map/reduce/pallas_call | solution.py:929
  119.7 1.1 broadcast_in_dim.6
  120.8 0.7 bitcast_dynamic-update-slice_fusion
  121.5 1.5 %collective-permute-start.11 = (bf16[2,16,4096]{2,1,0:T(8,128)(2,1)S(1)}, bf16[2,16,4096]{2,1,0:T(8,128)(2,1)S(1)}, u32[]{:S(2)}, u32[]{:S(2)}) collective-permute-start(bf16[2,16,4096]{2,1,0:T(8,128)(2,1)S(1)} %get-tuple-element.108), channel_id=1, source_target_pairs={{0,2},{1,3},{2,0},{3,1},{4,6},{5,7},{6,4},{7,5},{8,10},{9,11},{10,... | collective-permute-start | bytes 786440 | tf_op jit(solution)/shard_map/ppermute | solution.py:979
  123.0 0.9 add.14.refs_0_
  124.0 0.4 collective-permute-start.12
  124.4 1.0 convert_dynamic-update-slice_fusion.3
  125.4 1.6 %collective-permute-start.27 = (f32[344,128]{1,0:T(8,128)S(1)}, f32[344,128]{1,0:T(8,128)S(1)}, u32[]{:S(2)}, u32[]{:S(2)}) collective-permute-start(f32[344,128]{1,0:T(8,128)S(1)} %add.14.refs_0_), channel_id=1, source_target_pairs={{0,2},{1,3},{2,0},{3,1},{4,6},{5,7},{6,4},{7,5},{8,10},{9,11},{10,... | collective-permute-start | bytes 528392 | tf_op jit(solution)/shard_map/ppermute | solution.py:979
  127.0 1.0 convert_dynamic-update-slice_fusion.2
  128.0 1.0 convert_dynamic-update-slice_fusion.1
  129.0 0.8 constant_dynamic-update-slice_fusion.2
  129.8 1.8 %collective-permute-done.11 = bf16[2,16,4096]{2,1,0:T(8,128)(2,1)S(1)} collective-permute-done((bf16[2,16,4096]{2,1,0:T(8,128)(2,1)S(1)}, bf16[2,16,4096]{2,1,0:T(8,128)(2,1)S(1)}, u32[]{:S(2)}, u32[]{:S(2)}) %collective-permute-start.11) | collective-permute-done | bytes 262176 | tf_op jit(solution)/shard_map/ppermute | solution.py:979
  131.6 0.7 constant_dynamic-update-slice_fusion.1
  132.3 4.0 %collective-permute-done.12 = bf16[2,16,4096]{2,1,0:T(8,128)(2,1)S(1)} collective-permute-done((bf16[2,16,4096]{2,1,0:T(8,128)(2,1)S(1)}, bf16[2,16,4096]{2,1,0:T(8,128)(2,1)S(1)}, u32[]{:S(2)}, u32[]{:S(2)}) %collective-permute-start.12) | collective-permute-done | bytes 262176 | tf_op jit(solution)/shard_map/ppermute | solution.py:979
  136.3 0.7 constant_dynamic-update-slice_fusion
  137.0 3.5 %collective-permute-done.27.refs_1_ = f32[344,128]{1,0:T(8,128)S(1)} collective-permute-done((f32[344,128]{1,0:T(8,128)S(1)}, f32[344,128]{1,0:T(8,128)S(1)}, u32[]{:S(2)}, u32[]{:S(2)}) %collective-permute-start.27) | collective-permute-done | bytes 176160 | tf_op jit(solution)/shard_map/ppermute | solution.py:979
  140.5 0.7 copy-done.19
  141.2 1.7 %finish.1 = (f32[18,32]{1,0:T(8,128)}, f32[32,32]{1,0:T(8,128)}, f32[32,128]{1,0:T(8,128)}, f32[32,128]{1,0:T(8,128)}, f32[72,64]{1,0:T(8,128)}, /*index=5*/f32[...) custom-call(f32[344,128]{1,0:T(8,128)} %copy-done.7, f32[344,128]{1,0:T(8,128)} %copy-done.19), custom_call_target="tpu_custom_call" | custom-call | tf_op jit(solution)/shard_map/finish/pallas_call | solution.py:945
  142.9 1.6 %copy.38 = f32[144,64]{0,1:T(8,128)} copy(f32[144,64]{1,0:T(8,128)} %get-tuple-element.95) | data formatting | bytes 73728
  144.5 1.5 copy.35
  146.0 1.5 copy.36
  147.4 1.5 copy.37
  148.9 1.3 slice_bitcast_fusion.13
  (81 shorter events, 0.9 us)
Async XLA Ops:
  0.6 28.9 %copy-start.1 = (bf16[8,16,4096]{2,1,0:T(8,128)(2,1)S(1)}, bf16[8,16,4096]{2,1,0:T(8,128)(2,1)}, u32[]{:S(2)}) copy-start(bf16[8,16,4096]{2,1,0:T(8,128)(2,1)} %param.18) | copy-start | bytes 3145732
  10.5 10.8 %copy-start.8 = (bf16[288,128]{1,0:T(8,128)(2,1)S(1)}, bf16[288,128]{1,0:T(8,128)(2,1)}, u32[]{:S(2)}) copy-start(bf16[288,128]{1,0:T(8,128)(2,1)} %pack.1.refs_4_.refs_9_) | copy-start | bytes 221188
  10.5 10.8 %collective-permute-start.3 = (bf16[288,128]{1,0:T(8,128)(2,1)}, bf16[288,128]{1,0:T(8,128)(2,1)S(1)}, u32[]{:S(2)}, u32[]{:S(2)}) collective-permute-start(bf16[288,128]{1,0:T(8,128)(2,1)} %pack.1.refs_4_.refs_9_), channel_id=1, source_target_pairs={{0,4},{4,0},{8,12},{12,8},{16,20},{20,16},{24,28},{28,24},{1,5},{5... | collective-permute-start | bytes 221192 | tf_op jit(solution)/shard_map/ppermute | solution.py:1002
  13.5 11.5 %collective-permute-start.4 = (bf16[288,128]{1,0:T(8,128)(2,1)}, bf16[288,128]{1,0:T(8,128)(2,1)S(1)}, u32[]{:S(2)}, u32[]{:S(2)}) collective-permute-start(bf16[288,128]{1,0:T(8,128)(2,1)} %pack.1.refs_4_.refs_9_), channel_id=1, source_target_pairs={{0,8},{4,12},{8,0},{12,4},{16,24},{20,28},{24,16},{28,20},{1,9},{5... | collective-permute-start | bytes 221192 | tf_op jit(solution)/shard_map/ppermute | solution.py:1002
  15.1 10.0 %collective-permute-start.5 = (bf16[288,128]{1,0:T(8,128)(2,1)}, bf16[288,128]{1,0:T(8,128)(2,1)S(1)}, u32[]{:S(2)}, u32[]{:S(2)}) collective-permute-start(bf16[288,128]{1,0:T(8,128)(2,1)} %pack.1.refs_4_.refs_9_), channel_id=1, source_target_pairs={{0,12},{4,8},{8,4},{12,0},{16,28},{20,24},{24,20},{28,16},{1,13},{... | collective-permute-start | bytes 221192 | tf_op jit(solution)/shard_map/ppermute | solution.py:1002
  15.1 10.0 %collective-permute-start.6 = (bf16[288,128]{1,0:T(8,128)(2,1)}, bf16[288,128]{1,0:T(8,128)(2,1)S(1)}, u32[]{:S(2)}, u32[]{:S(2)}) collective-permute-start(bf16[288,128]{1,0:T(8,128)(2,1)} %pack.1.refs_4_.refs_9_), channel_id=1, source_target_pairs={{0,16},{4,20},{8,24},{12,28},{16,0},{20,4},{24,8},{28,12},{1,17},{... | collective-permute-start | bytes 221192 | tf_op jit(solution)/shard_map/ppermute | solution.py:1002
  18.1 11.4 %collective-permute-start.7 = (bf16[288,128]{1,0:T(8,128)(2,1)}, bf16[288,128]{1,0:T(8,128)(2,1)S(1)}, u32[]{:S(2)}, u32[]{:S(2)}) collective-permute-start(bf16[288,128]{1,0:T(8,128)(2,1)} %pack.1.refs_4_.refs_9_), channel_id=1, source_target_pairs={{0,20},{4,16},{8,28},{12,24},{16,4},{20,0},{24,12},{28,8},{1,21},{... | collective-permute-start | bytes 221192 | tf_op jit(solution)/shard_map/ppermute | solution.py:1002
  21.3 13.0 %copy-start.9 = (bf16[288,128]{1,0:T(8,128)(2,1)}, bf16[288,128]{1,0:T(8,128)(2,1)S(1)}, u32[]{:S(2)}) copy-start(bf16[288,128]{1,0:T(8,128)(2,1)S(1)} %collective-permute-done.3.refs_5_.refs_10_) | copy-start | bytes 221188
  21.3 9.1 %collective-permute-start.8 = (bf16[288,128]{1,0:T(8,128)(2,1)S(1)}, bf16[288,128]{1,0:T(8,128)(2,1)S(1)}, u32[]{:S(2)}, u32[]{:S(2)}) collective-permute-start(bf16[288,128]{1,0:T(8,128)(2,1)S(1)} %copy-done.8), channel_id=1, source_target_pairs={{0,24},{4,28},{8,16},{12,20},{16,8},{20,12},{24,0},{28,4},{1,25},{... | collective-permute-start | bytes 221192 | tf_op jit(solution)/shard_map/ppermute | solution.py:1002
  25.0 9.3 %copy-start.10 = (bf16[288,128]{1,0:T(8,128)(2,1)}, bf16[288,128]{1,0:T(8,128)(2,1)S(1)}, u32[]{:S(2)}) copy-start(bf16[288,128]{1,0:T(8,128)(2,1)S(1)} %collective-permute-done.4.refs_6_.refs_11_) | copy-start | bytes 221188
  25.0 7.2 %collective-permute-start.9 = (bf16[288,128]{1,0:T(8,128)(2,1)S(1)}, bf16[288,128]{1,0:T(8,128)(2,1)S(1)}, u32[]{:S(2)}, u32[]{:S(2)}) collective-permute-start(bf16[288,128]{1,0:T(8,128)(2,1)S(1)} %copy-done.8), channel_id=1, source_target_pairs={{0,28},{4,24},{8,20},{12,16},{16,12},{20,8},{24,4},{28,0},{1,29},{... | collective-permute-start | bytes 221192 | tf_op jit(solution)/shard_map/ppermute | solution.py:1002
  25.1 9.2 %copy-start.11 = (bf16[288,128]{1,0:T(8,128)(2,1)}, bf16[288,128]{1,0:T(8,128)(2,1)S(1)}, u32[]{:S(2)}) copy-start(bf16[288,128]{1,0:T(8,128)(2,1)S(1)} %collective-permute-done.5.refs_7_.refs_12_) | copy-start | bytes 221188
  25.1 8.6 %collective-permute-start = (bf16[2,16,4096]{2,1,0:T(8,128)(2,1)S(1)}, bf16[2,16,4096]{2,1,0:T(8,128)(2,1)S(1)}, u32[]{:S(2)}, u32[]{:S(2)}) collective-permute-start(bf16[2,16,4096]{2,1,0:T(8,128)(2,1)S(1)} %get-tuple-element.111), channel_id=1, source_target_pairs={{0,1},{1,0},{2,3},{3,2},{4,5},{5,4},{6,7},{7,6},{8,9},{9,8},{10,11... | collective-permute-start | bytes 786440 | tf_op jit(solution)/shard_map/ppermute | solution.py:979
  25.1 9.2 %copy-start.12 = (bf16[288,128]{1,0:T(8,128)(2,1)}, bf16[288,128]{1,0:T(8,128)(2,1)S(1)}, u32[]{:S(2)}) copy-start(bf16[288,128]{1,0:T(8,128)(2,1)S(1)} %collective-permute-done.6.refs_8_.refs_13_) | copy-start | bytes 221188
  25.1 12.9 %collective-permute-start.1 = (bf16[2,16,4096]{2,1,0:T(8,128)(2,1)S(1)}, bf16[2,16,4096]{2,1,0:T(8,128)(2,1)S(1)}, u32[]{:S(2)}, u32[]{:S(2)}) collective-permute-start(bf16[2,16,4096]{2,1,0:T(8,128)(2,1)S(1)} %get-tuple-element.113), channel_id=1, source_target_pairs={{0,2},{1,3},{2,0},{3,1},{4,6},{5,7},{6,4},{7,5},{8,10},{9,11},{10,... | collective-permute-start | bytes 786440 | tf_op jit(solution)/shard_map/ppermute | solution.py:979
  29.5 4.8 %copy-start.13 = (bf16[288,128]{1,0:T(8,128)(2,1)}, bf16[288,128]{1,0:T(8,128)(2,1)S(1)}, u32[]{:S(2)}) copy-start(bf16[288,128]{1,0:T(8,128)(2,1)S(1)} %collective-permute-done.7.refs_9_.refs_14_) | copy-start | bytes 221188
  29.5 9.5 %collective-permute-start.2 = (bf16[2,16,4096]{2,1,0:T(8,128)(2,1)S(1)}, bf16[2,16,4096]{2,1,0:T(8,128)(2,1)S(1)}, u32[]{:S(2)}, u32[]{:S(2)}) collective-permute-start(bf16[2,16,4096]{2,1,0:T(8,128)(2,1)S(1)} %get-tuple-element.110), channel_id=1, source_target_pairs={{0,3},{1,2},{2,1},{3,0},{4,7},{5,6},{6,5},{7,4},{8,11},{9,10},{10,... | collective-permute-start | bytes 786440 | tf_op jit(solution)/shard_map/ppermute | solution.py:979
  30.4 3.9 %copy-start.14 = (bf16[288,128]{1,0:T(8,128)(2,1)}, bf16[288,128]{1,0:T(8,128)(2,1)S(1)}, u32[]{:S(2)}) copy-start(bf16[288,128]{1,0:T(8,128)(2,1)S(1)} %collective-permute-done.8.refs_10_.refs_15_) | copy-start | bytes 221188
  30.4 31.7 %collective-permute-start.13 = (bf16[2,16,4096]{2,1,0:T(8,128)(2,1)}, bf16[2,16,4096]{2,1,0:T(8,128)(2,1)S(1)}, u32[]{:S(2)}, u32[]{:S(2)}) collective-permute-start(bf16[2,16,4096]{2,1,0:T(8,128)(2,1)} %get-tuple-element.104), channel_id=1, source_target_pairs={{0,1},{1,0},{2,3},{3,2},{4,5},{5,4},{6,7},{7,6},{8,9},{9,8},{10,11... | collective-permute-start | bytes 786440 | tf_op jit(solution)/shard_map/ppermute | solution.py:979
  32.1 2.2 %copy-start.15 = (bf16[288,128]{1,0:T(8,128)(2,1)}, bf16[288,128]{1,0:T(8,128)(2,1)S(1)}, u32[]{:S(2)}) copy-start(bf16[288,128]{1,0:T(8,128)(2,1)S(1)} %collective-permute-done.9.refs_11_.refs_16_) | copy-start | bytes 221188
  32.1 30.0 %collective-permute-start.14 = (bf16[2,16,4096]{2,1,0:T(8,128)(2,1)S(1)}, bf16[2,16,4096]{2,1,0:T(8,128)(2,1)S(1)}, u32[]{:S(2)}, u32[]{:S(2)}) collective-permute-start(bf16[2,16,4096]{2,1,0:T(8,128)(2,1)S(1)} %get-tuple-element.106), channel_id=1, source_target_pairs={{0,2},{1,3},{2,0},{3,1},{4,6},{5,7},{6,4},{7,5},{8,10},{9,11},{10,... | collective-permute-start | bytes 786440 | tf_op jit(solution)/shard_map/ppermute | solution.py:979
  33.7 5.4 %copy-start.4 = (bf16[2,16,4096]{2,1,0:T(8,128)(2,1)}, bf16[2,16,4096]{2,1,0:T(8,128)(2,1)S(1)}, u32[]{:S(2)}) copy-start(bf16[2,16,4096]{2,1,0:T(8,128)(2,1)S(1)} %collective-permute-done.refs_2_.refs_6_) | copy-start | bytes 786436
  33.7 28.5 %collective-permute-start.15 = (bf16[2,16,4096]{2,1,0:T(8,128)(2,1)S(1)}, bf16[2,16,4096]{2,1,0:T(8,128)(2,1)S(1)}, u32[]{:S(2)}, u32[]{:S(2)}) collective-permute-start(bf16[2,16,4096]{2,1,0:T(8,128)(2,1)S(1)} %get-tuple-element.103), channel_id=1, source_target_pairs={{0,3},{1,2},{2,1},{3,0},{4,7},{5,6},{6,5},{7,4},{8,11},{9,10},{10,... | collective-permute-start | bytes 786440 | tf_op jit(solution)/shard_map/ppermute | solution.py:979
  38.0 1.0 copy-start.5
  39.0 0.7 copy-start.6
  62.2 0.7 copy-start.16
  62.2 0.8 copy-start.17
  62.2 0.8 copy-start.18
  84.6 19.7 %copy-start.3 = (bf16[4,2,16,4096]{3,2,1,0:T(8,128)(2,1)S(1)}, bf16[4,2,16,4096]{3,2,1,0:T(8,128)(2,1)}, u32[]{:S(2)}) copy-start(bf16[4,2,16,4096]{3,2,1,0:T(8,128)(2,1)} %get-tuple-element.64) | copy-start | bytes 3145732
  95.6 9.6 %copy-start.2 = (bf16[4,2,16,4096]{3,2,1,0:T(8,128)(2,1)S(1)}, bf16[4,2,16,4096]{3,2,1,0:T(8,128)(2,1)}, u32[]{:S(2)}) copy-start(bf16[4,2,16,4096]{3,2,1,0:T(8,128)(2,1)} %get-tuple-element.56) | copy-start | bytes 3145732
  96.7 9.2 %collective-permute-start.19 = (bf16[216,128]{1,0:T(8,128)(2,1)S(1)}, bf16[216,128]{1,0:T(8,128)(2,1)S(1)}, u32[]{:S(2)}, u32[]{:S(2)}) collective-permute-start(bf16[216,128]{1,0:T(8,128)(2,1)S(1)} %get-tuple-element.120), channel_id=1, source_target_pairs={{0,4},{4,0},{8,12},{12,8},{16,20},{20,16},{24,28},{28,24},{1,5},{5... | collective-permute-start | bytes 165896 | tf_op jit(solution)/shard_map/ppermute | solution.py:1002
  98.5 11.0 %collective-permute-start.20 = (bf16[216,128]{1,0:T(8,128)(2,1)S(1)}, bf16[216,128]{1,0:T(8,128)(2,1)S(1)}, u32[]{:S(2)}, u32[]{:S(2)}) collective-permute-start(bf16[216,128]{1,0:T(8,128)(2,1)S(1)} %get-tuple-element.119), channel_id=1, source_target_pairs={{0,8},{4,12},{8,0},{12,4},{16,24},{20,28},{24,16},{28,20},{1,9},{5... | collective-permute-start | bytes 165896 | tf_op jit(solution)/shard_map/ppermute | solution.py:1002
  98.5 12.4 %collective-permute-start.21 = (bf16[216,128]{1,0:T(8,128)(2,1)S(1)}, bf16[216,128]{1,0:T(8,128)(2,1)S(1)}, u32[]{:S(2)}, u32[]{:S(2)}) collective-permute-start(bf16[216,128]{1,0:T(8,128)(2,1)S(1)} %get-tuple-element.118), channel_id=1, source_target_pairs={{0,12},{4,8},{8,4},{12,0},{16,28},{20,24},{24,20},{28,16},{1,13},{... | collective-permute-start | bytes 165896 | tf_op jit(solution)/shard_map/ppermute | solution.py:1002
  100.3 10.6 %collective-permute-start.22 = (bf16[216,128]{1,0:T(8,128)(2,1)S(1)}, bf16[216,128]{1,0:T(8,128)(2,1)S(1)}, u32[]{:S(2)}, u32[]{:S(2)}) collective-permute-start(bf16[216,128]{1,0:T(8,128)(2,1)S(1)} %get-tuple-element.117), channel_id=1, source_target_pairs={{0,16},{4,20},{8,24},{12,28},{16,0},{20,4},{24,8},{28,12},{1,17},{... | collective-permute-start | bytes 165896 | tf_op jit(solution)/shard_map/ppermute | solution.py:1002
  102.5 10.1 %collective-permute-start.23 = (bf16[216,128]{1,0:T(8,128)(2,1)S(1)}, bf16[216,128]{1,0:T(8,128)(2,1)S(1)}, u32[]{:S(2)}, u32[]{:S(2)}) collective-permute-start(bf16[216,128]{1,0:T(8,128)(2,1)S(1)} %get-tuple-element.116), channel_id=1, source_target_pairs={{0,20},{4,16},{8,28},{12,24},{16,4},{20,0},{24,12},{28,8},{1,21},{... | collective-permute-start | bytes 165896 | tf_op jit(solution)/shard_map/ppermute | solution.py:1002
  106.0 11.0 %copy-start.20 = (bf16[216,128]{1,0:T(8,128)(2,1)}, bf16[216,128]{1,0:T(8,128)(2,1)S(1)}, u32[]{:S(2)}) copy-start(bf16[216,128]{1,0:T(8,128)(2,1)S(1)} %collective-permute-done.19.refs_2_) | copy-start | bytes 165892
  106.0 6.8 %collective-permute-start.24 = (bf16[216,128]{1,0:T(8,128)(2,1)S(1)}, bf16[216,128]{1,0:T(8,128)(2,1)S(1)}, u32[]{:S(2)}, u32[]{:S(2)}) collective-permute-start(bf16[216,128]{1,0:T(8,128)(2,1)S(1)} %get-tuple-element.115), channel_id=1, source_target_pairs={{0,24},{4,28},{8,16},{12,20},{16,8},{20,12},{24,0},{28,4},{1,25},{... | collective-permute-start | bytes 165896 | tf_op jit(solution)/shard_map/ppermute | solution.py:1002
  109.5 7.5 %copy-start.21 = (bf16[216,128]{1,0:T(8,128)(2,1)}, bf16[216,128]{1,0:T(8,128)(2,1)S(1)}, u32[]{:S(2)}) copy-start(bf16[216,128]{1,0:T(8,128)(2,1)S(1)} %collective-permute-done.20.refs_3_) | copy-start | bytes 165892
  109.5 6.9 %collective-permute-start.25 = (bf16[216,128]{1,0:T(8,128)(2,1)S(1)}, bf16[216,128]{1,0:T(8,128)(2,1)S(1)}, u32[]{:S(2)}, u32[]{:S(2)}) collective-permute-start(bf16[216,128]{1,0:T(8,128)(2,1)S(1)} %get-tuple-element.114), channel_id=1, source_target_pairs={{0,28},{4,24},{8,20},{12,16},{16,12},{20,8},{24,4},{28,0},{1,29},{... | collective-permute-start | bytes 165896 | tf_op jit(solution)/shard_map/ppermute | solution.py:1002
  110.8 5.5 %copy-start.22 = (bf16[216,128]{1,0:T(8,128)(2,1)}, bf16[216,128]{1,0:T(8,128)(2,1)S(1)}, u32[]{:S(2)}) copy-start(bf16[216,128]{1,0:T(8,128)(2,1)S(1)} %collective-permute-done.21.refs_4_) | copy-start | bytes 165892
  110.8 13.2 %collective-permute-start.16 = (bf16[2,16,4096]{2,1,0:T(8,128)(2,1)}, bf16[2,16,4096]{2,1,0:T(8,128)(2,1)}, u32[]{:S(2)}, u32[]{:S(2)}) collective-permute-start(bf16[2,16,4096]{2,1,0:T(8,128)(2,1)} %get-tuple-element.102), channel_id=1, source_target_pairs={{0,1},{1,0},{2,3},{3,2},{4,5},{5,4},{6,7},{7,6},{8,9},{9,8},{10,11... | collective-permute-start | bytes 786440 | tf_op jit(solution)/shard_map/ppermute | solution.py:979
  110.9 5.4 %copy-start.23 = (bf16[216,128]{1,0:T(8,128)(2,1)}, bf16[216,128]{1,0:T(8,128)(2,1)S(1)}, u32[]{:S(2)}) copy-start(bf16[216,128]{1,0:T(8,128)(2,1)S(1)} %collective-permute-done.22.refs_5_) | copy-start | bytes 165892
  110.9 14.4 %collective-permute-start.17 = (bf16[2,16,4096]{2,1,0:T(8,128)(2,1)}, bf16[2,16,4096]{2,1,0:T(8,128)(2,1)}, u32[]{:S(2)}, u32[]{:S(2)}) collective-permute-start(bf16[2,16,4096]{2,1,0:T(8,128)(2,1)} %get-tuple-element.101), channel_id=1, source_target_pairs={{0,2},{1,3},{2,0},{3,1},{4,6},{5,7},{6,4},{7,5},{8,10},{9,11},{10,... | collective-permute-start | bytes 786440 | tf_op jit(solution)/shard_map/ppermute | solution.py:979
  112.6 3.8 %copy-start.24 = (bf16[216,128]{1,0:T(8,128)(2,1)}, bf16[216,128]{1,0:T(8,128)(2,1)S(1)}, u32[]{:S(2)}) copy-start(bf16[216,128]{1,0:T(8,128)(2,1)S(1)} %collective-permute-done.23.refs_6_) | copy-start | bytes 165892
  112.6 15.4 %collective-permute-start.18 = (bf16[2,16,4096]{2,1,0:T(8,128)(2,1)}, bf16[2,16,4096]{2,1,0:T(8,128)(2,1)}, u32[]{:S(2)}, u32[]{:S(2)}) collective-permute-start(bf16[2,16,4096]{2,1,0:T(8,128)(2,1)} %get-tuple-element.100), channel_id=1, source_target_pairs={{0,3},{1,2},{2,1},{3,0},{4,7},{5,6},{6,5},{7,4},{8,11},{9,10},{10,... | collective-permute-start | bytes 786440 | tf_op jit(solution)/shard_map/ppermute | solution.py:979
  112.8 0.6 copy-start.25
  113.4 15.6 %collective-permute-start.10 = (bf16[2,16,4096]{2,1,0:T(8,128)(2,1)}, bf16[2,16,4096]{2,1,0:T(8,128)(2,1)S(1)}, u32[]{:S(2)}, u32[]{:S(2)}) collective-permute-start(bf16[2,16,4096]{2,1,0:T(8,128)(2,1)} %get-tuple-element.109), channel_id=1, source_target_pairs={{0,1},{1,0},{2,3},{3,2},{4,5},{5,4},{6,7},{7,6},{8,9},{9,8},{10,11... | collective-permute-start | bytes 786440 | tf_op jit(solution)/shard_map/ppermute | solution.py:979
  116.3 0.6 copy-start.26
  119.7 1.8 %collective-permute-start.26 = (f32[344,128]{1,0:T(8,128)}, f32[344,128]{1,0:T(8,128)S(1)}, u32[]{:S(2)}, u32[]{:S(2)}) collective-permute-start(f32[344,128]{1,0:T(8,128)} %reduce.1), channel_id=1, source_target_pairs={{0,1},{1,0},{2,3},{3,2},{4,5},{5,4},{6,7},{7,6},{8,9},{9,8},{10,11... | collective-permute-start | bytes 528392 | tf_op jit(solution)/shard_map/ppermute | solution.py:979
  121.5 10.1 %collective-permute-start.11 = (bf16[2,16,4096]{2,1,0:T(8,128)(2,1)S(1)}, bf16[2,16,4096]{2,1,0:T(8,128)(2,1)S(1)}, u32[]{:S(2)}, u32[]{:S(2)}) collective-permute-start(bf16[2,16,4096]{2,1,0:T(8,128)(2,1)S(1)} %get-tuple-element.108), channel_id=1, source_target_pairs={{0,2},{1,3},{2,0},{3,1},{4,6},{5,7},{6,4},{7,5},{8,10},{9,11},{10,... | collective-permute-start | bytes 786440 | tf_op jit(solution)/shard_map/ppermute | solution.py:979
  124.0 16.5 %copy-start.7 = (f32[344,128]{1,0:T(8,128)}, f32[344,128]{1,0:T(8,128)S(1)}, u32[]{:S(2)}) copy-start(f32[344,128]{1,0:T(8,128)S(1)} %add.14.refs_0_) | copy-start | bytes 528388
  124.0 12.3 %collective-permute-start.12 = (bf16[2,16,4096]{2,1,0:T(8,128)(2,1)S(1)}, bf16[2,16,4096]{2,1,0:T(8,128)(2,1)S(1)}, u32[]{:S(2)}, u32[]{:S(2)}) collective-permute-start(bf16[2,16,4096]{2,1,0:T(8,128)(2,1)S(1)} %get-tuple-element.107), channel_id=1, source_target_pairs={{0,3},{1,2},{2,1},{3,0},{4,7},{5,6},{6,5},{7,4},{8,11},{9,10},{10,... | collective-permute-start | bytes 786440 | tf_op jit(solution)/shard_map/ppermute | solution.py:979
  125.4 15.1 %collective-permute-start.27 = (f32[344,128]{1,0:T(8,128)S(1)}, f32[344,128]{1,0:T(8,128)S(1)}, u32[]{:S(2)}, u32[]{:S(2)}) collective-permute-start(f32[344,128]{1,0:T(8,128)S(1)} %add.14.refs_0_), channel_id=1, source_target_pairs={{0,2},{1,3},{2,0},{3,1},{4,6},{5,7},{6,4},{7,5},{8,10},{9,11},{10,... | collective-permute-start | bytes 528392 | tf_op jit(solution)/shard_map/ppermute | solution.py:979
  129.0 21.3 %copy-start = (f32[8,16,4096]{2,1,0:T(8,128)}, f32[8,16,4096]{2,1,0:T(8,128)S(1)}, u32[]{:S(2)}) copy-start(f32[8,16,4096]{2,1,0:T(8,128)S(1)} %convert_dynamic-update-slice_fusion.1) | copy-start | bytes 6291460
  140.5 0.7 copy-start.19

commit v2 on v1

--- a/solution.py
+++ b/solution.py
@@ -112,11 +112,11 @@
 
 
 def store_strips(member, image, strips):
-    for offset in range(strips.shape[0]):
-        rows = strips.shape[2]
+    for offset, strip in enumerate(strips):
+        rows = strip.shape[1]
         start = strip_start(member, offset, rows)
         for j in range(PAIRS):
-            strips[offset, 0, :, j * LANES : (j + 1) * LANES] = image[j, pl.ds(start, rows), :].astype(strips.dtype)
+            strip[0, :, j * LANES : (j + 1) * LANES] = image[j, pl.ds(start, rows), :].astype(strip.dtype)
 
 
 def parity_rows(image, parity, j):
@@ -127,8 +127,9 @@
     member_ref = refs[0]
     strips = refs[1 : 1 + count]
     styles, biases, w_one, w_two, w_down, w_up = refs[1 + count : 7 + count]
-    out, win_one, win_two, win_level, win_coarse, middle, down, stats = refs[7 + count : 15 + count]
-    image, level = refs[15 + count :]
+    out = refs[7 + count : 7 + 2 * count]
+    win_one, win_two, win_level, win_coarse, middle, down, stats = refs[7 + 2 * count : 14 + 2 * count]
+    image, level = refs[14 + 2 * count :]
     member = member_ref[0]
     win_one, win_two, win_level, win_coarse = (ref.at[0] for ref in (win_one, win_two, win_level, win_coarse))
     middle, down = middle.at[0], down.at[0]
@@ -220,8 +221,9 @@
     cot_strips = refs[1 : 1 + count]
     frame_strips = refs[1 + count : 1 + 2 * count]
     styles, stats, middle, down, w_up, w_down, w_two, w_one = refs[1 + 2 * count : 9 + 2 * count]
-    out, tile_out, tile_level, tile_mid, coarse_pairs, pieces, bias_sums = refs[9 + 2 * count : 16 + 2 * count]
-    image, level_grad, pre_grad, windows, coarse_below, row_sums = refs[16 + 2 * count :]
+    out = refs[9 + 2 * count : 9 + 3 * count]
+    tile_out, tile_level, tile_mid, coarse_pairs, pieces, bias_sums = refs[9 + 3 * count : 15 + 3 * count]
+    image, level_grad, pre_grad, windows, coarse_below, row_sums = refs[15 + 3 * count :]
     member = member_ref[0]
     tile_out, tile_level, tile_mid, coarse_pairs = (ref.at[0] for ref in (tile_out, tile_level, tile_mid, coarse_pairs))
     middle, down = middle.at[0], down.at[0]
@@ -400,9 +402,10 @@
 
 def message_kernel(count, rows, *refs):
     where_ref, wins, tiles = refs[0], refs[1:5], refs[5:9]
-    pieces, bias_sums, own, messages = refs[9:13]
-    sums = refs[13:17]
-    g_pair, g_up, g_down, small = refs[17:]
+    pieces, bias_sums = refs[9:11]
+    outs = refs[11 : 11 + count]
+    sums = refs[11 + count : 15 + count]
+    g_pair, g_up, g_down, small = refs[15 + count :]
     sum_one, sum_two, sum_down, sum_up = sums
     accumulate(wins, tiles, sums)
 
@@ -450,10 +453,7 @@
                 ],
                 axis=0,
             )
-            if offset == 0:
-                own[...] = block
-            else:
-                messages[offset - 1] = block.astype(bf16)
+            outs[offset][...] = block.astype(outs[offset].dtype)
 
 
 def reduce_kernel(count, rows, cells, frames, *refs):
@@ -516,16 +516,20 @@
     out[at : at + 8, :] = pltpu.roll(bias, (C - place * width) % LANES, axis=1)
 
 
-def finish_kernel(rows, cells, width, first, second, *outs):
+def finish_kernel(rows, cells, first, second, *outs):
     act_grad, noise_grad, ada_one, ada_two, g_one, g_two, g_down, g_up = outs[:8]
-    bias_grads = outs[8]
+    bias_grads = outs[8:12]
     sums = first[...] + second[...]
-    pair, halves, down = (sums[k * rows : (k + 1) * rows] for k in range(3))
-    g_one[...] = pair[:, :C]
-    g_two[...] = swap_halves(pair)[:, :C]
-    g_up[:rows, :] = halves[:, :C]
-    g_up[rows:, :] = swap_halves(halves)[:, :C]
-    g_down[...] = down[:, :C]
+
+    def turn(block):
+        return jnp.concatenate([block, jnp.zeros((LANES - rows, LANES), f32)], axis=0).T[:, :rows]
+
+    pair, halves, down = (turn(sums[k * rows : (k + 1) * rows]) for k in range(3))
+    g_one[...] = pair[:C]
+    g_two[...] = pair[C:]
+    g_up[:, :rows] = halves[:C]
+    g_up[:, rows:] = halves[C:]
+    g_down[...] = down[:C]
     at = 3 * rows
     ada_one[...] = sums[at : at + cells]
     ada_two[...] = sums[at + cells : at + 2 * cells]
@@ -533,7 +537,8 @@
     act_grad[...] = sums[at + ACT_ROW : at + ACT_ROW + NACT, :cells]
     noise_grad[...] = sums[at + NOISE_ROW : at + NOISE_ROW + NLEV, :cells]
     at = at + TABLE_ROWS
-    bias_grads[...] = sums[at : at + 4, :width]
+    for k, ref in enumerate(bias_grads):
+        ref[...] = sums[at + k : at + k + 1, : ref.shape[0]].reshape(ref.shape)
 
 
 def write_operands(block, f_one, f_two, f_down, f_up, b_one, b_two, b_down, b_up):
@@ -620,17 +625,42 @@
     return 3 * rows, 3 * rows + 2 * cells, -(-(3 * rows + 2 * cells) // 16) * 16
 
 
-def pack_kernel(conv_one, conv_two, down_kernel, up_kernel, ada_one, ada_two, act_table, noise_table, biases, ids, out, work):
-    rows, cells = conv_one.shape[0], ada_one.shape[0]
+def turned(values):
+    wide = jnp.concatenate([values, jnp.zeros((C, LANES - values.shape[1]), f32)], axis=1)
+    return jnp.concatenate([wide, jnp.zeros((C, LANES), f32)], axis=0).T[: values.shape[1]]
+
+
+def pack_kernel(*refs):
+    actions, noise_ids, valid, conv_one, conv_two, down_kernel, up_kernel, ada_one, ada_two = refs[:9]
+    act_table, noise_table = refs[9:11]
+    biases = refs[11:15]
+    out, work = refs[15:]
+    rows, cells = conv_one.shape[1], ada_one.shape[0]
     style_at, end, _ = pack_sizes(rows, cells)
+    wide = lambda ref: ref[...].astype(f32)
+    low_lanes = lane_ids((rows, LANES)) < C
+    up = wide(up_kernel)
     work[...] = jnp.zeros_like(work)
-    wide = lambda ref: ref[...].astype(f32)
-    work[:rows, :] = jnp.concatenate([wide(conv_one), wide(conv_two)], axis=1)
-    work[rows : 2 * rows, :] = jnp.concatenate([wide(up_kernel)[:rows], wide(up_kernel)[rows:]], axis=1)
-    work[2 * rows : 3 * rows, :C] = wide(down_kernel)
-    for at, ref in ((ACT_ROW, act_table), (NOISE_ROW, noise_table), (BIAS_ROW, biases), (ID_ROW, ids)):
+    for at, low, high in (
+        (0, turned(wide(conv_one)), turned(wide(conv_two))),
+        (rows, turned(up[:, :rows]), turned(up[:, rows:])),
+    ):
+        work[at : at + rows, :] = jnp.where(low_lanes, low, swap_halves(high))
+    work[2 * rows : 3 * rows, :] = turned(wide(down_kernel))
+    extra = 2 * rows
+    for at, ref in ((ACT_ROW, act_table), (NOISE_ROW, noise_table)):
         size = ref.shape
-        work[2 * rows + at : 2 * rows + at + size[0], C : C + size[1]] = wide(ref)
+        work[extra + at : extra + at + size[0], C : C + size[1]] = wide(ref)
+    for k, ref in enumerate(biases):
+        at = extra + BIAS_ROW + k
+        work[at : at + 1, C : C + ref.shape[0]] = wide(ref).reshape(1, ref.shape[0])
+    lanes = lane_ids((1, LANES))
+    for k, ref in enumerate((actions, noise_ids, valid)):
+        line = jnp.zeros((1, LANES), jnp.int32)
+        for f in range(ref.shape[0]):
+            line = jnp.where(lanes == C + f, ref[f], line)
+        at = extra + ID_ROW + k
+        work[at : at + 1, C:] = line.astype(f32)[:, C:]
     work[style_at : style_at + cells, :] = wide(ada_one)
     work[style_at + cells : end, :] = wide(ada_two)
     out[...] = work[...].astype(bf16)
@@ -724,10 +754,6 @@
     return [pl.BlockSpec((1, strip, W * C), lambda f: (f, 0, 0))] * count
 
 
-def out_strips(count, strip):
-    return pl.BlockSpec((count, 1, strip, W * C), lambda f: (0, f, 0, 0))
-
-
 SMALL = (8, LANES)
 WINDOWS = (4, PAIRS + 1, HALF, LANES)
 COARSE_WINDOWS = (3, PAIRS + 1, HALF, LANES)
@@ -739,6 +765,10 @@
 
 def params():
     return pltpu.CompilerParams(vmem_limit_bytes=VMEM_LIMIT)
+
+
+def cost(macs, moved):
+    return pl.CostEstimate(flops=2 * macs, bytes_accessed=moved, transcendentals=0)
 
 
 def expand(conv_one, conv_two, down_kernel, up_kernel):
@@ -772,10 +802,10 @@
         + strip_specs(count, strip)
         + [per_frame(SMALL), whole(SMALL)]
         + [whole(w.shape) for w in (w_one, w_two, w_down, w_up)],
-        out_specs=[out_strips(count, strip)]
+        out_specs=strip_specs(count, strip)
         + [per_frame(d) for d in (WINDOWS, WINDOWS, WINDOWS, COARSE_WINDOWS, TILES, COARSE, SMALL)],
-        out_shape=[
-            shape((count, frames, strip, W * C), bf16),
+        out_shape=[shape((frames, strip, W * C), bf16)] * count
+        + [
             shape((frames,) + WINDOWS, bf16),
             shape((frames,) + WINDOWS, bf16),
             shape((frames,) + WINDOWS, bf16),
@@ -786,6 +816,7 @@
         ],
         scratch_shapes=[pltpu.VMEM(IMAGE, f32), pltpu.VMEM(TILES, f32)],
         compiler_params=params(),
+        cost_estimate=cost(frames * BLOCK * KEYS * 2 * LANES * 5, frames * (14 << 20)),
         name="forward",
     )(member, *strips, styles, biases, w_one, w_two, w_down, w_up)
 
@@ -800,10 +831,10 @@
         + strip_specs(2 * count, strip)
         + [per_frame(d) for d in (SMALL, SMALL, TILES, COARSE)]
         + [whole(w.shape) for w in (w_up, w_down, w_two, w_one)],
-        out_specs=[out_strips(count, strip)]
+        out_specs=strip_specs(count, strip)
         + [per_frame(d) for d in (TILES, TILES, TILES, COARSE, SMALL, SMALL)],
-        out_shape=[
-            shape((count, frames, strip, W * C), bf16),
+        out_shape=[shape((frames, strip, W * C), bf16)] * count
+        + [
             shape((frames,) + TILES, bf16),
             shape((frames,) + TILES, bf16),
             shape((frames,) + TILES, bf16),
@@ -820,6 +851,7 @@
             pltpu.VMEM((HALF, LANES), f32),
         ],
         compiler_params=params(),
+        cost_estimate=cost(frames * BLOCK * KEYS * 2 * LANES * 5, frames * (10 << 20)),
         name="backward",
     )(member, *cot_strips, *frame_strips, styles, stats, middle, down, w_up, w_down, w_two, w_one)
 
@@ -841,6 +873,7 @@
             pltpu.VMEM((2 * KEYS, 2 * LANES), f32),
         ],
         compiler_params=params(),
+        cost_estimate=cost(frames * BLOCK * KEYS * 2 * LANES * 5, frames * (6 << 20)),
         name="weights",
     )(win_one, win_two, win_level, win_coarse, tile_out, tile_level, tile_mid, coarse_pairs)
 
@@ -853,18 +886,19 @@
     return pl.BlockSpec(memory_space=pltpu.SMEM)
 
 
-def pack(conv_one, conv_two, down_kernel, up_kernel, ada_one, ada_two, act_table, noise_table, biases, ids):
-    args = (conv_one, conv_two, down_kernel, up_kernel, ada_one, ada_two, act_table, noise_table, biases, ids)
+def pack(actions, noise_ids, valid, conv_one, conv_two, down_kernel, up_kernel, ada_one, ada_two, act_table, noise_table, *biases):
     _, _, size = pack_sizes(conv_one.shape[0], ada_one.shape[0])
+    kernels = [kernel.T for kernel in (conv_one, conv_two, down_kernel, up_kernel)]
+    args = (*kernels, ada_one, ada_two, act_table, noise_table, *biases)
     return pl.pallas_call(
         pack_kernel,
-        in_specs=[in_vmem()] * len(args),
+        in_specs=[in_smem()] * 3 + [in_vmem()] * len(args),
         out_specs=in_vmem(),
         out_shape=shape((size, LANES), bf16),
         scratch_shapes=[pltpu.VMEM((size, LANES), f32)],
         compiler_params=params(),
         name="pack",
-    )(*args)
+    )(actions, noise_ids, valid, *args)
 
 
 OPERANDS = (
@@ -907,8 +941,8 @@
         in_specs=[in_smem()]
         + [per_frame(d) for d in (WINDOWS, WINDOWS, WINDOWS, COARSE_WINDOWS, TILES, TILES, TILES, COARSE)]
         + [whole((frames,) + SMALL)] * 2,
-        out_specs=[whole((3 * rows, LANES)), whole((count - 1, 3 * rows, LANES))],
-        out_shape=[shape((3 * rows, LANES), f32), shape((count - 1, 3 * rows, LANES), bf16)],
+        out_specs=[whole((3 * rows, LANES))] * count,
+        out_shape=[shape((3 * rows, LANES), f32)] + [shape((3 * rows, LANES), bf16)] * (count - 1),
         scratch_shapes=[
             pltpu.VMEM((KEYS, 2 * LANES), f32),
             pltpu.VMEM((KEYS, 2 * LANES), f32),
@@ -920,6 +954,7 @@
             pltpu.VMEM((PARTS, LANES), f32),
         ],
         compiler_params=params(),
+        cost_estimate=cost(frames * BLOCK * KEYS * 2 * LANES * 5, frames * (6 << 20)),
         name="weights",
     )(where, *wins, *tiles, pieces, bias_sums)
 
@@ -942,24 +977,50 @@
 
 
 def finish(first, second, rows, cells, width):
-    return pl.pallas_call(
-        lambda *refs: finish_kernel(rows, cells, width, *refs),
+    act_grad, noise_grad, one, two, *rest = pl.pallas_call(
+        lambda *refs: finish_kernel(rows, cells, *refs),
         in_specs=[in_vmem()] * 2,
-        out_specs=[in_vmem()] * 9,
+        out_specs=[in_vmem()] * 12,
         out_shape=[
             shape((NACT, cells), f32),
             shape((NLEV, cells), f32),
             shape((cells, LANES), f32),
             shape((cells, LANES), f32),
-            shape((rows, C), f32),
-            shape((rows, C), f32),
-            shape((rows, C), f32),
-            shape((2 * rows, C), f32),
-            shape((4, width), f32),
-        ],
+            shape((C, rows), f32),
+            shape((C, rows), f32),
+            shape((C, rows), f32),
+            shape((C, 2 * rows), f32),
+        ]
+        + [shape((width,), f32)] * 4,
         compiler_params=params(),
         name="finish",
     )(first, second)
+    return (act_grad, noise_grad, one, two, *[grad.T for grad in rest[:4]], *rest[4:])
+
+
+def collect_kernel(member_ref, *refs):
+    strips, out = refs[:-1], refs[-1]
+    for offset, strip in enumerate(strips):
+        out[member_ref[0] ^ offset, 0] = strip[0].astype(out.dtype)
+
+
+def return_strips(strips):
+    return tuple(trade(strip, offset) for offset, strip in enumerate(strips))
+
+
+def collect_strips(member_box, strips, kind):
+    count = len(strips)
+    frames, rows, columns = strips[0].shape
+    whole_strips = pl.pallas_call(
+        collect_kernel,
+        grid=(frames,),
+        in_specs=[in_smem()] + [pl.BlockSpec((1, rows, columns), lambda f: (f, 0, 0))] * count,
+        out_specs=pl.BlockSpec((count, 1, rows, columns), lambda f: (0, f, 0, 0)),
+        out_shape=shape((count, frames, rows, columns), kind),
+        compiler_params=params(),
+        name="collect",
+    )(member_box, *strips)
+    return whole_strips.reshape(count * frames, rows, columns)
 
 
 def twice(values):
@@ -988,15 +1049,6 @@
     ]
 
 
-def collect_strips(strips, member, kind):
-    count, share = strips.shape[:2]
-    result = jnp.zeros((count * share,) + strips.shape[2:], kind)
-    for offset in range(count):
-        part = trade(strips[offset], offset).astype(kind)
-        result = lax.dynamic_update_slice_in_dim(result, part, (member ^ offset) * share, axis=0)
-    return result
-
-
 def seq_trade(value, offset):
     count = lax.axis_size("seq")
     return lax.ppermute(value, "seq", [(i, i ^ offset) for i in range(count)])
@@ -1005,17 +1057,18 @@
 def layers(member_box, frame_strips, cot_strips, styles, bias_rows, operands):
     f_one, f_two, f_down, f_up, b_one, b_two, b_down, b_up = operands
     member = member_box[0]
-    out, win_one, win_two, win_level, win_coarse, middle, down, stats = forward(
+    *out, win_one, win_two, win_level, win_coarse, middle, down, stats = forward(
         member_box, frame_strips, styles, bias_rows, f_one, f_two, f_down, f_up
     )
-    result = collect_strips(out, member, bf16)
-    grad_strips, tile_out, tile_level, tile_mid, coarse_pairs, pieces, bias_sums = backward(
+    out = return_strips(out)
+    *grad_strips, tile_out, tile_level, tile_mid, coarse_pairs, pieces, bias_sums = backward(
         member_box, cot_strips, frame_strips, styles, stats, middle, down, b_up, b_down, b_two, b_one
     )
-    frames_grad = collect_strips(grad_strips, member, f32)
+    grad_strips = return_strips(grad_strips)
     wins = (win_one, win_two, win_level, win_coarse)
     tiles = (tile_out, tile_level, tile_mid, coarse_pairs)
-    return result, frames_grad, wins, tiles, pieces, bias_sums
+    pieces, out = lax.optimization_barrier((pieces, out))
+    return out, grad_strips, wins, tiles, pieces, bias_sums
 
 
 def local_direct(
@@ -1044,25 +1097,41 @@
     rows, cells, width = conv_one.shape[0], ada_one.shape[0], bias_one.shape[0]
     member_box = member.reshape(1)
     where = jnp.stack([place, member])
-    biases = jnp.stack([bias_one, bias_two, bias_down, bias_up])
-    ids = jnp.stack([actions, noise_ids, valid])
-    packed = pack(conv_one, conv_two, down_kernel, up_kernel, ada_one, ada_two, act_table, noise_table, biases, ids)
+    packed = pack(
+        actions,
+        noise_ids,
+        valid,
+        conv_one,
+        conv_two,
+        down_kernel,
+        up_kernel,
+        ada_one,
+        ada_two,
+        act_table,
+        noise_table,
+        bias_one,
+        bias_two,
+        bias_down,
+        bias_up,
+    )
     packs = [packed] + [seq_trade(packed, offset) for offset in range(1, count)]
     frame_strips = spread_strips(frames, member)
     cot_strips = spread_strips(cotangent, member)
     *operands, styles, bias_rows = prepare(where, actions, noise_ids, valid, packs, rows, cells, share)
-    result, frames_grad, wins, tiles, pieces, bias_sums = layers(
+    out, grad_strips, wins, tiles, pieces, bias_sums = layers(
         member_box, frame_strips, cot_strips, styles, bias_rows, operands
     )
-    own, messages = weight_messages(where, wins, tiles, pieces, bias_sums, count, rows)
+    own, *messages = weight_messages(where, wins, tiles, pieces, bias_sums, count, rows)
+    messages, grad_strips = lax.optimization_barrier((messages, grad_strips))
     received = [seq_trade(messages[offset - 1], offset) for offset in range(1, count)]
     sums = reduce_messages(where, own, received, packs, act_table, noise_table, ada_one, ada_two, rows, cells, share)
     offset = 1
     while 2 * offset < lax.axis_size("rows"):
         sums = sums + trade(sums, offset)
         offset *= 2
-    *grads, bias_grads = finish(sums, trade(sums, offset), rows, cells, width)
-    return (result, frames_grad, *grads, bias_grads[0], bias_grads[1], bias_grads[2], bias_grads[3])
+    result = collect_strips(member_box, out, bf16)
+    frames_grad = collect_strips(member_box, grad_strips, f32)
+    return (result, frames_grad, *finish(sums, trade(sums, offset), rows, cells, width))
 
 
 def local_general(
@@ -1118,10 +1187,12 @@
         ]
     )
     bias_rows = pad_small([twice(biases[k]) for k in range(4)])
-    result, frames_grad, wins, tiles, pieces, bias_sums = layers(
+    out, grad_strips, wins, tiles, pieces, bias_sums = layers(
         member_box, frame_strips, cot_strips, styles, bias_rows, operands
     )
     g_one, g_two, g_down, g_up = weight_grads(*wins, *tiles)
+    result = collect_strips(member_box, out, bf16)
+    frames_grad = collect_strips(member_box, grad_strips, f32)
 
     pieces_one = jnp.concatenate([pieces[:, 0, :C], pieces[:, 1, :C]], axis=1)
     pieces_two = jnp.concatenate([pieces[:, 2, :C], pieces[:, 3, :C]], axis=1)

time: 151 us -> 125 us (0.83)
  local copies, waits for them, and re-layouts: 26.5 us -> 4.98 us
  other arithmetic: 8.04 us -> 1.52 us
  Pallas kernels: 64.7 us -> 68.4 us
    unnamed x62 -> x56, local copies, waits for them, and re-layouts: 15.3 us -> 2.2 us
    ppermute x14, waiting for transfers between devices: 10.3 us -> 3.24 us  [trade(): return lax.ppermute(value, 'rows', [(i, i ^ offset) for i in range(count)])]
    ppermute x14, waiting for transfers between devices: 5.37 us -> 11.1 us  [seq_trade(): return lax.ppermute(value, 'seq', [(i, i ^ offset) for i in range(count)])]
    pallas_call x2 -> x4, Pallas kernels: 3.28 us -> 8.31 us  [the longest x2 4.61 us: collect_strips(): pl.pallas_call(collect_kernel, grid=(frames,), in_specs=[in_smem()] + [pl...]
    squeeze x4 -> x0, local copies, waits for them, and re-layouts: 4.09 us -> none  [the longest x2 1.66 us: collect_strips(): part = trade(strips[offset], offset).astype(kind)]
    dynamic_update_slice x4 -> x0, other arithmetic: 3.95 us -> none  [collect_strips(): lax.dynamic_update_slice_in_dim(result, part, (member ^ offset) * share,...]
    dynamic_update_slice x4 -> x0, local copies, waits for them, and re-layouts: 2.95 us -> none  [collect_strips(): lax.dynamic_update_slice_in_dim(result, part, (member ^ offset) * share,...]
    another operation x2 -> x0, other arithmetic: 2.55 us -> none  [the longest x1 1.28 us: local_direct(): biases = jnp.stack([bias_one, bias_two, bias_down, bias_up])]
  transfers between devices with their start and end apart: 28 -> 28, of which waited for: 7 -> 8; matrix products, arithmetic and copies ran while one was open for 9% -> 3% of each run, Pallas kernels for 19% -> 50%
where the time goes in v2:
time: 125 us; the launch traced here: 124 us
  Pallas kernels  68.4 us (55%)
  starting transfers between devices  34.1 us (27%)
  waiting for transfers between devices  14.4 us (12%)
  local copies, waits for them, and re-layouts  4.98 us (4%)
  other arithmetic  1.52 us (1%)
    ppermute x14, starting transfers between devices, seq_trade(): return lax.ppermute(value, 'seq', [(i, i ^ offset) for i in range(count)])  24 us
    pallas_call x1, Pallas kernels, backward(): pl.pallas_call(lambda *refs: backward_kernel(count, *refs), grid=(frames,...  21.5 us
    pallas_call x1, Pallas kernels, forward(): pl.pallas_call(lambda *refs: forward_kernel(count, *refs), grid=(frames,)...  21.1 us
    ppermute x14, waiting for transfers between devices, seq_trade(): return lax.ppermute(value, 'seq', [(i, i ^ offset) for i in range(count)])  11.1 us
    pallas_call x1, Pallas kernels, weight_messages(): pl.pallas_call(lambda *refs: message_kernel(count, rows, *refs), grid=(fr...  11.1 us
    ppermute x14, starting transfers between devices, trade(): return lax.ppermute(value, 'rows', [(i, i ^ offset) for i in range(count)])  10.2 us
    pallas_call x2, Pallas kernels, collect_strips(): pl.pallas_call(collect_kernel, grid=(frames,), in_specs=[in_smem()] + [pl...  4.61 us
    pallas_call x1, Pallas kernels, prepare(): pl.pallas_call(lambda *refs: prepare_kernel(count, rows, cells, *refs), i...  3.67 us
  transfers between devices with their start and end apart: 28, of which 8 were waited for; matrix products, arithmetic and copies ran while one was open for 3% of the time, Pallas kernels for 50%

profile of v2, /device:TPU:0, one launch (start us, length us, event | category | flops | bytes accessed | tf_op | source)
XLA Modules:
  0.0 124.5 jit_solution(14819562695825032924)
XLA Ops:
  0.7 1.9 %pack.1.refs_4_.refs_9_ = bf16[288,128]{1,0:T(8,128)(2,1)} custom-call(s32[8]{0:T(128)} %refs_1_.3, s32[8]{0:T(128)} %refs_2_.3, s32[8]{0:T(128)} %refs_3_.1, bf16[64,72]{1,0:T(8,128)(2,1)} %bitcast.15, bf16[64,72]{1,0:T(8,128)(2,1)} %bitcast.16, bf16[64,72]{1,0:T(8,128)(2,1)} %bitcast.17, bf16[64,144]{1,0:T(8,128)(2,1)} %bitcast.14, ...), custom_call_target="tpu_custom_call" | custom-call | tf_op jit(solution)/shard_map/pack/pallas_call | solution.py:893
  2.5 6.0 %collective-permute-start.12 = (bf16[288,128]{1,0:T(8,128)(2,1)}, bf16[288,128]{1,0:T(8,128)(2,1)S(1)}, u32[]{:S(2)}, u32[]{:S(2)}) collective-permute-start(bf16[288,128]{1,0:T(8,128)(2,1)} %pack.1.refs_4_.refs_9_), channel_id=1, source_target_pairs={{0,28},{4,24},{8,20},{12,16},{16,12},{20,8},{24,4},{28,0},{1,29},{... | collective-permute-start | bytes 221192 | tf_op jit(solution)/shard_map/ppermute | solution.py:1054
  8.5 0.2 collective-permute-start.11
  8.7 0.8 collective-permute-start.10
  9.5 2.0 %collective-permute-start.9 = (bf16[288,128]{1,0:T(8,128)(2,1)}, bf16[288,128]{1,0:T(8,128)(2,1)S(1)}, u32[]{:S(2)}, u32[]{:S(2)}) collective-permute-start(bf16[288,128]{1,0:T(8,128)(2,1)} %pack.1.refs_4_.refs_9_), channel_id=1, source_target_pairs={{0,16},{4,20},{8,24},{12,28},{16,0},{20,4},{24,8},{28,12},{1,17},{... | collective-permute-start | bytes 221192 | tf_op jit(solution)/shard_map/ppermute | solution.py:1054
  11.5 2.3 %collective-permute-start.8 = (bf16[288,128]{1,0:T(8,128)(2,1)}, bf16[288,128]{1,0:T(8,128)(2,1)S(1)}, u32[]{:S(2)}, u32[]{:S(2)}) collective-permute-start(bf16[288,128]{1,0:T(8,128)(2,1)} %pack.1.refs_4_.refs_9_), channel_id=1, source_target_pairs={{0,12},{4,8},{8,4},{12,0},{16,28},{20,24},{24,20},{28,16},{1,13},{... | collective-permute-start | bytes 221192 | tf_op jit(solution)/shard_map/ppermute | solution.py:1054
  13.8 2.0 %constant_dynamic-slice_fusion = (bf16[2,16,4096]{2,1,0:T(8,128)(2,1)S(1)}, bf16[2,16,4096]{2,1,0:T(8,128)(2,1)S(1)}, bf16[2,16,4096]{2,1,0:T(8,128)(2,1)}, bf16[2,16,4096]{2,1,0:T(8,128)(2,1)S(1)}) fusion(bf16[8,16,4096]{2,1,0:T(8,128)(2,1)} %param.17, s32[]{:T(128)S(6)} %select_n.19, s32[]{:T(128)S(6)} %select_n.17, s32[]{:T(128)S(6)} %select_n.16, ...), kind=kLoop, calls=%fused_computation | loop fusion | bytes 2097168 | tf_op jit(solution)/shard_map/dynamic_slice | solution.py:1047
  15.8 0.0 collective-permute-done.12.refs_11_.refs_16_
  15.8 0.0 collective-permute-start.5
  15.8 1.6 %collective-permute-start.3 = (bf16[2,16,4096]{2,1,0:T(8,128)(2,1)S(1)}, bf16[2,16,4096]{2,1,0:T(8,128)(2,1)}, u32[]{:S(2)}, u32[]{:S(2)}) collective-permute-start(bf16[2,16,4096]{2,1,0:T(8,128)(2,1)S(1)} %get-tuple-element.149), channel_id=1, source_target_pairs={{0,1},{1,0},{2,3},{3,2},{4,5},{5,4},{6,7},{7,6},{8,9},{9,8},{10,11... | collective-permute-start | bytes 786440 | tf_op jit(solution)/shard_map/ppermute | solution.py:1040
  17.4 3.0 %collective-permute-done.10.refs_9_.refs_14_ = bf16[288,128]{1,0:T(8,128)(2,1)S(1)} collective-permute-done((bf16[288,128]{1,0:T(8,128)(2,1)}, bf16[288,128]{1,0:T(8,128)(2,1)S(1)}, u32[]{:S(2)}, u32[]{:S(2)}) %collective-permute-start.10) | collective-permute-done | bytes 73760 | tf_op jit(solution)/shard_map/ppermute | solution.py:1054
  20.4 1.5 %collective-permute-start.4 = (bf16[2,16,4096]{2,1,0:T(8,128)(2,1)S(1)}, bf16[2,16,4096]{2,1,0:T(8,128)(2,1)}, u32[]{:S(2)}, u32[]{:S(2)}) collective-permute-start(bf16[2,16,4096]{2,1,0:T(8,128)(2,1)S(1)} %get-tuple-element.151), channel_id=1, source_target_pairs={{0,2},{1,3},{2,0},{3,1},{4,6},{5,7},{6,4},{7,5},{8,10},{9,11},{10,... | collective-permute-start | bytes 786440 | tf_op jit(solution)/shard_map/ppermute | solution.py:1040
  22.0 0.8 constant_dynamic-slice_fusion.4
  22.8 0.1 collective-permute-start.7
  22.8 0.0 collective-permute-done.8.refs_7_.refs_12_
  22.9 1.5 %collective-permute-start.6 = (bf16[288,128]{1,0:T(8,128)(2,1)S(1)}, bf16[288,128]{1,0:T(8,128)(2,1)S(1)}, u32[]{:S(2)}, u32[]{:S(2)}) collective-permute-start(bf16[288,128]{1,0:T(8,128)(2,1)S(1)} %copy-done.2), channel_id=1, source_target_pairs={{0,4},{4,0},{8,12},{12,8},{16,20},{20,16},{24,28},{28,24},{1,5},{5... | collective-permute-start | bytes 221192 | tf_op jit(solution)/shard_map/ppermute | solution.py:1054
  24.3 0.6 pad_add_fusion.refs_0_
  24.9 2.3 %collective-permute-done.7.refs_6_.refs_11_ = bf16[288,128]{1,0:T(8,128)(2,1)S(1)} collective-permute-done((bf16[288,128]{1,0:T(8,128)(2,1)S(1)}, bf16[288,128]{1,0:T(8,128)(2,1)S(1)}, u32[]{:S(2)}, u32[]{:S(2)}) %collective-permute-start.7) | collective-permute-done | bytes 73760 | tf_op jit(solution)/shard_map/ppermute | solution.py:1054
  27.2 0.0 collective-permute-start.2
  27.2 0.1 collective-permute-done.6.refs_5_.refs_10_
  27.3 0.5 collective-permute-start
  27.8 0.1 copy-done.9
  27.9 3.7 %prepare.1 = (bf16[1024,256]{1,0:T(8,128)(2,1)}, bf16[1024,256]{1,0:T(8,128)(2,1)}, bf16[768,128]{1,0:T(8,128)(2,1)}, bf16[2048,256]{1,0:T(8,128)(2,1)}, bf16[10...) custom-call(s32[2]{0:T(128)} %pad_add_fusion.refs_0_, ...), custom_call_target="tpu_custom_call" | custom-call | tf_op jit(solution)/shard_map/prepare/pallas_call | solution.py:918
  31.6 1.5 %collective-permute-start.1 = (bf16[2,16,4096]{2,1,0:T(8,128)(2,1)S(1)}, bf16[2,16,4096]{2,1,0:T(8,128)(2,1)S(1)}, u32[]{:S(2)}, u32[]{:S(2)}) collective-permute-start(bf16[2,16,4096]{2,1,0:T(8,128)(2,1)S(1)} %get-tuple-element.155), channel_id=1, source_target_pairs={{0,2},{1,3},{2,0},{3,1},{4,6},{5,7},{6,4},{7,5},{8,10},{9,11},{10,... | collective-permute-start | bytes 786440 | tf_op jit(solution)/shard_map/ppermute | solution.py:1040
  33.1 0.0 collective-permute-done.3.refs_2_.refs_6_
  33.1 0.0 collective-permute-done.4.refs_3_.refs_7_
  33.2 21.1 %forward.1 = (bf16[2,16,4096]{2,1,0:T(8,128)(2,1)}, bf16[2,16,4096]{2,1,0:T(8,128)(2,1)}, bf16[2,16,4096]{2,1,0:T(8,128)(2,1)}, bf16[2,16,4096]{2,1,0:T(8,128)(2...) custom-call(s32[1]{0:T(128)} %bitcast.refs_0_.member_ref, ...), custom_call_target="tpu_custom_call" | custom-call | flops 5368709120 | bytes 29360128 | tf_op jit(solution)/shard_map/forward/pallas_call | solution.py:798
  54.2 0.4 collective-permute-start.13
  54.6 0.9 collective-permute-start.14
  55.5 0.7 collective-permute-start.15
  56.1 0.0 collective-permute-done.refs_2_
  56.2 0.0 collective-permute-done.1.refs_3_
  56.2 0.0 copy-done.25
  56.2 0.7 copy-done.26
  56.9 0.1 copy-done.27
  57.0 21.5 %backward.1 = (bf16[2,16,4096]{2,1,0:T(8,128)(2,1)}, bf16[2,16,4096]{2,1,0:T(8,128)(2,1)}, bf16[2,16,4096]{2,1,0:T(8,128)(2,1)}, bf16[2,16,4096]{2,1,0:T(8,128)(...) custom-call(s32[1]{0:T(128)} %bitcast.refs_0_.member_ref, ...), custom_call_target="tpu_custom_call" | custom-call | flops 5368709120 | bytes 20971520 | tf_op jit(solution)/shard_map/backward/pallas_call | solution.py:827
  78.5 0.6 collective-permute-start.16
  79.2 0.9 collective-permute-start.17
  80.1 0.0 collective-permute-done.13.refs_1_
  80.1 0.5 collective-permute-start.18
  80.6 0.0 collective-permute-done.15.refs_3_
  80.6 11.1 %weights.1 = (f32[216,128]{1,0:T(8,128)}, bf16[216,128]{1,0:T(8,128)(2,1)}, bf16[216,128]{1,0:T(8,128)(2,1)}, bf16[216,128]{1,0:T(8,128)(2,1)}, bf16[216,128]{1,...) custom-call(s32[2]{0:T(128)} %pad_add_fusion.refs_0_, ...), custom_call_target="tpu_custom_call" | custom-call | flops 5368709120 | bytes 12582912 | tf_op jit(solution)/shard_map/weights/pallas_call | solution.py:938
  91.8 0.0 collective-permute-done.17.refs_2_
  91.8 0.6 collective-permute-done.18.refs_3_
  92.4 1.4 %collective-permute-start.19 = (bf16[216,128]{1,0:T(8,128)(2,1)}, bf16[216,128]{1,0:T(8,128)(2,1)S(1)}, u32[]{:S(2)}, u32[]{:S(2)}) collective-permute-start(bf16[216,128]{1,0:T(8,128)(2,1)} %get-tuple-element.129), channel_id=1, source_target_pairs={{0,4},{4,0},{8,12},{12,8},{16,20},{20,16},{24,28},{28,24},{1,5},{5... | collective-permute-start | bytes 165896 | tf_op jit(solution)/shard_map/ppermute | solution.py:1054
  93.8 1.0 collective-permute-start.20
  94.9 1.0 collective-permute-start.21
  95.9 2.0 %collective-permute-start.22 = (bf16[216,128]{1,0:T(8,128)(2,1)}, bf16[216,128]{1,0:T(8,128)(2,1)S(1)}, u32[]{:S(2)}, u32[]{:S(2)}) collective-permute-start(bf16[216,128]{1,0:T(8,128)(2,1)} %get-tuple-element.132), channel_id=1, source_target_pairs={{0,16},{4,20},{8,24},{12,28},{16,0},{20,4},{24,8},{28,12},{1,17},{... | collective-permute-start | bytes 165896 | tf_op jit(solution)/shard_map/ppermute | solution.py:1054
  97.9 1.8 %collective-permute-start.23 = (bf16[216,128]{1,0:T(8,128)(2,1)}, bf16[216,128]{1,0:T(8,128)(2,1)S(1)}, u32[]{:S(2)}, u32[]{:S(2)}) collective-permute-start(bf16[216,128]{1,0:T(8,128)(2,1)} %get-tuple-element.133), channel_id=1, source_target_pairs={{0,20},{4,16},{8,28},{12,24},{16,4},{20,0},{24,12},{28,8},{1,21},{... | collective-permute-start | bytes 165896 | tf_op jit(solution)/shard_map/ppermute | solution.py:1054
  99.7 0.0 collective-permute-done.19.refs_2_
  99.7 2.5 %collective-permute-start.24 = (bf16[216,128]{1,0:T(8,128)(2,1)}, bf16[216,128]{1,0:T(8,128)(2,1)S(1)}, u32[]{:S(2)}, u32[]{:S(2)}) collective-permute-start(bf16[216,128]{1,0:T(8,128)(2,1)} %get-tuple-element.134), channel_id=1, source_target_pairs={{0,24},{4,28},{8,16},{12,20},{16,8},{20,12},{24,0},{28,4},{1,25},{... | collective-permute-start | bytes 165896 | tf_op jit(solution)/shard_map/ppermute | solution.py:1054
  102.2 1.4 %collective-permute-start.25 = (bf16[216,128]{1,0:T(8,128)(2,1)}, bf16[216,128]{1,0:T(8,128)(2,1)S(1)}, u32[]{:S(2)}, u32[]{:S(2)}) collective-permute-start(bf16[216,128]{1,0:T(8,128)(2,1)} %get-tuple-element.135), channel_id=1, source_target_pairs={{0,28},{4,24},{8,20},{12,16},{16,12},{20,8},{24,4},{28,0},{1,29},{... | collective-permute-start | bytes 165896 | tf_op jit(solution)/shard_map/ppermute | solution.py:1054
  103.6 3.0 %collective-permute-done.23.refs_6_ = bf16[216,128]{1,0:T(8,128)(2,1)S(1)} collective-permute-done((bf16[216,128]{1,0:T(8,128)(2,1)}, bf16[216,128]{1,0:T(8,128)(2,1)S(1)}, u32[]{:S(2)}, u32[]{:S(2)}) %collective-permute-start.23) | collective-permute-done | bytes 55328 | tf_op jit(solution)/shard_map/ppermute | solution.py:1054
  106.6 2.7 %collective-permute-done.25.refs_8_ = bf16[216,128]{1,0:T(8,128)(2,1)S(1)} collective-permute-done((bf16[216,128]{1,0:T(8,128)(2,1)}, bf16[216,128]{1,0:T(8,128)(2,1)S(1)}, u32[]{:S(2)}, u32[]{:S(2)}) %collective-permute-start.25) | collective-permute-done | bytes 55328 | tf_op jit(solution)/shard_map/ppermute | solution.py:1054
  109.4 0.6 copy-done.23
  110.0 2.8 %reduce.1 = f32[344,128]{1,0:T(8,128)} custom-call(s32[2]{0:T(128)} %pad_add_fusion.refs_0_, f32[216,128]{1,0:T(8,128)} %get-tuple-element.128.refs_1_, bf16[216,128]{1,0:T(8,128)(2,1)} %copy-done.17, bf16[216,128]{1,0:T(8,128)(2,1)} %copy-done.18, bf16[216,128]{1,0:T(8,128)(2,1)} %copy-done.19, bf16[216,128]{1,0:T(8,128)(2,1)} %copy-done.20, ...), custom_call_target="tpu_custom_call" | custom-call | tf_op jit(solution)/shard_map/reduce/pallas_call | solution.py:964
  112.7 1.6 %collective-permute-done.26 = f32[344,128]{1,0:T(8,128)S(1)} collective-permute-done((f32[344,128]{1,0:T(8,128)}, f32[344,128]{1,0:T(8,128)S(1)}, u32[]{:S(2)}, u32[]{:S(2)}) %collective-permute-start.26) | collective-permute-done | bytes 176160 | tf_op jit(solution)/shard_map/ppermute | solution.py:1040
  114.3 0.9 add.23.refs_0_
  115.3 1.0 collective-permute-start.27
  116.2 2.1 %collect.2 = bf16[4,2,16,4096]{3,2,1,0:T(8,128)(2,1)} custom-call(s32[1]{0:T(128)} %bitcast.refs_0_.member_ref, bf16[2,16,4096]{2,1,0:T(8,128)(2,1)} %get-tuple-element.99.refs_0_, bf16[2,16,4096]{2,1,0:T(8,128)(2,1)} %copy-done.10, bf16[2,16,4096]{2,1,0:T(8,128)(2,1)} %copy-done.11, bf16[2,16,4096]{2,1,0:T(8,128)(2,1)} %copy-done.12), custom_call_target="tpu_custom_call" | custom-call | tf_op jit(solution)/shard_map/collect/pallas_call | solution.py:1014
  118.4 2.5 %collect.3 = f32[4,2,16,4096]{3,2,1,0:T(8,128)} custom-call(s32[1]{0:T(128)} %bitcast.refs_0_.member_ref, bf16[2,16,4096]{2,1,0:T(8,128)(2,1)} %get-tuple-element.124.refs_0_, bf16[2,16,4096]{2,1,0:T(8,128)(2,1)} %copy-done.13, bf16[2,16,4096]{2,1,0:T(8,128)(2,1)} %copy-done.14, bf16[2,16,4096]{2,1,0:T(8,128)(2,1)} %copy-done.15), custom_call_target="tpu_custom_call" | custom-call | tf_op jit(solution)/shard_map/collect/pallas_call | solution.py:1014
  120.9 1.0 collective-permute-done.27.refs_1_
  121.9 0.7 copy-done.16
  122.5 1.8 %finish.1 = (f32[18,32]{1,0:T(8,128)}, f32[32,32]{1,0:T(8,128)}, f32[32,128]{1,0:T(8,128)}, f32[32,128]{1,0:T(8,128)}, f32[64,72]{1,0:T(8,128)}, /*index=5*/f32[...) custom-call(f32[344,128]{1,0:T(8,128)} %copy-done.1, ...), custom_call_target="tpu_custom_call" | custom-call | tf_op jit(solution)/shard_map/finish/pallas_call | solution.py:980
  (61 shorter events, 0.1 us)
Async XLA Ops:
  0.6 21.3 %copy-start = (bf16[8,16,4096]{2,1,0:T(8,128)(2,1)S(1)}, bf16[8,16,4096]{2,1,0:T(8,128)(2,1)}, u32[]{:S(2)}) copy-start(bf16[8,16,4096]{2,1,0:T(8,128)(2,1)} %param.18) | copy-start | bytes 3145732
  2.5 20.2 %copy-start.2 = (bf16[288,128]{1,0:T(8,128)(2,1)S(1)}, bf16[288,128]{1,0:T(8,128)(2,1)}, u32[]{:S(2)}) copy-start(bf16[288,128]{1,0:T(8,128)(2,1)} %pack.1.refs_4_.refs_9_) | copy-start | bytes 221188
  2.5 13.3 %collective-permute-start.12 = (bf16[288,128]{1,0:T(8,128)(2,1)}, bf16[288,128]{1,0:T(8,128)(2,1)S(1)}, u32[]{:S(2)}, u32[]{:S(2)}) collective-permute-start(bf16[288,128]{1,0:T(8,128)(2,1)} %pack.1.refs_4_.refs_9_), channel_id=1, source_target_pairs={{0,28},{4,24},{8,20},{12,16},{16,12},{20,8},{24,4},{28,0},{1,29},{... | collective-permute-start | bytes 221192 | tf_op jit(solution)/shard_map/ppermute | solution.py:1054
  8.5 7.3 %collective-permute-start.11 = (bf16[288,128]{1,0:T(8,128)(2,1)}, bf16[288,128]{1,0:T(8,128)(2,1)S(1)}, u32[]{:S(2)}, u32[]{:S(2)}) collective-permute-start(bf16[288,128]{1,0:T(8,128)(2,1)} %pack.1.refs_4_.refs_9_), channel_id=1, source_target_pairs={{0,24},{4,28},{8,16},{12,20},{16,8},{20,12},{24,0},{28,4},{1,25},{... | collective-permute-start | bytes 221192 | tf_op jit(solution)/shard_map/ppermute | solution.py:1054
  8.7 11.7 %collective-permute-start.10 = (bf16[288,128]{1,0:T(8,128)(2,1)}, bf16[288,128]{1,0:T(8,128)(2,1)S(1)}, u32[]{:S(2)}, u32[]{:S(2)}) collective-permute-start(bf16[288,128]{1,0:T(8,128)(2,1)} %pack.1.refs_4_.refs_9_), channel_id=1, source_target_pairs={{0,20},{4,16},{8,28},{12,24},{16,4},{20,0},{24,12},{28,8},{1,21},{... | collective-permute-start | bytes 221192 | tf_op jit(solution)/shard_map/ppermute | solution.py:1054
  9.5 13.3 %collective-permute-start.9 = (bf16[288,128]{1,0:T(8,128)(2,1)}, bf16[288,128]{1,0:T(8,128)(2,1)S(1)}, u32[]{:S(2)}, u32[]{:S(2)}) collective-permute-start(bf16[288,128]{1,0:T(8,128)(2,1)} %pack.1.refs_4_.refs_9_), channel_id=1, source_target_pairs={{0,16},{4,20},{8,24},{12,28},{16,0},{20,4},{24,8},{28,12},{1,17},{... | collective-permute-start | bytes 221192 | tf_op jit(solution)/shard_map/ppermute | solution.py:1054
  11.5 11.3 %collective-permute-start.8 = (bf16[288,128]{1,0:T(8,128)(2,1)}, bf16[288,128]{1,0:T(8,128)(2,1)S(1)}, u32[]{:S(2)}, u32[]{:S(2)}) collective-permute-start(bf16[288,128]{1,0:T(8,128)(2,1)} %pack.1.refs_4_.refs_9_), channel_id=1, source_target_pairs={{0,12},{4,8},{8,4},{12,0},{16,28},{20,24},{24,20},{28,16},{1,13},{... | collective-permute-start | bytes 221192 | tf_op jit(solution)/shard_map/ppermute | solution.py:1054
  15.8 12.0 %copy-start.3 = (bf16[288,128]{1,0:T(8,128)(2,1)}, bf16[288,128]{1,0:T(8,128)(2,1)S(1)}, u32[]{:S(2)}) copy-start(bf16[288,128]{1,0:T(8,128)(2,1)S(1)} %collective-permute-done.12.refs_11_.refs_16_) | copy-start | bytes 221188
  15.8 15.8 %collective-permute-start.5 = (bf16[2,16,4096]{2,1,0:T(8,128)(2,1)S(1)}, bf16[2,16,4096]{2,1,0:T(8,128)(2,1)S(1)}, u32[]{:S(2)}, u32[]{:S(2)}) collective-permute-start(bf16[2,16,4096]{2,1,0:T(8,128)(2,1)S(1)} %get-tuple-element.148), channel_id=1, source_target_pairs={{0,3},{1,2},{2,1},{3,0},{4,7},{5,6},{6,5},{7,4},{8,11},{9,10},{10,... | collective-permute-start | bytes 786440 | tf_op jit(solution)/shard_map/ppermute | solution.py:1040
  15.8 12.0 %copy-start.4 = (bf16[288,128]{1,0:T(8,128)(2,1)}, bf16[288,128]{1,0:T(8,128)(2,1)S(1)}, u32[]{:S(2)}) copy-start(bf16[288,128]{1,0:T(8,128)(2,1)S(1)} %collective-permute-done.11.refs_10_.refs_15_) | copy-start | bytes 221188
  15.8 17.3 %collective-permute-start.3 = (bf16[2,16,4096]{2,1,0:T(8,128)(2,1)S(1)}, bf16[2,16,4096]{2,1,0:T(8,128)(2,1)}, u32[]{:S(2)}, u32[]{:S(2)}) collective-permute-start(bf16[2,16,4096]{2,1,0:T(8,128)(2,1)S(1)} %get-tuple-element.149), channel_id=1, source_target_pairs={{0,1},{1,0},{2,3},{3,2},{4,5},{5,4},{6,7},{7,6},{8,9},{9,8},{10,11... | collective-permute-start | bytes 786440 | tf_op jit(solution)/shard_map/ppermute | solution.py:1040
  20.4 7.4 %copy-start.5 = (bf16[288,128]{1,0:T(8,128)(2,1)}, bf16[288,128]{1,0:T(8,128)(2,1)S(1)}, u32[]{:S(2)}) copy-start(bf16[288,128]{1,0:T(8,128)(2,1)S(1)} %collective-permute-done.10.refs_9_.refs_14_) | copy-start | bytes 221188
  20.4 12.7 %collective-permute-start.4 = (bf16[2,16,4096]{2,1,0:T(8,128)(2,1)S(1)}, bf16[2,16,4096]{2,1,0:T(8,128)(2,1)}, u32[]{:S(2)}, u32[]{:S(2)}) collective-permute-start(bf16[2,16,4096]{2,1,0:T(8,128)(2,1)S(1)} %get-tuple-element.151), channel_id=1, source_target_pairs={{0,2},{1,3},{2,0},{3,1},{4,6},{5,7},{6,4},{7,5},{8,10},{9,11},{10,... | collective-permute-start | bytes 786440 | tf_op jit(solution)/shard_map/ppermute | solution.py:1040
  22.8 5.1 %copy-start.6 = (bf16[288,128]{1,0:T(8,128)(2,1)}, bf16[288,128]{1,0:T(8,128)(2,1)S(1)}, u32[]{:S(2)}) copy-start(bf16[288,128]{1,0:T(8,128)(2,1)S(1)} %collective-permute-done.9.refs_8_.refs_13_) | copy-start | bytes 221188
  22.8 4.4 %collective-permute-start.7 = (bf16[288,128]{1,0:T(8,128)(2,1)S(1)}, bf16[288,128]{1,0:T(8,128)(2,1)S(1)}, u32[]{:S(2)}, u32[]{:S(2)}) collective-permute-start(bf16[288,128]{1,0:T(8,128)(2,1)S(1)} %copy-done.2), channel_id=1, source_target_pairs={{0,8},{4,12},{8,0},{12,4},{16,24},{20,28},{24,16},{28,20},{1,9},{5... | collective-permute-start | bytes 221192 | tf_op jit(solution)/shard_map/ppermute | solution.py:1054
  22.8 5.0 %copy-start.7 = (bf16[288,128]{1,0:T(8,128)(2,1)}, bf16[288,128]{1,0:T(8,128)(2,1)S(1)}, u32[]{:S(2)}) copy-start(bf16[288,128]{1,0:T(8,128)(2,1)S(1)} %collective-permute-done.8.refs_7_.refs_12_) | copy-start | bytes 221188
  22.9 4.4 %collective-permute-start.6 = (bf16[288,128]{1,0:T(8,128)(2,1)S(1)}, bf16[288,128]{1,0:T(8,128)(2,1)S(1)}, u32[]{:S(2)}, u32[]{:S(2)}) collective-permute-start(bf16[288,128]{1,0:T(8,128)(2,1)S(1)} %copy-done.2), channel_id=1, source_target_pairs={{0,4},{4,0},{8,12},{12,8},{16,20},{20,16},{24,28},{28,24},{1,5},{5... | collective-permute-start | bytes 221192 | tf_op jit(solution)/shard_map/ppermute | solution.py:1054
  27.2 0.7 copy-start.8
  27.2 28.3 %collective-permute-start.2 = (bf16[2,16,4096]{2,1,0:T(8,128)(2,1)S(1)}, bf16[2,16,4096]{2,1,0:T(8,128)(2,1)S(1)}, u32[]{:S(2)}, u32[]{:S(2)}) collective-permute-start(bf16[2,16,4096]{2,1,0:T(8,128)(2,1)S(1)} %get-tuple-element.152), channel_id=1, source_target_pairs={{0,3},{1,2},{2,1},{3,0},{4,7},{5,6},{6,5},{7,4},{8,11},{9,10},{10,... | collective-permute-start | bytes 786440 | tf_op jit(solution)/shard_map/ppermute | solution.py:1040
  27.3 0.6 copy-start.9
  27.3 28.9 %collective-permute-start = (bf16[2,16,4096]{2,1,0:T(8,128)(2,1)S(1)}, bf16[2,16,4096]{2,1,0:T(8,128)(2,1)S(1)}, u32[]{:S(2)}, u32[]{:S(2)}) collective-permute-start(bf16[2,16,4096]{2,1,0:T(8,128)(2,1)S(1)} %get-tuple-element.153), channel_id=1, source_target_pairs={{0,1},{1,0},{2,3},{3,2},{4,5},{5,4},{6,7},{7,6},{8,9},{9,8},{10,11... | collective-permute-start | bytes 786440 | tf_op jit(solution)/shard_map/ppermute | solution.py:1040
  31.6 1.6 %copy-start.24 = (bf16[2,16,4096]{2,1,0:T(8,128)(2,1)}, bf16[2,16,4096]{2,1,0:T(8,128)(2,1)S(1)}, u32[]{:S(2)}) copy-start(bf16[2,16,4096]{2,1,0:T(8,128)(2,1)S(1)} %collective-permute-done.5.refs_4_.refs_8_) | copy-start | bytes 786436
  31.6 24.5 %collective-permute-start.1 = (bf16[2,16,4096]{2,1,0:T(8,128)(2,1)S(1)}, bf16[2,16,4096]{2,1,0:T(8,128)(2,1)S(1)}, u32[]{:S(2)}, u32[]{:S(2)}) collective-permute-start(bf16[2,16,4096]{2,1,0:T(8,128)(2,1)S(1)} %get-tuple-element.155), channel_id=1, source_target_pairs={{0,2},{1,3},{2,0},{3,1},{4,6},{5,7},{6,4},{7,5},{8,10},{9,11},{10,... | collective-permute-start | bytes 786440 | tf_op jit(solution)/shard_map/ppermute | solution.py:1040
  54.2 25.8 %collective-permute-start.13 = (bf16[2,16,4096]{2,1,0:T(8,128)(2,1)}, bf16[2,16,4096]{2,1,0:T(8,128)(2,1)S(1)}, u32[]{:S(2)}, u32[]{:S(2)}) collective-permute-start(bf16[2,16,4096]{2,1,0:T(8,128)(2,1)} %get-tuple-element.96), channel_id=1, source_target_pairs={{0,1},{1,0},{2,3},{3,2},{4,5},{5,4},{6,7},{7,6},{8,9},{9,8},{10,11... | collective-permute-start | bytes 786440 | tf_op jit(solution)/shard_map/ppermute | solution.py:1040
  54.6 26.0 %collective-permute-start.14 = (bf16[2,16,4096]{2,1,0:T(8,128)(2,1)}, bf16[2,16,4096]{2,1,0:T(8,128)(2,1)S(1)}, u32[]{:S(2)}, u32[]{:S(2)}) collective-permute-start(bf16[2,16,4096]{2,1,0:T(8,128)(2,1)} %get-tuple-element.97), channel_id=1, source_target_pairs={{0,2},{1,3},{2,0},{3,1},{4,6},{5,7},{6,4},{7,5},{8,10},{9,11},{10,... | collective-permute-start | bytes 786440 | tf_op jit(solution)/shard_map/ppermute | solution.py:1040
  55.5 0.7 copy-start.25
  55.5 25.1 %collective-permute-start.15 = (bf16[2,16,4096]{2,1,0:T(8,128)(2,1)}, bf16[2,16,4096]{2,1,0:T(8,128)(2,1)S(1)}, u32[]{:S(2)}, u32[]{:S(2)}) collective-permute-start(bf16[2,16,4096]{2,1,0:T(8,128)(2,1)} %get-tuple-element.98), channel_id=1, source_target_pairs={{0,3},{1,2},{2,1},{3,0},{4,7},{5,6},{6,5},{7,4},{8,11},{9,10},{10,... | collective-permute-start | bytes 786440 | tf_op jit(solution)/shard_map/ppermute | solution.py:1040
  56.2 0.7 copy-start.26
  56.2 0.8 copy-start.27
  78.5 13.2 %collective-permute-start.16 = (bf16[2,16,4096]{2,1,0:T(8,128)(2,1)}, bf16[2,16,4096]{2,1,0:T(8,128)(2,1)S(1)}, u32[]{:S(2)}, u32[]{:S(2)}) collective-permute-start(bf16[2,16,4096]{2,1,0:T(8,128)(2,1)} %get-tuple-element.121), channel_id=1, source_target_pairs={{0,1},{1,0},{2,3},{3,2},{4,5},{5,4},{6,7},{7,6},{8,9},{9,8},{10,11... | collective-permute-start | bytes 786440 | tf_op jit(solution)/shard_map/ppermute | solution.py:1040
  79.2 12.6 %collective-permute-start.17 = (bf16[2,16,4096]{2,1,0:T(8,128)(2,1)}, bf16[2,16,4096]{2,1,0:T(8,128)(2,1)S(1)}, u32[]{:S(2)}, u32[]{:S(2)}) collective-permute-start(bf16[2,16,4096]{2,1,0:T(8,128)(2,1)} %get-tuple-element.122), channel_id=1, source_target_pairs={{0,2},{1,3},{2,0},{3,1},{4,6},{5,7},{6,4},{7,5},{8,10},{9,11},{10,... | collective-permute-start | bytes 786440 | tf_op jit(solution)/shard_map/ppermute | solution.py:1040
  80.1 11.7 %copy-start.10 = (bf16[2,16,4096]{2,1,0:T(8,128)(2,1)}, bf16[2,16,4096]{2,1,0:T(8,128)(2,1)S(1)}, u32[]{:S(2)}) copy-start(bf16[2,16,4096]{2,1,0:T(8,128)(2,1)S(1)} %collective-permute-done.13.refs_1_) | copy-start | bytes 786436
  80.1 12.3 %collective-permute-start.18 = (bf16[2,16,4096]{2,1,0:T(8,128)(2,1)}, bf16[2,16,4096]{2,1,0:T(8,128)(2,1)S(1)}, u32[]{:S(2)}, u32[]{:S(2)}) collective-permute-start(bf16[2,16,4096]{2,1,0:T(8,128)(2,1)} %get-tuple-element.123), channel_id=1, source_target_pairs={{0,3},{1,2},{2,1},{3,0},{4,7},{5,6},{6,5},{7,4},{8,11},{9,10},{10,... | collective-permute-start | bytes 786440 | tf_op jit(solution)/shard_map/ppermute | solution.py:1040
  80.6 11.1 %copy-start.11 = (bf16[2,16,4096]{2,1,0:T(8,128)(2,1)}, bf16[2,16,4096]{2,1,0:T(8,128)(2,1)S(1)}, u32[]{:S(2)}) copy-start(bf16[2,16,4096]{2,1,0:T(8,128)(2,1)S(1)} %collective-permute-done.14.refs_2_) | copy-start | bytes 786436
  80.6 11.1 %copy-start.12 = (bf16[2,16,4096]{2,1,0:T(8,128)(2,1)}, bf16[2,16,4096]{2,1,0:T(8,128)(2,1)S(1)}, u32[]{:S(2)}) copy-start(bf16[2,16,4096]{2,1,0:T(8,128)(2,1)S(1)} %collective-permute-done.15.refs_3_) | copy-start | bytes 786436
  91.8 26.6 %copy-start.13 = (bf16[2,16,4096]{2,1,0:T(8,128)(2,1)}, bf16[2,16,4096]{2,1,0:T(8,128)(2,1)S(1)}, u32[]{:S(2)}) copy-start(bf16[2,16,4096]{2,1,0:T(8,128)(2,1)S(1)} %collective-permute-done.16.refs_1_) | copy-start | bytes 786436
  91.8 26.6 %copy-start.14 = (bf16[2,16,4096]{2,1,0:T(8,128)(2,1)}, bf16[2,16,4096]{2,1,0:T(8,128)(2,1)S(1)}, u32[]{:S(2)}) copy-start(bf16[2,16,4096]{2,1,0:T(8,128)(2,1)S(1)} %collective-permute-done.17.refs_2_) | copy-start | bytes 786436
  92.4 26.0 %copy-start.15 = (bf16[2,16,4096]{2,1,0:T(8,128)(2,1)}, bf16[2,16,4096]{2,1,0:T(8,128)(2,1)S(1)}, u32[]{:S(2)}) copy-start(bf16[2,16,4096]{2,1,0:T(8,128)(2,1)S(1)} %collective-permute-done.18.refs_3_) | copy-start | bytes 786436
  92.4 7.3 %collective-permute-start.19 = (bf16[216,128]{1,0:T(8,128)(2,1)}, bf16[216,128]{1,0:T(8,128)(2,1)S(1)}, u32[]{:S(2)}, u32[]{:S(2)}) collective-permute-start(bf16[216,128]{1,0:T(8,128)(2,1)} %get-tuple-element.129), channel_id=1, source_target_pairs={{0,4},{4,0},{8,12},{12,8},{16,20},{20,16},{24,28},{28,24},{1,5},{5... | collective-permute-start | bytes 165896 | tf_op jit(solution)/shard_map/ppermute | solution.py:1054
  93.8 8.4 %collective-permute-start.20 = (bf16[216,128]{1,0:T(8,128)(2,1)}, bf16[216,128]{1,0:T(8,128)(2,1)S(1)}, u32[]{:S(2)}, u32[]{:S(2)}) collective-permute-start(bf16[216,128]{1,0:T(8,128)(2,1)} %get-tuple-element.130), channel_id=1, source_target_pairs={{0,8},{4,12},{8,0},{12,4},{16,24},{20,28},{24,16},{28,20},{1,9},{5... | collective-permute-start | bytes 165896 | tf_op jit(solution)/shard_map/ppermute | solution.py:1054
  94.9 8.7 %collective-permute-start.21 = (bf16[216,128]{1,0:T(8,128)(2,1)}, bf16[216,128]{1,0:T(8,128)(2,1)S(1)}, u32[]{:S(2)}, u32[]{:S(2)}) collective-permute-start(bf16[216,128]{1,0:T(8,128)(2,1)} %get-tuple-element.131), channel_id=1, source_target_pairs={{0,12},{4,8},{8,4},{12,0},{16,28},{20,24},{24,20},{28,16},{1,13},{... | collective-permute-start | bytes 165896 | tf_op jit(solution)/shard_map/ppermute | solution.py:1054
  95.9 7.7 %collective-permute-start.22 = (bf16[216,128]{1,0:T(8,128)(2,1)}, bf16[216,128]{1,0:T(8,128)(2,1)S(1)}, u32[]{:S(2)}, u32[]{:S(2)}) collective-permute-start(bf16[216,128]{1,0:T(8,128)(2,1)} %get-tuple-element.132), channel_id=1, source_target_pairs={{0,16},{4,20},{8,24},{12,28},{16,0},{20,4},{24,8},{28,12},{1,17},{... | collective-permute-start | bytes 165896 | tf_op jit(solution)/shard_map/ppermute | solution.py:1054
  97.9 8.7 %collective-permute-start.23 = (bf16[216,128]{1,0:T(8,128)(2,1)}, bf16[216,128]{1,0:T(8,128)(2,1)S(1)}, u32[]{:S(2)}, u32[]{:S(2)}) collective-permute-start(bf16[216,128]{1,0:T(8,128)(2,1)} %get-tuple-element.133), channel_id=1, source_target_pairs={{0,20},{4,16},{8,28},{12,24},{16,4},{20,0},{24,12},{28,8},{1,21},{... | collective-permute-start | bytes 165896 | tf_op jit(solution)/shard_map/ppermute | solution.py:1054
  99.7 9.7 %copy-start.17 = (bf16[216,128]{1,0:T(8,128)(2,1)}, bf16[216,128]{1,0:T(8,128)(2,1)S(1)}, u32[]{:S(2)}) copy-start(bf16[216,128]{1,0:T(8,128)(2,1)S(1)} %collective-permute-done.19.refs_2_) | copy-start | bytes 165892
  99.7 6.9 %collective-permute-start.24 = (bf16[216,128]{1,0:T(8,128)(2,1)}, bf16[216,128]{1,0:T(8,128)(2,1)S(1)}, u32[]{:S(2)}, u32[]{:S(2)}) collective-permute-start(bf16[216,128]{1,0:T(8,128)(2,1)} %get-tuple-element.134), channel_id=1, source_target_pairs={{0,24},{4,28},{8,16},{12,20},{16,8},{20,12},{24,0},{28,4},{1,25},{... | collective-permute-start | bytes 165896 | tf_op jit(solution)/shard_map/ppermute | solution.py:1054
  102.2 7.2 %copy-start.18 = (bf16[216,128]{1,0:T(8,128)(2,1)}, bf16[216,128]{1,0:T(8,128)(2,1)S(1)}, u32[]{:S(2)}) copy-start(bf16[216,128]{1,0:T(8,128)(2,1)S(1)} %collective-permute-done.20.refs_3_) | copy-start | bytes 165892
  102.2 7.2 %collective-permute-start.25 = (bf16[216,128]{1,0:T(8,128)(2,1)}, bf16[216,128]{1,0:T(8,128)(2,1)S(1)}, u32[]{:S(2)}, u32[]{:S(2)}) collective-permute-start(bf16[216,128]{1,0:T(8,128)(2,1)} %get-tuple-element.135), channel_id=1, source_target_pairs={{0,28},{4,24},{8,20},{12,16},{16,12},{20,8},{24,4},{28,0},{1,29},{... | collective-permute-start | bytes 165896 | tf_op jit(solution)/shard_map/ppermute | solution.py:1054
  103.6 5.8 %copy-start.19 = (bf16[216,128]{1,0:T(8,128)(2,1)}, bf16[216,128]{1,0:T(8,128)(2,1)S(1)}, u32[]{:S(2)}) copy-start(bf16[216,128]{1,0:T(8,128)(2,1)S(1)} %collective-permute-done.21.refs_4_) | copy-start | bytes 165892
  103.6 5.8 %copy-start.20 = (bf16[216,128]{1,0:T(8,128)(2,1)}, bf16[216,128]{1,0:T(8,128)(2,1)S(1)}, u32[]{:S(2)}) copy-start(bf16[216,128]{1,0:T(8,128)(2,1)S(1)} %collective-permute-done.22.refs_5_) | copy-start | bytes 165892
  106.6 2.7 %copy-start.21 = (bf16[216,128]{1,0:T(8,128)(2,1)}, bf16[216,128]{1,0:T(8,128)(2,1)S(1)}, u32[]{:S(2)}) copy-start(bf16[216,128]{1,0:T(8,128)(2,1)S(1)} %collective-permute-done.23.refs_6_) | copy-start | bytes 165892
  106.6 2.8 %copy-start.22 = (bf16[216,128]{1,0:T(8,128)(2,1)}, bf16[216,128]{1,0:T(8,128)(2,1)S(1)}, u32[]{:S(2)}) copy-start(bf16[216,128]{1,0:T(8,128)(2,1)S(1)} %collective-permute-done.24.refs_7_) | copy-start | bytes 165892
  109.3 0.6 copy-start.23
  112.7 1.6 %collective-permute-start.26 = (f32[344,128]{1,0:T(8,128)}, f32[344,128]{1,0:T(8,128)S(1)}, u32[]{:S(2)}, u32[]{:S(2)}) collective-permute-start(f32[344,128]{1,0:T(8,128)} %reduce.1), channel_id=1, source_target_pairs={{0,1},{1,0},{2,3},{3,2},{4,5},{5,4},{6,7},{7,6},{8,9},{9,8},{10,11... | collective-permute-start | bytes 528392 | tf_op jit(solution)/shard_map/ppermute | solution.py:1040
  115.3 5.6 %copy-start.1 = (f32[344,128]{1,0:T(8,128)}, f32[344,128]{1,0:T(8,128)S(1)}, u32[]{:S(2)}) copy-start(f32[344,128]{1,0:T(8,128)S(1)} %add.23.refs_0_) | copy-start | bytes 528388
  115.3 6.6 %collective-permute-start.27 = (f32[344,128]{1,0:T(8,128)S(1)}, f32[344,128]{1,0:T(8,128)S(1)}, u32[]{:S(2)}, u32[]{:S(2)}) collective-permute-start(f32[344,128]{1,0:T(8,128)S(1)} %add.23.refs_0_), channel_id=1, source_target_pairs={{0,2},{1,3},{2,0},{3,1},{4,6},{5,7},{6,4},{7,5},{8,10},{9,11},{10,... | collective-permute-start | bytes 528392 | tf_op jit(solution)/shard_map/ppermute | solution.py:1040
  121.9 0.7 copy-start.16

commit v3 on v2

--- a/solution.py
+++ b/solution.py
@@ -21,7 +21,8 @@
 precise = lax.Precision.HIGHEST
 f32 = jnp.float32
 bf16 = jnp.bfloat16
-VMEM_LIMIT = 60 * 2**20
+VMEM_LIMIT = 24 * 2**20
+VMEM_MOST = 60 * 2**20
 
 
 def lane_ids(shape):
@@ -54,6 +55,12 @@
 
 def total(x):
     return jnp.sum(x, axis=0, keepdims=True)
+
+
+def over_pairs(body, carry):
+    for j in range(PAIRS):
+        carry = body(j, carry)
+    return carry
 
 
 def build_windows(windows, tile):
@@ -73,7 +80,7 @@
         write(j, jnp.where(low_lanes, even_past, even), jnp.where(low_lanes, odd_past, odd))
         return even, odd
 
-    even, odd = lax.fori_loop(0, PAIRS, body, (zero, zero), unroll=4)
+    even, odd = over_pairs(body, (zero, zero))
     write(PAIRS, jnp.where(low_lanes, even, 0.0), jnp.where(low_lanes, odd, 0.0))
 
 
@@ -103,24 +110,35 @@
     return pl.multiple_of((member ^ offset) * strip, strip)
 
 
-def load_strips(member, strips, image):
+def load_strips(member, strips, f, image):
     for offset, strip in enumerate(strips):
         rows = strip.shape[1]
         start = strip_start(member, offset, rows)
         for j in range(PAIRS):
-            image[j, pl.ds(start, rows), :] = strip[0, :, j * LANES : (j + 1) * LANES].astype(f32)
-
-
-def store_strips(member, image, strips):
+            image[j, pl.ds(start, rows), :] = strip[f, :, j * LANES : (j + 1) * LANES].astype(f32)
+
+
+def store_strips(member, image, f, strips):
     for offset, strip in enumerate(strips):
         rows = strip.shape[1]
         start = strip_start(member, offset, rows)
         for j in range(PAIRS):
-            strip[0, :, j * LANES : (j + 1) * LANES] = image[j, pl.ds(start, rows), :].astype(strip.dtype)
+            strip[f, :, j * LANES : (j + 1) * LANES] = image[j, pl.ds(start, rows), :].astype(strip.dtype)
 
 
 def parity_rows(image, parity, j):
     return image[j, pl.ds(parity, HALF, stride=2), :]
+
+
+def staggered(steps):
+    steps = list(steps)
+    started = []
+    while steps or started:
+        if steps:
+            started.append(steps.pop(0))
+        for step in list(started):
+            if next(step, "end") == "end":
+                started.remove(step)
 
 
 def forward_kernel(count, *refs):
@@ -128,87 +146,95 @@
     strips = refs[1 : 1 + count]
     styles, biases, w_one, w_two, w_down, w_up = refs[1 + count : 7 + count]
     out = refs[7 + count : 7 + 2 * count]
-    win_one, win_two, win_level, win_coarse, middle, down, stats = refs[7 + 2 * count : 14 + 2 * count]
-    image, level = refs[14 + 2 * count :]
+    outs = refs[7 + 2 * count : 14 + 2 * count]
+    images, levels = refs[14 + 2 * count :]
     member = member_ref[0]
-    win_one, win_two, win_level, win_coarse = (ref.at[0] for ref in (win_one, win_two, win_level, win_coarse))
-    middle, down = middle.at[0], down.at[0]
-
-    load_strips(member, strips, image)
-
-    def add_stats(j, carry):
-        x = image[j]
-        s, q = carry
-        return s + x, q + x * x
-
-    zero = jnp.zeros((H, LANES), f32)
-    s, q = lax.fori_loop(0, PAIRS, add_stats, (zero, zero), unroll=4)
-    average_one, inverse_one = norm_stats(total(s), total(q))
-    gain_one = inverse_one * styles[0, 0:1, :]
-    half_gain = 0.5 * gain_one[0:1]
-    half_shift = 0.5 * (styles[0, 1:2, :] - average_one[0:1] * gain_one[0:1])
-
-    def act_one(parity, j):
-        h = parity_rows(image, parity, j) * half_gain + half_shift
-        return h * jnp.tanh(h) + h
-
-    build_windows(win_one, act_one)
-    y = matmul(window_operand(win_one, range(4)), w_one[...])
-    sums = jnp.zeros((1, LANES), f32)
-    squares = jnp.zeros((1, LANES), f32)
-    for a in range(2):
-        v = y[:, a * LANES : (a + 1) * LANES] + biases[0:1, :]
-        sums = sums + total(v)
-        squares = squares + total(v * v)
-        middle[a] = tiles_of(v)
-    average_two, inverse_two = norm_stats(sums, squares)
-    stats[0, 0:1, :] = average_one[0:1]
-    stats[0, 1:2, :] = inverse_one[0:1]
-    stats[0, 2:3, :] = average_two[0:1]
-    stats[0, 3:4, :] = inverse_two[0:1]
-    stats[0, 4:8, :] = jnp.zeros((4, LANES), f32)
-    gain_two = inverse_two * styles[0, 2:3, :]
-    half_gain_two = 0.5 * gain_two[0:1]
-    half_shift_two = 0.5 * (styles[0, 3:4, :] - average_two[0:1] * gain_two[0:1])
-
-    def act_two(parity, j):
-        h = middle[parity, j] * half_gain_two + half_shift_two
-        return h * jnp.tanh(h) + h
-
-    build_windows(win_two, act_two)
-    y = matmul(window_operand(win_two, range(4)), w_two[...])
-    for a in range(2):
-        v = y[:, a * LANES : (a + 1) * LANES] + biases[1:2, :]
-        level[a] = tiles_of(v) + image[:, pl.ds(a, HALF, stride=2), :]
-
-    build_windows(win_level, lambda parity, j: level[parity, j])
-    operand = window_operand(win_level, range(4))
-    y = matmul(operand[:, : 6 * LANES], w_down[...]) + biases[2:3, :]
-    down[...] = tiles_of(y)
-
     low_lanes = lane_ids((HALF, LANES)) < C
 
-    def write_coarse(j, cells):
-        win_coarse[0, j] = row_before(cells).astype(bf16)
-        win_coarse[1, j] = cells.astype(bf16)
-        win_coarse[2, j] = row_after(cells).astype(bf16)
-
-    def coarse_body(j, past):
-        h = down[j] * 0.5
-        coarse = h * jnp.tanh(h) + h
-        write_coarse(j, jnp.where(low_lanes, past, coarse))
-        return coarse
-
-    past = lax.fori_loop(0, PAIRS, coarse_body, jnp.zeros((HALF, LANES), f32), unroll=4)
-    write_coarse(PAIRS, jnp.where(low_lanes, past, 0.0))
-
-    operand = window_operand(win_level, range(4))
-    coarse_operand = window_operand(win_coarse, (0, 1, 1, 2))
-    y = matmul(operand, w_up[: 16 * C, :]) + matmul(coarse_operand, w_up[16 * C :, :])
-    for a in range(2):
-        v = y[:, a * LANES : (a + 1) * LANES] + biases[3:4, :]
-        image[:, pl.ds(a, HALF, stride=2), :] = tiles_of(v) + level[a]
-    store_strips(member, image, out)
+    def frame(f):
+        win_one, win_two, win_level, win_coarse, middle, down, stats = (ref.at[f] for ref in outs)
+        image, level, style = images.at[f], levels.at[f], styles.at[f]
+        load_strips(member, strips, f, image)
+
+        def add_stats(j, carry):
+            x = image[j]
+            s, q = carry
+            return s + x, q + x * x
+
+        zero = jnp.zeros((H, LANES), f32)
+        s, q = over_pairs(add_stats, (zero, zero))
+        average_one, inverse_one = norm_stats(total(s), total(q))
+        gain_one = inverse_one * style[0:1, :]
+        half_gain = 0.5 * gain_one[0:1]
+        half_shift = 0.5 * (style[1:2, :] - average_one[0:1] * gain_one[0:1])
+
+        def act_one(parity, j):
+            h = parity_rows(image, parity, j) * half_gain + half_shift
+            return h * jnp.tanh(h) + h
+
+        build_windows(win_one, act_one)
+        yield
+        y = matmul(window_operand(win_one, range(4)), w_one[...])
+        sums = jnp.zeros((1, LANES), f32)
+        squares = jnp.zeros((1, LANES), f32)
+        for a in range(2):
+            v = y[:, a * LANES : (a + 1) * LANES] + biases[0:1, :]
+            sums = sums + total(v)
+            squares = squares + total(v * v)
+            middle[a] = tiles_of(v)
+        yield
+        average_two, inverse_two = norm_stats(sums, squares)
+        stats[0:1, :] = average_one[0:1]
+        stats[1:2, :] = inverse_one[0:1]
+        stats[2:3, :] = average_two[0:1]
+        stats[3:4, :] = inverse_two[0:1]
+        stats[4:8, :] = jnp.zeros((4, LANES), f32)
+        gain_two = inverse_two * style[2:3, :]
+        half_gain_two = 0.5 * gain_two[0:1]
+        half_shift_two = 0.5 * (style[3:4, :] - average_two[0:1] * gain_two[0:1])
+
+        def act_two(parity, j):
+            h = middle[parity, j] * half_gain_two + half_shift_two
+            return h * jnp.tanh(h) + h
+
+        build_windows(win_two, act_two)
+        yield
+        y = matmul(window_operand(win_two, range(4)), w_two[...])
+        for a in range(2):
+            v = y[:, a * LANES : (a + 1) * LANES] + biases[1:2, :]
+            level[a] = tiles_of(v) + image[:, pl.ds(a, HALF, stride=2), :]
+        yield
+        build_windows(win_level, lambda parity, j: level[parity, j])
+        yield
+        operand = window_operand(win_level, range(4))
+        y = matmul(operand[:, : 6 * LANES], w_down[...]) + biases[2:3, :]
+        down[...] = tiles_of(y)
+        yield
+
+        def write_coarse(j, cells):
+            win_coarse[0, j] = row_before(cells).astype(bf16)
+            win_coarse[1, j] = cells.astype(bf16)
+            win_coarse[2, j] = row_after(cells).astype(bf16)
+
+        def coarse_body(j, past):
+            h = down[j] * 0.5
+            coarse = h * jnp.tanh(h) + h
+            write_coarse(j, jnp.where(low_lanes, past, coarse))
+            return coarse
+
+        past = over_pairs(coarse_body, jnp.zeros((HALF, LANES), f32))
+        write_coarse(PAIRS, jnp.where(low_lanes, past, 0.0))
+        yield
+        operand = window_operand(win_level, range(4))
+        coarse_operand = window_operand(win_coarse, (0, 1, 1, 2))
+        y = matmul(operand, w_up[: 16 * C, :]) + matmul(coarse_operand, w_up[16 * C :, :])
+        for a in range(2):
+            v = y[:, a * LANES : (a + 1) * LANES] + biases[3:4, :]
+            image[:, pl.ds(a, HALF, stride=2), :] = tiles_of(v) + level[a]
+        yield
+        store_strips(member, image, f, out)
+
+    staggered(frame(f) for f in range(styles.shape[0]))
 
 
 def slope_twice(h):
@@ -220,128 +246,135 @@
     member_ref = refs[0]
     cot_strips = refs[1 : 1 + count]
     frame_strips = refs[1 + count : 1 + 2 * count]
-    styles, stats, middle, down, w_up, w_down, w_two, w_one = refs[1 + 2 * count : 9 + 2 * count]
+    styles, all_stats, all_middle, all_down, w_up, w_down, w_two, w_one = refs[1 + 2 * count : 9 + 2 * count]
     out = refs[9 + 2 * count : 9 + 3 * count]
-    tile_out, tile_level, tile_mid, coarse_pairs, pieces, bias_sums = refs[9 + 3 * count : 15 + 3 * count]
-    image, level_grad, pre_grad, windows, coarse_below, row_sums = refs[15 + 3 * count :]
+    outs = refs[9 + 3 * count : 15 + 3 * count]
+    scratch = refs[15 + 3 * count :]
     member = member_ref[0]
-    tile_out, tile_level, tile_mid, coarse_pairs = (ref.at[0] for ref in (tile_out, tile_level, tile_mid, coarse_pairs))
-    middle, down = middle.at[0], down.at[0]
     low_lanes = lane_ids((HALF, LANES)) < C
 
-    load_strips(member, cot_strips, image)
-
-    def add_rows(j, s):
-        return s + image[j]
-
-    sums = lax.fori_loop(0, PAIRS, add_rows, jnp.zeros((H, LANES), f32), unroll=4)
-    bias_up_sum = both_parities(total(sums))
-
-    def out_tile(parity, j):
-        x = parity_rows(image, parity, j)
-        tile_out[parity, j] = x.astype(bf16)
-        return x
-
-    build_windows(windows, out_tile)
-    y = matmul(window_operand(windows, range(4)), w_up[...])
-    for a in range(2):
-        level_grad[a] = tiles_of(y[:, (2 + a) * LANES : (3 + a) * LANES]) + image[:, pl.ds(a, HALF, stride=2), :]
-    coarse = y[:, :LANES] + y[:, LANES : 2 * LANES]
-    pre_grad[0] = tiles_of(coarse)
-
-    def coarse_body(t, carry):
-        after, sums = carry
-        j = PAIRS - 1 - t
-        g = pre_grad[0, j]
-        g = g + swap_halves(g)
-        h = down[j] * 0.5
-        d = 0.5 * g * slope_twice(h)
-        pair = jnp.where(low_lanes, d, after)
-        coarse_pairs[j] = pair.astype(bf16)
-        coarse_below[j] = row_after(pair).astype(bf16)
-        return d, sums + d
-
-    zero = jnp.zeros((HALF, LANES), f32)
-    _, sums = lax.fori_loop(0, PAIRS, coarse_body, (zero, zero), unroll=4)
-    bias_down_sum = jnp.broadcast_to(total(sums), (8, LANES))
-
-    operand = jnp.concatenate(
-        [coarse_pairs[...].reshape(BLOCK, LANES), coarse_below[...].reshape(BLOCK, LANES)], axis=1
-    )
-    y = matmul(operand, w_down[...])
-    sums = jnp.zeros((1, LANES), f32)
-    for a in range(2):
-        v = y[:, a * LANES : (a + 1) * LANES] + level_grad[a].reshape(BLOCK, LANES)
-        sums = sums + total(v)
-        level_grad[a] = tiles_of(v)
-    bias_two_sum = both_parities(sums)
-
-    def level_tile(parity, j):
-        x = level_grad[parity, j]
-        tile_level[parity, j] = x.astype(bf16)
-        return x
-
-    build_windows(windows, level_tile)
-
-    def norm_slopes(y, value, k):
-        average, inverse = stats[0, 2 * k : 2 * k + 1, :], stats[0, 2 * k + 1 : 2 * k + 2, :]
-        gain = inverse * styles[0, 2 * k : 2 * k + 1, :]
-        half_gain = 0.5 * gain
-        half_shift = 0.5 * (styles[0, 2 * k + 1 : 2 * k + 2, :] - average * gain)
-        scale_sum = jnp.zeros((1, LANES), f32)
-        shift_sum = jnp.zeros((1, LANES), f32)
+    def frame(f):
+        tile_out, tile_level, tile_mid, coarse_pairs, pieces, bias_sums = (ref.at[f] for ref in outs)
+        image, level_grad, pre_grad, windows, coarse_below = (ref.at[f] for ref in scratch)
+        style, stats, middle, down = (ref.at[f] for ref in (styles, all_stats, all_middle, all_down))
+        load_strips(member, cot_strips, f, image)
+
+        def add_rows(j, s):
+            return s + image[j]
+
+        sums = over_pairs(add_rows, jnp.zeros((H, LANES), f32))
+        bias_up_sum = both_parities(total(sums))
+
+        def out_tile(parity, j):
+            x = parity_rows(image, parity, j)
+            tile_out[parity, j] = x.astype(bf16)
+            return x
+
+        build_windows(windows, out_tile)
+        yield
+        y = matmul(window_operand(windows, range(4)), w_up[...])
         for a in range(2):
-            v = value(a)
-            g = 0.5 * y[:, a * LANES : (a + 1) * LANES] * slope_twice(v * half_gain + half_shift)
-            pre_grad[a] = tiles_of(g)
-            shift_sum = shift_sum + total(g)
-            scale_sum = scale_sum + total(g * ((v - average) * inverse))
-        scale_sum, shift_sum = both_parities(scale_sum), both_parities(shift_sum)
-        factor = styles[0, 2 * k : 2 * k + 1, :]
-        center = group_sum(factor * shift_sum) / MEMBERS
-        tilt = group_sum(factor * scale_sum) / MEMBERS
-        return scale_sum, shift_sum, gain, (inverse * center)[0:1], (inverse * tilt)[0:1], average, inverse
-
-    y = matmul(window_operand(windows, range(4)), w_two[...])
-    scale_two, shift_two, gain, center, tilt, average, inverse = norm_slopes(
-        y, lambda a: middle[a].reshape(BLOCK, LANES), 1
-    )
-    tilt_slope = tilt * inverse
-    constant = tilt_slope * average - center
-
-    def mid_tile(parity, j):
-        x = pre_grad[parity, j] * gain + (constant - middle[parity, j] * tilt_slope)
-        tile_mid[parity, j] = x.astype(bf16)
-        row_sums[...] += x
-        return x
-
-    row_sums[...] = jnp.zeros_like(row_sums)
-    build_windows(windows, mid_tile)
-    bias_one_sum = both_parities(total(row_sums[...]))
-
-    load_strips(member, frame_strips, image)
-    y = matmul(window_operand(windows, range(4)), w_one[...])
-    scale_one, shift_one, gain_one, center_one, tilt_one, average_one, inverse_one = norm_slopes(
-        y, lambda a: image[:, pl.ds(a, HALF, stride=2), :].reshape(BLOCK, LANES), 0
-    )
-    slope_one = tilt_one * inverse_one
-    constant_one = slope_one * average_one - center_one
-
-    def frame_body(j, carry):
-        for parity in range(2):
-            x = parity_rows(image, parity, j)
-            g = pre_grad[parity, j] * gain_one + (constant_one - x * slope_one) + level_grad[parity, j]
-            image[j, pl.ds(parity, HALF, stride=2), :] = g
-        return carry
-
-    lax.fori_loop(0, PAIRS, frame_body, 0, unroll=4)
-    store_strips(member, image, out)
-    for k, value in enumerate((scale_one, shift_one, scale_two, shift_two)):
-        pieces[0, k : k + 1, :] = value[0:1]
-    pieces[0, 4:8, :] = jnp.zeros((4, LANES), f32)
-    for k, value in enumerate((bias_one_sum, bias_two_sum, bias_down_sum, bias_up_sum)):
-        bias_sums[0, k : k + 1, :] = value[0:1]
-    bias_sums[0, 4:8, :] = jnp.zeros((4, LANES), f32)
+            level_grad[a] = tiles_of(y[:, (2 + a) * LANES : (3 + a) * LANES]) + image[:, pl.ds(a, HALF, stride=2), :]
+        coarse = y[:, :LANES] + y[:, LANES : 2 * LANES]
+        pre_grad[0] = tiles_of(coarse)
+        yield
+
+        def coarse_body(t, carry):
+            after, sums = carry
+            j = PAIRS - 1 - t
+            g = pre_grad[0, j]
+            g = g + swap_halves(g)
+            h = down[j] * 0.5
+            d = 0.5 * g * slope_twice(h)
+            pair = jnp.where(low_lanes, d, after)
+            coarse_pairs[j] = pair.astype(bf16)
+            coarse_below[j] = row_after(pair).astype(bf16)
+            return d, sums + d
+
+        zero = jnp.zeros((HALF, LANES), f32)
+        _, sums = over_pairs(coarse_body, (zero, zero))
+        bias_down_sum = jnp.broadcast_to(total(sums), (8, LANES))
+        load_strips(member, frame_strips, f, image)
+        yield
+        operand = jnp.concatenate(
+            [coarse_pairs[...].reshape(BLOCK, LANES), coarse_below[...].reshape(BLOCK, LANES)], axis=1
+        )
+        y = matmul(operand, w_down[...])
+        sums = jnp.zeros((1, LANES), f32)
+        for a in range(2):
+            v = y[:, a * LANES : (a + 1) * LANES] + level_grad[a].reshape(BLOCK, LANES)
+            sums = sums + total(v)
+            level_grad[a] = tiles_of(v)
+        bias_two_sum = both_parities(sums)
+        yield
+
+        def level_tile(parity, j):
+            x = level_grad[parity, j]
+            tile_level[parity, j] = x.astype(bf16)
+            return x
+
+        build_windows(windows, level_tile)
+        yield
+
+        def norm_slopes(y, value, k):
+            average, inverse = stats[2 * k : 2 * k + 1, :], stats[2 * k + 1 : 2 * k + 2, :]
+            gain = inverse * style[2 * k : 2 * k + 1, :]
+            half_gain = 0.5 * gain
+            half_shift = 0.5 * (style[2 * k + 1 : 2 * k + 2, :] - average * gain)
+            scale_sum = jnp.zeros((1, LANES), f32)
+            shift_sum = jnp.zeros((1, LANES), f32)
+            for a in range(2):
+                v = value(a)
+                g = 0.5 * y[:, a * LANES : (a + 1) * LANES] * slope_twice(v * half_gain + half_shift)
+                pre_grad[a] = tiles_of(g)
+                shift_sum = shift_sum + total(g)
+                scale_sum = scale_sum + total(g * ((v - average) * inverse))
+            scale_sum, shift_sum = both_parities(scale_sum), both_parities(shift_sum)
+            factor = style[2 * k : 2 * k + 1, :]
+            center = group_sum(factor * shift_sum) / MEMBERS
+            tilt = group_sum(factor * scale_sum) / MEMBERS
+            slope = (inverse * tilt)[0:1] * inverse
+            return scale_sum, shift_sum, gain, slope, slope * average - (inverse * center)[0:1]
+
+        y = matmul(window_operand(windows, range(4)), w_two[...])
+        scale_two, shift_two, gain_two, slope_two, constant_two = norm_slopes(
+            y, lambda a: middle[a].reshape(BLOCK, LANES), 1
+        )
+        yield
+        row_sums = [zero]
+
+        def mid_tile(parity, j):
+            x = pre_grad[parity, j] * gain_two + (constant_two - middle[parity, j] * slope_two)
+            tile_mid[parity, j] = x.astype(bf16)
+            row_sums[0] = row_sums[0] + x
+            return x
+
+        build_windows(windows, mid_tile)
+        bias_one_sum = both_parities(total(row_sums[0]))
+        yield
+        y = matmul(window_operand(windows, range(4)), w_one[...])
+        scale_one, shift_one, gain_one, slope_one, constant_one = norm_slopes(
+            y, lambda a: image[:, pl.ds(a, HALF, stride=2), :].reshape(BLOCK, LANES), 0
+        )
+        yield
+
+        def frame_body(j, carry):
+            for parity in range(2):
+                x = parity_rows(image, parity, j)
+                g = pre_grad[parity, j] * gain_one + (constant_one - x * slope_one) + level_grad[parity, j]
+                image[j, pl.ds(parity, HALF, stride=2), :] = g
+            return carry
+
+        over_pairs(frame_body, 0)
+        store_strips(member, image, f, out)
+        for k, value in enumerate((scale_one, shift_one, scale_two, shift_two)):
+            pieces[k : k + 1, :] = value[0:1]
+        pieces[4:8, :] = jnp.zeros((4, LANES), f32)
+        for k, value in enumerate((bias_one_sum, bias_two_sum, bias_down_sum, bias_up_sum)):
+            bias_sums[k : k + 1, :] = value[0:1]
+        bias_sums[4:8, :] = jnp.zeros((4, LANES), f32)
+
+    staggered(frame(f) for f in range(styles.shape[0]))
 
 
 def outer(left, right):
@@ -763,8 +796,16 @@
 KEYS = 16 * C
 
 
-def params():
-    return pltpu.CompilerParams(vmem_limit_bytes=VMEM_LIMIT)
+def in_vmem():
+    return pl.BlockSpec(memory_space=pltpu.VMEM)
+
+
+def in_smem():
+    return pl.BlockSpec(memory_space=pltpu.SMEM)
+
+
+def params(limit=VMEM_LIMIT):
+    return pltpu.CompilerParams(vmem_limit_bytes=limit)
 
 
 def cost(macs, moved):
@@ -797,13 +838,8 @@
     frames, strip, _ = strips[0].shape
     return pl.pallas_call(
         lambda *refs: forward_kernel(count, *refs),
-        grid=(frames,),
-        in_specs=[pl.BlockSpec(memory_space=pltpu.SMEM)]
-        + strip_specs(count, strip)
-        + [per_frame(SMALL), whole(SMALL)]
-        + [whole(w.shape) for w in (w_one, w_two, w_down, w_up)],
-        out_specs=strip_specs(count, strip)
-        + [per_frame(d) for d in (WINDOWS, WINDOWS, WINDOWS, COARSE_WINDOWS, TILES, COARSE, SMALL)],
+        in_specs=[in_smem()] + [in_vmem()] * (count + 6),
+        out_specs=[in_vmem()] * (count + 7),
         out_shape=[shape((frames, strip, W * C), bf16)] * count
         + [
             shape((frames,) + WINDOWS, bf16),
@@ -814,7 +850,7 @@
             shape((frames,) + COARSE, f32),
             shape((frames,) + SMALL, f32),
         ],
-        scratch_shapes=[pltpu.VMEM(IMAGE, f32), pltpu.VMEM(TILES, f32)],
+        scratch_shapes=[pltpu.VMEM((frames,) + IMAGE, f32), pltpu.VMEM((frames,) + TILES, f32)],
         compiler_params=params(),
         cost_estimate=cost(frames * BLOCK * KEYS * 2 * LANES * 5, frames * (14 << 20)),
         name="forward",
@@ -826,13 +862,8 @@
     frames, strip, _ = cot_strips[0].shape
     return pl.pallas_call(
         lambda *refs: backward_kernel(count, *refs),
-        grid=(frames,),
-        in_specs=[pl.BlockSpec(memory_space=pltpu.SMEM)]
-        + strip_specs(2 * count, strip)
-        + [per_frame(d) for d in (SMALL, SMALL, TILES, COARSE)]
-        + [whole(w.shape) for w in (w_up, w_down, w_two, w_one)],
-        out_specs=strip_specs(count, strip)
-        + [per_frame(d) for d in (TILES, TILES, TILES, COARSE, SMALL, SMALL)],
+        in_specs=[in_smem()] + [in_vmem()] * (2 * count + 8),
+        out_specs=[in_vmem()] * (count + 6),
         out_shape=[shape((frames, strip, W * C), bf16)] * count
         + [
             shape((frames,) + TILES, bf16),
@@ -843,12 +874,11 @@
             shape((frames,) + SMALL, f32),
         ],
         scratch_shapes=[
-            pltpu.VMEM(IMAGE, f32),
-            pltpu.VMEM(TILES, f32),
-            pltpu.VMEM(TILES, f32),
-            pltpu.VMEM(WINDOWS, bf16),
-            pltpu.VMEM(COARSE, bf16),
-            pltpu.VMEM((HALF, LANES), f32),
+            pltpu.VMEM((frames,) + IMAGE, f32),
+            pltpu.VMEM((frames,) + TILES, f32),
+            pltpu.VMEM((frames,) + TILES, f32),
+            pltpu.VMEM((frames,) + WINDOWS, bf16),
+            pltpu.VMEM((frames,) + COARSE, bf16),
         ],
         compiler_params=params(),
         cost_estimate=cost(frames * BLOCK * KEYS * 2 * LANES * 5, frames * (10 << 20)),
@@ -878,14 +908,6 @@
     )(win_one, win_two, win_level, win_coarse, tile_out, tile_level, tile_mid, coarse_pairs)
 
 
-def in_vmem():
-    return pl.BlockSpec(memory_space=pltpu.VMEM)
-
-
-def in_smem():
-    return pl.BlockSpec(memory_space=pltpu.SMEM)
-
-
 def pack(actions, noise_ids, valid, conv_one, conv_two, down_kernel, up_kernel, ada_one, ada_two, act_table, noise_table, *biases):
     _, _, size = pack_sizes(conv_one.shape[0], ada_one.shape[0])
     kernels = [kernel.T for kernel in (conv_one, conv_two, down_kernel, up_kernel)]
@@ -896,7 +918,7 @@
         out_specs=in_vmem(),
         out_shape=shape((size, LANES), bf16),
         scratch_shapes=[pltpu.VMEM((size, LANES), f32)],
-        compiler_params=params(),
+        compiler_params=params(VMEM_MOST),
         name="pack",
     )(actions, noise_ids, valid, *args)
 
@@ -1122,8 +1144,8 @@
         member_box, frame_strips, cot_strips, styles, bias_rows, operands
     )
     own, *messages = weight_messages(where, wins, tiles, pieces, bias_sums, count, rows)
-    messages, grad_strips = lax.optimization_barrier((messages, grad_strips))
     received = [seq_trade(messages[offset - 1], offset) for offset in range(1, count)]
+    received, grad_strips = lax.optimization_barrier((received, grad_strips))
     sums = reduce_messages(where, own, received, packs, act_table, noise_table, ada_one, ada_two, rows, cells, share)
     offset = 1
     while 2 * offset < lax.axis_size("rows"):

time: 125 us -> 87.9 us (0.70)
  Pallas kernels: 68.4 us -> 32.9 us
  local copies, waits for them, and re-layouts: 4.98 us -> 2.9 us
  waiting for transfers between devices: 14.4 us -> 16.3 us
  other arithmetic: 1.52 us -> 0.09 us
    pallas_call x2, Pallas kernels: 42.6 us -> 16.8 us  [the longest x1 9.25 us: backward(): pl.pallas_call(lambda *refs: backward_kernel(count, *refs), in_specs=[in_...]
    pallas_call x1, Pallas kernels: 11.1 us -> 7.58 us  [weight_messages(): pl.pallas_call(lambda *refs: message_kernel(count, rows, *refs), grid=(fr...]
    ppermute x14, waiting for transfers between devices: 3.24 us -> 5.86 us  [trade(): return lax.ppermute(value, 'rows', [(i, i ^ offset) for i in range(count)])]
    pallas_call x2, Pallas kernels: 4.61 us -> 2.38 us  [collect_strips(): pl.pallas_call(collect_kernel, grid=(frames,), in_specs=[in_smem()] + [pl...]
    unnamed x56 -> x18, local copies, waits for them, and re-layouts: 2.2 us -> 0.04 us
    pallas_call x1, Pallas kernels: 3.67 us -> 2.12 us  [prepare(): pl.pallas_call(lambda *refs: prepare_kernel(count, rows, cells, *refs), i...]
    pallas_call x1, Pallas kernels: 2.75 us -> 1.29 us  [reduce_messages(): pl.pallas_call(lambda *refs: reduce_kernel(count, rows, cells, frames, *r...]
  transfers between devices with their start and end apart: 28 -> 28, of which waited for: 8 -> 9; matrix products, arithmetic and copies ran while one was open for 3% -> 3% of each run, Pallas kernels for 50% -> 33%
where the time goes in v3:
time: 87.9 us; the launch traced here: 87.7 us
  starting transfers between devices  34.7 us (39%)
  Pallas kernels  32.9 us (37%)
  waiting for transfers between devices  16.3 us (19%)
  local copies, waits for them, and re-layouts  2.9 us (3%)
  between operations  0.89 us (1%)
    ppermute x14, starting transfers between devices, seq_trade(): return lax.ppermute(value, 'seq', [(i, i ^ offset) for i in range(count)])  25 us
    ppermute x14, waiting for transfers between devices, seq_trade(): return lax.ppermute(value, 'seq', [(i, i ^ offset) for i in range(count)])  10.4 us
    ppermute x14, starting transfers between devices, trade(): return lax.ppermute(value, 'rows', [(i, i ^ offset) for i in range(count)])  9.73 us
    pallas_call x1, Pallas kernels, backward(): pl.pallas_call(lambda *refs: backward_kernel(count, *refs), in_specs=[in_...  9.25 us
    pallas_call x1, Pallas kernels, weight_messages(): pl.pallas_call(lambda *refs: message_kernel(count, rows, *refs), grid=(fr...  7.58 us
    pallas_call x1, Pallas kernels, forward(): pl.pallas_call(lambda *refs: forward_kernel(count, *refs), in_specs=[in_s...  7.52 us
    ppermute x14, waiting for transfers between devices, trade(): return lax.ppermute(value, 'rows', [(i, i ^ offset) for i in range(count)])  5.86 us
    dynamic_slice x2, local copies, waits for them, and re-layouts, spread_strips(): lax.dynamic_slice_in_dim(array, (member ^ offset) * share, share, axis=0)  2.86 us
  transfers between devices with their start and end apart: 28, of which 9 were waited for; matrix products, arithmetic and copies ran while one was open for 3% of the time, Pallas kernels for 33%

profile of v3, /device:TPU:0, one launch (start us, length us, event | category | flops | bytes accessed | tf_op | source)
XLA Modules:
  0.0 87.7 jit_solution(12881085905464235578)
XLA Ops:
  0.7 1.9 %pack.1.refs_4_.refs_9_ = bf16[288,128]{1,0:T(8,128)(2,1)} custom-call(s32[8]{0:T(128)} %refs_1_.3, s32[8]{0:T(128)} %refs_2_.3, s32[8]{0:T(128)} %refs_3_.1, bf16[64,72]{1,0:T(8,128)(2,1)} %bitcast.15, bf16[64,72]{1,0:T(8,128)(2,1)} %bitcast.16, bf16[64,72]{1,0:T(8,128)(2,1)} %bitcast.17, bf16[64,144]{1,0:T(8,128)(2,1)} %bitcast.14, ...), custom_call_target="tpu_custom_call" | custom-call | tf_op jit(solution)/shard_map/pack/pallas_call | solution.py:915
  2.5 0.0 copy-start.6
  2.5 0.0 copy-start.7
  2.6 6.0 %collective-permute-start.12 = (bf16[288,128]{1,0:T(8,128)(2,1)}, bf16[288,128]{1,0:T(8,128)(2,1)S(1)}, u32[]{:S(2)}, u32[]{:S(2)}) collective-permute-start(bf16[288,128]{1,0:T(8,128)(2,1)} %pack.1.refs_4_.refs_9_), channel_id=1, source_target_pairs={{0,28},{4,24},{8,20},{12,16},{16,12},{20,8},{24,4},{28,0},{1,29},{... | collective-permute-start | bytes 221192 | tf_op jit(solution)/shard_map/ppermute | solution.py:1076
  8.6 0.2 collective-permute-start.11
  8.8 0.8 collective-permute-start.10
  9.6 2.0 %collective-permute-start.9 = (bf16[288,128]{1,0:T(8,128)(2,1)}, bf16[288,128]{1,0:T(8,128)(2,1)S(1)}, u32[]{:S(2)}, u32[]{:S(2)}) collective-permute-start(bf16[288,128]{1,0:T(8,128)(2,1)} %pack.1.refs_4_.refs_9_), channel_id=1, source_target_pairs={{0,16},{4,20},{8,24},{12,28},{16,0},{20,4},{24,8},{28,12},{1,17},{... | collective-permute-start | bytes 221192 | tf_op jit(solution)/shard_map/ppermute | solution.py:1076
  11.6 2.3 %collective-permute-start.8 = (bf16[288,128]{1,0:T(8,128)(2,1)}, bf16[288,128]{1,0:T(8,128)(2,1)S(1)}, u32[]{:S(2)}, u32[]{:S(2)}) collective-permute-start(bf16[288,128]{1,0:T(8,128)(2,1)} %pack.1.refs_4_.refs_9_), channel_id=1, source_target_pairs={{0,12},{4,8},{8,4},{12,0},{16,28},{20,24},{24,20},{28,16},{1,13},{... | collective-permute-start | bytes 221192 | tf_op jit(solution)/shard_map/ppermute | solution.py:1076
  13.9 2.1 %constant_dynamic-slice_fusion = (bf16[2,16,4096]{2,1,0:T(8,128)(2,1)}, bf16[2,16,4096]{2,1,0:T(8,128)(2,1)}, bf16[2,16,4096]{2,1,0:T(8,128)(2,1)S(1)}, bf16[2,16,4096]{2,1,0:T(8,128)(2,1)}) fusion(bf16[8,16,4096]{2,1,0:T(8,128)(2,1)} %param.17, s32[]{:T(128)S(6)} %select_n.19, s32[]{:T(128)S(6)} %select_n.17, s32[]{:T(128)S(6)} %select_n.16, s32[]{:T(128)S(6)} %select_n.18), kind=kLoop, calls=%fused_computation | loop fusion | bytes 2097168 | tf_op jit(solution)/shard_map/dynamic_slice | solution.py:1069
  16.0 0.0 collective-permute-done.12.refs_11_.refs_16_
  16.0 0.0 collective-permute-start.5
  16.0 0.0 collective-permute-done.11.refs_10_.refs_15_
  16.0 1.6 %collective-permute-start.3 = (bf16[2,16,4096]{2,1,0:T(8,128)(2,1)}, bf16[2,16,4096]{2,1,0:T(8,128)(2,1)S(1)}, u32[]{:S(2)}, u32[]{:S(2)}) collective-permute-start(bf16[2,16,4096]{2,1,0:T(8,128)(2,1)} %get-tuple-element.149), channel_id=1, source_target_pairs={{0,1},{1,0},{2,3},{3,2},{4,5},{5,4},{6,7},{7,6},{8,9},{9,8},{10,11... | collective-permute-start | bytes 786440 | tf_op jit(solution)/shard_map/ppermute | solution.py:1062
  17.6 2.8 %collective-permute-done.10.refs_9_.refs_14_ = bf16[288,128]{1,0:T(8,128)(2,1)S(1)} collective-permute-done((bf16[288,128]{1,0:T(8,128)(2,1)}, bf16[288,128]{1,0:T(8,128)(2,1)S(1)}, u32[]{:S(2)}, u32[]{:S(2)}) %collective-permute-start.10) | collective-permute-done | bytes 73760 | tf_op jit(solution)/shard_map/ppermute | solution.py:1076
  20.4 1.5 %collective-permute-start.4 = (bf16[2,16,4096]{2,1,0:T(8,128)(2,1)}, bf16[2,16,4096]{2,1,0:T(8,128)(2,1)S(1)}, u32[]{:S(2)}, u32[]{:S(2)}) collective-permute-start(bf16[2,16,4096]{2,1,0:T(8,128)(2,1)} %get-tuple-element.151), channel_id=1, source_target_pairs={{0,2},{1,3},{2,0},{3,1},{4,6},{5,7},{6,4},{7,5},{8,10},{9,11},{10,... | collective-permute-start | bytes 786440 | tf_op jit(solution)/shard_map/ppermute | solution.py:1062
  21.9 0.8 constant_dynamic-slice_fusion.4
  22.7 0.0 collective-permute-done.9.refs_8_.refs_13_
  22.7 0.0 collective-permute-start.7
  22.7 0.0 collective-permute-done.8.refs_7_.refs_12_
  22.7 1.6 %collective-permute-start.6 = (bf16[288,128]{1,0:T(8,128)(2,1)S(1)}, bf16[288,128]{1,0:T(8,128)(2,1)S(1)}, u32[]{:S(2)}, u32[]{:S(2)}) collective-permute-start(bf16[288,128]{1,0:T(8,128)(2,1)S(1)} %copy-done), channel_id=1, source_target_pairs={{0,4},{4,0},{8,12},{12,8},{16,20},{20,16},{24,28},{28,24},{1,5},{5... | collective-permute-start | bytes 221192 | tf_op jit(solution)/shard_map/ppermute | solution.py:1076
  24.4 0.1 pad_add_fusion.refs_0_
  24.4 2.6 %collective-permute-done.7.refs_6_.refs_11_ = bf16[288,128]{1,0:T(8,128)(2,1)S(1)} collective-permute-done((bf16[288,128]{1,0:T(8,128)(2,1)S(1)}, bf16[288,128]{1,0:T(8,128)(2,1)S(1)}, u32[]{:S(2)}, u32[]{:S(2)}) %collective-permute-start.7) | collective-permute-done | bytes 73760 | tf_op jit(solution)/shard_map/ppermute | solution.py:1076
  27.1 0.0 collective-permute-start.2
  27.1 0.1 collective-permute-done.6.refs_5_.refs_10_
  27.2 0.5 collective-permute-start
  27.7 2.1 %prepare.1 = (bf16[1024,256]{1,0:T(8,128)(2,1)S(1)}, bf16[1024,256]{1,0:T(8,128)(2,1)S(1)}, bf16[768,128]{1,0:T(8,128)(2,1)S(1)}, bf16[2048,256]{1,0:T(8,128)(2,...) custom-call(s32[2]{0:T(128)S(1)} %pad_add_fusion.refs_0_, ...), custom_call_target="tpu_custom_call" | custom-call | tf_op jit(solution)/shard_map/prepare/pallas_call | solution.py:940
  29.8 0.0 collective-permute-done.5.refs_4_.refs_8_
  29.8 1.6 %collective-permute-start.1 = (bf16[2,16,4096]{2,1,0:T(8,128)(2,1)S(1)}, bf16[2,16,4096]{2,1,0:T(8,128)(2,1)S(1)}, u32[]{:S(2)}, u32[]{:S(2)}) collective-permute-start(bf16[2,16,4096]{2,1,0:T(8,128)(2,1)S(1)} %get-tuple-element.155), channel_id=1, source_target_pairs={{0,2},{1,3},{2,0},{3,1},{4,6},{5,7},{6,4},{7,5},{8,10},{9,11},{10,... | collective-permute-start | bytes 786440 | tf_op jit(solution)/shard_map/ppermute | solution.py:1062
  31.4 0.0 collective-permute-done.3.refs_2_.refs_6_
  31.4 0.0 collective-permute-done.4.refs_3_.refs_7_
  31.4 7.5 %forward.1 = (bf16[2,16,4096]{2,1,0:T(8,128)(2,1)S(1)}, bf16[2,16,4096]{2,1,0:T(8,128)(2,1)S(1)}, bf16[2,16,4096]{2,1,0:T(8,128)(2,1)S(1)}, bf16[2,16,4096]{2,1,...) custom-call(s32[1]{0:T(128)} %bitcast.refs_0_.member_ref, ...), custom_call_target="tpu_custom_call" | custom-call | flops 5368709120 | bytes 29360128 | tf_op jit(solution)/shard_map/forward/pallas_call | solution.py:839
  39.0 0.1 collective-permute-start.13
  39.0 0.6 collective-permute-start.14
  39.6 0.0 collective-permute-done.2.refs_4_
  39.6 1.3 %collective-permute-start.15 = (bf16[2,16,4096]{2,1,0:T(8,128)(2,1)S(1)}, bf16[2,16,4096]{2,1,0:T(8,128)(2,1)S(1)}, u32[]{:S(2)}, u32[]{:S(2)}) collective-permute-start(bf16[2,16,4096]{2,1,0:T(8,128)(2,1)S(1)} %get-tuple-element.98), channel_id=1, source_target_pairs={{0,3},{1,2},{2,1},{3,0},{4,7},{5,6},{6,5},{7,4},{8,11},{9,10},{10,... | collective-permute-start | bytes 786440 | tf_op jit(solution)/shard_map/ppermute | solution.py:1062
  40.9 0.0 collective-permute-done.refs_2_
  40.9 0.7 collective-permute-done.1.refs_3_
  41.6 9.2 %backward.1 = (bf16[2,16,4096]{2,1,0:T(8,128)(2,1)S(1)}, bf16[2,16,4096]{2,1,0:T(8,128)(2,1)S(1)}, bf16[2,16,4096]{2,1,0:T(8,128)(2,1)S(1)}, bf16[2,16,4096]{2,1...) custom-call(s32[1]{0:T(128)} %bitcast.refs_0_.member_ref, ...), custom_call_target="tpu_custom_call" | custom-call | flops 5368709120 | bytes 20971520 | tf_op jit(solution)/shard_map/backward/pallas_call | solution.py:863
  50.9 0.1 collective-permute-start.23
  51.0 0.6 collective-permute-start.24
  51.6 0.0 collective-permute-done.13.refs_1_
  51.6 1.2 %collective-permute-start.25 = (bf16[2,16,4096]{2,1,0:T(8,128)(2,1)S(1)}, bf16[2,16,4096]{2,1,0:T(8,128)(2,1)S(1)}, u32[]{:S(2)}, u32[]{:S(2)}) collective-permute-start(bf16[2,16,4096]{2,1,0:T(8,128)(2,1)S(1)} %get-tuple-element.123), channel_id=1, source_target_pairs={{0,3},{1,2},{2,1},{3,0},{4,7},{5,6},{6,5},{7,4},{8,11},{9,10},{10,... | collective-permute-start | bytes 786440 | tf_op jit(solution)/shard_map/ppermute | solution.py:1062
  52.9 0.1 collective-permute-done.15.refs_3_
  52.9 7.6 %weights.1 = (f32[216,128]{1,0:T(8,128)S(1)}, bf16[216,128]{1,0:T(8,128)(2,1)S(1)}, bf16[216,128]{1,0:T(8,128)(2,1)S(1)}, bf16[216,128]{1,0:T(8,128)(2,1)S(1)}, ...) custom-call(s32[2]{0:T(128)S(1)} %pad_add_fusion.refs_0_, ...), custom_call_target="tpu_custom_call" | custom-call | flops 5368709120 | bytes 12582912 | tf_op jit(solution)/shard_map/weights/pallas_call | solution.py:960
  60.5 1.6 %collective-permute-start.16 = (bf16[216,128]{1,0:T(8,128)(2,1)S(1)}, bf16[216,128]{1,0:T(8,128)(2,1)S(1)}, u32[]{:S(2)}, u32[]{:S(2)}) collective-permute-start(bf16[216,128]{1,0:T(8,128)(2,1)S(1)} %get-tuple-element.113), channel_id=1, source_target_pairs={{0,4},{4,0},{8,12},{12,8},{16,20},{20,16},{24,28},{28,24},{1,5},{5... | collective-permute-start | bytes 165896 | tf_op jit(solution)/shard_map/ppermute | solution.py:1076
  62.1 0.2 collective-permute-start.17
  62.4 1.7 %collective-permute-start.18 = (bf16[216,128]{1,0:T(8,128)(2,1)S(1)}, bf16[216,128]{1,0:T(8,128)(2,1)S(1)}, u32[]{:S(2)}, u32[]{:S(2)}) collective-permute-start(bf16[216,128]{1,0:T(8,128)(2,1)S(1)} %get-tuple-element.115), channel_id=1, source_target_pairs={{0,12},{4,8},{8,4},{12,0},{16,28},{20,24},{24,20},{28,16},{1,13},{... | collective-permute-start | bytes 165896 | tf_op jit(solution)/shard_map/ppermute | solution.py:1076
  64.1 3.0 %collective-permute-start.19 = (bf16[216,128]{1,0:T(8,128)(2,1)S(1)}, bf16[216,128]{1,0:T(8,128)(2,1)S(1)}, u32[]{:S(2)}, u32[]{:S(2)}) collective-permute-start(bf16[216,128]{1,0:T(8,128)(2,1)S(1)} %get-tuple-element.116), channel_id=1, source_target_pairs={{0,16},{4,20},{8,24},{12,28},{16,0},{20,4},{24,8},{28,12},{1,17},{... | collective-permute-start | bytes 165896 | tf_op jit(solution)/shard_map/ppermute | solution.py:1076
  67.0 0.0 collective-permute-done.25.refs_3_
  67.1 1.6 %collective-permute-start.20 = (bf16[216,128]{1,0:T(8,128)(2,1)S(1)}, bf16[216,128]{1,0:T(8,128)(2,1)S(1)}, u32[]{:S(2)}, u32[]{:S(2)}) collective-permute-start(bf16[216,128]{1,0:T(8,128)(2,1)S(1)} %get-tuple-element.117), channel_id=1, source_target_pairs={{0,20},{4,16},{8,28},{12,24},{16,4},{20,0},{24,12},{28,8},{1,21},{... | collective-permute-start | bytes 165896 | tf_op jit(solution)/shard_map/ppermute | solution.py:1076
  68.7 1.8 %collective-permute-start.21 = (bf16[216,128]{1,0:T(8,128)(2,1)S(1)}, bf16[216,128]{1,0:T(8,128)(2,1)S(1)}, u32[]{:S(2)}, u32[]{:S(2)}) collective-permute-start(bf16[216,128]{1,0:T(8,128)(2,1)S(1)} %get-tuple-element.118), channel_id=1, source_target_pairs={{0,24},{4,28},{8,16},{12,20},{16,8},{20,12},{24,0},{28,4},{1,25},{... | collective-permute-start | bytes 165896 | tf_op jit(solution)/shard_map/ppermute | solution.py:1076
  70.5 0.0 collective-permute-done.17.refs_3_
  70.5 2.1 %collective-permute-start.22 = (bf16[216,128]{1,0:T(8,128)(2,1)S(1)}, bf16[216,128]{1,0:T(8,128)(2,1)S(1)}, u32[]{:S(2)}, u32[]{:S(2)}) collective-permute-start(bf16[216,128]{1,0:T(8,128)(2,1)S(1)} %get-tuple-element.119), channel_id=1, source_target_pairs={{0,28},{4,24},{8,20},{12,16},{16,12},{20,8},{24,4},{28,0},{1,29},{... | collective-permute-start | bytes 165896 | tf_op jit(solution)/shard_map/ppermute | solution.py:1076
  72.6 3.0 %collective-permute-done.20.refs_6_ = bf16[216,128]{1,0:T(8,128)(2,1)S(1)} collective-permute-done((bf16[216,128]{1,0:T(8,128)(2,1)S(1)}, bf16[216,128]{1,0:T(8,128)(2,1)S(1)}, u32[]{:S(2)}, u32[]{:S(2)}) %collective-permute-start.20) | collective-permute-done | bytes 55328 | tf_op jit(solution)/shard_map/ppermute | solution.py:1076
  75.6 0.0 collective-permute-done.21.refs_7_
  75.6 1.8 %collective-permute-done.22.refs_8_ = bf16[216,128]{1,0:T(8,128)(2,1)S(1)} collective-permute-done((bf16[216,128]{1,0:T(8,128)(2,1)S(1)}, bf16[216,128]{1,0:T(8,128)(2,1)S(1)}, u32[]{:S(2)}, u32[]{:S(2)}) %collective-permute-start.22) | collective-permute-done | bytes 55328 | tf_op jit(solution)/shard_map/ppermute | solution.py:1076
  77.5 1.3 %reduce.1 = f32[344,128]{1,0:T(8,128)S(1)} custom-call(s32[2]{0:T(128)S(1)} %pad_add_fusion.refs_0_, f32[216,128]{1,0:T(8,128)S(1)} %get-tuple-element.128.refs_1_, bf16[216,128]{1,0:T(8,128)(2,1)S(1)} %collective-permute-done.16.refs_2_, bf16[216,128]{1,0:T(8,128)(2,1)S(1)} %collective-permute-done.17.refs_3_, ...), custom_call_target="tpu_custom_call" | custom-call | tf_op jit(solution)/shard_map/reduce/pallas_call | solution.py:986
  78.8 0.0 collective-permute-start.26
  78.8 1.4 %collective-permute-done.26 = f32[344,128]{1,0:T(8,128)S(1)} collective-permute-done((f32[344,128]{1,0:T(8,128)S(1)}, f32[344,128]{1,0:T(8,128)S(1)}, u32[]{:S(2)}, u32[]{:S(2)}) %collective-permute-start.26) | collective-permute-done | bytes 176160 | tf_op jit(solution)/shard_map/ppermute | solution.py:1062
  80.2 0.6 collective-permute-start.27
  80.8 1.0 %collect.2 = bf16[4,2,16,4096]{3,2,1,0:T(8,128)(2,1)} custom-call(s32[1]{0:T(128)} %bitcast.refs_0_.member_ref, bf16[2,16,4096]{2,1,0:T(8,128)(2,1)S(1)} %get-tuple-element.99.refs_0_, bf16[2,16,4096]{2,1,0:T(8,128)(2,1)S(1)} %collective-permute-done.13.refs_1_, bf16[2,16,4096]{2,1,0:T(8,128)(2,1)S(1)} %collective-permute-done.14.refs_2_, ...), custom_call_target="tpu_custom_call" | custom-call | tf_op jit(solution)/shard_map/collect/pallas_call | solution.py:1036
  81.8 1.4 %collect.3 = f32[4,2,16,4096]{3,2,1,0:T(8,128)} custom-call(s32[1]{0:T(128)} %bitcast.refs_0_.member_ref, bf16[2,16,4096]{2,1,0:T(8,128)(2,1)S(1)} %get-tuple-element.124.refs_0_, bf16[2,16,4096]{2,1,0:T(8,128)(2,1)S(1)} %collective-permute-done.23.refs_1_, bf16[2,16,4096]{2,1,0:T(8,128)(2,1)S(1)} %collective-permute-done.24.refs_2_, ...), custom_call_target="tpu_custom_call" | custom-call | tf_op jit(solution)/shard_map/collect/pallas_call | solution.py:1036
  83.2 3.6 %collective-permute-done.27.refs_1_ = f32[344,128]{1,0:T(8,128)S(1)} collective-permute-done((f32[344,128]{1,0:T(8,128)S(1)}, f32[344,128]{1,0:T(8,128)S(1)}, u32[]{:S(2)}, u32[]{:S(2)}) %collective-permute-start.27) | collective-permute-done | bytes 176160 | tf_op jit(solution)/shard_map/ppermute | solution.py:1062
  86.8 0.8 finish.1
  (23 shorter events, 0.1 us)
Async XLA Ops:
  0.6 21.3 %copy-start.8 = (bf16[8,16,4096]{2,1,0:T(8,128)(2,1)S(1)}, bf16[8,16,4096]{2,1,0:T(8,128)(2,1)}, u32[]{:S(2)}) copy-start(bf16[8,16,4096]{2,1,0:T(8,128)(2,1)} %param.18) | copy-start | bytes 3145732
  2.5 20.2 %copy-start = (bf16[288,128]{1,0:T(8,128)(2,1)S(1)}, bf16[288,128]{1,0:T(8,128)(2,1)}, u32[]{:S(2)}) copy-start(bf16[288,128]{1,0:T(8,128)(2,1)} %pack.1.refs_4_.refs_9_) | copy-start | bytes 221188
  2.5 25.2 %copy-start.5 = (s32[8]{0:T(128)S(1)}, s32[8]{0:T(128)}, u32[]{:S(2)}) copy-start(s32[8]{0:T(128)} %refs_1_.3) | copy-start | bytes 100
  2.5 25.2 %copy-start.6 = (s32[8]{0:T(128)S(1)}, s32[8]{0:T(128)}, u32[]{:S(2)}) copy-start(s32[8]{0:T(128)} %refs_2_.3) | copy-start | bytes 100
  2.5 25.2 %copy-start.7 = (s32[8]{0:T(128)S(1)}, s32[8]{0:T(128)}, u32[]{:S(2)}) copy-start(s32[8]{0:T(128)} %refs_3_.1) | copy-start | bytes 100
  2.6 13.4 %collective-permute-start.12 = (bf16[288,128]{1,0:T(8,128)(2,1)}, bf16[288,128]{1,0:T(8,128)(2,1)S(1)}, u32[]{:S(2)}, u32[]{:S(2)}) collective-permute-start(bf16[288,128]{1,0:T(8,128)(2,1)} %pack.1.refs_4_.refs_9_), channel_id=1, source_target_pairs={{0,28},{4,24},{8,20},{12,16},{16,12},{20,8},{24,4},{28,0},{1,29},{... | collective-permute-start | bytes 221192 | tf_op jit(solution)/shard_map/ppermute | solution.py:1076
  8.6 7.4 %collective-permute-start.11 = (bf16[288,128]{1,0:T(8,128)(2,1)}, bf16[288,128]{1,0:T(8,128)(2,1)S(1)}, u32[]{:S(2)}, u32[]{:S(2)}) collective-permute-start(bf16[288,128]{1,0:T(8,128)(2,1)} %pack.1.refs_4_.refs_9_), channel_id=1, source_target_pairs={{0,24},{4,28},{8,16},{12,20},{16,8},{20,12},{24,0},{28,4},{1,25},{... | collective-permute-start | bytes 221192 | tf_op jit(solution)/shard_map/ppermute | solution.py:1076
  8.8 11.6 %collective-permute-start.10 = (bf16[288,128]{1,0:T(8,128)(2,1)}, bf16[288,128]{1,0:T(8,128)(2,1)S(1)}, u32[]{:S(2)}, u32[]{:S(2)}) collective-permute-start(bf16[288,128]{1,0:T(8,128)(2,1)} %pack.1.refs_4_.refs_9_), channel_id=1, source_target_pairs={{0,20},{4,16},{8,28},{12,24},{16,4},{20,0},{24,12},{28,8},{1,21},{... | collective-permute-start | bytes 221192 | tf_op jit(solution)/shard_map/ppermute | solution.py:1076
  9.6 13.1 %collective-permute-start.9 = (bf16[288,128]{1,0:T(8,128)(2,1)}, bf16[288,128]{1,0:T(8,128)(2,1)S(1)}, u32[]{:S(2)}, u32[]{:S(2)}) collective-permute-start(bf16[288,128]{1,0:T(8,128)(2,1)} %pack.1.refs_4_.refs_9_), channel_id=1, source_target_pairs={{0,16},{4,20},{8,24},{12,28},{16,0},{20,4},{24,8},{28,12},{1,17},{... | collective-permute-start | bytes 221192 | tf_op jit(solution)/shard_map/ppermute | solution.py:1076
  11.6 11.1 %collective-permute-start.8 = (bf16[288,128]{1,0:T(8,128)(2,1)}, bf16[288,128]{1,0:T(8,128)(2,1)S(1)}, u32[]{:S(2)}, u32[]{:S(2)}) collective-permute-start(bf16[288,128]{1,0:T(8,128)(2,1)} %pack.1.refs_4_.refs_9_), channel_id=1, source_target_pairs={{0,12},{4,8},{8,4},{12,0},{16,28},{20,24},{24,20},{28,16},{1,13},{... | collective-permute-start | bytes 221192 | tf_op jit(solution)/shard_map/ppermute | solution.py:1076
  16.0 13.9 %collective-permute-start.5 = (bf16[2,16,4096]{2,1,0:T(8,128)(2,1)}, bf16[2,16,4096]{2,1,0:T(8,128)(2,1)S(1)}, u32[]{:S(2)}, u32[]{:S(2)}) collective-permute-start(bf16[2,16,4096]{2,1,0:T(8,128)(2,1)} %get-tuple-element.148), channel_id=1, source_target_pairs={{0,3},{1,2},{2,1},{3,0},{4,7},{5,6},{6,5},{7,4},{8,11},{9,10},{10,... | collective-permute-start | bytes 786440 | tf_op jit(solution)/shard_map/ppermute | solution.py:1062
  16.0 15.4 %collective-permute-start.3 = (bf16[2,16,4096]{2,1,0:T(8,128)(2,1)}, bf16[2,16,4096]{2,1,0:T(8,128)(2,1)S(1)}, u32[]{:S(2)}, u32[]{:S(2)}) collective-permute-start(bf16[2,16,4096]{2,1,0:T(8,128)(2,1)} %get-tuple-element.149), channel_id=1, source_target_pairs={{0,1},{1,0},{2,3},{3,2},{4,5},{5,4},{6,7},{7,6},{8,9},{9,8},{10,11... | collective-permute-start | bytes 786440 | tf_op jit(solution)/shard_map/ppermute | solution.py:1062
  20.4 11.0 %collective-permute-start.4 = (bf16[2,16,4096]{2,1,0:T(8,128)(2,1)}, bf16[2,16,4096]{2,1,0:T(8,128)(2,1)S(1)}, u32[]{:S(2)}, u32[]{:S(2)}) collective-permute-start(bf16[2,16,4096]{2,1,0:T(8,128)(2,1)} %get-tuple-element.151), channel_id=1, source_target_pairs={{0,2},{1,3},{2,0},{3,1},{4,6},{5,7},{6,4},{7,5},{8,10},{9,11},{10,... | collective-permute-start | bytes 786440 | tf_op jit(solution)/shard_map/ppermute | solution.py:1062
  22.7 4.4 %collective-permute-start.7 = (bf16[288,128]{1,0:T(8,128)(2,1)S(1)}, bf16[288,128]{1,0:T(8,128)(2,1)S(1)}, u32[]{:S(2)}, u32[]{:S(2)}) collective-permute-start(bf16[288,128]{1,0:T(8,128)(2,1)S(1)} %copy-done), channel_id=1, source_target_pairs={{0,8},{4,12},{8,0},{12,4},{16,24},{20,28},{24,16},{28,20},{1,9},{5... | collective-permute-start | bytes 221192 | tf_op jit(solution)/shard_map/ppermute | solution.py:1076
  22.7 4.4 %collective-permute-start.6 = (bf16[288,128]{1,0:T(8,128)(2,1)S(1)}, bf16[288,128]{1,0:T(8,128)(2,1)S(1)}, u32[]{:S(2)}, u32[]{:S(2)}) collective-permute-start(bf16[288,128]{1,0:T(8,128)(2,1)S(1)} %copy-done), channel_id=1, source_target_pairs={{0,4},{4,0},{8,12},{12,8},{16,20},{20,16},{24,28},{28,24},{1,5},{5... | collective-permute-start | bytes 221192 | tf_op jit(solution)/shard_map/ppermute | solution.py:1076
  27.1 12.5 %collective-permute-start.2 = (bf16[2,16,4096]{2,1,0:T(8,128)(2,1)}, bf16[2,16,4096]{2,1,0:T(8,128)(2,1)S(1)}, u32[]{:S(2)}, u32[]{:S(2)}) collective-permute-start(bf16[2,16,4096]{2,1,0:T(8,128)(2,1)} %get-tuple-element.152), channel_id=1, source_target_pairs={{0,3},{1,2},{2,1},{3,0},{4,7},{5,6},{6,5},{7,4},{8,11},{9,10},{10,... | collective-permute-start | bytes 786440 | tf_op jit(solution)/shard_map/ppermute | solution.py:1062
  27.2 13.8 %collective-permute-start = (bf16[2,16,4096]{2,1,0:T(8,128)(2,1)S(1)}, bf16[2,16,4096]{2,1,0:T(8,128)(2,1)S(1)}, u32[]{:S(2)}, u32[]{:S(2)}) collective-permute-start(bf16[2,16,4096]{2,1,0:T(8,128)(2,1)S(1)} %get-tuple-element.153), channel_id=1, source_target_pairs={{0,1},{1,0},{2,3},{3,2},{4,5},{5,4},{6,7},{7,6},{8,9},{9,8},{10,11... | collective-permute-start | bytes 786440 | tf_op jit(solution)/shard_map/ppermute | solution.py:1062
  29.8 11.8 %collective-permute-start.1 = (bf16[2,16,4096]{2,1,0:T(8,128)(2,1)S(1)}, bf16[2,16,4096]{2,1,0:T(8,128)(2,1)S(1)}, u32[]{:S(2)}, u32[]{:S(2)}) collective-permute-start(bf16[2,16,4096]{2,1,0:T(8,128)(2,1)S(1)} %get-tuple-element.155), channel_id=1, source_target_pairs={{0,2},{1,3},{2,0},{3,1},{4,6},{5,7},{6,4},{7,5},{8,10},{9,11},{10,... | collective-permute-start | bytes 786440 | tf_op jit(solution)/shard_map/ppermute | solution.py:1062
  39.0 12.7 %collective-permute-start.13 = (bf16[2,16,4096]{2,1,0:T(8,128)(2,1)S(1)}, bf16[2,16,4096]{2,1,0:T(8,128)(2,1)S(1)}, u32[]{:S(2)}, u32[]{:S(2)}) collective-permute-start(bf16[2,16,4096]{2,1,0:T(8,128)(2,1)S(1)} %get-tuple-element.96), channel_id=1, source_target_pairs={{0,1},{1,0},{2,3},{3,2},{4,5},{5,4},{6,7},{7,6},{8,9},{9,8},{10,11... | collective-permute-start | bytes 786440 | tf_op jit(solution)/shard_map/ppermute | solution.py:1062
  39.0 13.8 %collective-permute-start.14 = (bf16[2,16,4096]{2,1,0:T(8,128)(2,1)S(1)}, bf16[2,16,4096]{2,1,0:T(8,128)(2,1)S(1)}, u32[]{:S(2)}, u32[]{:S(2)}) collective-permute-start(bf16[2,16,4096]{2,1,0:T(8,128)(2,1)S(1)} %get-tuple-element.97), channel_id=1, source_target_pairs={{0,2},{1,3},{2,0},{3,1},{4,6},{5,7},{6,4},{7,5},{8,10},{9,11},{10,... | collective-permute-start | bytes 786440 | tf_op jit(solution)/shard_map/ppermute | solution.py:1062
  39.6 13.3 %collective-permute-start.15 = (bf16[2,16,4096]{2,1,0:T(8,128)(2,1)S(1)}, bf16[2,16,4096]{2,1,0:T(8,128)(2,1)S(1)}, u32[]{:S(2)}, u32[]{:S(2)}) collective-permute-start(bf16[2,16,4096]{2,1,0:T(8,128)(2,1)S(1)} %get-tuple-element.98), channel_id=1, source_target_pairs={{0,3},{1,2},{2,1},{3,0},{4,7},{5,6},{6,5},{7,4},{8,11},{9,10},{10,... | collective-permute-start | bytes 786440 | tf_op jit(solution)/shard_map/ppermute | solution.py:1062
  50.9 11.5 %collective-permute-start.23 = (bf16[2,16,4096]{2,1,0:T(8,128)(2,1)S(1)}, bf16[2,16,4096]{2,1,0:T(8,128)(2,1)S(1)}, u32[]{:S(2)}, u32[]{:S(2)}) collective-permute-start(bf16[2,16,4096]{2,1,0:T(8,128)(2,1)S(1)} %get-tuple-element.121), channel_id=1, source_target_pairs={{0,1},{1,0},{2,3},{3,2},{4,5},{5,4},{6,7},{7,6},{8,9},{9,8},{10,11... | collective-permute-start | bytes 786440 | tf_op jit(solution)/shard_map/ppermute | solution.py:1062
  51.0 13.1 %collective-permute-start.24 = (bf16[2,16,4096]{2,1,0:T(8,128)(2,1)S(1)}, bf16[2,16,4096]{2,1,0:T(8,128)(2,1)S(1)}, u32[]{:S(2)}, u32[]{:S(2)}) collective-permute-start(bf16[2,16,4096]{2,1,0:T(8,128)(2,1)S(1)} %get-tuple-element.122), channel_id=1, source_target_pairs={{0,2},{1,3},{2,0},{3,1},{4,6},{5,7},{6,4},{7,5},{8,10},{9,11},{10,... | collective-permute-start | bytes 786440 | tf_op jit(solution)/shard_map/ppermute | solution.py:1062
  51.6 15.4 %collective-permute-start.25 = (bf16[2,16,4096]{2,1,0:T(8,128)(2,1)S(1)}, bf16[2,16,4096]{2,1,0:T(8,128)(2,1)S(1)}, u32[]{:S(2)}, u32[]{:S(2)}) collective-permute-start(bf16[2,16,4096]{2,1,0:T(8,128)(2,1)S(1)} %get-tuple-element.123), channel_id=1, source_target_pairs={{0,3},{1,2},{2,1},{3,0},{4,7},{5,6},{6,5},{7,4},{8,11},{9,10},{10,... | collective-permute-start | bytes 786440 | tf_op jit(solution)/shard_map/ppermute | solution.py:1062
  52.9 24.5 %copy-start.1 = (bf16[32,128]{1,0:T(8,128)(2,1)S(1)}, bf16[32,128]{1,0:T(8,128)(2,1)}, u32[]{:S(2)}) copy-start(bf16[32,128]{1,0:T(8,128)(2,1)} %refs_19_.1) | copy-start | bytes 24580
  52.9 24.5 %copy-start.2 = (bf16[32,128]{1,0:T(8,128)(2,1)S(1)}, bf16[32,128]{1,0:T(8,128)(2,1)}, u32[]{:S(2)}) copy-start(bf16[32,128]{1,0:T(8,128)(2,1)} %refs_20_.1) | copy-start | bytes 24580
  52.9 24.5 %copy-start.3 = (bf16[32,32]{1,0:T(8,128)(2,1)S(1)}, bf16[32,32]{1,0:T(8,128)(2,1)}, u32[]{:S(2)}) copy-start(bf16[32,32]{1,0:T(8,128)(2,1)} %refs_18_.1) | copy-start | bytes 6148
  52.9 24.5 %copy-start.4 = (bf16[18,32]{1,0:T(8,128)(2,1)S(1)}, bf16[18,32]{1,0:T(8,128)(2,1)}, u32[]{:S(2)}) copy-start(bf16[18,32]{1,0:T(8,128)(2,1)} %refs_17_.1) | copy-start | bytes 3460
  60.5 8.1 %collective-permute-start.16 = (bf16[216,128]{1,0:T(8,128)(2,1)S(1)}, bf16[216,128]{1,0:T(8,128)(2,1)S(1)}, u32[]{:S(2)}, u32[]{:S(2)}) collective-permute-start(bf16[216,128]{1,0:T(8,128)(2,1)S(1)} %get-tuple-element.113), channel_id=1, source_target_pairs={{0,4},{4,0},{8,12},{12,8},{16,20},{20,16},{24,28},{28,24},{1,5},{5... | collective-permute-start | bytes 165896 | tf_op jit(solution)/shard_map/ppermute | solution.py:1076
  62.1 8.4 %collective-permute-start.17 = (bf16[216,128]{1,0:T(8,128)(2,1)S(1)}, bf16[216,128]{1,0:T(8,128)(2,1)S(1)}, u32[]{:S(2)}, u32[]{:S(2)}) collective-permute-start(bf16[216,128]{1,0:T(8,128)(2,1)S(1)} %get-tuple-element.114), channel_id=1, source_target_pairs={{0,8},{4,12},{8,0},{12,4},{16,24},{20,28},{24,16},{28,20},{1,9},{5... | collective-permute-start | bytes 165896 | tf_op jit(solution)/shard_map/ppermute | solution.py:1076
  62.4 10.2 %collective-permute-start.18 = (bf16[216,128]{1,0:T(8,128)(2,1)S(1)}, bf16[216,128]{1,0:T(8,128)(2,1)S(1)}, u32[]{:S(2)}, u32[]{:S(2)}) collective-permute-start(bf16[216,128]{1,0:T(8,128)(2,1)S(1)} %get-tuple-element.115), channel_id=1, source_target_pairs={{0,12},{4,8},{8,4},{12,0},{16,28},{20,24},{24,20},{28,16},{1,13},{... | collective-permute-start | bytes 165896 | tf_op jit(solution)/shard_map/ppermute | solution.py:1076
  64.1 8.5 %collective-permute-start.19 = (bf16[216,128]{1,0:T(8,128)(2,1)S(1)}, bf16[216,128]{1,0:T(8,128)(2,1)S(1)}, u32[]{:S(2)}, u32[]{:S(2)}) collective-permute-start(bf16[216,128]{1,0:T(8,128)(2,1)S(1)} %get-tuple-element.116), channel_id=1, source_target_pairs={{0,16},{4,20},{8,24},{12,28},{16,0},{20,4},{24,8},{28,12},{1,17},{... | collective-permute-start | bytes 165896 | tf_op jit(solution)/shard_map/ppermute | solution.py:1076
  67.1 8.6 %collective-permute-start.20 = (bf16[216,128]{1,0:T(8,128)(2,1)S(1)}, bf16[216,128]{1,0:T(8,128)(2,1)S(1)}, u32[]{:S(2)}, u32[]{:S(2)}) collective-permute-start(bf16[216,128]{1,0:T(8,128)(2,1)S(1)} %get-tuple-element.117), channel_id=1, source_target_pairs={{0,20},{4,16},{8,28},{12,24},{16,4},{20,0},{24,12},{28,8},{1,21},{... | collective-permute-start | bytes 165896 | tf_op jit(solution)/shard_map/ppermute | solution.py:1076
  68.7 7.0 %collective-permute-start.21 = (bf16[216,128]{1,0:T(8,128)(2,1)S(1)}, bf16[216,128]{1,0:T(8,128)(2,1)S(1)}, u32[]{:S(2)}, u32[]{:S(2)}) collective-permute-start(bf16[216,128]{1,0:T(8,128)(2,1)S(1)} %get-tuple-element.118), channel_id=1, source_target_pairs={{0,24},{4,28},{8,16},{12,20},{16,8},{20,12},{24,0},{28,4},{1,25},{... | collective-permute-start | bytes 165896 | tf_op jit(solution)/shard_map/ppermute | solution.py:1076
  70.5 7.0 %collective-permute-start.22 = (bf16[216,128]{1,0:T(8,128)(2,1)S(1)}, bf16[216,128]{1,0:T(8,128)(2,1)S(1)}, u32[]{:S(2)}, u32[]{:S(2)}) collective-permute-start(bf16[216,128]{1,0:T(8,128)(2,1)S(1)} %get-tuple-element.119), channel_id=1, source_target_pairs={{0,28},{4,24},{8,20},{12,16},{16,12},{20,8},{24,4},{28,0},{1,29},{... | collective-permute-start | bytes 165896 | tf_op jit(solution)/shard_map/ppermute | solution.py:1076
  78.8 1.4 %collective-permute-start.26 = (f32[344,128]{1,0:T(8,128)S(1)}, f32[344,128]{1,0:T(8,128)S(1)}, u32[]{:S(2)}, u32[]{:S(2)}) collective-permute-start(f32[344,128]{1,0:T(8,128)S(1)} %reduce.1), channel_id=1, source_target_pairs={{0,1},{1,0},{2,3},{3,2},{4,5},{5,4},{6,7},{7,6},{8,9},{9,8},{10,11... | collective-permute-start | bytes 528392 | tf_op jit(solution)/shard_map/ppermute | solution.py:1062
  80.2 6.6 %collective-permute-start.27 = (f32[344,128]{1,0:T(8,128)S(1)}, f32[344,128]{1,0:T(8,128)S(1)}, u32[]{:S(2)}, u32[]{:S(2)}) collective-permute-start(f32[344,128]{1,0:T(8,128)S(1)} %add.23.refs_0_), channel_id=1, source_target_pairs={{0,2},{1,3},{2,0},{3,1},{4,6},{5,7},{6,4},{7,5},{8,10},{9,11},{10,... | collective-permute-start | bytes 528392 | tf_op jit(solution)/shard_map/ppermute | solution.py:1062

commit v4 on v3

--- a/solution.py
+++ b/solution.py
@@ -21,7 +21,7 @@
 precise = lax.Precision.HIGHEST
 f32 = jnp.float32
 bf16 = jnp.bfloat16
-VMEM_LIMIT = 24 * 2**20
+VMEM_LIMIT = 16 * 2**20
 VMEM_MOST = 60 * 2**20
 
 
@@ -110,12 +110,12 @@
     return pl.multiple_of((member ^ offset) * strip, strip)
 
 
-def load_strips(member, strips, f, image):
+def load_strips(member, strips, image):
     for offset, strip in enumerate(strips):
-        rows = strip.shape[1]
+        rows = strip.shape[0]
         start = strip_start(member, offset, rows)
         for j in range(PAIRS):
-            image[j, pl.ds(start, rows), :] = strip[f, :, j * LANES : (j + 1) * LANES].astype(f32)
+            image[j, pl.ds(start, rows), :] = strip[:, j * LANES : (j + 1) * LANES].astype(f32)
 
 
 def store_strips(member, image, f, strips):
@@ -141,35 +141,53 @@
                 started.remove(step)
 
 
+def gather_frame(member, strips, image, stats):
+    load_strips(member, strips, image)
+
+    def add_stats(j, carry):
+        x = image[j]
+        s, q = carry
+        return s + x, q + x * x
+
+    zero = jnp.zeros((H, LANES), f32)
+    s, q = over_pairs(add_stats, (zero, zero))
+    average, inverse = norm_stats(total(s), total(q))
+    stats[0:1, :] = average[0:1]
+    stats[1:2, :] = inverse[0:1]
+    stats[2:3, :] = both_parities(total(s))[0:1]
+    stats[3:8, :] = jnp.zeros((5, LANES), f32)
+
+
+def gather_kernel(member_ref, array, far, near, images, all_stats, own, sent):
+    member = member_ref[0]
+    frames = images.shape[0]
+    copy = pltpu.make_async_copy(array.at[pl.ds(member * frames, frames)], own, sent)
+    copy.start()
+    first = member % 2 * frames
+    copy.wait()
+    for f in range(frames):
+        strips = (own.at[f], near.at[f], far.at[first + f], near.at[frames + f])
+        gather_frame(member, strips, images.at[f], all_stats.at[f])
+
+
 def forward_kernel(count, *refs):
-    member_ref = refs[0]
-    strips = refs[1 : 1 + count]
-    styles, biases, w_one, w_two, w_down, w_up = refs[1 + count : 7 + count]
-    out = refs[7 + count : 7 + 2 * count]
-    outs = refs[7 + 2 * count : 14 + 2 * count]
-    images, levels = refs[14 + 2 * count :]
+    member_ref, frame_images, frame_stats, styles, biases, w_one, w_two, w_down, w_up = refs[:9]
+    out = refs[9 : 9 + count]
+    outs = refs[9 + count : 16 + count]
+    images, levels = refs[16 + count :]
     member = member_ref[0]
     low_lanes = lane_ids((HALF, LANES)) < C
 
     def frame(f):
         win_one, win_two, win_level, win_coarse, middle, down, stats = (ref.at[f] for ref in outs)
-        image, level, style = images.at[f], levels.at[f], styles.at[f]
-        load_strips(member, strips, f, image)
-
-        def add_stats(j, carry):
-            x = image[j]
-            s, q = carry
-            return s + x, q + x * x
-
-        zero = jnp.zeros((H, LANES), f32)
-        s, q = over_pairs(add_stats, (zero, zero))
-        average_one, inverse_one = norm_stats(total(s), total(q))
+        frame_image, image, level, style = frame_images.at[f], images.at[f], levels.at[f], styles.at[f]
+        average_one, inverse_one = frame_stats[f, 0:1, :], frame_stats[f, 1:2, :]
         gain_one = inverse_one * style[0:1, :]
-        half_gain = 0.5 * gain_one[0:1]
-        half_shift = 0.5 * (style[1:2, :] - average_one[0:1] * gain_one[0:1])
+        half_gain = 0.5 * gain_one
+        half_shift = 0.5 * (style[1:2, :] - average_one * gain_one)
 
         def act_one(parity, j):
-            h = parity_rows(image, parity, j) * half_gain + half_shift
+            h = parity_rows(frame_image, parity, j) * half_gain + half_shift
             return h * jnp.tanh(h) + h
 
         build_windows(win_one, act_one)
@@ -184,8 +202,8 @@
             middle[a] = tiles_of(v)
         yield
         average_two, inverse_two = norm_stats(sums, squares)
-        stats[0:1, :] = average_one[0:1]
-        stats[1:2, :] = inverse_one[0:1]
+        stats[0:1, :] = average_one
+        stats[1:2, :] = inverse_one
         stats[2:3, :] = average_two[0:1]
         stats[3:4, :] = inverse_two[0:1]
         stats[4:8, :] = jnp.zeros((4, LANES), f32)
@@ -202,7 +220,7 @@
         y = matmul(window_operand(win_two, range(4)), w_two[...])
         for a in range(2):
             v = y[:, a * LANES : (a + 1) * LANES] + biases[1:2, :]
-            level[a] = tiles_of(v) + image[:, pl.ds(a, HALF, stride=2), :]
+            level[a] = tiles_of(v) + frame_image[:, pl.ds(a, HALF, stride=2), :]
         yield
         build_windows(win_level, lambda parity, j: level[parity, j])
         yield
@@ -244,29 +262,24 @@
 
 def backward_kernel(count, *refs):
     member_ref = refs[0]
-    cot_strips = refs[1 : 1 + count]
-    frame_strips = refs[1 + count : 1 + 2 * count]
-    styles, all_stats, all_middle, all_down, w_up, w_down, w_two, w_one = refs[1 + 2 * count : 9 + 2 * count]
-    out = refs[9 + 2 * count : 9 + 3 * count]
-    outs = refs[9 + 3 * count : 15 + 3 * count]
-    scratch = refs[15 + 3 * count :]
+    cot_images, cot_stats, frame_images, styles, all_stats, all_middle, all_down = refs[1:8]
+    w_up, w_down, w_two, w_one = refs[8:12]
+    out = refs[12 : 12 + count]
+    outs = refs[12 + count : 18 + count]
+    scratch = refs[18 + count :]
     member = member_ref[0]
     low_lanes = lane_ids((HALF, LANES)) < C
 
     def frame(f):
         tile_out, tile_level, tile_mid, coarse_pairs, pieces, bias_sums = (ref.at[f] for ref in outs)
         image, level_grad, pre_grad, windows, coarse_below = (ref.at[f] for ref in scratch)
-        style, stats, middle, down = (ref.at[f] for ref in (styles, all_stats, all_middle, all_down))
-        load_strips(member, cot_strips, f, image)
-
-        def add_rows(j, s):
-            return s + image[j]
-
-        sums = over_pairs(add_rows, jnp.zeros((H, LANES), f32))
-        bias_up_sum = both_parities(total(sums))
+        style, stats, middle, down, frame_image = (
+            ref.at[f] for ref in (styles, all_stats, all_middle, all_down, frame_images)
+        )
+        cot_image = cot_images.at[f]
 
         def out_tile(parity, j):
-            x = parity_rows(image, parity, j)
+            x = parity_rows(cot_image, parity, j)
             tile_out[parity, j] = x.astype(bf16)
             return x
 
@@ -274,7 +287,9 @@
         yield
         y = matmul(window_operand(windows, range(4)), w_up[...])
         for a in range(2):
-            level_grad[a] = tiles_of(y[:, (2 + a) * LANES : (3 + a) * LANES]) + image[:, pl.ds(a, HALF, stride=2), :]
+            level_grad[a] = (
+                tiles_of(y[:, (2 + a) * LANES : (3 + a) * LANES]) + cot_image[:, pl.ds(a, HALF, stride=2), :]
+            )
         coarse = y[:, :LANES] + y[:, LANES : 2 * LANES]
         pre_grad[0] = tiles_of(coarse)
         yield
@@ -294,7 +309,6 @@
         zero = jnp.zeros((HALF, LANES), f32)
         _, sums = over_pairs(coarse_body, (zero, zero))
         bias_down_sum = jnp.broadcast_to(total(sums), (8, LANES))
-        load_strips(member, frame_strips, f, image)
         yield
         operand = jnp.concatenate(
             [coarse_pairs[...].reshape(BLOCK, LANES), coarse_below[...].reshape(BLOCK, LANES)], axis=1
@@ -354,13 +368,13 @@
         yield
         y = matmul(window_operand(windows, range(4)), w_one[...])
         scale_one, shift_one, gain_one, slope_one, constant_one = norm_slopes(
-            y, lambda a: image[:, pl.ds(a, HALF, stride=2), :].reshape(BLOCK, LANES), 0
+            y, lambda a: frame_image[:, pl.ds(a, HALF, stride=2), :].reshape(BLOCK, LANES), 0
         )
         yield
 
         def frame_body(j, carry):
             for parity in range(2):
-                x = parity_rows(image, parity, j)
+                x = parity_rows(frame_image, parity, j)
                 g = pre_grad[parity, j] * gain_one + (constant_one - x * slope_one) + level_grad[parity, j]
                 image[j, pl.ds(parity, HALF, stride=2), :] = g
             return carry
@@ -370,7 +384,7 @@
         for k, value in enumerate((scale_one, shift_one, scale_two, shift_two)):
             pieces[k : k + 1, :] = value[0:1]
         pieces[4:8, :] = jnp.zeros((4, LANES), f32)
-        for k, value in enumerate((bias_one_sum, bias_two_sum, bias_down_sum, bias_up_sum)):
+        for k, value in enumerate((bias_one_sum, bias_two_sum, bias_down_sum, cot_stats[f, 2:3, :])):
             bias_sums[k : k + 1, :] = value[0:1]
         bias_sums[4:8, :] = jnp.zeros((4, LANES), f32)
 
@@ -431,14 +445,28 @@
 
 
 PARTS = 16
+FAR_HINT = 90
+PAIR_PARTS = 24
+
+
+def three_parts(exact):
+    high = exact.astype(bf16).astype(f32)
+    rest = exact - high
+    mid = rest.astype(bf16).astype(f32)
+    return jnp.concatenate([high, mid, rest - mid], axis=0)
+
+
+def below(block, rows):
+    if block.shape[0] == rows:
+        return block
+    return jnp.concatenate([block, jnp.zeros((rows - block.shape[0], LANES), f32)], axis=0)
 
 
 def message_kernel(count, rows, *refs):
     where_ref, wins, tiles = refs[0], refs[1:5], refs[5:9]
-    pieces, bias_sums = refs[9:11]
-    outs = refs[11 : 11 + count]
-    sums = refs[11 + count : 15 + count]
-    g_pair, g_up, g_down, small = refs[15 + count :]
+    pieces, bias_sums, kept, small, theirs = refs[9:14]
+    sums = refs[14:18]
+    g_pair, g_up, g_down = refs[18:]
     sum_one, sum_two, sum_down, sum_up = sums
     accumulate(wins, tiles, sums)
 
@@ -463,69 +491,81 @@
             if f > 0:
                 total_bias = total_bias + bias_sums[f, 0:4, :]
         small[4 * frames : 4 * frames + 4, :] = total_bias
-        exact = small[...]
-        high = exact.astype(bf16).astype(f32)
-        rest = exact - high
-        mid = rest.astype(bf16).astype(f32)
-        parts = (high, mid, rest - mid)
+        sent = below(three_parts(small[...]), rows)
         low_lanes = lane_ids((rows, LANES)) < C
-        nothing = jnp.zeros((rows - 3 * PARTS, LANES), f32)
-        sent = jnp.concatenate([*parts, nothing], axis=0)
-        kept = jnp.concatenate([exact, jnp.zeros((2 * PARTS, LANES), f32), nothing], axis=0)
-        for offset in range(count):
-            start = pl.multiple_of(seq_owner(where_ref[0], offset) * rows, 8)
-            block = jnp.concatenate(
-                [
+        half = count // 2
+        for at in range(half):
+            for ref, mine in ((kept, True), (theirs, False)):
+                start = pl.multiple_of(seq_owner(where_ref[0], where_ref[1], half, at, mine) * rows, 8)
+                blocks = (
                     g_pair[pl.ds(start, rows), :],
                     jnp.where(
                         low_lanes,
                         g_up[pl.ds(pl.multiple_of(2 * start, 8), rows), :],
                         swap_halves(g_up[pl.ds(pl.multiple_of(2 * start + rows, 8), rows), :]),
                     ),
-                    jnp.where(low_lanes, g_down[pl.ds(start, rows), :], kept if offset == 0 else sent),
-                ],
-                axis=0,
-            )
-            outs[offset][...] = block.astype(outs[offset].dtype)
-
-
-def reduce_kernel(count, rows, cells, frames, *refs):
+                    jnp.where(low_lanes, g_down[pl.ds(start, rows), :], 0.0 if mine else sent),
+                )
+                ref[at * 3 * rows : (at + 1) * 3 * rows, :] = jnp.concatenate(blocks, axis=0).astype(ref.dtype)
+
+
+def join_kernel(half, rows, frames, where_ref, kept, small, theirs, own, *messages):
+    first = where_ref[1] % 2 == 0
+    at = 2 * rows
+    other = theirs[at : at + 3 * PARTS, :].astype(f32)
+    other = other[:PARTS] + other[PARTS : 2 * PARTS] + other[2 * PARTS :]
+    mine = small[...]
+    n = 4 * frames
+    exact = jnp.concatenate(
+        [
+            jnp.where(first, mine[:n], other[:n]),
+            jnp.where(first, other[:n], mine[:n]),
+            mine[n : n + 4] + other[n : n + 4],
+            jnp.zeros((PAIR_PARTS - 2 * n - 4, LANES), f32),
+        ],
+        axis=0,
+    )
+    low_lanes = lane_ids((rows, LANES)) < C
+    sent = below(three_parts(exact), rows)
+    size = 3 * rows
+    for k, message in enumerate(messages):
+        block = kept[k * size : (k + 1) * size, :] + theirs[k * size : (k + 1) * size, :].astype(f32)
+        message[:at, :] = block[:at].astype(bf16)
+        message[at:, :] = jnp.where(low_lanes, block[at:], sent).astype(bf16)
+        if k == 0:
+            own[:at, :] = block[:at]
+            own[at:, :] = jnp.where(low_lanes, block[at:], below(exact, rows))
+
+
+def reduce_kernel(half, rows, cells, frames, *refs):
     where_ref, own = refs[:2]
-    messages = refs[2 : 1 + count]
-    packs = refs[1 + count : 1 + 2 * count]
-    act_table, noise_table, ada_one, ada_two, out, pieces_one, pieces_two, table = refs[1 + 2 * count :]
+    messages = refs[2 : 2 + half]
+    hots, act_table, noise_table, ada_one, ada_two, out, pieces_one, pieces_two, table = refs[2 + half :]
     place, member = where_ref[0], where_ref[1]
     taken = 4 * frames
     bias = jnp.zeros((4, LANES), f32)
-    sums = own[...]
+    sums = None
     lanes = lane_ids((1, LANES))
     low_lanes = lanes < C
-    hot = []
-    for offset in range(count):
-        if offset == 0:
-            small = sums[2 * rows : 2 * rows + PARTS]
-        else:
-            message = messages[offset - 1][...].astype(f32)
-            sums = sums + message
-            first = 2 * rows
-            small = (
-                message[first : first + PARTS]
-                + message[first + PARTS : first + 2 * PARTS]
-                + message[first + 2 * PARTS : first + 3 * PARTS]
-            )
+    at = 2 * rows
+    for k, ref in enumerate(messages):
+        message = ref[...].astype(f32)
+        if k == 0:
+            message = jnp.where(member % 2 == 0, own[...], message)
+        sums = message if sums is None else sums + message
+        small = (
+            message[at : at + PAIR_PARTS]
+            + message[at + PAIR_PARTS : at + 2 * PAIR_PARTS]
+            + message[at + 2 * PAIR_PARTS : at + 3 * PAIR_PARTS]
+        )
         turned = swap_halves(small)
         bias = bias + small[taken : taken + 4]
-        ids = packs[offset][2 * rows + ID_ROW : 2 * rows + ID_ROW + 8, :].astype(f32)
         for f in range(frames):
-            at = offset * frames + f
-            for k, ref in ((0, pieces_one), (2, pieces_two)):
-                ref[at : at + 1, :] = jnp.where(low_lanes, turned[4 * f + k : 4 * f + k + 1], small[4 * f + k + 1 : 4 * f + k + 2])
-            mine = jnp.where(lane_ids(ids.shape) == C + member * frames + f, ids, 0.0)
-            mine = jnp.sum(mine, axis=1, keepdims=True)
-            action, noise, valid = mine[0:1], mine[1:2], mine[2:3]
-            place_at = lanes.astype(f32)
-            hot.append(jnp.where(place_at == action + ACT_ROW, valid, 0.0) + jnp.where(place_at == noise + NOISE_ROW, 1.0, 0.0))
-    hot = jnp.concatenate(hot, axis=0)[:, :TABLE_ROWS]
+            row = k * frames + f
+            for kind, piece in ((0, pieces_one), (2, pieces_two)):
+                low, high = 4 * f + kind, 4 * f + kind + 1
+                piece[row : row + 1, :] = jnp.where(low_lanes, turned[low : low + 1], small[high : high + 1])
+    hot = hots[:, :TABLE_ROWS]
     table[...] = jnp.zeros_like(table)
     table[ACT_ROW : ACT_ROW + NACT, :] = act_table[...].astype(f32)
     table[NOISE_ROW : NOISE_ROW + NLEV, :] = noise_table[...].astype(f32)
@@ -545,7 +585,7 @@
     out[at : at + TABLE_ROWS, :cells] = exact(hot, embed_grad, ((0,), (0,)))
     at = at + TABLE_ROWS
     bias = jnp.concatenate([bias, jnp.zeros((4, LANES), f32)], axis=0)
-    width = C // count
+    width = C // (2 * half)
     out[at : at + 8, :] = pltpu.roll(bias, (C - place * width) % LANES, axis=1)
 
 
@@ -661,6 +701,22 @@
 def turned(values):
     wide = jnp.concatenate([values, jnp.zeros((C, LANES - values.shape[1]), f32)], axis=1)
     return jnp.concatenate([wide, jnp.zeros((C, LANES), f32)], axis=0).T[: values.shape[1]]
+
+
+def far_kernel(member_ref, array, out, sent):
+    half = array.shape[0] // 2
+    copy = pltpu.make_async_copy(array.at[pl.ds((1 - member_ref[0] // 2) * half, half)], out, sent)
+    copy.start()
+    copy.wait()
+
+
+def near_kernel(member_ref, array, far, out, sent):
+    share = out.shape[0] // 2
+    other = member_ref[0] ^ 1
+    copy = pltpu.make_async_copy(array.at[pl.ds(other * share, share)], out.at[pl.ds(0, share)], sent)
+    copy.start()
+    out[share:] = far[pl.ds(other % 2 * share, share)]
+    copy.wait()
 
 
 def pack_kernel(*refs):
@@ -699,22 +755,44 @@
     out[...] = work[...].astype(bf16)
 
 
-def seq_owner(place, offset):
-    return place ^ offset
+def seq_owner(place, member, half, at, mine=True):
+    side = member % 2 if mine else 1 - member % 2
+    even, odd = sides(2 * half)
+    return place ^ (even[at] + side * (odd[at] - even[at]))
+
+
+def sides(count):
+    ones = lambda offset: bin(offset).count("1") % 2
+    return tuple([offset for offset in range(count) if ones(offset) == side] for side in (0, 1))
+
+
+def write_hots(hots, at, first, frames, ids):
+    lanes = lane_ids((1, LANES)).astype(f32)
+    for f in range(frames):
+        mine = jnp.where(lane_ids(ids.shape) == C + first + f, ids, 0.0)
+        mine = jnp.sum(mine, axis=1, keepdims=True)
+        action, noise, valid = mine[0:1], mine[1:2], mine[2:3]
+        hots[at + f : at + f + 1, :] = jnp.where(lanes == action + ACT_ROW, valid, 0.0) + jnp.where(
+            lanes == noise + NOISE_ROW, 1.0, 0.0
+        )
 
 
 def prepare_kernel(count, rows, cells, *refs):
-    where_ref, actions, noise_ids, valid = refs[:4]
-    packs = refs[4 : 4 + count]
-    outs = refs[4 + count : 12 + count]
-    styles, biases = refs[12 + count : 14 + count]
-    work_pair, work_up, work_down, work_one, work_two, work_table = refs[14 + count :]
+    where_ref, actions, noise_ids, valid, packed, mine, other = refs[:7]
+    outs = refs[7:15]
+    styles, biases, hots = refs[15:18]
+    work_pair, work_up, work_down, work_one, work_two, work_table = refs[18:]
     place, member, frames = where_ref[0], where_ref[1], styles.shape[0]
-    style_at, _, _ = pack_sizes(rows, cells)
+    style_at, _, size = pack_sizes(rows, cells)
     bias_rows = jnp.zeros(SMALL, f32)
-    for offset, ref in enumerate(packs):
-        pack = ref[...].astype(f32)
-        owner = seq_owner(place, offset)
+    half = count // 2
+    for offset in range(count):
+        ref = mine if offset < half else other
+        at = offset % half
+        pack = ref[at * size : (at + 1) * size, :].astype(f32)
+        if at == 0:
+            pack = jnp.where(member % 2 == offset // half, packed[...].astype(f32), pack)
+        owner = seq_owner(place, member, half, at, offset < half)
         start = pl.multiple_of(owner * rows, 8)
         work_pair[pl.ds(start, rows), :] = pack[:rows]
         halves = pack[rows : 2 * rows]
@@ -737,6 +815,8 @@
         width = C // count
         slots = jnp.where((lane_ids(SMALL) >= C) & (lane_ids(SMALL) < C + width), slots, 0.0)
         bias_rows = bias_rows + pltpu.roll(slots, (owner * width + C) % LANES, axis=1)
+        if offset < half:
+            write_hots(hots, at * 2 * frames, member // 2 * 2 * frames, 2 * frames, extra[ID_ROW : ID_ROW + 8])
     biases[...] = bias_rows + swap_halves(bias_rows)
 
     lanes = lane_ids((8, LANES))
@@ -833,12 +913,26 @@
     )(conv_one, conv_two, down_kernel, up_kernel)
 
 
-def forward(member, strips, styles, biases, w_one, w_two, w_down, w_up):
-    count = len(strips)
-    frames, strip, _ = strips[0].shape
+def gather_frames(member, array, far, hint=0):
+    frames = array.shape[0] // lax.axis_size("rows")
+    near = trade(cut_near(member, array, far, hint), 1)
+    return pl.pallas_call(
+        gather_kernel,
+        in_specs=[in_smem(), in_place()] + [in_vmem()] * 2,
+        out_specs=[in_vmem()] * 2,
+        out_shape=[shape((frames,) + IMAGE, f32), shape((frames,) + SMALL, f32)],
+        scratch_shapes=[pltpu.VMEM((frames,) + array.shape[1:], array.dtype), pltpu.SemaphoreType.DMA],
+        compiler_params=params(),
+        name="frames",
+    )(member, array, far, near)
+
+
+def forward(member, frame_images, frame_stats, styles, biases, w_one, w_two, w_down, w_up, count):
+    frames = frame_images.shape[0]
+    strip = H // count
     return pl.pallas_call(
         lambda *refs: forward_kernel(count, *refs),
-        in_specs=[in_smem()] + [in_vmem()] * (count + 6),
+        in_specs=[in_smem()] + [in_vmem()] * 8,
         out_specs=[in_vmem()] * (count + 7),
         out_shape=[shape((frames, strip, W * C), bf16)] * count
         + [
@@ -852,17 +946,17 @@
         ],
         scratch_shapes=[pltpu.VMEM((frames,) + IMAGE, f32), pltpu.VMEM((frames,) + TILES, f32)],
         compiler_params=params(),
-        cost_estimate=cost(frames * BLOCK * KEYS * 2 * LANES * 5, frames * (14 << 20)),
+        cost_estimate=cost(1 << 10, 1 << 10),
         name="forward",
-    )(member, *strips, styles, biases, w_one, w_two, w_down, w_up)
-
-
-def backward(member, cot_strips, frame_strips, styles, stats, middle, down, w_up, w_down, w_two, w_one):
-    count = len(cot_strips)
-    frames, strip, _ = cot_strips[0].shape
+    )(member, frame_images, frame_stats, styles, biases, w_one, w_two, w_down, w_up)
+
+
+def backward(member, cot, frame_images, styles, stats, middle, down, w_up, w_down, w_two, w_one, count):
+    frames = frame_images.shape[0]
+    strip = H // count
     return pl.pallas_call(
         lambda *refs: backward_kernel(count, *refs),
-        in_specs=[in_smem()] + [in_vmem()] * (2 * count + 8),
+        in_specs=[in_smem()] + [in_vmem()] * 11,
         out_specs=[in_vmem()] * (count + 6),
         out_shape=[shape((frames, strip, W * C), bf16)] * count
         + [
@@ -883,7 +977,7 @@
         compiler_params=params(),
         cost_estimate=cost(frames * BLOCK * KEYS * 2 * LANES * 5, frames * (10 << 20)),
         name="backward",
-    )(member, *cot_strips, *frame_strips, styles, stats, middle, down, w_up, w_down, w_two, w_one)
+    )(member, *cot, frame_images, styles, stats, middle, down, w_up, w_down, w_two, w_one)
 
 
 def weight_grads(win_one, win_two, win_level, win_coarse, tile_out, tile_level, tile_mid, coarse_pairs):
@@ -908,10 +1002,39 @@
     )(win_one, win_two, win_level, win_coarse, tile_out, tile_level, tile_mid, coarse_pairs)
 
 
-def pack(actions, noise_ids, valid, conv_one, conv_two, down_kernel, up_kernel, ada_one, ada_two, act_table, noise_table, *biases):
-    _, _, size = pack_sizes(conv_one.shape[0], ada_one.shape[0])
-    kernels = [kernel.T for kernel in (conv_one, conv_two, down_kernel, up_kernel)]
-    args = (*kernels, ada_one, ada_two, act_table, noise_table, *biases)
+def in_place(space=pl.ANY):
+    return pl.BlockSpec(memory_space=space)
+
+
+def cut_far(member, array):
+    array = pltpu.with_memory_space_constraint(array, pltpu.HBM)
+    return pl.pallas_call(
+        far_kernel,
+        in_specs=[in_smem(), in_place(pltpu.HBM)],
+        out_specs=in_vmem(),
+        out_shape=shape((array.shape[0] // 2,) + array.shape[1:], array.dtype),
+        scratch_shapes=[pltpu.SemaphoreType.DMA],
+        compiler_params=params(),
+        name="far",
+    )(member, array)
+
+
+def cut_near(member, array, far, hint):
+    return pl.pallas_call(
+        near_kernel,
+        in_specs=[in_smem(), in_place(), in_vmem()],
+        out_specs=in_vmem(),
+        out_shape=shape(far.shape, array.dtype),
+        scratch_shapes=[pltpu.SemaphoreType.DMA],
+        compiler_params=params(),
+        cost_estimate=cost(BLOCK * KEYS * 2 * LANES * hint, 1 << 20),
+        name="near",
+    )(member, array, far)
+
+
+def pack(ids, kernels, ada_one, ada_two, act_table, noise_table, biases):
+    _, _, size = pack_sizes(kernels[0].shape[0], ada_one.shape[0])
+    args = (*[kernel.T for kernel in kernels], ada_one, ada_two, act_table, noise_table, *biases)
     return pl.pallas_call(
         pack_kernel,
         in_specs=[in_smem()] * 3 + [in_vmem()] * len(args),
@@ -919,8 +1042,9 @@
         out_shape=shape((size, LANES), bf16),
         scratch_shapes=[pltpu.VMEM((size, LANES), f32)],
         compiler_params=params(VMEM_MOST),
+        cost_estimate=cost(BLOCK * KEYS * 2 * LANES * 30, 1 << 20),
         name="pack",
-    )(actions, noise_ids, valid, *args)
+    )(*ids, *args)
 
 
 OPERANDS = (
@@ -935,13 +1059,13 @@
 )
 
 
-def prepare(where, actions, noise_ids, valid, packs, rows, cells, frames):
-    count = len(packs)
+def prepare(where, ids, packed, mine, other, count, rows, cells, frames):
     return pl.pallas_call(
         lambda *refs: prepare_kernel(count, rows, cells, *refs),
-        in_specs=[in_smem()] * 4 + [in_vmem()] * count,
-        out_specs=[in_vmem()] * 10,
-        out_shape=[shape(d, bf16) for d in OPERANDS] + [shape((frames,) + SMALL, f32), shape(SMALL, f32)],
+        in_specs=[in_smem()] * 4 + [in_vmem()] * 3,
+        out_specs=[in_vmem()] * 11,
+        out_shape=[shape(d, bf16) for d in OPERANDS]
+        + [shape((frames,) + SMALL, f32), shape(SMALL, f32), shape((count * frames, LANES), f32)],
         scratch_shapes=[
             pltpu.VMEM((9 * C, LANES), f32),
             pltpu.VMEM((18 * C, LANES), f32),
@@ -952,19 +1076,20 @@
         ],
         compiler_params=params(),
         name="prepare",
-    )(where, actions, noise_ids, valid, *packs)
+    )(where, *ids, packed, mine, other)
 
 
 def weight_messages(where, wins, tiles, pieces, bias_sums, count, rows):
     frames = pieces.shape[0]
+    size = count // 2 * 3 * rows
     return pl.pallas_call(
         lambda *refs: message_kernel(count, rows, *refs),
         grid=(frames,),
         in_specs=[in_smem()]
         + [per_frame(d) for d in (WINDOWS, WINDOWS, WINDOWS, COARSE_WINDOWS, TILES, TILES, TILES, COARSE)]
         + [whole((frames,) + SMALL)] * 2,
-        out_specs=[whole((3 * rows, LANES))] * count,
-        out_shape=[shape((3 * rows, LANES), f32)] + [shape((3 * rows, LANES), bf16)] * (count - 1),
+        out_specs=[whole((size, LANES)), whole((PARTS, LANES)), whole((size, LANES))],
+        out_shape=[shape((size, LANES), f32), shape((PARTS, LANES), f32), shape((size, LANES), bf16)],
         scratch_shapes=[
             pltpu.VMEM((KEYS, 2 * LANES), f32),
             pltpu.VMEM((KEYS, 2 * LANES), f32),
@@ -973,7 +1098,6 @@
             pltpu.VMEM((9 * C, LANES), f32),
             pltpu.VMEM((18 * C, LANES), f32),
             pltpu.VMEM((9 * C, LANES), f32),
-            pltpu.VMEM((PARTS, LANES), f32),
         ],
         compiler_params=params(),
         cost_estimate=cost(frames * BLOCK * KEYS * 2 * LANES * 5, frames * (6 << 20)),
@@ -981,21 +1105,32 @@
     )(where, *wins, *tiles, pieces, bias_sums)
 
 
-def reduce_messages(where, own, messages, packs, act_table, noise_table, ada_one, ada_two, rows, cells, frames):
-    count = len(packs)
+def join_messages(where, kept, small, theirs, half, rows, frames):
     return pl.pallas_call(
-        lambda *refs: reduce_kernel(count, rows, cells, frames, *refs),
-        in_specs=[in_smem()] + [in_vmem()] * (2 * count + 4),
+        lambda *refs: join_kernel(half, rows, frames, *refs),
+        in_specs=[in_smem()] + [in_vmem()] * 3,
+        out_specs=[in_vmem()] * (1 + half),
+        out_shape=[shape((3 * rows, LANES), f32)] + [shape((3 * rows, LANES), bf16)] * half,
+        compiler_params=params(),
+        name="join",
+    )(where, kept, small, theirs)
+
+
+def reduce_messages(where, own, messages, hots, act_table, noise_table, ada_one, ada_two, rows, cells, frames):
+    half = len(messages)
+    return pl.pallas_call(
+        lambda *refs: reduce_kernel(half, rows, cells, frames, *refs),
+        in_specs=[in_smem()] + [in_vmem()] * (half + 6),
         out_specs=in_vmem(),
         out_shape=shape((3 * rows + 2 * cells + TABLE_ROWS + 8, LANES), f32),
         scratch_shapes=[
-            pltpu.VMEM((count * frames, LANES), f32),
-            pltpu.VMEM((count * frames, LANES), f32),
+            pltpu.VMEM((half * frames, LANES), f32),
+            pltpu.VMEM((half * frames, LANES), f32),
             pltpu.VMEM((TABLE_ROWS, cells), f32),
         ],
         compiler_params=params(),
         name="reduce",
-    )(where, own, *messages, *packs, act_table, noise_table, ada_one, ada_two)
+    )(where, own, *messages, hots, act_table, noise_table, ada_one, ada_two)
 
 
 def finish(first, second, rows, cells, width):
@@ -1026,7 +1161,7 @@
         out[member_ref[0] ^ offset, 0] = strip[0].astype(out.dtype)
 
 
-def return_strips(strips):
+def trade_strips(strips):
     return tuple(trade(strip, offset) for offset, strip in enumerate(strips))
 
 
@@ -1062,34 +1197,32 @@
     return lax.ppermute(value, "rows", [(i, i ^ offset) for i in range(count)])
 
 
-def spread_strips(array, member):
+def half_trade(value, at):
+    count, members = lax.axis_size("seq"), lax.axis_size("rows")
+    pairs = []
+    for place in range(count):
+        for member in range(members):
+            offset = sides(count)[member % 2][at]
+            if offset:
+                pairs.append((place * members + member, (place ^ offset) * members + member))
+    return lax.ppermute(value, ("seq", "rows"), pairs)
+
+
+def layers(member_box, frame_images, frame_stats, cotangent, cot_far, styles, bias_rows, operands):
+    f_one, f_two, f_down, f_up, b_one, b_two, b_down, b_up = operands
     count = lax.axis_size("rows")
-    share = array.shape[0] // count
-    return [
-        trade(lax.dynamic_slice_in_dim(array, (member ^ offset) * share, share, axis=0), offset)
-        for offset in range(count)
-    ]
-
-
-def seq_trade(value, offset):
-    count = lax.axis_size("seq")
-    return lax.ppermute(value, "seq", [(i, i ^ offset) for i in range(count)])
-
-
-def layers(member_box, frame_strips, cot_strips, styles, bias_rows, operands):
-    f_one, f_two, f_down, f_up, b_one, b_two, b_down, b_up = operands
-    member = member_box[0]
     *out, win_one, win_two, win_level, win_coarse, middle, down, stats = forward(
-        member_box, frame_strips, styles, bias_rows, f_one, f_two, f_down, f_up
+        member_box, frame_images, frame_stats, styles, bias_rows, f_one, f_two, f_down, f_up, count
     )
-    out = return_strips(out)
+    out = trade_strips(out)
+    down, cot_far = lax.optimization_barrier((down, cot_far))
+    cot = gather_frames(member_box, cotangent, cot_far)
     *grad_strips, tile_out, tile_level, tile_mid, coarse_pairs, pieces, bias_sums = backward(
-        member_box, cot_strips, frame_strips, styles, stats, middle, down, b_up, b_down, b_two, b_one
+        member_box, cot, frame_images, styles, stats, middle, down, b_up, b_down, b_two, b_one, count
     )
-    grad_strips = return_strips(grad_strips)
+    grad_strips = trade_strips(grad_strips)
     wins = (win_one, win_two, win_level, win_coarse)
     tiles = (tile_out, tile_level, tile_mid, coarse_pairs)
-    pieces, out = lax.optimization_barrier((pieces, out))
     return out, grad_strips, wins, tiles, pieces, bias_sums
 
 
@@ -1117,36 +1250,30 @@
     count = lax.axis_size("seq")
     share = frames.shape[0] // lax.axis_size("rows")
     rows, cells, width = conv_one.shape[0], ada_one.shape[0], bias_one.shape[0]
+    half = count // 2
     member_box = member.reshape(1)
     where = jnp.stack([place, member])
-    packed = pack(
-        actions,
-        noise_ids,
-        valid,
-        conv_one,
-        conv_two,
-        down_kernel,
-        up_kernel,
-        ada_one,
-        ada_two,
-        act_table,
-        noise_table,
-        bias_one,
-        bias_two,
-        bias_down,
-        bias_up,
+    ids = (actions, noise_ids, valid)
+    kernels = (conv_one, conv_two, down_kernel, up_kernel)
+    biases = (bias_one, bias_two, bias_down, bias_up)
+    far = trade(cut_far(member_box, frames), 2)
+    packed = pack(ids, kernels, ada_one, ada_two, act_table, noise_table, biases)
+    mine = jnp.concatenate([half_trade(packed, at) for at in range(half)], axis=0)
+    other = trade(mine, 1)
+    cot_far = trade(cut_far(member_box, cotangent), 2)
+    frame_images, frame_stats = gather_frames(member_box, frames, far, FAR_HINT)
+    *operands, styles, bias_rows, hots = prepare(where, ids, packed, mine, other, count, rows, cells, share)
+    out, grad_strips, wins, tiles, pieces, bias_sums = layers(
+        member_box, frame_images, frame_stats, cotangent, cot_far, styles, bias_rows, operands
     )
-    packs = [packed] + [seq_trade(packed, offset) for offset in range(1, count)]
-    frame_strips = spread_strips(frames, member)
-    cot_strips = spread_strips(cotangent, member)
-    *operands, styles, bias_rows = prepare(where, actions, noise_ids, valid, packs, rows, cells, share)
-    out, grad_strips, wins, tiles, pieces, bias_sums = layers(
-        member_box, frame_strips, cot_strips, styles, bias_rows, operands
+    kept, small, theirs = weight_messages(where, wins, tiles, pieces, bias_sums, count, rows)
+    theirs, out = lax.optimization_barrier((theirs, out))
+    own, *messages = join_messages(where, kept, small, trade(theirs, 1), half, rows, share)
+    received = [half_trade(message, at) for at, message in enumerate(messages)]
+    received, grad_strips = lax.optimization_barrier((received, grad_strips))
+    sums = reduce_messages(
+        where, own, received, hots, act_table, noise_table, ada_one, ada_two, rows, cells, 2 * share
     )
-    own, *messages = weight_messages(where, wins, tiles, pieces, bias_sums, count, rows)
-    received = [seq_trade(messages[offset - 1], offset) for offset in range(1, count)]
-    received, grad_strips = lax.optimization_barrier((received, grad_strips))
-    sums = reduce_messages(where, own, received, packs, act_table, noise_table, ada_one, ada_two, rows, cells, share)
     offset = 1
     while 2 * offset < lax.axis_size("rows"):
         sums = sums + trade(sums, offset)
@@ -1182,8 +1309,9 @@
     def gathered(value, axis):
         return lax.all_gather(value, "seq", axis=axis, tiled=True)
 
-    frame_strips = spread_strips(frames, member)
-    cot_strips = spread_strips(cotangent, member)
+    cot_far = trade(cut_far(member_box, cotangent), 2)
+    far = trade(cut_far(member_box, frames), 2)
+    frame_images, frame_stats = gather_frames(member_box, frames, far)
     act_full = gathered(act_table, 1)
     noise_full = gathered(noise_table, 1)
     ada_full = gathered(jnp.concatenate([ada_one, ada_two], axis=1), 0).astype(f32)
@@ -1210,7 +1338,7 @@
     )
     bias_rows = pad_small([twice(biases[k]) for k in range(4)])
     out, grad_strips, wins, tiles, pieces, bias_sums = layers(
-        member_box, frame_strips, cot_strips, styles, bias_rows, operands
+        member_box, frame_images, frame_stats, cotangent, cot_far, styles, bias_rows, operands
     )
     g_one, g_two, g_down, g_up = weight_grads(*wins, *tiles)
     result = collect_strips(member_box, out, bf16)

time: 87.9 us -> 78.5 us (0.89)
  starting transfers between devices: 34.7 us -> 22.5 us
  Pallas kernels: 32.9 us -> 36.9 us
  local copies, waits for them, and re-layouts: 2.9 us -> 0.1 us
  waiting for transfers between devices: 16.3 us -> 17.6 us
    ppermute x14 -> x8, starting transfers between devices: 25 us -> 12 us  [half_trade(): return lax.ppermute(value, ('seq', 'rows'), pairs)]
    pallas_call x1 -> x8, Pallas kernels: 1.29 us -> 6.1 us  [the longest x2 2.11 us: cut_far(): pl.pallas_call(far_kernel, in_specs=[in_smem(), in_place(pltpu.HBM)], out...]
    ppermute x14, waiting for transfers between devices: 5.86 us -> 10.5 us  [trade(): return lax.ppermute(value, 'rows', [(i, i ^ offset) for i in range(count)])]
    ppermute x14 -> x8, waiting for transfers between devices: 10.4 us -> 7.15 us  [half_trade(): return lax.ppermute(value, ('seq', 'rows'), pairs)]
    dynamic_slice x2 -> x0, local copies, waits for them, and re-layouts: 2.86 us -> none  [spread_strips(): lax.dynamic_slice_in_dim(array, (member ^ offset) * share, share, axis=0)]
  transfers between devices with their start and end apart: 28 -> 22, of which waited for: 9 -> 8; matrix products, arithmetic and copies ran while one was open for 3% -> 0% of each run, Pallas kernels for 33% -> 43%
where the time goes in v4:
time: 78.5 us; the launch traced here: 78.2 us
  Pallas kernels  36.9 us (47%)
  starting transfers between devices  22.5 us (29%)
  waiting for transfers between devices  17.6 us (22%)
  between operations  1.03 us (1%)
    ppermute x8, starting transfers between devices, half_trade(): return lax.ppermute(value, ('seq', 'rows'), pairs)  12 us
    ppermute x14, waiting for transfers between devices, trade(): return lax.ppermute(value, 'rows', [(i, i ^ offset) for i in range(count)])  10.5 us
    ppermute x14, starting transfers between devices, trade(): return lax.ppermute(value, 'rows', [(i, i ^ offset) for i in range(count)])  10.5 us
    pallas_call x1, Pallas kernels, backward(): pl.pallas_call(lambda *refs: backward_kernel(count, *refs), in_specs=[in_...  8.43 us
    pallas_call x1, Pallas kernels, weight_messages(): pl.pallas_call(lambda *refs: message_kernel(count, rows, *refs), grid=(fr...  7.62 us
    ppermute x8, waiting for transfers between devices, half_trade(): return lax.ppermute(value, ('seq', 'rows'), pairs)  7.15 us
    pallas_call x1, Pallas kernels, forward(): pl.pallas_call(lambda *refs: forward_kernel(count, *refs), in_specs=[in_s...  7.02 us
    pallas_call x1, Pallas kernels, prepare(): pl.pallas_call(lambda *refs: prepare_kernel(count, rows, cells, *refs), i...  2.63 us
  transfers between devices with their start and end apart: 22, of which 8 were waited for; matrix products, arithmetic and copies ran while one was open for 0% of the time, Pallas kernels for 43%

profile of v4, /device:TPU:0, one launch (start us, length us, event | category | flops | bytes accessed | tf_op | source)
XLA Modules:
  0.0 78.2 jit_solution(11341914752738646994)
XLA Ops:
  0.6 1.1 %far.2 = bf16[4,16,4096]{2,1,0:T(8,128)(2,1)S(1)} custom-call(s32[1]{0:T(128)} %bitcast.member_ref.refs_0_, bf16[8,16,4096]{2,1,0:T(8,128)(2,1)} %array.8), custom_call_target="tpu_custom_call" | custom-call | tf_op jit(solution)/shard_map/far/pallas_call | solution.py:1011
  1.7 3.0 %collective-permute-start = (bf16[4,16,4096]{2,1,0:T(8,128)(2,1)S(1)}, bf16[4,16,4096]{2,1,0:T(8,128)(2,1)S(1)}, u32[]{:S(2)}, u32[]{:S(2)}) collective-permute-start(bf16[4,16,4096]{2,1,0:T(8,128)(2,1)S(1)} %far.2), channel_id=1, source_target_pairs={{0,2},{1,3},{2,0},{3,1},{4,6},{5,7},{6,4},{7,5},{8,10},{9,11},{10,... | collective-permute-start | bytes 1572872 | tf_op jit(solution)/shard_map/ppermute | solution.py:1197
  4.7 1.9 %pack.1.refs_4_ = bf16[288,128]{1,0:T(8,128)(2,1)} custom-call(s32[8]{0:T(128)} %refs_1_.3, s32[8]{0:T(128)} %refs_2_.3, s32[8]{0:T(128)} %refs_3_.1, bf16[64,72]{1,0:T(8,128)(2,1)} %bitcast.19, bf16[64,72]{1,0:T(8,128)(2,1)} %bitcast.20, bf16[64,72]{1,0:T(8,128)(2,1)} %bitcast.21, bf16[64,144]{1,0:T(8,128)(2,1)} %bitcast.15, bf16[32,128]{1,0:T(8,128)(2,1)} %refs_9_.3, ...), custom_call_target="tpu_custom_call" | custom-call | flops 16106127360 | bytes 1048576 | tf_op jit(solution)/shard_map/pack/pallas_call | solution.py:1038
  6.6 0.7 collective-permute-start.2
  7.3 3.7 %collective-permute-start.5 = (bf16[288,128]{1,0:T(8,128)(2,1)}, bf16[288,128]{1,0:T(8,128)(2,1)S(1)}, u32[]{:S(2)}, u32[]{:S(2)}) collective-permute-start(bf16[288,128]{1,0:T(8,128)(2,1)} %pack.1.refs_4_), channel_id=1, source_target_pairs={{0,24},{1,29},{2,26},{3,31},{4,28},{5,25},{6,30},{7,27},{8,16},{9,... | collective-permute-start | bytes 221192 | tf_op jit(solution)/shard_map/ppermute | solution.py:1208
  10.9 0.4 collective-permute-start.4
  11.3 1.3 %collective-permute-start.3 = (bf16[288,128]{1,0:T(8,128)(2,1)}, bf16[288,128]{1,0:T(8,128)(2,1)S(1)}, u32[]{:S(2)}, u32[]{:S(2)}) collective-permute-start(bf16[288,128]{1,0:T(8,128)(2,1)} %pack.1.refs_4_), channel_id=1, source_target_pairs={{0,12},{1,9},{2,14},{3,11},{4,8},{5,13},{6,10},{7,15},{8,4},{9,1},... | collective-permute-start | bytes 221192 | tf_op jit(solution)/shard_map/ppermute | solution.py:1208
  12.6 1.0 %far.3 = bf16[4,16,4096]{2,1,0:T(8,128)(2,1)S(1)} custom-call(s32[1]{0:T(128)} %bitcast.member_ref.refs_0_, bf16[8,16,4096]{2,1,0:T(8,128)(2,1)} %array.11), custom_call_target="tpu_custom_call" | custom-call | tf_op jit(solution)/shard_map/far/pallas_call | solution.py:1011
  13.7 0.0 collective-permute-done.2
  13.7 0.4 collective-permute-start.7
  14.1 0.0 copy-start.7
  14.1 0.0 copy-start.8
  14.2 0.0 copy-start.9
  14.2 2.8 %collective-permute-done.far = bf16[4,16,4096]{2,1,0:T(8,128)(2,1)S(1)} collective-permute-done((bf16[4,16,4096]{2,1,0:T(8,128)(2,1)S(1)}, bf16[4,16,4096]{2,1,0:T(8,128)(2,1)S(1)}, u32[]{:S(2)}, u32[]{:S(2)}) %collective-permute-start) | collective-permute-done | bytes 524320 | tf_op jit(solution)/shard_map/ppermute | solution.py:1197
  17.0 0.8 %near.2 = bf16[4,16,4096]{2,1,0:T(8,128)(2,1)} custom-call(s32[1]{0:T(128)} %bitcast.member_ref.refs_0_, bf16[8,16,4096]{2,1,0:T(8,128)(2,1)S(1)} %copy-done.1, bf16[4,16,4096]{2,1,0:T(8,128)(2,1)S(1)} %collective-permute-done.far), custom_call_target="tpu_custom_call" | custom-call | flops 48318382080 | bytes 1048576 | tf_op jit(solution)/shard_map/near/pallas_call | solution.py:1023
  17.9 0.1 collective-permute-start.1
  17.9 0.0 collective-permute-done.3
  18.0 0.8 %collective-permute-done.4 = bf16[288,128]{1,0:T(8,128)(2,1)S(1)} collective-permute-done((bf16[288,128]{1,0:T(8,128)(2,1)}, bf16[288,128]{1,0:T(8,128)(2,1)S(1)}, u32[]{:S(2)}, u32[]{:S(2)}) %collective-permute-start.4) | collective-permute-done | bytes 73760 | tf_op jit(solution)/shard_map/ppermute | solution.py:1208
  18.8 0.0 collective-permute-done.5
  18.8 0.1 collective-permute-start.6
  18.9 0.1 pad_add_fusion.refs_0_
  19.0 1.6 %collective-permute-done.6.refs_6_ = bf16[1152,128]{1,0:T(8,128)(2,1)} collective-permute-done((bf16[1152,128]{1,0:T(8,128)(2,1)S(1)}, bf16[1152,128]{1,0:T(8,128)(2,1)}, u32[]{:S(2)}, u32[]{:S(2)}) %collective-permute-start.6) | collective-permute-done | bytes 294944 | tf_op jit(solution)/shard_map/ppermute | solution.py:1197
  20.6 2.6 %prepare.1 = (bf16[1024,256]{1,0:T(8,128)(2,1)S(1)}, bf16[1024,256]{1,0:T(8,128)(2,1)S(1)}, bf16[768,128]{1,0:T(8,128)(2,1)S(1)}, bf16[2048,256]{1,0:T(8,128)(2,...) custom-call(s32[2]{0:T(128)S(1)} %pad_add_fusion.refs_0_, ...), custom_call_target="tpu_custom_call" | custom-call | tf_op jit(solution)/shard_map/prepare/pallas_call | solution.py:1063
  23.3 0.0 collective-permute-done.1.near
  23.3 0.6 frames.2
  23.9 0.0 copy-start
  23.9 7.0 %forward.1 = (bf16[2,16,4096]{2,1,0:T(8,128)(2,1)S(1)}, bf16[2,16,4096]{2,1,0:T(8,128)(2,1)S(1)}, bf16[2,16,4096]{2,1,0:T(8,128)(2,1)S(1)}, bf16[2,16,4096]{2,1,...) custom-call(s32[1]{0:T(128)} %bitcast.member_ref.refs_0_, ...), custom_call_target="tpu_custom_call" | custom-call | flops 2048 | bytes 1024 | tf_op jit(solution)/shard_map/forward/pallas_call | solution.py:933
  30.9 0.0 collective-permute-done.7.far
  30.9 0.1 near.3
  31.0 0.2 collective-permute-start.8
  31.2 0.4 collective-permute-start.9
  31.6 2.2 %collective-permute-start.10 = (bf16[2,16,4096]{2,1,0:T(8,128)(2,1)S(1)}, bf16[2,16,4096]{2,1,0:T(8,128)(2,1)S(1)}, u32[]{:S(2)}, u32[]{:S(2)}) collective-permute-start(bf16[2,16,4096]{2,1,0:T(8,128)(2,1)S(1)} %get-tuple-element.117), channel_id=1, source_target_pairs={{0,2},{1,3},{2,0},{3,1},{4,6},{5,7},{6,4},{7,5},{8,10},{9,11},{10,... | collective-permute-start | bytes 786440 | tf_op jit(solution)/shard_map/ppermute | solution.py:1197
  33.8 0.0 collective-permute-start.11
  33.8 0.0 collective-permute-done.8.near
  33.8 0.7 frames.3
  34.6 8.4 %backward.1 = (bf16[2,16,4096]{2,1,0:T(8,128)(2,1)S(1)}, bf16[2,16,4096]{2,1,0:T(8,128)(2,1)S(1)}, bf16[2,16,4096]{2,1,0:T(8,128)(2,1)S(1)}, bf16[2,16,4096]{2,1...) custom-call(s32[1]{0:T(128)} %bitcast.member_ref.refs_0_, ...), custom_call_target="tpu_custom_call" | custom-call | flops 5368709120 | bytes 20971520 | tf_op jit(solution)/shard_map/backward/pallas_call | solution.py:957
  43.0 0.2 collective-permute-start.17
  43.2 2.0 %collective-permute-start.18 = (bf16[2,16,4096]{2,1,0:T(8,128)(2,1)S(1)}, bf16[2,16,4096]{2,1,0:T(8,128)(2,1)S(1)}, u32[]{:S(2)}, u32[]{:S(2)}) collective-permute-start(bf16[2,16,4096]{2,1,0:T(8,128)(2,1)S(1)} %get-tuple-element.132), channel_id=1, source_target_pairs={{0,2},{1,3},{2,0},{3,1},{4,6},{5,7},{6,4},{7,5},{8,10},{9,11},{10,... | collective-permute-start | bytes 786440 | tf_op jit(solution)/shard_map/ppermute | solution.py:1197
  45.2 7.6 %weights.1 = (f32[864,128]{1,0:T(8,128)S(1)}, f32[16,128]{1,0:T(8,128)S(1)}, bf16[864,128]{1,0:T(8,128)(2,1)S(1)}) custom-call(s32[2]{0:T(128)S(1)} %pad_add_fusion.refs_0_, bf16[2,4,33,32,128]{4,3,2,1,0:T(8,128)(2,1)S(1)} %get-tuple-element.93.refs_1_, bf16[2,4,33,32,128]{4,3,2,1,0:T(8,128)(2,1)S(1)} %get-tuple-element.94.refs_2_, ...), custom_call_target="tpu_custom_call" | custom-call | flops 5368709120 | bytes 12582912 | tf_op jit(solution)/shard_map/weights/pallas_call | solution.py:1085
  52.9 0.0 collective-permute-done.9.refs_1_
  52.9 0.0 collective-permute-done.10.refs_2_
  52.9 0.0 collective-permute-done.11.refs_3_
  52.9 0.1 collective-permute-start.12
  53.0 0.2 collective-permute-start.19
  53.1 1.3 %collective-permute-done.12.refs_3_ = bf16[864,128]{1,0:T(8,128)(2,1)S(1)} collective-permute-done((bf16[864,128]{1,0:T(8,128)(2,1)S(1)}, bf16[864,128]{1,0:T(8,128)(2,1)S(1)}, u32[]{:S(2)}, u32[]{:S(2)}) %collective-permute-start.12) | collective-permute-done | bytes 221216 | tf_op jit(solution)/shard_map/ppermute | solution.py:1197
  54.4 0.6 join.1
  55.0 0.7 collective-permute-start.13
  55.7 2.6 %collective-permute-start.14 = (bf16[216,128]{1,0:T(8,128)(2,1)S(1)}, bf16[216,128]{1,0:T(8,128)(2,1)S(1)}, u32[]{:S(2)}, u32[]{:S(2)}) collective-permute-start(bf16[216,128]{1,0:T(8,128)(2,1)S(1)} %get-tuple-element.127), channel_id=1, source_target_pairs={{0,12},{1,9},{2,14},{3,11},{4,8},{5,13},{6,10},{7,15},{8,4},{9,1},... | collective-permute-start | bytes 165896 | tf_op jit(solution)/shard_map/ppermute | solution.py:1208
  58.3 0.0 collective-permute-done.17.refs_1_
  58.3 2.6 %collective-permute-start.15 = (bf16[216,128]{1,0:T(8,128)(2,1)S(1)}, bf16[216,128]{1,0:T(8,128)(2,1)S(1)}, u32[]{:S(2)}, u32[]{:S(2)}) collective-permute-start(bf16[216,128]{1,0:T(8,128)(2,1)S(1)} %get-tuple-element.128), channel_id=1, source_target_pairs={{0,20},{1,17},{2,22},{3,19},{4,16},{5,21},{6,18},{7,23},{8,28},{9,... | collective-permute-start | bytes 165896 | tf_op jit(solution)/shard_map/ppermute | solution.py:1208
  60.9 0.0 collective-permute-done.18.refs_2_
  60.9 0.2 collective-permute-start.16
  61.1 0.0 collective-permute-done.19.refs_3_
  61.1 0.0 collective-permute-done.13.refs_2_
  61.1 4.6 %collective-permute-done.15.refs_4_ = bf16[216,128]{1,0:T(8,128)(2,1)S(1)} collective-permute-done((bf16[216,128]{1,0:T(8,128)(2,1)S(1)}, bf16[216,128]{1,0:T(8,128)(2,1)S(1)}, u32[]{:S(2)}, u32[]{:S(2)}) %collective-permute-start.15) | collective-permute-done | bytes 55328 | tf_op jit(solution)/shard_map/ppermute | solution.py:1208
  65.6 1.7 %collective-permute-done.16.refs_5_ = bf16[216,128]{1,0:T(8,128)(2,1)S(1)} collective-permute-done((bf16[216,128]{1,0:T(8,128)(2,1)S(1)}, bf16[216,128]{1,0:T(8,128)(2,1)S(1)}, u32[]{:S(2)}, u32[]{:S(2)}) %collective-permute-start.16) | collective-permute-done | bytes 55328 | tf_op jit(solution)/shard_map/ppermute | solution.py:1208
  67.4 1.2 %reduce.1 = f32[344,128]{1,0:T(8,128)S(1)} custom-call(s32[2]{0:T(128)S(1)} %pad_add_fusion.refs_0_, f32[216,128]{1,0:T(8,128)S(1)} %get-tuple-element.138.refs_1_, bf16[216,128]{1,0:T(8,128)(2,1)S(1)} %collective-permute-done.13.refs_2_, bf16[216,128]{1,0:T(8,128)(2,1)S(1)} %collective-permute-done.14.refs_3_, ...), custom_call_target="tpu_custom_call" | custom-call | tf_op jit(solution)/shard_map/reduce/pallas_call | solution.py:1121
  68.6 0.8 %collective-permute-start.20 = (f32[344,128]{1,0:T(8,128)S(1)}, f32[344,128]{1,0:T(8,128)S(1)}, u32[]{:S(2)}, u32[]{:S(2)}) collective-permute-start(f32[344,128]{1,0:T(8,128)S(1)} %reduce.1), channel_id=1, source_target_pairs={{0,1},{1,0},{2,3},{3,2},{4,5},{5,4},{6,7},{7,6},{8,9},{9,8},{10,11... | collective-permute-start | bytes 528392 | tf_op jit(solution)/shard_map/ppermute | solution.py:1197
  69.4 1.0 %collective-permute-done.20 = f32[344,128]{1,0:T(8,128)S(1)} collective-permute-done((f32[344,128]{1,0:T(8,128)S(1)}, f32[344,128]{1,0:T(8,128)S(1)}, u32[]{:S(2)}, u32[]{:S(2)}) %collective-permute-start.20) | collective-permute-done | bytes 176160 | tf_op jit(solution)/shard_map/ppermute | solution.py:1197
  70.5 0.8 collective-permute-start.21
  71.3 1.0 %collect.2 = bf16[4,2,16,4096]{3,2,1,0:T(8,128)(2,1)} custom-call(s32[1]{0:T(128)} %bitcast.member_ref.refs_0_, bf16[2,16,4096]{2,1,0:T(8,128)(2,1)S(1)} %get-tuple-element.119.refs_0_, bf16[2,16,4096]{2,1,0:T(8,128)(2,1)S(1)} %collective-permute-done.9.refs_1_, bf16[2,16,4096]{2,1,0:T(8,128)(2,1)S(1)} %collective-permute-done.10.refs_2_, ...), custom_call_target="tpu_custom_call" | custom-call | tf_op jit(solution)/shard_map/collect/pallas_call | solution.py:1171
  72.3 1.4 %collect.3 = f32[4,2,16,4096]{3,2,1,0:T(8,128)} custom-call(s32[1]{0:T(128)} %bitcast.member_ref.refs_0_, bf16[2,16,4096]{2,1,0:T(8,128)(2,1)S(1)} %get-tuple-element.134.refs_0_, bf16[2,16,4096]{2,1,0:T(8,128)(2,1)S(1)} %collective-permute-done.17.refs_1_, bf16[2,16,4096]{2,1,0:T(8,128)(2,1)S(1)} %collective-permute-done.18.refs_2_, ...), custom_call_target="tpu_custom_call" | custom-call | tf_op jit(solution)/shard_map/collect/pallas_call | solution.py:1171
  73.7 3.7 %collective-permute-done.21.refs_1_ = f32[344,128]{1,0:T(8,128)S(1)} collective-permute-done((f32[344,128]{1,0:T(8,128)S(1)}, f32[344,128]{1,0:T(8,128)S(1)}, u32[]{:S(2)}, u32[]{:S(2)}) %collective-permute-start.21) | collective-permute-done | bytes 176160 | tf_op jit(solution)/shard_map/ppermute | solution.py:1197
  77.3 0.8 %finish.1 = (f32[18,32]{1,0:T(8,128)}, f32[32,32]{1,0:T(8,128)}, f32[32,128]{1,0:T(8,128)}, f32[32,128]{1,0:T(8,128)}, f32[64,72]{1,0:T(8,128)}, /*index=5*/f32[...) custom-call(f32[344,128]{1,0:T(8,128)S(1)} %add.3.refs_0_, ...), custom_call_target="tpu_custom_call" | custom-call | tf_op jit(solution)/shard_map/finish/pallas_call | solution.py:1137
  (22 shorter events, 0.1 us)
Async XLA Ops:
  1.7 15.3 %collective-permute-start = (bf16[4,16,4096]{2,1,0:T(8,128)(2,1)S(1)}, bf16[4,16,4096]{2,1,0:T(8,128)(2,1)S(1)}, u32[]{:S(2)}, u32[]{:S(2)}) collective-permute-start(bf16[4,16,4096]{2,1,0:T(8,128)(2,1)S(1)} %far.2), channel_id=1, source_target_pairs={{0,2},{1,3},{2,0},{3,1},{4,6},{5,7},{6,4},{7,5},{8,10},{9,11},{10,... | collective-permute-start | bytes 1572872 | tf_op jit(solution)/shard_map/ppermute | solution.py:1197
  4.7 12.3 %copy-start.1 = (bf16[8,16,4096]{2,1,0:T(8,128)(2,1)S(1)}, bf16[8,16,4096]{2,1,0:T(8,128)(2,1)}, u32[]{:S(2)}) copy-start(bf16[8,16,4096]{2,1,0:T(8,128)(2,1)} %array.8) | copy-start | bytes 3145732
  6.6 7.1 %collective-permute-start.2 = (bf16[288,128]{1,0:T(8,128)(2,1)}, bf16[288,128]{1,0:T(8,128)(2,1)S(1)}, u32[]{:S(2)}, u32[]{:S(2)}) collective-permute-start(bf16[288,128]{1,0:T(8,128)(2,1)} %pack.1.refs_4_), channel_id=1, source_target_pairs={{1,5},{3,7},{5,1},{7,3},{9,13},{11,15},{13,9},{15,11},{17,21},{19,... | collective-permute-start | bytes 221192 | tf_op jit(solution)/shard_map/ppermute | solution.py:1208
  7.3 11.5 %collective-permute-start.5 = (bf16[288,128]{1,0:T(8,128)(2,1)}, bf16[288,128]{1,0:T(8,128)(2,1)S(1)}, u32[]{:S(2)}, u32[]{:S(2)}) collective-permute-start(bf16[288,128]{1,0:T(8,128)(2,1)} %pack.1.refs_4_), channel_id=1, source_target_pairs={{0,24},{1,29},{2,26},{3,31},{4,28},{5,25},{6,30},{7,27},{8,16},{9,... | collective-permute-start | bytes 221192 | tf_op jit(solution)/shard_map/ppermute | solution.py:1208
  10.9 7.9 %collective-permute-start.4 = (bf16[288,128]{1,0:T(8,128)(2,1)}, bf16[288,128]{1,0:T(8,128)(2,1)S(1)}, u32[]{:S(2)}, u32[]{:S(2)}) collective-permute-start(bf16[288,128]{1,0:T(8,128)(2,1)} %pack.1.refs_4_), channel_id=1, source_target_pairs={{0,20},{1,17},{2,22},{3,19},{4,16},{5,21},{6,18},{7,23},{8,28},{9,... | collective-permute-start | bytes 221192 | tf_op jit(solution)/shard_map/ppermute | solution.py:1208
  11.3 6.6 %collective-permute-start.3 = (bf16[288,128]{1,0:T(8,128)(2,1)}, bf16[288,128]{1,0:T(8,128)(2,1)S(1)}, u32[]{:S(2)}, u32[]{:S(2)}) collective-permute-start(bf16[288,128]{1,0:T(8,128)(2,1)} %pack.1.refs_4_), channel_id=1, source_target_pairs={{0,12},{1,9},{2,14},{3,11},{4,8},{5,13},{6,10},{7,15},{8,4},{9,1},... | collective-permute-start | bytes 221192 | tf_op jit(solution)/shard_map/ppermute | solution.py:1208
  13.7 17.2 %collective-permute-start.7 = (bf16[4,16,4096]{2,1,0:T(8,128)(2,1)S(1)}, bf16[4,16,4096]{2,1,0:T(8,128)(2,1)S(1)}, u32[]{:S(2)}, u32[]{:S(2)}) collective-permute-start(bf16[4,16,4096]{2,1,0:T(8,128)(2,1)S(1)} %far.3), channel_id=1, source_target_pairs={{0,2},{1,3},{2,0},{3,1},{4,6},{5,7},{6,4},{7,5},{8,10},{9,11},{10,... | collective-permute-start | bytes 1572872 | tf_op jit(solution)/shard_map/ppermute | solution.py:1197
  14.1 6.5 %copy-start.2 = (bf16[288,128]{1,0:T(8,128)(2,1)S(1)}, bf16[288,128]{1,0:T(8,128)(2,1)}, u32[]{:S(2)}) copy-start(bf16[288,128]{1,0:T(8,128)(2,1)} %pack.1.refs_4_) | copy-start | bytes 221188
  14.1 6.5 %copy-start.7 = (s32[8]{0:T(128)S(1)}, s32[8]{0:T(128)}, u32[]{:S(2)}) copy-start(s32[8]{0:T(128)} %refs_1_.3) | copy-start | bytes 100
  14.1 6.5 %copy-start.8 = (s32[8]{0:T(128)S(1)}, s32[8]{0:T(128)}, u32[]{:S(2)}) copy-start(s32[8]{0:T(128)} %refs_2_.3) | copy-start | bytes 100
  14.2 6.5 %copy-start.9 = (s32[8]{0:T(128)S(1)}, s32[8]{0:T(128)}, u32[]{:S(2)}) copy-start(s32[8]{0:T(128)} %refs_3_.1) | copy-start | bytes 100
  17.9 5.4 %collective-permute-start.1 = (bf16[4,16,4096]{2,1,0:T(8,128)(2,1)}, bf16[4,16,4096]{2,1,0:T(8,128)(2,1)S(1)}, u32[]{:S(2)}, u32[]{:S(2)}) collective-permute-start(bf16[4,16,4096]{2,1,0:T(8,128)(2,1)} %near.2), channel_id=1, source_target_pairs={{0,1},{1,0},{2,3},{3,2},{4,5},{5,4},{6,7},{7,6},{8,9},{9,8},{10,11... | collective-permute-start | bytes 1572872 | tf_op jit(solution)/shard_map/ppermute | solution.py:1197
  18.8 1.8 %collective-permute-start.6 = (bf16[1152,128]{1,0:T(8,128)(2,1)S(1)}, bf16[1152,128]{1,0:T(8,128)(2,1)}, u32[]{:S(2)}, u32[]{:S(2)}) collective-permute-start(bf16[1152,128]{1,0:T(8,128)(2,1)S(1)} %constant_dynamic-update-slice_fusion.refs_5_), channel_id=1, source_target_pairs={{0,1},{1,0},{2,3},{3,2},{4,5},{5,4},{6,7},{7,6},{8,9},{9,8},{10,11... | collective-permute-start | bytes 884744 | tf_op jit(solution)/shard_map/ppermute | solution.py:1197
  23.9 7.0 %copy-start = (bf16[8,16,4096]{2,1,0:T(8,128)(2,1)S(1)}, bf16[8,16,4096]{2,1,0:T(8,128)(2,1)}, u32[]{:S(2)}) copy-start(bf16[8,16,4096]{2,1,0:T(8,128)(2,1)} %array.11) | copy-start | bytes 3145732
  31.0 2.8 %collective-permute-start.8 = (bf16[4,16,4096]{2,1,0:T(8,128)(2,1)S(1)}, bf16[4,16,4096]{2,1,0:T(8,128)(2,1)S(1)}, u32[]{:S(2)}, u32[]{:S(2)}) collective-permute-start(bf16[4,16,4096]{2,1,0:T(8,128)(2,1)S(1)} %near.3), channel_id=1, source_target_pairs={{0,1},{1,0},{2,3},{3,2},{4,5},{5,4},{6,7},{7,6},{8,9},{9,8},{10,11... | collective-permute-start | bytes 1572872 | tf_op jit(solution)/shard_map/ppermute | solution.py:1197
  31.2 21.7 %collective-permute-start.9 = (bf16[2,16,4096]{2,1,0:T(8,128)(2,1)S(1)}, bf16[2,16,4096]{2,1,0:T(8,128)(2,1)S(1)}, u32[]{:S(2)}, u32[]{:S(2)}) collective-permute-start(bf16[2,16,4096]{2,1,0:T(8,128)(2,1)S(1)} %get-tuple-element.116), channel_id=1, source_target_pairs={{0,1},{1,0},{2,3},{3,2},{4,5},{5,4},{6,7},{7,6},{8,9},{9,8},{10,11... | collective-permute-start | bytes 786440 | tf_op jit(solution)/shard_map/ppermute | solution.py:1197
  31.6 21.3 %collective-permute-start.10 = (bf16[2,16,4096]{2,1,0:T(8,128)(2,1)S(1)}, bf16[2,16,4096]{2,1,0:T(8,128)(2,1)S(1)}, u32[]{:S(2)}, u32[]{:S(2)}) collective-permute-start(bf16[2,16,4096]{2,1,0:T(8,128)(2,1)S(1)} %get-tuple-element.117), channel_id=1, source_target_pairs={{0,2},{1,3},{2,0},{3,1},{4,6},{5,7},{6,4},{7,5},{8,10},{9,11},{10,... | collective-permute-start | bytes 786440 | tf_op jit(solution)/shard_map/ppermute | solution.py:1197
  33.8 19.1 %collective-permute-start.11 = (bf16[2,16,4096]{2,1,0:T(8,128)(2,1)S(1)}, bf16[2,16,4096]{2,1,0:T(8,128)(2,1)S(1)}, u32[]{:S(2)}, u32[]{:S(2)}) collective-permute-start(bf16[2,16,4096]{2,1,0:T(8,128)(2,1)S(1)} %get-tuple-element.118), channel_id=1, source_target_pairs={{0,3},{1,2},{2,1},{3,0},{4,7},{5,6},{6,5},{7,4},{8,11},{9,10},{10,... | collective-permute-start | bytes 786440 | tf_op jit(solution)/shard_map/ppermute | solution.py:1197
  43.0 15.3 %collective-permute-start.17 = (bf16[2,16,4096]{2,1,0:T(8,128)(2,1)S(1)}, bf16[2,16,4096]{2,1,0:T(8,128)(2,1)S(1)}, u32[]{:S(2)}, u32[]{:S(2)}) collective-permute-start(bf16[2,16,4096]{2,1,0:T(8,128)(2,1)S(1)} %get-tuple-element.131), channel_id=1, source_target_pairs={{0,1},{1,0},{2,3},{3,2},{4,5},{5,4},{6,7},{7,6},{8,9},{9,8},{10,11... | collective-permute-start | bytes 786440 | tf_op jit(solution)/shard_map/ppermute | solution.py:1197
  43.2 17.7 %collective-permute-start.18 = (bf16[2,16,4096]{2,1,0:T(8,128)(2,1)S(1)}, bf16[2,16,4096]{2,1,0:T(8,128)(2,1)S(1)}, u32[]{:S(2)}, u32[]{:S(2)}) collective-permute-start(bf16[2,16,4096]{2,1,0:T(8,128)(2,1)S(1)} %get-tuple-element.132), channel_id=1, source_target_pairs={{0,2},{1,3},{2,0},{3,1},{4,6},{5,7},{6,4},{7,5},{8,10},{9,11},{10,... | collective-permute-start | bytes 786440 | tf_op jit(solution)/shard_map/ppermute | solution.py:1197
  45.2 22.2 %copy-start.3 = (bf16[32,128]{1,0:T(8,128)(2,1)S(1)}, bf16[32,128]{1,0:T(8,128)(2,1)}, u32[]{:S(2)}) copy-start(bf16[32,128]{1,0:T(8,128)(2,1)} %refs_9_.3) | copy-start | bytes 24580
  45.2 22.2 %copy-start.4 = (bf16[32,128]{1,0:T(8,128)(2,1)S(1)}, bf16[32,128]{1,0:T(8,128)(2,1)}, u32[]{:S(2)}) copy-start(bf16[32,128]{1,0:T(8,128)(2,1)} %refs_10_.3) | copy-start | bytes 24580
  45.2 22.2 %copy-start.5 = (bf16[32,32]{1,0:T(8,128)(2,1)S(1)}, bf16[32,32]{1,0:T(8,128)(2,1)}, u32[]{:S(2)}) copy-start(bf16[32,32]{1,0:T(8,128)(2,1)} %refs_8_.3) | copy-start | bytes 6148
  45.2 22.2 %copy-start.6 = (bf16[18,32]{1,0:T(8,128)(2,1)S(1)}, bf16[18,32]{1,0:T(8,128)(2,1)}, u32[]{:S(2)}) copy-start(bf16[18,32]{1,0:T(8,128)(2,1)} %refs_7_.3) | copy-start | bytes 3460
  52.9 1.5 %collective-permute-start.12 = (bf16[864,128]{1,0:T(8,128)(2,1)S(1)}, bf16[864,128]{1,0:T(8,128)(2,1)S(1)}, u32[]{:S(2)}, u32[]{:S(2)}) collective-permute-start(bf16[864,128]{1,0:T(8,128)(2,1)S(1)} %get-tuple-element.125), channel_id=1, source_target_pairs={{0,1},{1,0},{2,3},{3,2},{4,5},{5,4},{6,7},{7,6},{8,9},{9,8},{10,11... | collective-permute-start | bytes 663560 | tf_op jit(solution)/shard_map/ppermute | solution.py:1197
  53.0 8.1 %collective-permute-start.19 = (bf16[2,16,4096]{2,1,0:T(8,128)(2,1)S(1)}, bf16[2,16,4096]{2,1,0:T(8,128)(2,1)S(1)}, u32[]{:S(2)}, u32[]{:S(2)}) collective-permute-start(bf16[2,16,4096]{2,1,0:T(8,128)(2,1)S(1)} %get-tuple-element.133), channel_id=1, source_target_pairs={{0,3},{1,2},{2,1},{3,0},{4,7},{5,6},{6,5},{7,4},{8,11},{9,10},{10,... | collective-permute-start | bytes 786440 | tf_op jit(solution)/shard_map/ppermute | solution.py:1197
  55.0 6.0 %collective-permute-start.13 = (bf16[216,128]{1,0:T(8,128)(2,1)S(1)}, bf16[216,128]{1,0:T(8,128)(2,1)S(1)}, u32[]{:S(2)}, u32[]{:S(2)}) collective-permute-start(bf16[216,128]{1,0:T(8,128)(2,1)S(1)} %get-tuple-element.126), channel_id=1, source_target_pairs={{1,5},{3,7},{5,1},{7,3},{9,13},{11,15},{13,9},{15,11},{17,21},{19,... | collective-permute-start | bytes 165896 | tf_op jit(solution)/shard_map/ppermute | solution.py:1208
  55.7 5.4 %collective-permute-start.14 = (bf16[216,128]{1,0:T(8,128)(2,1)S(1)}, bf16[216,128]{1,0:T(8,128)(2,1)S(1)}, u32[]{:S(2)}, u32[]{:S(2)}) collective-permute-start(bf16[216,128]{1,0:T(8,128)(2,1)S(1)} %get-tuple-element.127), channel_id=1, source_target_pairs={{0,12},{1,9},{2,14},{3,11},{4,8},{5,13},{6,10},{7,15},{8,4},{9,1},... | collective-permute-start | bytes 165896 | tf_op jit(solution)/shard_map/ppermute | solution.py:1208
  58.3 7.3 %collective-permute-start.15 = (bf16[216,128]{1,0:T(8,128)(2,1)S(1)}, bf16[216,128]{1,0:T(8,128)(2,1)S(1)}, u32[]{:S(2)}, u32[]{:S(2)}) collective-permute-start(bf16[216,128]{1,0:T(8,128)(2,1)S(1)} %get-tuple-element.128), channel_id=1, source_target_pairs={{0,20},{1,17},{2,22},{3,19},{4,16},{5,21},{6,18},{7,23},{8,28},{9,... | collective-permute-start | bytes 165896 | tf_op jit(solution)/shard_map/ppermute | solution.py:1208
  60.9 6.5 %collective-permute-start.16 = (bf16[216,128]{1,0:T(8,128)(2,1)S(1)}, bf16[216,128]{1,0:T(8,128)(2,1)S(1)}, u32[]{:S(2)}, u32[]{:S(2)}) collective-permute-start(bf16[216,128]{1,0:T(8,128)(2,1)S(1)} %get-tuple-element.129), channel_id=1, source_target_pairs={{0,24},{1,29},{2,26},{3,31},{4,28},{5,25},{6,30},{7,27},{8,16},{9,... | collective-permute-start | bytes 165896 | tf_op jit(solution)/shard_map/ppermute | solution.py:1208
  68.6 1.9 %collective-permute-start.20 = (f32[344,128]{1,0:T(8,128)S(1)}, f32[344,128]{1,0:T(8,128)S(1)}, u32[]{:S(2)}, u32[]{:S(2)}) collective-permute-start(f32[344,128]{1,0:T(8,128)S(1)} %reduce.1), channel_id=1, source_target_pairs={{0,1},{1,0},{2,3},{3,2},{4,5},{5,4},{6,7},{7,6},{8,9},{9,8},{10,11... | collective-permute-start | bytes 528392 | tf_op jit(solution)/shard_map/ppermute | solution.py:1197
  70.5 6.8 %collective-permute-start.21 = (f32[344,128]{1,0:T(8,128)S(1)}, f32[344,128]{1,0:T(8,128)S(1)}, u32[]{:S(2)}, u32[]{:S(2)}) collective-permute-start(f32[344,128]{1,0:T(8,128)S(1)} %add.3.refs_0_), channel_id=1, source_target_pairs={{0,2},{1,3},{2,0},{3,1},{4,6},{5,7},{6,4},{7,5},{8,10},{9,11},{10,... | collective-permute-start | bytes 528392 | tf_op jit(solution)/shard_map/ppermute | solution.py:1197

commit v5 on v4

--- a/solution.py
+++ b/solution.py
@@ -158,13 +158,10 @@
     stats[3:8, :] = jnp.zeros((5, LANES), f32)
 
 
-def gather_kernel(member_ref, array, far, near, images, all_stats, own, sent):
+def gather_kernel(member_ref, own, far, near, images, all_stats):
     member = member_ref[0]
     frames = images.shape[0]
-    copy = pltpu.make_async_copy(array.at[pl.ds(member * frames, frames)], own, sent)
-    copy.start()
     first = member % 2 * frames
-    copy.wait()
     for f in range(frames):
         strips = (own.at[f], near.at[f], far.at[first + f], near.at[frames + f])
         gather_frame(member, strips, images.at[f], all_stats.at[f])
@@ -399,28 +396,38 @@
     win_one, win_two, win_level, win_coarse = wins
     tile_out, tile_level, tile_mid, coarse_pairs = tiles
     sum_one, sum_two, sum_down, sum_up = sums
-
-    @pl.when(pl.program_id(0) == 0)
-    def _():
-        for ref in sums:
-            ref[...] = jnp.zeros_like(ref)
+    cells = win_one.shape[0] * BLOCK
+
+    def operand(windows, slots):
+        parts = []
+        for slot in slots:
+            for shift in (0, 1):
+                parts.append(windows[:, slot, shift : shift + PAIRS].reshape(cells, LANES))
+        return jnp.concatenate(parts, axis=1)
 
     def blocks(tiles):
-        return jnp.concatenate([tiles[0, a].reshape(BLOCK, LANES) for a in range(2)], axis=1)
-
-    level_operand = window_operand(win_level.at[0], range(4))
+        return jnp.concatenate([tiles[:, a].reshape(cells, LANES) for a in range(2)], axis=1)
+
     out_blocks = blocks(tile_out)
-    sum_up[16 * C :, :] += outer(window_operand(win_coarse.at[0], (0, 1, 1, 2)), out_blocks)
-    sum_up[: 16 * C, :] += outer(level_operand, out_blocks)
-    sum_down[...] += outer(level_operand[:, : 6 * LANES], coarse_pairs[0].reshape(BLOCK, LANES))
-    sum_two[...] += outer(window_operand(win_two.at[0], range(4)), blocks(tile_level))
-    sum_one[...] += outer(window_operand(win_one.at[0], range(4)), blocks(tile_mid))
-
-
-def fold(sums, base, p, q):
+    sum_up[16 * C :, :] = outer(operand(win_coarse, range(3)), out_blocks)
+    sum_up[: 16 * C, :] = outer(operand(win_level, range(4)), out_blocks)
+    sum_down[...] = outer(operand(win_level, range(3)), coarse_pairs[...].reshape(cells, LANES))
+    sum_two[...] = outer(operand(win_two, range(4)), blocks(tile_level))
+    sum_one[...] = outer(operand(win_one, range(4)), blocks(tile_mid))
+
+
+def fold(sums, p, q):
+    return fold_slots(sums, 0, p, q, range(4))
+
+
+def fold_coarse(sums, p, q):
+    return fold_slots(sums, 16 * C, p, q, (0, 1, 1, 2))
+
+
+def fold_slots(sums, base, p, q, slots):
     halves = []
     for b in range(2):
-        rows = [base + ((a + p) * 4 + b + q) * C for a in range(2)]
+        rows = [base + (slots[a + p] * 4 + b + q) * C for a in range(2)]
         halves.append(sums[rows[0] : rows[0] + C, :LANES] + sums[rows[1] : rows[1] + C, LANES:])
     return halves[0] + swap_halves(halves[1])
 
@@ -430,22 +437,19 @@
     g_one, g_two, g_down, g_up = grads
     sum_one, sum_two, sum_down, sum_up = sums
     accumulate(wins, tiles, sums)
-
-    @pl.when(pl.program_id(0) == pl.num_programs(0) - 1)
-    def _():
-        for p in range(3):
-            for q in range(3):
-                at = (3 * p + q) * C
-                g_one[at : at + C, :] = fold(sum_one, 0, p, q)[:, :C]
-                g_two[at : at + C, :] = fold(sum_two, 0, p, q)[:, :C]
-                g_up[2 * at : 2 * at + C, :] = fold(sum_up, 16 * C, p, q)[:, :C]
-                g_up[2 * at + C : 2 * at + 2 * C, :] = fold(sum_up, 0, p, q)[:, :C]
-                place = (p * 4 + q) * C
-                g_down[at : at + C, :] = sum_down[place : place + C, :C]
+    for p in range(3):
+        for q in range(3):
+            at = (3 * p + q) * C
+            g_one[at : at + C, :] = fold(sum_one, p, q)[:, :C]
+            g_two[at : at + C, :] = fold(sum_two, p, q)[:, :C]
+            g_up[2 * at : 2 * at + C, :] = fold_coarse(sum_up, p, q)[:, :C]
+            g_up[2 * at + C : 2 * at + 2 * C, :] = fold(sum_up, p, q)[:, :C]
+            place = (p * 4 + q) * C
+            g_down[at : at + C, :] = sum_down[place : place + C, :C]
 
 
 PARTS = 16
-FAR_HINT = 90
+FAR_HINTS = 0, 90
 PAIR_PARTS = 24
 
 
@@ -469,44 +473,41 @@
     g_pair, g_up, g_down = refs[18:]
     sum_one, sum_two, sum_down, sum_up = sums
     accumulate(wins, tiles, sums)
-
-    @pl.when(pl.program_id(0) == pl.num_programs(0) - 1)
-    def _():
-        low_lanes = lane_ids((C, LANES)) < C
-        for p in range(3):
-            for q in range(3):
-                at = (3 * p + q) * C
-                g_pair[at : at + C, :] = jnp.where(
-                    low_lanes, fold(sum_one, 0, p, q), swap_halves(fold(sum_two, 0, p, q))
-                )
-                g_up[2 * at : 2 * at + C, :] = fold(sum_up, 16 * C, p, q)
-                g_up[2 * at + C : 2 * at + 2 * C, :] = fold(sum_up, 0, p, q)
-                place = (p * 4 + q) * C
-                g_down[at : at + C, :] = sum_down[place : place + C, :]
-        frames = pieces.shape[0]
-        small[...] = jnp.zeros_like(small)
-        total_bias = bias_sums[0, 0:4, :]
-        for f in range(frames):
-            small[4 * f : 4 * f + 4, :] = pieces[f, 0:4, :]
-            if f > 0:
-                total_bias = total_bias + bias_sums[f, 0:4, :]
-        small[4 * frames : 4 * frames + 4, :] = total_bias
-        sent = below(three_parts(small[...]), rows)
-        low_lanes = lane_ids((rows, LANES)) < C
-        half = count // 2
-        for at in range(half):
-            for ref, mine in ((kept, True), (theirs, False)):
-                start = pl.multiple_of(seq_owner(where_ref[0], where_ref[1], half, at, mine) * rows, 8)
-                blocks = (
-                    g_pair[pl.ds(start, rows), :],
-                    jnp.where(
-                        low_lanes,
-                        g_up[pl.ds(pl.multiple_of(2 * start, 8), rows), :],
-                        swap_halves(g_up[pl.ds(pl.multiple_of(2 * start + rows, 8), rows), :]),
-                    ),
-                    jnp.where(low_lanes, g_down[pl.ds(start, rows), :], 0.0 if mine else sent),
-                )
-                ref[at * 3 * rows : (at + 1) * 3 * rows, :] = jnp.concatenate(blocks, axis=0).astype(ref.dtype)
+    low_lanes = lane_ids((C, LANES)) < C
+    for p in range(3):
+        for q in range(3):
+            at = (3 * p + q) * C
+            g_pair[at : at + C, :] = jnp.where(
+                low_lanes, fold(sum_one, p, q), swap_halves(fold(sum_two, p, q))
+            )
+            g_up[2 * at : 2 * at + C, :] = fold_coarse(sum_up, p, q)
+            g_up[2 * at + C : 2 * at + 2 * C, :] = fold(sum_up, p, q)
+            place = (p * 4 + q) * C
+            g_down[at : at + C, :] = sum_down[place : place + C, :]
+    frames = pieces.shape[0]
+    small[...] = jnp.zeros_like(small)
+    total_bias = bias_sums[0, 0:4, :]
+    for f in range(frames):
+        small[4 * f : 4 * f + 4, :] = pieces[f, 0:4, :]
+        if f > 0:
+            total_bias = total_bias + bias_sums[f, 0:4, :]
+    small[4 * frames : 4 * frames + 4, :] = total_bias
+    sent = below(three_parts(small[...]), rows)
+    low_lanes = lane_ids((rows, LANES)) < C
+    half = count // 2
+    for at in range(half):
+        for ref, mine in ((kept, True), (theirs, False)):
+            start = pl.multiple_of(seq_owner(where_ref[0], where_ref[1], half, at, mine) * rows, 8)
+            blocks = (
+                g_pair[pl.ds(start, rows), :],
+                jnp.where(
+                    low_lanes,
+                    g_up[pl.ds(pl.multiple_of(2 * start, 8), rows), :],
+                    swap_halves(g_up[pl.ds(pl.multiple_of(2 * start + rows, 8), rows), :]),
+                ),
+                jnp.where(low_lanes, g_down[pl.ds(start, rows), :], 0.0 if mine else sent),
+            )
+            ref[at * 3 * rows : (at + 1) * 3 * rows, :] = jnp.concatenate(blocks, axis=0).astype(ref.dtype)
 
 
 def join_kernel(half, rows, frames, where_ref, kept, small, theirs, own, *messages):
@@ -540,7 +541,7 @@
 def reduce_kernel(half, rows, cells, frames, *refs):
     where_ref, own = refs[:2]
     messages = refs[2 : 2 + half]
-    hots, act_table, noise_table, ada_one, ada_two, out, pieces_one, pieces_two, table = refs[2 + half :]
+    hots, act_table, noise_table, ada_one, ada_two, out, pieces_one, pieces_two, table, high_one, high_two = refs[2 + half :]
     place, member = where_ref[0], where_ref[1]
     taken = 4 * frames
     bias = jnp.zeros((4, LANES), f32)
@@ -575,24 +576,25 @@
         return lax.dot_general(left, right, (dims, ((), ())), precision=precise, preferred_element_type=f32)
 
     one, two = pieces_one[...], pieces_two[...]
-    at = 3 * rows
-    out[:at, :] = sums
+    for ref, ada in ((high_one, ada_one), (high_two, ada_two)):
+        ref[...] = jnp.zeros_like(ref)
+        ref[C : C + cells, :] = ada[...].astype(f32)
+    embed_grad = exact(one, high_one[...], ((1,), (1,))) + exact(two, high_two[...], ((1,), (1,)))
+    width = C // (2 * half)
+    bias = pltpu.roll(jnp.concatenate([bias, bias], axis=0), (LANES - place * width) % LANES, axis=1)
+    extra = below(jnp.concatenate([exact(hot, embed_grad, ((0,), (0,))), bias], axis=0), rows)
+    at = 2 * rows
+    out[:at, :] = sums[:at]
+    out[at : at + rows, :] = jnp.where(lane_ids((rows, LANES)) < C, sums[at:], extra)
+    at = at + rows
     out[at : at + cells, :] = exact(embed, one, ((0,), (0,)))
     out[at + cells : at + 2 * cells, :] = exact(embed, two, ((0,), (0,)))
-    embed_grad = exact(one, ada_one[...].astype(f32), ((1,), (1,))) + exact(two, ada_two[...].astype(f32), ((1,), (1,)))
-    at = at + 2 * cells
-    out[at : at + TABLE_ROWS, :] = jnp.zeros((TABLE_ROWS, LANES), f32)
-    out[at : at + TABLE_ROWS, :cells] = exact(hot, embed_grad, ((0,), (0,)))
-    at = at + TABLE_ROWS
-    bias = jnp.concatenate([bias, jnp.zeros((4, LANES), f32)], axis=0)
-    width = C // (2 * half)
-    out[at : at + 8, :] = pltpu.roll(bias, (C - place * width) % LANES, axis=1)
 
 
 def finish_kernel(rows, cells, first, second, *outs):
     act_grad, noise_grad, ada_one, ada_two, g_one, g_two, g_down, g_up = outs[:8]
     bias_grads = outs[8:12]
-    sums = first[...] + second[...]
+    sums = first[...].astype(f32) + second[...].astype(f32)
 
     def turn(block):
         return jnp.concatenate([block, jnp.zeros((LANES - rows, LANES), f32)], axis=0).T[:, :rows]
@@ -606,25 +608,28 @@
     at = 3 * rows
     ada_one[...] = sums[at : at + cells]
     ada_two[...] = sums[at + cells : at + 2 * cells]
-    at = at + 2 * cells
-    act_grad[...] = sums[at + ACT_ROW : at + ACT_ROW + NACT, :cells]
-    noise_grad[...] = sums[at + NOISE_ROW : at + NOISE_ROW + NLEV, :cells]
-    at = at + TABLE_ROWS
+    extra = swap_halves(sums[2 * rows : 3 * rows])
+    act_grad[...] = extra[ACT_ROW : ACT_ROW + NACT, :cells]
+    noise_grad[...] = extra[NOISE_ROW : NOISE_ROW + NLEV, :cells]
     for k, ref in enumerate(bias_grads):
-        ref[...] = sums[at + k : at + k + 1, : ref.shape[0]].reshape(ref.shape)
-
-
-def write_operands(block, f_one, f_two, f_down, f_up, b_one, b_two, b_down, b_up):
+        ref[...] = extra[BIAS_ROW + k : BIAS_ROW + k + 1, : ref.shape[0]].reshape(ref.shape)
+
+
+def write_operands(block, turned_pairs, f_one, f_two, f_down, f_up, b_one, b_two, b_down, b_up):
     low_lanes = lane_ids((C, LANES)) < C
     zero = jnp.zeros((C, LANES), f32)
+
+    pairs = {name: turned_pairs(name) for name in ("one", "two", "down", "up")}
 
     def taps(name, base, step):
         plain, turned = {}, {}
         for p in range(3):
             for q in range(3):
-                k = block(name, (3 * p + q) * step + base)
-                plain[p, q] = k
-                turned[p, q] = jnp.concatenate([k, k], axis=0).T[:C]
+                at = (3 * p + q) * step + base
+                plain[p, q] = block(name, at)
+                pair = pairs[name][at // LANES]
+                other = swap_halves(pair)
+                turned[p, q] = jnp.where(low_lanes, pair, other) if at % LANES == 0 else jnp.where(low_lanes, other, pair)
         return plain, turned
 
     def write_forward(ref, base, plain):
@@ -687,7 +692,17 @@
         k = kernels[name][row : row + C, :].astype(f32)
         return jnp.concatenate([k, k], axis=1)
 
-    write_operands(block, *outs)
+    def turned_pairs(name):
+        found = []
+        for at in range(0, kernels[name].shape[0], LANES):
+            k = kernels[name][at : at + LANES, :].astype(f32)
+            k = jnp.concatenate([k, jnp.zeros(k.shape, f32)], axis=1)
+            if k.shape[0] < LANES:
+                k = jnp.concatenate([k, jnp.zeros((LANES - k.shape[0], LANES), f32)], axis=0)
+            found.append(k.T[:C])
+        return found
+
+    write_operands(block, turned_pairs, *outs)
 
 
 ACT_ROW, NOISE_ROW, TABLE_ROWS = 0, 24, 56
@@ -703,20 +718,30 @@
     return jnp.concatenate([wide, jnp.zeros((C, LANES), f32)], axis=0).T[: values.shape[1]]
 
 
-def far_kernel(member_ref, array, out, sent):
-    half = array.shape[0] // 2
-    copy = pltpu.make_async_copy(array.at[pl.ds((1 - member_ref[0] // 2) * half, half)], out, sent)
-    copy.start()
-    copy.wait()
-
-
-def near_kernel(member_ref, array, far, out, sent):
+def far_kernel(member_ref, array, out, own, other, sent):
+    half, share = out.shape[0], own.shape[0]
+    member = member_ref[0]
+    copies = [
+        pltpu.make_async_copy(array.at[pl.ds(first, ref.shape[0])], ref, sent.at[k])
+        for k, (first, ref) in enumerate(
+            (((1 - member // 2) * half, out), (member * share, own), ((member ^ 1) * share, other))
+        )
+    ]
+    for copy in copies:
+        copy.start()
+    for copy in copies:
+        copy.wait()
+
+
+def share_kernel(member_ref, far, out):
+    share = out.shape[0]
+    out[...] = far[pl.ds((member_ref[0] ^ 1) % 2 * share, share)]
+
+
+def near_kernel(other, shared, out):
     share = out.shape[0] // 2
-    other = member_ref[0] ^ 1
-    copy = pltpu.make_async_copy(array.at[pl.ds(other * share, share)], out.at[pl.ds(0, share)], sent)
-    copy.start()
-    out[share:] = far[pl.ds(other % 2 * share, share)]
-    copy.wait()
+    out[:share] = other[...]
+    out[share:] = shared[...]
 
 
 def pack_kernel(*refs):
@@ -848,7 +873,22 @@
             return jnp.where(low, swap_halves(k), k)
         return jnp.where(low, k, swap_halves(k))
 
-    write_operands(block, *outs)
+    both = {}
+
+    def turned_pairs(name):
+        work = {"one": work_pair, "two": work_pair, "down": work_down, "up": work_up}[name]
+        if name not in both:
+            found = []
+            for at in range(0, work.shape[0], LANES):
+                k = work[at : min(at + LANES, work.shape[0]), :]
+                if k.shape[0] < LANES:
+                    k = below(k, LANES)
+                found.append(k.T)
+            both["one" if name == "two" else name] = [k[:C] for k in found]
+            both["two" if name == "one" else name] = [k[C:] for k in found] if name in ("one", "two") else both[name]
+        return both[name]
+
+    write_operands(block, turned_pairs, *outs)
 
 
 def shape(dims, kind):
@@ -913,18 +953,22 @@
     )(conv_one, conv_two, down_kernel, up_kernel)
 
 
-def gather_frames(member, array, far, hint=0):
-    frames = array.shape[0] // lax.axis_size("rows")
-    near = trade(cut_near(member, array, far, hint), 1)
+def fetch_far(member, array):
+    far, own, other = cut_far(member, array, lax.axis_size("rows"))
+    return trade(far, 2), own, other
+
+
+def gather_frames(member, far, own, other, hints=(0, 0)):
+    near = trade(cut_near(member, other, far, hints), 1)
+    frames = own.shape[0]
     return pl.pallas_call(
         gather_kernel,
-        in_specs=[in_smem(), in_place()] + [in_vmem()] * 2,
+        in_specs=[in_smem()] + [in_vmem()] * 3,
         out_specs=[in_vmem()] * 2,
         out_shape=[shape((frames,) + IMAGE, f32), shape((frames,) + SMALL, f32)],
-        scratch_shapes=[pltpu.VMEM((frames,) + array.shape[1:], array.dtype), pltpu.SemaphoreType.DMA],
         compiler_params=params(),
         name="frames",
-    )(member, array, far, near)
+    )(member, own, far, near)
 
 
 def forward(member, frame_images, frame_stats, styles, biases, w_one, w_two, w_down, w_up, count):
@@ -980,56 +1024,65 @@
     )(member, *cot, frame_images, styles, stats, middle, down, w_up, w_down, w_two, w_one)
 
 
-def weight_grads(win_one, win_two, win_level, win_coarse, tile_out, tile_level, tile_mid, coarse_pairs):
-    frames = win_one.shape[0]
+def sum_scratch():
+    return [
+        pltpu.VMEM((KEYS, 2 * LANES), f32),
+        pltpu.VMEM((KEYS, 2 * LANES), f32),
+        pltpu.VMEM((6 * LANES, LANES), f32),
+        pltpu.VMEM((KEYS + 6 * LANES, 2 * LANES), f32),
+    ]
+
+
+def weight_grads(wins, tiles):
     return pl.pallas_call(
         weight_kernel,
-        grid=(frames,),
-        in_specs=[
-            per_frame(d) for d in (WINDOWS, WINDOWS, WINDOWS, COARSE_WINDOWS, TILES, TILES, TILES, COARSE)
-        ],
-        out_specs=[whole((9 * C, C)), whole((9 * C, C)), whole((9 * C, C)), whole((18 * C, C))],
+        in_specs=[in_vmem()] * 8,
+        out_specs=[in_vmem()] * 4,
         out_shape=[shape((9 * C, C), f32)] * 3 + [shape((18 * C, C), f32)],
-        scratch_shapes=[
-            pltpu.VMEM((KEYS, 2 * LANES), f32),
-            pltpu.VMEM((KEYS, 2 * LANES), f32),
-            pltpu.VMEM((6 * LANES, LANES), f32),
-            pltpu.VMEM((2 * KEYS, 2 * LANES), f32),
-        ],
+        scratch_shapes=sum_scratch(),
         compiler_params=params(),
-        cost_estimate=cost(frames * BLOCK * KEYS * 2 * LANES * 5, frames * (6 << 20)),
         name="weights",
-    )(win_one, win_two, win_level, win_coarse, tile_out, tile_level, tile_mid, coarse_pairs)
+    )(*wins, *tiles)
 
 
 def in_place(space=pl.ANY):
     return pl.BlockSpec(memory_space=space)
 
 
-def cut_far(member, array):
+def cut_far(member, array, count):
+    half, share = ((array.shape[0] // n,) + array.shape[1:] for n in (2, count))
     array = pltpu.with_memory_space_constraint(array, pltpu.HBM)
     return pl.pallas_call(
         far_kernel,
         in_specs=[in_smem(), in_place(pltpu.HBM)],
-        out_specs=in_vmem(),
-        out_shape=shape((array.shape[0] // 2,) + array.shape[1:], array.dtype),
-        scratch_shapes=[pltpu.SemaphoreType.DMA],
+        out_specs=[in_vmem()] * 3,
+        out_shape=[shape(half, array.dtype), shape(share, array.dtype), shape(share, array.dtype)],
+        scratch_shapes=[pltpu.SemaphoreType.DMA((3,))],
         compiler_params=params(),
         name="far",
     )(member, array)
 
 
-def cut_near(member, array, far, hint):
+def cut_near(member, other, far, hints):
+    other = pltpu.with_memory_space_constraint(other, pltpu.VMEM)
+    shared = pl.pallas_call(
+        share_kernel,
+        in_specs=[in_smem(), in_vmem()],
+        out_specs=in_vmem(),
+        out_shape=shape(other.shape, other.dtype),
+        compiler_params=params(),
+        cost_estimate=cost(BLOCK * KEYS * 2 * LANES * hints[0], 1 << 20),
+        name="shared",
+    )(member, far)
     return pl.pallas_call(
         near_kernel,
-        in_specs=[in_smem(), in_place(), in_vmem()],
+        in_specs=[in_vmem()] * 2,
         out_specs=in_vmem(),
-        out_shape=shape(far.shape, array.dtype),
-        scratch_shapes=[pltpu.SemaphoreType.DMA],
+        out_shape=shape(far.shape, other.dtype),
         compiler_params=params(),
-        cost_estimate=cost(BLOCK * KEYS * 2 * LANES * hint, 1 << 20),
+        cost_estimate=cost(BLOCK * KEYS * 2 * LANES * hints[1], 1 << 20),
         name="near",
-    )(member, array, far)
+    )(other, shared)
 
 
 def pack(ids, kernels, ada_one, ada_two, act_table, noise_table, biases):
@@ -1084,21 +1137,11 @@
     size = count // 2 * 3 * rows
     return pl.pallas_call(
         lambda *refs: message_kernel(count, rows, *refs),
-        grid=(frames,),
-        in_specs=[in_smem()]
-        + [per_frame(d) for d in (WINDOWS, WINDOWS, WINDOWS, COARSE_WINDOWS, TILES, TILES, TILES, COARSE)]
-        + [whole((frames,) + SMALL)] * 2,
-        out_specs=[whole((size, LANES)), whole((PARTS, LANES)), whole((size, LANES))],
+        in_specs=[in_smem()] + [in_vmem()] * 10,
+        out_specs=[in_vmem()] * 3,
         out_shape=[shape((size, LANES), f32), shape((PARTS, LANES), f32), shape((size, LANES), bf16)],
-        scratch_shapes=[
-            pltpu.VMEM((KEYS, 2 * LANES), f32),
-            pltpu.VMEM((KEYS, 2 * LANES), f32),
-            pltpu.VMEM((6 * LANES, LANES), f32),
-            pltpu.VMEM((2 * KEYS, 2 * LANES), f32),
-            pltpu.VMEM((9 * C, LANES), f32),
-            pltpu.VMEM((18 * C, LANES), f32),
-            pltpu.VMEM((9 * C, LANES), f32),
-        ],
+        scratch_shapes=sum_scratch()
+        + [pltpu.VMEM((9 * C, LANES), f32), pltpu.VMEM((18 * C, LANES), f32), pltpu.VMEM((9 * C, LANES), f32)],
         compiler_params=params(),
         cost_estimate=cost(frames * BLOCK * KEYS * 2 * LANES * 5, frames * (6 << 20)),
         name="weights",
@@ -1122,11 +1165,13 @@
         lambda *refs: reduce_kernel(half, rows, cells, frames, *refs),
         in_specs=[in_smem()] + [in_vmem()] * (half + 6),
         out_specs=in_vmem(),
-        out_shape=shape((3 * rows + 2 * cells + TABLE_ROWS + 8, LANES), f32),
+        out_shape=shape((3 * rows + 2 * cells, LANES), f32),
         scratch_shapes=[
             pltpu.VMEM((half * frames, LANES), f32),
             pltpu.VMEM((half * frames, LANES), f32),
             pltpu.VMEM((TABLE_ROWS, cells), f32),
+            pltpu.VMEM((LANES, LANES), f32),
+            pltpu.VMEM((LANES, LANES), f32),
         ],
         compiler_params=params(),
         name="reduce",
@@ -1208,15 +1253,15 @@
     return lax.ppermute(value, ("seq", "rows"), pairs)
 
 
-def layers(member_box, frame_images, frame_stats, cotangent, cot_far, styles, bias_rows, operands):
+def layers(member_box, frame_images, frame_stats, cot_fetched, styles, bias_rows, operands):
     f_one, f_two, f_down, f_up, b_one, b_two, b_down, b_up = operands
     count = lax.axis_size("rows")
     *out, win_one, win_two, win_level, win_coarse, middle, down, stats = forward(
         member_box, frame_images, frame_stats, styles, bias_rows, f_one, f_two, f_down, f_up, count
     )
     out = trade_strips(out)
-    down, cot_far = lax.optimization_barrier((down, cot_far))
-    cot = gather_frames(member_box, cotangent, cot_far)
+    down, cot_fetched = lax.optimization_barrier((down, cot_fetched))
+    cot = gather_frames(member_box, *cot_fetched)
     *grad_strips, tile_out, tile_level, tile_mid, coarse_pairs, pieces, bias_sums = backward(
         member_box, cot, frame_images, styles, stats, middle, down, b_up, b_down, b_two, b_one, count
     )
@@ -1256,15 +1301,15 @@
     ids = (actions, noise_ids, valid)
     kernels = (conv_one, conv_two, down_kernel, up_kernel)
     biases = (bias_one, bias_two, bias_down, bias_up)
-    far = trade(cut_far(member_box, frames), 2)
+    fetched = fetch_far(member_box, frames)
     packed = pack(ids, kernels, ada_one, ada_two, act_table, noise_table, biases)
     mine = jnp.concatenate([half_trade(packed, at) for at in range(half)], axis=0)
     other = trade(mine, 1)
-    cot_far = trade(cut_far(member_box, cotangent), 2)
-    frame_images, frame_stats = gather_frames(member_box, frames, far, FAR_HINT)
+    cot_fetched = fetch_far(member_box, cotangent)
+    frame_images, frame_stats = gather_frames(member_box, *fetched, FAR_HINTS)
     *operands, styles, bias_rows, hots = prepare(where, ids, packed, mine, other, count, rows, cells, share)
     out, grad_strips, wins, tiles, pieces, bias_sums = layers(
-        member_box, frame_images, frame_stats, cotangent, cot_far, styles, bias_rows, operands
+        member_box, frame_images, frame_stats, cot_fetched, styles, bias_rows, operands
     )
     kept, small, theirs = weight_messages(where, wins, tiles, pieces, bias_sums, count, rows)
     theirs, out = lax.optimization_barrier((theirs, out))
@@ -1280,6 +1325,7 @@
         offset *= 2
     result = collect_strips(member_box, out, bf16)
     frames_grad = collect_strips(member_box, grad_strips, f32)
+    sums = sums.astype(bf16)
     return (result, frames_grad, *finish(sums, trade(sums, offset), rows, cells, width))
 
 
@@ -1309,9 +1355,8 @@
     def gathered(value, axis):
         return lax.all_gather(value, "seq", axis=axis, tiled=True)
 
-    cot_far = trade(cut_far(member_box, cotangent), 2)
-    far = trade(cut_far(member_box, frames), 2)
-    frame_images, frame_stats = gather_frames(member_box, frames, far)
+    cot_fetched = fetch_far(member_box, cotangent)
+    frame_images, frame_stats = gather_frames(member_box, *fetch_far(member_box, frames))
     act_full = gathered(act_table, 1)
     noise_full = gathered(noise_table, 1)
     ada_full = gathered(jnp.concatenate([ada_one, ada_two], axis=1), 0).astype(f32)
@@ -1338,9 +1383,9 @@
     )
     bias_rows = pad_small([twice(biases[k]) for k in range(4)])
     out, grad_strips, wins, tiles, pieces, bias_sums = layers(
-        member_box, frame_images, frame_stats, cotangent, cot_far, styles, bias_rows, operands
+        member_box, frame_images, frame_stats, cot_fetched, styles, bias_rows, operands
     )
-    g_one, g_two, g_down, g_up = weight_grads(*wins, *tiles)
+    g_one, g_two, g_down, g_up = weight_grads(wins, tiles)
     result = collect_strips(member_box, out, bf16)
     frames_grad = collect_strips(member_box, grad_strips, f32)
 

time: 78.5 us -> 73.7 us (0.939)
  waiting for transfers between devices: 17.6 us -> 13.6 us
    ppermute x14, waiting for transfers between devices: 10.5 us -> 6.15 us  [trade(): return lax.ppermute(value, 'rows', [(i, i ^ offset) for i in range(count)])]
    pallas_call x2, Pallas kernels: 2.11 us -> 3.24 us  [cut_far(): pl.pallas_call(far_kernel, in_specs=[in_smem(), in_place(pltpu.HBM)], out...]
    pallas_call x5 -> x7, Pallas kernels: 9.83 us -> 8.89 us  [the longest x1 6.94 us: weight_messages(): pl.pallas_call(lambda *refs: message_kernel(count, rows, *refs), in_specs...]
    pallas_call x1, Pallas kernels: 2.63 us -> 1.74 us  [prepare(): pl.pallas_call(lambda *refs: prepare_kernel(count, rows, cells, *refs), i...]
  transfers between devices with their start and end apart: 22 -> 22, of which waited for: 8 -> 8; matrix products, arithmetic and copies ran while one was open for 0% -> 0% of each run, Pallas kernels for 43% -> 45%
where the time goes in v5:
time: 73.7 us; the launch traced here: 73.4 us
  Pallas kernels  36.4 us (49%)
  starting transfers between devices  22.2 us (30%)
  waiting for transfers between devices  13.6 us (18%)
  between operations  1.06 us (1%)
    ppermute x8, starting transfers between devices, half_trade(): return lax.ppermute(value, ('seq', 'rows'), pairs)  12.1 us
    ppermute x14, starting transfers between devices, trade(): return lax.ppermute(value, 'rows', [(i, i ^ offset) for i in range(count)])  10.1 us
    pallas_call x1, Pallas kernels, backward(): pl.pallas_call(lambda *refs: backward_kernel(count, *refs), in_specs=[in_...  8.59 us
    ppermute x8, waiting for transfers between devices, half_trade(): return lax.ppermute(value, ('seq', 'rows'), pairs)  7.48 us
    pallas_call x1, Pallas kernels, forward(): pl.pallas_call(lambda *refs: forward_kernel(count, *refs), in_specs=[in_s...  7.06 us
    pallas_call x1, Pallas kernels, weight_messages(): pl.pallas_call(lambda *refs: message_kernel(count, rows, *refs), in_specs...  6.94 us
    ppermute x14, waiting for transfers between devices, trade(): return lax.ppermute(value, 'rows', [(i, i ^ offset) for i in range(count)])  6.15 us
    pallas_call x2, Pallas kernels, cut_far(): pl.pallas_call(far_kernel, in_specs=[in_smem(), in_place(pltpu.HBM)], out...  3.24 us
  transfers between devices with their start and end apart: 22, of which 8 were waited for; matrix products, arithmetic and copies ran while one was open for 0% of the time, Pallas kernels for 45%

profile of v5, /device:TPU:0, one launch (start us, length us, event | category | flops | bytes accessed | tf_op | source)
XLA Modules:
  0.0 73.4 jit_solution(9012954434669190431)
XLA Ops:
  0.6 1.2 %far.2 = (bf16[4,16,4096]{2,1,0:T(8,128)(2,1)S(1)}, bf16[2,16,4096]{2,1,0:T(8,128)(2,1)S(1)}, bf16[2,16,4096]{2,1,0:T(8,128)(2,1)S(1)}) custom-call(s32[1]{0:T(128)} %bitcast.member_ref.refs_0_, bf16[8,16,4096]{2,1,0:T(8,128)(2,1)} %array.2), custom_call_target="tpu_custom_call" | custom-call | tf_op jit(solution)/shard_map/far/pallas_call | solution.py:1055
  1.9 3.0 %collective-permute-start = (bf16[4,16,4096]{2,1,0:T(8,128)(2,1)S(1)}, bf16[4,16,4096]{2,1,0:T(8,128)(2,1)S(1)}, u32[]{:S(2)}, u32[]{:S(2)}) collective-permute-start(bf16[4,16,4096]{2,1,0:T(8,128)(2,1)S(1)} %get-tuple-element.94), channel_id=1, source_target_pairs={{0,2},{1,3},{2,0},{3,1},{4,6},{5,7},{6,4},{7,5},{8,10},{9,11},{10,... | collective-permute-start | bytes 1572872 | tf_op jit(solution)/shard_map/ppermute | solution.py:1242
  4.9 1.8 %pack.1.refs_4_ = bf16[288,128]{1,0:T(8,128)(2,1)} custom-call(s32[8]{0:T(128)} %refs_1_.3, s32[8]{0:T(128)} %refs_2_.3, s32[8]{0:T(128)} %refs_3_.1, bf16[64,72]{1,0:T(8,128)(2,1)} %bitcast.19, bf16[64,72]{1,0:T(8,128)(2,1)} %bitcast.20, bf16[64,72]{1,0:T(8,128)(2,1)} %bitcast.21, bf16[64,144]{1,0:T(8,128)(2,1)} %bitcast.15, bf16[32,128]{1,0:T(8,128)(2,1)} %refs_9_.3, ...), custom_call_target="tpu_custom_call" | custom-call | flops 16106127360 | bytes 1048576 | tf_op jit(solution)/shard_map/pack/pallas_call | solution.py:1091
  6.7 0.7 collective-permute-start.2
  7.3 3.7 %collective-permute-start.5 = (bf16[288,128]{1,0:T(8,128)(2,1)}, bf16[288,128]{1,0:T(8,128)(2,1)S(1)}, u32[]{:S(2)}, u32[]{:S(2)}) collective-permute-start(bf16[288,128]{1,0:T(8,128)(2,1)} %pack.1.refs_4_), channel_id=1, source_target_pairs={{0,24},{1,29},{2,26},{3,31},{4,28},{5,25},{6,30},{7,27},{8,16},{9,... | collective-permute-start | bytes 221192 | tf_op jit(solution)/shard_map/ppermute | solution.py:1253
  11.0 0.4 collective-permute-start.4
  11.4 1.3 %collective-permute-start.3 = (bf16[288,128]{1,0:T(8,128)(2,1)}, bf16[288,128]{1,0:T(8,128)(2,1)S(1)}, u32[]{:S(2)}, u32[]{:S(2)}) collective-permute-start(bf16[288,128]{1,0:T(8,128)(2,1)} %pack.1.refs_4_), channel_id=1, source_target_pairs={{0,12},{1,9},{2,14},{3,11},{4,8},{5,13},{6,10},{7,15},{8,4},{9,1},... | collective-permute-start | bytes 221192 | tf_op jit(solution)/shard_map/ppermute | solution.py:1253
  12.7 2.0 %far.3 = (bf16[4,16,4096]{2,1,0:T(8,128)(2,1)}, bf16[2,16,4096]{2,1,0:T(8,128)(2,1)S(1)}, bf16[2,16,4096]{2,1,0:T(8,128)(2,1)S(1)}) custom-call(s32[1]{0:T(128)} %bitcast.member_ref.refs_0_, bf16[8,16,4096]{2,1,0:T(8,128)(2,1)} %array.3), custom_call_target="tpu_custom_call" | custom-call | tf_op jit(solution)/shard_map/far/pallas_call | solution.py:1055
  14.7 0.0 collective-permute-done.2
  14.7 0.4 collective-permute-start.7
  15.2 1.7 %collective-permute-done.far = bf16[4,16,4096]{2,1,0:T(8,128)(2,1)S(1)} collective-permute-done((bf16[4,16,4096]{2,1,0:T(8,128)(2,1)S(1)}, bf16[4,16,4096]{2,1,0:T(8,128)(2,1)S(1)}, u32[]{:S(2)}, u32[]{:S(2)}) %collective-permute-start) | collective-permute-done | bytes 524320 | tf_op jit(solution)/shard_map/ppermute | solution.py:1242
  16.9 0.0 copy-start.5
  16.9 0.0 copy-start.6
  16.9 0.0 copy-start.7
  16.9 0.8 %near.2 = bf16[4,16,4096]{2,1,0:T(8,128)(2,1)} custom-call(bf16[2,16,4096]{2,1,0:T(8,128)(2,1)S(1)} %get-tuple-element.95.other, bf16[2,16,4096]{2,1,0:T(8,128)(2,1)S(1)} %shared.2), custom_call_target="tpu_custom_call" | custom-call | flops 48318382080 | bytes 1048576 | tf_op jit(solution)/shard_map/near/pallas_call | solution.py:1077
  17.7 0.0 collective-permute-start.1
  17.7 0.0 collective-permute-done.3
  17.8 1.1 %collective-permute-done.4 = bf16[288,128]{1,0:T(8,128)(2,1)S(1)} collective-permute-done((bf16[288,128]{1,0:T(8,128)(2,1)}, bf16[288,128]{1,0:T(8,128)(2,1)S(1)}, u32[]{:S(2)}, u32[]{:S(2)}) %collective-permute-start.4) | collective-permute-done | bytes 73760 | tf_op jit(solution)/shard_map/ppermute | solution.py:1253
  18.9 0.0 collective-permute-done.5
  18.9 0.1 collective-permute-start.6
  19.0 0.1 pad_add_fusion.refs_0_
  19.1 1.5 %collective-permute-done.6.refs_6_ = bf16[1152,128]{1,0:T(8,128)(2,1)S(1)} collective-permute-done((bf16[1152,128]{1,0:T(8,128)(2,1)S(1)}, bf16[1152,128]{1,0:T(8,128)(2,1)S(1)}, u32[]{:S(2)}, u32[]{:S(2)}) %collective-permute-start.6) | collective-permute-done | bytes 294944 | tf_op jit(solution)/shard_map/ppermute | solution.py:1242
  20.6 0.0 copy-done
  20.6 1.7 %prepare.1 = (bf16[1024,256]{1,0:T(8,128)(2,1)S(1)}, bf16[1024,256]{1,0:T(8,128)(2,1)S(1)}, bf16[768,128]{1,0:T(8,128)(2,1)S(1)}, bf16[2048,256]{1,0:T(8,128)(2,...) custom-call(s32[2]{0:T(128)S(1)} %pad_add_fusion.refs_0_, ...), custom_call_target="tpu_custom_call" | custom-call | tf_op jit(solution)/shard_map/prepare/pallas_call | solution.py:1116
  22.3 0.0 collective-permute-done.1.near
  22.3 0.5 frames.2
  22.9 7.1 %forward.1 = (bf16[2,16,4096]{2,1,0:T(8,128)(2,1)S(1)}, bf16[2,16,4096]{2,1,0:T(8,128)(2,1)S(1)}, bf16[2,16,4096]{2,1,0:T(8,128)(2,1)S(1)}, bf16[2,16,4096]{2,1,...) custom-call(s32[1]{0:T(128)} %bitcast.member_ref.refs_0_, ...), custom_call_target="tpu_custom_call" | custom-call | flops 2048 | bytes 1024 | tf_op jit(solution)/shard_map/forward/pallas_call | solution.py:977
  29.9 0.0 collective-permute-done.7.far
  30.0 0.2 collective-permute-start.8
  30.2 0.4 collective-permute-start.9
  30.6 1.2 %collective-permute-start.10 = (bf16[2,16,4096]{2,1,0:T(8,128)(2,1)S(1)}, bf16[2,16,4096]{2,1,0:T(8,128)(2,1)S(1)}, u32[]{:S(2)}, u32[]{:S(2)}) collective-permute-start(bf16[2,16,4096]{2,1,0:T(8,128)(2,1)S(1)} %get-tuple-element.133), channel_id=1, source_target_pairs={{0,2},{1,3},{2,0},{3,1},{4,6},{5,7},{6,4},{7,5},{8,10},{9,11},{10,... | collective-permute-start | bytes 786440 | tf_op jit(solution)/shard_map/ppermute | solution.py:1242
  31.8 0.2 collective-permute-start.11
  32.1 0.0 collective-permute-done.8.near
  32.1 0.5 frames.3
  32.6 8.6 %backward.1 = (bf16[2,16,4096]{2,1,0:T(8,128)(2,1)S(1)}, bf16[2,16,4096]{2,1,0:T(8,128)(2,1)S(1)}, bf16[2,16,4096]{2,1,0:T(8,128)(2,1)S(1)}, bf16[2,16,4096]{2,1...) custom-call(s32[1]{0:T(128)} %bitcast.member_ref.refs_0_, ...), custom_call_target="tpu_custom_call" | custom-call | flops 5368709120 | bytes 20971520 | tf_op jit(solution)/shard_map/backward/pallas_call | solution.py:1001
  41.2 0.7 collective-permute-start.17
  41.9 1.2 %collective-permute-start.18 = (bf16[2,16,4096]{2,1,0:T(8,128)(2,1)S(1)}, bf16[2,16,4096]{2,1,0:T(8,128)(2,1)S(1)}, u32[]{:S(2)}, u32[]{:S(2)}) collective-permute-start(bf16[2,16,4096]{2,1,0:T(8,128)(2,1)S(1)} %get-tuple-element.148), channel_id=1, source_target_pairs={{0,2},{1,3},{2,0},{3,1},{4,6},{5,7},{6,4},{7,5},{8,10},{9,11},{10,... | collective-permute-start | bytes 786440 | tf_op jit(solution)/shard_map/ppermute | solution.py:1242
  43.2 6.9 %weights.1 = (f32[864,128]{1,0:T(8,128)S(1)}, f32[16,128]{1,0:T(8,128)S(1)}, bf16[864,128]{1,0:T(8,128)(2,1)S(1)}) custom-call(s32[2]{0:T(128)S(1)} %pad_add_fusion.refs_0_, bf16[2,4,33,32,128]{4,3,2,1,0:T(8,128)(2,1)S(1)} %get-tuple-element.104.refs_1_, bf16[2,4,33,32,128]{4,3,2,1,0:T(8,128)(2,1)S(1)} %get-tuple-element.105.refs_2_, ...), custom_call_target="tpu_custom_call" | custom-call | flops 5368709120 | bytes 12582912 | tf_op jit(solution)/shard_map/weights/pallas_call | solution.py:1138
  50.1 0.0 collective-permute-done.9.refs_1_
  50.1 0.0 collective-permute-done.10.refs_2_
  50.1 0.0 collective-permute-done.11.refs_3_
  50.2 0.1 collective-permute-start.12
  50.2 0.9 %collective-permute-start.19 = (bf16[2,16,4096]{2,1,0:T(8,128)(2,1)S(1)}, bf16[2,16,4096]{2,1,0:T(8,128)(2,1)S(1)}, u32[]{:S(2)}, u32[]{:S(2)}) collective-permute-start(bf16[2,16,4096]{2,1,0:T(8,128)(2,1)S(1)} %get-tuple-element.149), channel_id=1, source_target_pairs={{0,3},{1,2},{2,1},{3,0},{4,7},{5,6},{6,5},{7,4},{8,11},{9,10},{10,... | collective-permute-start | bytes 786440 | tf_op jit(solution)/shard_map/ppermute | solution.py:1242
  51.1 0.6 collective-permute-done.12.refs_3_
  51.7 0.6 join.1
  52.3 0.7 collective-permute-start.13
  53.0 2.8 %collective-permute-start.14 = (bf16[216,128]{1,0:T(8,128)(2,1)S(1)}, bf16[216,128]{1,0:T(8,128)(2,1)S(1)}, u32[]{:S(2)}, u32[]{:S(2)}) collective-permute-start(bf16[216,128]{1,0:T(8,128)(2,1)S(1)} %get-tuple-element.143), channel_id=1, source_target_pairs={{0,12},{1,9},{2,14},{3,11},{4,8},{5,13},{6,10},{7,15},{8,4},{9,1},... | collective-permute-start | bytes 165896 | tf_op jit(solution)/shard_map/ppermute | solution.py:1253
  55.7 0.0 collective-permute-done.17.refs_1_
  55.7 2.5 %collective-permute-start.15 = (bf16[216,128]{1,0:T(8,128)(2,1)S(1)}, bf16[216,128]{1,0:T(8,128)(2,1)S(1)}, u32[]{:S(2)}, u32[]{:S(2)}) collective-permute-start(bf16[216,128]{1,0:T(8,128)(2,1)S(1)} %get-tuple-element.144), channel_id=1, source_target_pairs={{0,20},{1,17},{2,22},{3,19},{4,16},{5,21},{6,18},{7,23},{8,28},{9,... | collective-permute-start | bytes 165896 | tf_op jit(solution)/shard_map/ppermute | solution.py:1253
  58.3 0.0 collective-permute-done.18.refs_2_
  58.3 0.1 collective-permute-start.16
  58.4 0.0 collective-permute-done.19.refs_3_
  58.4 0.0 collective-permute-done.13.refs_2_
  58.4 0.0 collective-permute-done.14.refs_3_
  58.4 4.6 %collective-permute-done.15.refs_4_ = bf16[216,128]{1,0:T(8,128)(2,1)S(1)} collective-permute-done((bf16[216,128]{1,0:T(8,128)(2,1)S(1)}, bf16[216,128]{1,0:T(8,128)(2,1)S(1)}, u32[]{:S(2)}, u32[]{:S(2)}) %collective-permute-start.15) | collective-permute-done | bytes 55328 | tf_op jit(solution)/shard_map/ppermute | solution.py:1253
  63.0 1.8 %collective-permute-done.16.refs_5_ = bf16[216,128]{1,0:T(8,128)(2,1)S(1)} collective-permute-done((bf16[216,128]{1,0:T(8,128)(2,1)S(1)}, bf16[216,128]{1,0:T(8,128)(2,1)S(1)}, u32[]{:S(2)}, u32[]{:S(2)}) %collective-permute-start.16) | collective-permute-done | bytes 55328 | tf_op jit(solution)/shard_map/ppermute | solution.py:1253
  64.8 1.3 %reduce.1 = f32[280,128]{1,0:T(8,128)S(1)} custom-call(s32[2]{0:T(128)S(1)} %pad_add_fusion.refs_0_, f32[216,128]{1,0:T(8,128)S(1)} %get-tuple-element.154.refs_1_, bf16[216,128]{1,0:T(8,128)(2,1)S(1)} %collective-permute-done.13.refs_2_, bf16[216,128]{1,0:T(8,128)(2,1)S(1)} %collective-permute-done.14.refs_3_, ...), custom_call_target="tpu_custom_call" | custom-call | tf_op jit(solution)/shard_map/reduce/pallas_call | solution.py:1164
  66.1 0.8 %collective-permute-start.20 = (f32[280,128]{1,0:T(8,128)S(1)}, f32[280,128]{1,0:T(8,128)S(1)}, u32[]{:S(2)}, u32[]{:S(2)}) collective-permute-start(f32[280,128]{1,0:T(8,128)S(1)} %reduce.1), channel_id=1, source_target_pairs={{0,1},{1,0},{2,3},{3,2},{4,5},{5,4},{6,7},{7,6},{8,9},{9,8},{10,11... | collective-permute-start | bytes 430088 | tf_op jit(solution)/shard_map/ppermute | solution.py:1242
  66.9 1.0 %collective-permute-done.20 = f32[280,128]{1,0:T(8,128)S(1)} collective-permute-done((f32[280,128]{1,0:T(8,128)S(1)}, f32[280,128]{1,0:T(8,128)S(1)}, u32[]{:S(2)}, u32[]{:S(2)}) %collective-permute-start.20) | collective-permute-done | bytes 143392 | tf_op jit(solution)/shard_map/ppermute | solution.py:1242
  67.9 0.8 %collective-permute-start.21 = (bf16[280,128]{1,0:T(8,128)(2,1)S(1)}, bf16[280,128]{1,0:T(8,128)(2,1)S(1)}, u32[]{:S(2)}, u32[]{:S(2)}) collective-permute-start(bf16[280,128]{1,0:T(8,128)(2,1)S(1)} %add_convert_fusion.refs_0_), channel_id=1, source_target_pairs={{0,2},{1,3},{2,0},{3,1},{4,6},{5,7},{6,4},{7,5},{8,10},{9,11},{10,... | collective-permute-start | bytes 215048 | tf_op jit(solution)/shard_map/ppermute | solution.py:1242
  68.6 1.0 %collect.2 = bf16[4,2,16,4096]{3,2,1,0:T(8,128)(2,1)} custom-call(s32[1]{0:T(128)} %bitcast.member_ref.refs_0_, bf16[2,16,4096]{2,1,0:T(8,128)(2,1)S(1)} %get-tuple-element.135.refs_0_, bf16[2,16,4096]{2,1,0:T(8,128)(2,1)S(1)} %collective-permute-done.9.refs_1_, bf16[2,16,4096]{2,1,0:T(8,128)(2,1)S(1)} %collective-permute-done.10.refs_2_, ...), custom_call_target="tpu_custom_call" | custom-call | tf_op jit(solution)/shard_map/collect/pallas_call | solution.py:1216
  69.6 1.4 %collect.3 = f32[4,2,16,4096]{3,2,1,0:T(8,128)} custom-call(s32[1]{0:T(128)} %bitcast.member_ref.refs_0_, bf16[2,16,4096]{2,1,0:T(8,128)(2,1)S(1)} %get-tuple-element.150.refs_0_, bf16[2,16,4096]{2,1,0:T(8,128)(2,1)S(1)} %collective-permute-done.17.refs_1_, bf16[2,16,4096]{2,1,0:T(8,128)(2,1)S(1)} %collective-permute-done.18.refs_2_, ...), custom_call_target="tpu_custom_call" | custom-call | tf_op jit(solution)/shard_map/collect/pallas_call | solution.py:1216
  71.0 1.4 %collective-permute-done.21.refs_1_ = bf16[280,128]{1,0:T(8,128)(2,1)S(1)} collective-permute-done((bf16[280,128]{1,0:T(8,128)(2,1)S(1)}, bf16[280,128]{1,0:T(8,128)(2,1)S(1)}, u32[]{:S(2)}, u32[]{:S(2)}) %collective-permute-start.21) | collective-permute-done | bytes 71712 | tf_op jit(solution)/shard_map/ppermute | solution.py:1242
  72.4 0.8 %finish.1 = (f32[18,32]{1,0:T(8,128)}, f32[32,32]{1,0:T(8,128)}, f32[32,128]{1,0:T(8,128)}, f32[32,128]{1,0:T(8,128)}, f32[64,72]{1,0:T(8,128)}, /*index=5*/f32[...) custom-call(bf16[280,128]{1,0:T(8,128)(2,1)S(1)} %add_convert_fusion, ...), custom_call_target="tpu_custom_call" | custom-call | tf_op jit(solution)/shard_map/finish/pallas_call | solution.py:1182
  (20 shorter events, 0.2 us)
Async XLA Ops:
  1.9 15.0 %collective-permute-start = (bf16[4,16,4096]{2,1,0:T(8,128)(2,1)S(1)}, bf16[4,16,4096]{2,1,0:T(8,128)(2,1)S(1)}, u32[]{:S(2)}, u32[]{:S(2)}) collective-permute-start(bf16[4,16,4096]{2,1,0:T(8,128)(2,1)S(1)} %get-tuple-element.94), channel_id=1, source_target_pairs={{0,2},{1,3},{2,0},{3,1},{4,6},{5,7},{6,4},{7,5},{8,10},{9,11},{10,... | collective-permute-start | bytes 1572872 | tf_op jit(solution)/shard_map/ppermute | solution.py:1242
  6.7 8.0 %collective-permute-start.2 = (bf16[288,128]{1,0:T(8,128)(2,1)}, bf16[288,128]{1,0:T(8,128)(2,1)S(1)}, u32[]{:S(2)}, u32[]{:S(2)}) collective-permute-start(bf16[288,128]{1,0:T(8,128)(2,1)} %pack.1.refs_4_), channel_id=1, source_target_pairs={{1,5},{3,7},{5,1},{7,3},{9,13},{11,15},{13,9},{15,11},{17,21},{19,... | collective-permute-start | bytes 221192 | tf_op jit(solution)/shard_map/ppermute | solution.py:1253
  7.3 11.5 %collective-permute-start.5 = (bf16[288,128]{1,0:T(8,128)(2,1)}, bf16[288,128]{1,0:T(8,128)(2,1)S(1)}, u32[]{:S(2)}, u32[]{:S(2)}) collective-permute-start(bf16[288,128]{1,0:T(8,128)(2,1)} %pack.1.refs_4_), channel_id=1, source_target_pairs={{0,24},{1,29},{2,26},{3,31},{4,28},{5,25},{6,30},{7,27},{8,16},{9,... | collective-permute-start | bytes 221192 | tf_op jit(solution)/shard_map/ppermute | solution.py:1253
  11.0 7.9 %collective-permute-start.4 = (bf16[288,128]{1,0:T(8,128)(2,1)}, bf16[288,128]{1,0:T(8,128)(2,1)S(1)}, u32[]{:S(2)}, u32[]{:S(2)}) collective-permute-start(bf16[288,128]{1,0:T(8,128)(2,1)} %pack.1.refs_4_), channel_id=1, source_target_pairs={{0,20},{1,17},{2,22},{3,19},{4,16},{5,21},{6,18},{7,23},{8,28},{9,... | collective-permute-start | bytes 221192 | tf_op jit(solution)/shard_map/ppermute | solution.py:1253
  11.4 6.4 %collective-permute-start.3 = (bf16[288,128]{1,0:T(8,128)(2,1)}, bf16[288,128]{1,0:T(8,128)(2,1)S(1)}, u32[]{:S(2)}, u32[]{:S(2)}) collective-permute-start(bf16[288,128]{1,0:T(8,128)(2,1)} %pack.1.refs_4_), channel_id=1, source_target_pairs={{0,12},{1,9},{2,14},{3,11},{4,8},{5,13},{6,10},{7,15},{8,4},{9,1},... | collective-permute-start | bytes 221192 | tf_op jit(solution)/shard_map/ppermute | solution.py:1253
  14.7 15.2 %collective-permute-start.7 = (bf16[4,16,4096]{2,1,0:T(8,128)(2,1)}, bf16[4,16,4096]{2,1,0:T(8,128)(2,1)S(1)}, u32[]{:S(2)}, u32[]{:S(2)}) collective-permute-start(bf16[4,16,4096]{2,1,0:T(8,128)(2,1)} %get-tuple-element.109), channel_id=1, source_target_pairs={{0,2},{1,3},{2,0},{3,1},{4,6},{5,7},{6,4},{7,5},{8,10},{9,11},{10,... | collective-permute-start | bytes 1572872 | tf_op jit(solution)/shard_map/ppermute | solution.py:1242
  16.9 3.7 %copy-start = (bf16[288,128]{1,0:T(8,128)(2,1)S(1)}, bf16[288,128]{1,0:T(8,128)(2,1)}, u32[]{:S(2)}) copy-start(bf16[288,128]{1,0:T(8,128)(2,1)} %pack.1.refs_4_) | copy-start | bytes 221188
  16.9 3.7 %copy-start.5 = (s32[8]{0:T(128)S(1)}, s32[8]{0:T(128)}, u32[]{:S(2)}) copy-start(s32[8]{0:T(128)} %refs_1_.3) | copy-start | bytes 100
  16.9 3.7 %copy-start.6 = (s32[8]{0:T(128)S(1)}, s32[8]{0:T(128)}, u32[]{:S(2)}) copy-start(s32[8]{0:T(128)} %refs_2_.3) | copy-start | bytes 100
  16.9 3.7 %copy-start.7 = (s32[8]{0:T(128)S(1)}, s32[8]{0:T(128)}, u32[]{:S(2)}) copy-start(s32[8]{0:T(128)} %refs_3_.1) | copy-start | bytes 100
  17.7 4.6 %collective-permute-start.1 = (bf16[4,16,4096]{2,1,0:T(8,128)(2,1)}, bf16[4,16,4096]{2,1,0:T(8,128)(2,1)S(1)}, u32[]{:S(2)}, u32[]{:S(2)}) collective-permute-start(bf16[4,16,4096]{2,1,0:T(8,128)(2,1)} %near.2), channel_id=1, source_target_pairs={{0,1},{1,0},{2,3},{3,2},{4,5},{5,4},{6,7},{7,6},{8,9},{9,8},{10,11... | collective-permute-start | bytes 1572872 | tf_op jit(solution)/shard_map/ppermute | solution.py:1242
  18.9 1.6 %collective-permute-start.6 = (bf16[1152,128]{1,0:T(8,128)(2,1)S(1)}, bf16[1152,128]{1,0:T(8,128)(2,1)S(1)}, u32[]{:S(2)}, u32[]{:S(2)}) collective-permute-start(bf16[1152,128]{1,0:T(8,128)(2,1)S(1)} %constant_dynamic-update-slice_fusion.refs_5_), channel_id=1, source_target_pairs={{0,1},{1,0},{2,3},{3,2},{4,5},{5,4},{6,7},{7,6},{8,9},{9,8},{10,11... | collective-permute-start | bytes 884744 | tf_op jit(solution)/shard_map/ppermute | solution.py:1242
  30.0 2.1 %collective-permute-start.8 = (bf16[4,16,4096]{2,1,0:T(8,128)(2,1)S(1)}, bf16[4,16,4096]{2,1,0:T(8,128)(2,1)S(1)}, u32[]{:S(2)}, u32[]{:S(2)}) collective-permute-start(bf16[4,16,4096]{2,1,0:T(8,128)(2,1)S(1)} %near.3), channel_id=1, source_target_pairs={{0,1},{1,0},{2,3},{3,2},{4,5},{5,4},{6,7},{7,6},{8,9},{9,8},{10,11... | collective-permute-start | bytes 1572872 | tf_op jit(solution)/shard_map/ppermute | solution.py:1242
  30.2 19.9 %collective-permute-start.9 = (bf16[2,16,4096]{2,1,0:T(8,128)(2,1)S(1)}, bf16[2,16,4096]{2,1,0:T(8,128)(2,1)S(1)}, u32[]{:S(2)}, u32[]{:S(2)}) collective-permute-start(bf16[2,16,4096]{2,1,0:T(8,128)(2,1)S(1)} %get-tuple-element.132), channel_id=1, source_target_pairs={{0,1},{1,0},{2,3},{3,2},{4,5},{5,4},{6,7},{7,6},{8,9},{9,8},{10,11... | collective-permute-start | bytes 786440 | tf_op jit(solution)/shard_map/ppermute | solution.py:1242
  30.6 19.5 %collective-permute-start.10 = (bf16[2,16,4096]{2,1,0:T(8,128)(2,1)S(1)}, bf16[2,16,4096]{2,1,0:T(8,128)(2,1)S(1)}, u32[]{:S(2)}, u32[]{:S(2)}) collective-permute-start(bf16[2,16,4096]{2,1,0:T(8,128)(2,1)S(1)} %get-tuple-element.133), channel_id=1, source_target_pairs={{0,2},{1,3},{2,0},{3,1},{4,6},{5,7},{6,4},{7,5},{8,10},{9,11},{10,... | collective-permute-start | bytes 786440 | tf_op jit(solution)/shard_map/ppermute | solution.py:1242
  31.8 18.3 %collective-permute-start.11 = (bf16[2,16,4096]{2,1,0:T(8,128)(2,1)S(1)}, bf16[2,16,4096]{2,1,0:T(8,128)(2,1)S(1)}, u32[]{:S(2)}, u32[]{:S(2)}) collective-permute-start(bf16[2,16,4096]{2,1,0:T(8,128)(2,1)S(1)} %get-tuple-element.134), channel_id=1, source_target_pairs={{0,3},{1,2},{2,1},{3,0},{4,7},{5,6},{6,5},{7,4},{8,11},{9,10},{10,... | collective-permute-start | bytes 786440 | tf_op jit(solution)/shard_map/ppermute | solution.py:1242
  41.2 14.5 %collective-permute-start.17 = (bf16[2,16,4096]{2,1,0:T(8,128)(2,1)S(1)}, bf16[2,16,4096]{2,1,0:T(8,128)(2,1)S(1)}, u32[]{:S(2)}, u32[]{:S(2)}) collective-permute-start(bf16[2,16,4096]{2,1,0:T(8,128)(2,1)S(1)} %get-tuple-element.147), channel_id=1, source_target_pairs={{0,1},{1,0},{2,3},{3,2},{4,5},{5,4},{6,7},{7,6},{8,9},{9,8},{10,11... | collective-permute-start | bytes 786440 | tf_op jit(solution)/shard_map/ppermute | solution.py:1242
  41.9 16.3 %collective-permute-start.18 = (bf16[2,16,4096]{2,1,0:T(8,128)(2,1)S(1)}, bf16[2,16,4096]{2,1,0:T(8,128)(2,1)S(1)}, u32[]{:S(2)}, u32[]{:S(2)}) collective-permute-start(bf16[2,16,4096]{2,1,0:T(8,128)(2,1)S(1)} %get-tuple-element.148), channel_id=1, source_target_pairs={{0,2},{1,3},{2,0},{3,1},{4,6},{5,7},{6,4},{7,5},{8,10},{9,11},{10,... | collective-permute-start | bytes 786440 | tf_op jit(solution)/shard_map/ppermute | solution.py:1242
  43.2 21.6 %copy-start.1 = (bf16[32,128]{1,0:T(8,128)(2,1)S(1)}, bf16[32,128]{1,0:T(8,128)(2,1)}, u32[]{:S(2)}) copy-start(bf16[32,128]{1,0:T(8,128)(2,1)} %refs_9_.3) | copy-start | bytes 24580
  43.2 21.6 %copy-start.2 = (bf16[32,128]{1,0:T(8,128)(2,1)S(1)}, bf16[32,128]{1,0:T(8,128)(2,1)}, u32[]{:S(2)}) copy-start(bf16[32,128]{1,0:T(8,128)(2,1)} %refs_10_.3) | copy-start | bytes 24580
  43.2 21.6 %copy-start.3 = (bf16[32,32]{1,0:T(8,128)(2,1)S(1)}, bf16[32,32]{1,0:T(8,128)(2,1)}, u32[]{:S(2)}) copy-start(bf16[32,32]{1,0:T(8,128)(2,1)} %refs_8_.3) | copy-start | bytes 6148
  43.2 21.6 %copy-start.4 = (bf16[18,32]{1,0:T(8,128)(2,1)S(1)}, bf16[18,32]{1,0:T(8,128)(2,1)}, u32[]{:S(2)}) copy-start(bf16[18,32]{1,0:T(8,128)(2,1)} %refs_7_.3) | copy-start | bytes 3460
  50.2 1.5 %collective-permute-start.12 = (bf16[864,128]{1,0:T(8,128)(2,1)S(1)}, bf16[864,128]{1,0:T(8,128)(2,1)S(1)}, u32[]{:S(2)}, u32[]{:S(2)}) collective-permute-start(bf16[864,128]{1,0:T(8,128)(2,1)S(1)} %get-tuple-element.141), channel_id=1, source_target_pairs={{0,1},{1,0},{2,3},{3,2},{4,5},{5,4},{6,7},{7,6},{8,9},{9,8},{10,11... | collective-permute-start | bytes 663560 | tf_op jit(solution)/shard_map/ppermute | solution.py:1242
  50.2 8.2 %collective-permute-start.19 = (bf16[2,16,4096]{2,1,0:T(8,128)(2,1)S(1)}, bf16[2,16,4096]{2,1,0:T(8,128)(2,1)S(1)}, u32[]{:S(2)}, u32[]{:S(2)}) collective-permute-start(bf16[2,16,4096]{2,1,0:T(8,128)(2,1)S(1)} %get-tuple-element.149), channel_id=1, source_target_pairs={{0,3},{1,2},{2,1},{3,0},{4,7},{5,6},{6,5},{7,4},{8,11},{9,10},{10,... | collective-permute-start | bytes 786440 | tf_op jit(solution)/shard_map/ppermute | solution.py:1242
  52.3 6.1 %collective-permute-start.13 = (bf16[216,128]{1,0:T(8,128)(2,1)S(1)}, bf16[216,128]{1,0:T(8,128)(2,1)S(1)}, u32[]{:S(2)}, u32[]{:S(2)}) collective-permute-start(bf16[216,128]{1,0:T(8,128)(2,1)S(1)} %get-tuple-element.142), channel_id=1, source_target_pairs={{1,5},{3,7},{5,1},{7,3},{9,13},{11,15},{13,9},{15,11},{17,21},{19,... | collective-permute-start | bytes 165896 | tf_op jit(solution)/shard_map/ppermute | solution.py:1253
  53.0 5.4 %collective-permute-start.14 = (bf16[216,128]{1,0:T(8,128)(2,1)S(1)}, bf16[216,128]{1,0:T(8,128)(2,1)S(1)}, u32[]{:S(2)}, u32[]{:S(2)}) collective-permute-start(bf16[216,128]{1,0:T(8,128)(2,1)S(1)} %get-tuple-element.143), channel_id=1, source_target_pairs={{0,12},{1,9},{2,14},{3,11},{4,8},{5,13},{6,10},{7,15},{8,4},{9,1},... | collective-permute-start | bytes 165896 | tf_op jit(solution)/shard_map/ppermute | solution.py:1253
  55.7 7.2 %collective-permute-start.15 = (bf16[216,128]{1,0:T(8,128)(2,1)S(1)}, bf16[216,128]{1,0:T(8,128)(2,1)S(1)}, u32[]{:S(2)}, u32[]{:S(2)}) collective-permute-start(bf16[216,128]{1,0:T(8,128)(2,1)S(1)} %get-tuple-element.144), channel_id=1, source_target_pairs={{0,20},{1,17},{2,22},{3,19},{4,16},{5,21},{6,18},{7,23},{8,28},{9,... | collective-permute-start | bytes 165896 | tf_op jit(solution)/shard_map/ppermute | solution.py:1253
  58.3 6.5 %collective-permute-start.16 = (bf16[216,128]{1,0:T(8,128)(2,1)S(1)}, bf16[216,128]{1,0:T(8,128)(2,1)S(1)}, u32[]{:S(2)}, u32[]{:S(2)}) collective-permute-start(bf16[216,128]{1,0:T(8,128)(2,1)S(1)} %get-tuple-element.145), channel_id=1, source_target_pairs={{0,24},{1,29},{2,26},{3,31},{4,28},{5,25},{6,30},{7,27},{8,16},{9,... | collective-permute-start | bytes 165896 | tf_op jit(solution)/shard_map/ppermute | solution.py:1253
  66.1 1.8 %collective-permute-start.20 = (f32[280,128]{1,0:T(8,128)S(1)}, f32[280,128]{1,0:T(8,128)S(1)}, u32[]{:S(2)}, u32[]{:S(2)}) collective-permute-start(f32[280,128]{1,0:T(8,128)S(1)} %reduce.1), channel_id=1, source_target_pairs={{0,1},{1,0},{2,3},{3,2},{4,5},{5,4},{6,7},{7,6},{8,9},{9,8},{10,11... | collective-permute-start | bytes 430088 | tf_op jit(solution)/shard_map/ppermute | solution.py:1242
  67.9 4.6 %collective-permute-start.21 = (bf16[280,128]{1,0:T(8,128)(2,1)S(1)}, bf16[280,128]{1,0:T(8,128)(2,1)S(1)}, u32[]{:S(2)}, u32[]{:S(2)}) collective-permute-start(bf16[280,128]{1,0:T(8,128)(2,1)S(1)} %add_convert_fusion.refs_0_), channel_id=1, source_target_pairs={{0,2},{1,3},{2,0},{3,1},{4,6},{5,7},{6,4},{7,5},{8,10},{9,11},{10,... | collective-permute-start | bytes 215048 | tf_op jit(solution)/shard_map/ppermute | solution.py:1242

commit v6 on v5

--- a/solution.py
+++ b/solution.py
@@ -168,11 +168,34 @@
 
 
 def forward_kernel(count, *refs):
-    member_ref, frame_images, frame_stats, styles, biases, w_one, w_two, w_down, w_up = refs[:9]
-    out = refs[9 : 9 + count]
-    outs = refs[9 + count : 16 + count]
-    images, levels = refs[16 + count :]
+    member_ref, frame_images, frame_stats, styles, biases, work_pair, work_up, work_down = refs[:8]
+    out = refs[8 : 8 + count]
+    outs = refs[8 + count : 15 + count]
+    turned_operands = refs[15 + count : 19 + count]
+    images, levels, w_one, w_two, w_down, w_up = refs[19 + count :]
     member = member_ref[0]
+    works = {"one": work_pair, "two": work_pair, "down": work_down, "up": work_up}
+    found = {}
+
+    def block(name, row):
+        k = works[name][row : row + C, :]
+        low = lane_ids(k.shape) < C
+        if name == "two":
+            return jnp.where(low, swap_halves(k), k)
+        return jnp.where(low, k, swap_halves(k))
+
+    def turned_pairs(name):
+        work = works[name]
+        key = "one" if name == "two" else name
+        if key not in found:
+            blocks = [work[at : min(at + LANES, work.shape[0]), :] for at in range(0, work.shape[0], LANES)]
+            found[key] = [below(block, LANES).T for block in blocks]
+        return [k[C:] if name == "two" else k[:C] for k in found[key]]
+
+    def operands():
+        yield from write_forward_operands(block, w_one, w_two, w_down, w_up)
+        yield from write_backward_operands(turned_pairs, *turned_operands)
+
     low_lanes = lane_ids((HALF, LANES)) < C
 
     def frame(f):
@@ -249,7 +272,7 @@
         yield
         store_strips(member, image, f, out)
 
-    staggered(frame(f) for f in range(styles.shape[0]))
+    staggered([operands()] + [frame(f) for f in range(styles.shape[0])])
 
 
 def slope_twice(h):
@@ -306,7 +329,6 @@
         zero = jnp.zeros((HALF, LANES), f32)
         _, sums = over_pairs(coarse_body, (zero, zero))
         bias_down_sum = jnp.broadcast_to(total(sums), (8, LANES))
-        yield
         operand = jnp.concatenate(
             [coarse_pairs[...].reshape(BLOCK, LANES), coarse_below[...].reshape(BLOCK, LANES)], axis=1
         )
@@ -317,7 +339,6 @@
             sums = sums + total(v)
             level_grad[a] = tiles_of(v)
         bias_two_sum = both_parities(sums)
-        yield
 
         def level_tile(parity, j):
             x = level_grad[parity, j]
@@ -449,7 +470,7 @@
 
 
 PARTS = 16
-FAR_HINTS = 0, 90
+FAR_HINT = 90
 PAIR_PARTS = 24
 
 
@@ -468,10 +489,13 @@
 
 def message_kernel(count, rows, *refs):
     where_ref, wins, tiles = refs[0], refs[1:5], refs[5:9]
-    pieces, bias_sums, kept, small, theirs = refs[9:14]
-    sums = refs[14:18]
-    g_pair, g_up, g_down = refs[18:]
+    pieces, bias_sums, ids, kept, small, theirs, hots = refs[9:16]
+    sums = refs[16:20]
+    g_pair, g_up, g_down = refs[20:]
     sum_one, sum_two, sum_down, sum_up = sums
+    taken = 2 * pieces.shape[0]
+    for at in range(ids.shape[0]):
+        write_hots(hots, at * taken, where_ref[1] // 2 * taken, taken, ids[at])
     accumulate(wins, tiles, sums)
     low_lanes = lane_ids((C, LANES)) < C
     for p in range(3):
@@ -533,7 +557,7 @@
         block = kept[k * size : (k + 1) * size, :] + theirs[k * size : (k + 1) * size, :].astype(f32)
         message[:at, :] = block[:at].astype(bf16)
         message[at:, :] = jnp.where(low_lanes, block[at:], sent).astype(bf16)
-        if k == 0:
+        if k == half - 1:
             own[:at, :] = block[:at]
             own[at:, :] = jnp.where(low_lanes, block[at:], below(exact, rows))
 
@@ -551,7 +575,7 @@
     at = 2 * rows
     for k, ref in enumerate(messages):
         message = ref[...].astype(f32)
-        if k == 0:
+        if k == half - 1:
             message = jnp.where(member % 2 == 0, own[...], message)
         sums = message if sums is None else sums + message
         small = (
@@ -584,17 +608,22 @@
     bias = pltpu.roll(jnp.concatenate([bias, bias], axis=0), (LANES - place * width) % LANES, axis=1)
     extra = below(jnp.concatenate([exact(hot, embed_grad, ((0,), (0,))), bias], axis=0), rows)
     at = 2 * rows
-    out[:at, :] = sums[:at]
-    out[at : at + rows, :] = jnp.where(lane_ids((rows, LANES)) < C, sums[at:], extra)
-    at = at + rows
-    out[at : at + cells, :] = exact(embed, one, ((0,), (0,)))
-    out[at + cells : at + 2 * cells, :] = exact(embed, two, ((0,), (0,)))
-
-
-def finish_kernel(rows, cells, first, second, *outs):
+    blocks = (
+        sums[:at],
+        jnp.where(lane_ids((rows, LANES)) < C, sums[at:], extra),
+        exact(embed, one, ((0,), (0,))),
+        exact(embed, two, ((0,), (0,))),
+    )
+    out[...] = jnp.concatenate(blocks, axis=0).astype(out.dtype)
+
+
+def finish_kernel(rows, cells, count, *refs):
+    parts, outs = [ref[...].astype(f32) for ref in refs[:count]], refs[count:]
     act_grad, noise_grad, ada_one, ada_two, g_one, g_two, g_down, g_up = outs[:8]
     bias_grads = outs[8:12]
-    sums = first[...].astype(f32) + second[...].astype(f32)
+    while len(parts) > 1:
+        parts = [parts[k] + parts[k + 1] for k in range(0, len(parts), 2)]
+    sums = parts[0]
 
     def turn(block):
         return jnp.concatenate([block, jnp.zeros((LANES - rows, LANES), f32)], axis=0).T[:, :rows]
@@ -615,27 +644,17 @@
         ref[...] = extra[BIAS_ROW + k : BIAS_ROW + k + 1, : ref.shape[0]].reshape(ref.shape)
 
 
-def write_operands(block, turned_pairs, f_one, f_two, f_down, f_up, b_one, b_two, b_down, b_up):
+def write_forward_operands(block, f_one, f_two, f_down, f_up):
     low_lanes = lane_ids((C, LANES)) < C
     zero = jnp.zeros((C, LANES), f32)
 
-    pairs = {name: turned_pairs(name) for name in ("one", "two", "down", "up")}
-
     def taps(name, base, step):
-        plain, turned = {}, {}
-        for p in range(3):
-            for q in range(3):
-                at = (3 * p + q) * step + base
-                plain[p, q] = block(name, at)
-                pair = pairs[name][at // LANES]
-                other = swap_halves(pair)
-                turned[p, q] = jnp.where(low_lanes, pair, other) if at % LANES == 0 else jnp.where(low_lanes, other, pair)
-        return plain, turned
-
-    def write_forward(ref, base, plain):
+        return {(p, q): block(name, (3 * p + q) * step + base) for p in range(3) for q in range(3)}
+
+    def write(ref, base, found):
         for w in range(4):
             for p in range(3):
-                tile = jnp.where(low_lanes, plain.get((p, w), zero), plain.get((p, w - 1), zero)).astype(bf16)
+                tile = jnp.where(low_lanes, found.get((p, w), zero), found.get((p, w - 1), zero)).astype(bf16)
                 for a in range(2):
                     at = base + ((a + p) * 4 + w) * C
                     ref[at : at + C, a * LANES : (a + 1) * LANES] = tile
@@ -645,10 +664,40 @@
                         at = base + (r * 4 + w) * C
                         ref[at : at + C, a * LANES : (a + 1) * LANES] = zero.astype(bf16)
 
-    def write_backward(ref, lane, turned):
+    write(f_one, 0, taps("one", 0, C))
+    yield
+    write(f_two, 0, taps("two", 0, C))
+    yield
+    found = taps("down", 0, C)
+    for p in range(3):
+        for w in range(4):
+            at = (p * 4 + w) * C
+            f_down[at : at + C, :] = found.get((p, w), zero).astype(bf16)
+    yield
+    write(f_up, 0, taps("up", C, 2 * C))
+    yield
+    write(f_up, 16 * C, taps("up", 0, 2 * C))
+    yield
+
+
+def write_backward_operands(turned_pairs, b_one, b_two, b_down, b_up):
+    low_lanes = lane_ids((C, LANES)) < C
+    zero = jnp.zeros((C, LANES), f32)
+    def taps(pairs, base, step):
+        found = {}
+        for p in range(3):
+            for q in range(3):
+                at = (3 * p + q) * step + base
+                pair = pairs[at // LANES]
+                other = swap_halves(pair)
+                low, high = (pair, other) if at % LANES == 0 else (other, pair)
+                found[p, q] = jnp.where(low_lanes, low, high)
+        return found
+
+    def write(ref, lane, found):
         for w in range(4):
             for p in range(3):
-                tile = jnp.where(low_lanes, turned.get((p, 2 - w), zero), turned.get((p, 3 - w), zero)).astype(bf16)
+                tile = jnp.where(low_lanes, found.get((p, 2 - w), zero), found.get((p, 3 - w), zero)).astype(bf16)
                 for a in range(2):
                     at = ((a + 2 - p) * 4 + w) * C
                     ref[at : at + C, lane + a * LANES : lane + (a + 1) * LANES] = tile
@@ -658,51 +707,27 @@
                         at = (r * 4 + w) * C
                         ref[at : at + C, lane + a * LANES : lane + (a + 1) * LANES] = zero.astype(bf16)
 
-    for name, forward_ref, backward_ref in (("one", f_one, b_one), ("two", f_two, b_two)):
-        plain, turned = taps(name, 0, C)
-        write_forward(forward_ref, 0, plain)
-        write_backward(backward_ref, 0, turned)
-    plain, turned = taps("up", 0, 2 * C)
-    write_forward(f_up, 16 * C, plain)
-    write_backward(b_up, 0, turned)
-    plain, turned = taps("up", C, 2 * C)
-    write_forward(f_up, 0, plain)
-    write_backward(b_up, 2 * LANES, turned)
-    plain, turned = taps("down", 0, C)
-    for p in range(3):
-        for w in range(4):
-            at = (p * 4 + w) * C
-            f_down[at : at + C, :] = plain.get((p, w), zero).astype(bf16)
-    for below in range(2):
+    one, two = turned_pairs("one"), turned_pairs("two")
+    write(b_one, 0, taps(one, 0, C))
+    yield
+    write(b_two, 0, taps(two, 0, C))
+    yield
+    pairs = turned_pairs("up")
+    write(b_up, 0, taps(pairs, 0, 2 * C))
+    yield
+    write(b_up, 2 * LANES, taps(pairs, C, 2 * C))
+    yield
+    found = taps(turned_pairs("down"), 0, C)
+    for under in range(2):
         for right in range(2):
-            at = (below * 2 + right) * C
+            at = (under * 2 + right) * C
             for a in range(2):
-                p = {(0, 0): 1, (0, 1): 2, (1, 1): 0}.get((below, a))
+                p = {(0, 0): 1, (0, 1): 2, (1, 1): 0}.get((under, a))
                 first, second = zero, zero
                 if p is not None:
-                    first = turned[p, 1] if right == 0 else zero
-                    second = turned[p, 2] if right == 0 else turned[p, 0]
+                    first = found[p, 1] if right == 0 else zero
+                    second = found[p, 2] if right == 0 else found[p, 0]
                 b_down[at : at + C, a * LANES : (a + 1) * LANES] = jnp.where(low_lanes, first, second).astype(bf16)
-
-
-def expand_kernel(conv_one, conv_two, down_kernel, up_kernel, *outs):
-    kernels = {"one": conv_one, "two": conv_two, "down": down_kernel, "up": up_kernel}
-
-    def block(name, row):
-        k = kernels[name][row : row + C, :].astype(f32)
-        return jnp.concatenate([k, k], axis=1)
-
-    def turned_pairs(name):
-        found = []
-        for at in range(0, kernels[name].shape[0], LANES):
-            k = kernels[name][at : at + LANES, :].astype(f32)
-            k = jnp.concatenate([k, jnp.zeros(k.shape, f32)], axis=1)
-            if k.shape[0] < LANES:
-                k = jnp.concatenate([k, jnp.zeros((LANES - k.shape[0], LANES), f32)], axis=0)
-            found.append(k.T[:C])
-        return found
-
-    write_operands(block, turned_pairs, *outs)
 
 
 ACT_ROW, NOISE_ROW, TABLE_ROWS = 0, 24, 56
@@ -738,7 +763,11 @@
     out[...] = far[pl.ds((member_ref[0] ^ 1) % 2 * share, share)]
 
 
-def near_kernel(other, shared, out):
+def mark_kernel(far, out):
+    out[...] = far[0, :8, :LANES].astype(f32)
+
+
+def near_kernel(other, shared, mark, out):
     share = out.shape[0] // 2
     out[:share] = other[...]
     out[share:] = shared[...]
@@ -788,7 +817,7 @@
 
 def sides(count):
     ones = lambda offset: bin(offset).count("1") % 2
-    return tuple([offset for offset in range(count) if ones(offset) == side] for side in (0, 1))
+    return tuple([offset for offset in reversed(range(count)) if ones(offset) == side] for side in (0, 1))
 
 
 def write_hots(hots, at, first, frames, ids):
@@ -804,9 +833,7 @@
 
 def prepare_kernel(count, rows, cells, *refs):
     where_ref, actions, noise_ids, valid, packed, mine, other = refs[:7]
-    outs = refs[7:15]
-    styles, biases, hots = refs[15:18]
-    work_pair, work_up, work_down, work_one, work_two, work_table = refs[18:]
+    styles, biases, ids, work_pair, work_up, work_down, work_one, work_two, work_table = refs[7:]
     place, member, frames = where_ref[0], where_ref[1], styles.shape[0]
     style_at, _, size = pack_sizes(rows, cells)
     bias_rows = jnp.zeros(SMALL, f32)
@@ -815,7 +842,7 @@
         ref = mine if offset < half else other
         at = offset % half
         pack = ref[at * size : (at + 1) * size, :].astype(f32)
-        if at == 0:
+        if at == half - 1:
             pack = jnp.where(member % 2 == offset // half, packed[...].astype(f32), pack)
         owner = seq_owner(place, member, half, at, offset < half)
         start = pl.multiple_of(owner * rows, 8)
@@ -841,7 +868,7 @@
         slots = jnp.where((lane_ids(SMALL) >= C) & (lane_ids(SMALL) < C + width), slots, 0.0)
         bias_rows = bias_rows + pltpu.roll(slots, (owner * width + C) % LANES, axis=1)
         if offset < half:
-            write_hots(hots, at * 2 * frames, member // 2 * 2 * frames, 2 * frames, extra[ID_ROW : ID_ROW + 8])
+            ids[at] = extra[ID_ROW : ID_ROW + 8]
     biases[...] = bias_rows + swap_halves(bias_rows)
 
     lanes = lane_ids((8, LANES))
@@ -865,31 +892,6 @@
     for f in range(frames):
         styles[f, 4:8, :] = jnp.zeros((4, LANES), f32)
 
-    def block(name, row):
-        work = {"one": work_pair, "two": work_pair, "down": work_down, "up": work_up}[name]
-        k = work[row : row + C, :]
-        low = lane_ids(k.shape) < C
-        if name == "two":
-            return jnp.where(low, swap_halves(k), k)
-        return jnp.where(low, k, swap_halves(k))
-
-    both = {}
-
-    def turned_pairs(name):
-        work = {"one": work_pair, "two": work_pair, "down": work_down, "up": work_up}[name]
-        if name not in both:
-            found = []
-            for at in range(0, work.shape[0], LANES):
-                k = work[at : min(at + LANES, work.shape[0]), :]
-                if k.shape[0] < LANES:
-                    k = below(k, LANES)
-                found.append(k.T)
-            both["one" if name == "two" else name] = [k[:C] for k in found]
-            both["two" if name == "one" else name] = [k[C:] for k in found] if name in ("one", "two") else both[name]
-        return both[name]
-
-    write_operands(block, turned_pairs, *outs)
-
 
 def shape(dims, kind):
     return jax.ShapeDtypeStruct(dims, kind)
@@ -932,34 +934,13 @@
     return pl.CostEstimate(flops=2 * macs, bytes_accessed=moved, transcendentals=0)
 
 
-def expand(conv_one, conv_two, down_kernel, up_kernel):
-    vmem = pl.BlockSpec(memory_space=pltpu.VMEM)
-    return pl.pallas_call(
-        expand_kernel,
-        in_specs=[vmem] * 4,
-        out_specs=[vmem] * 8,
-        out_shape=[
-            shape((KEYS, 2 * LANES), bf16),
-            shape((KEYS, 2 * LANES), bf16),
-            shape((6 * LANES, LANES), bf16),
-            shape((2 * KEYS, 2 * LANES), bf16),
-            shape((KEYS, 2 * LANES), bf16),
-            shape((KEYS, 2 * LANES), bf16),
-            shape((2 * LANES, 2 * LANES), bf16),
-            shape((KEYS, 4 * LANES), bf16),
-        ],
-        compiler_params=params(),
-        name="expand",
-    )(conv_one, conv_two, down_kernel, up_kernel)
-
-
 def fetch_far(member, array):
     far, own, other = cut_far(member, array, lax.axis_size("rows"))
     return trade(far, 2), own, other
 
 
-def gather_frames(member, far, own, other, hints=(0, 0)):
-    near = trade(cut_near(member, other, far, hints), 1)
+def gather_frames(member, far, own, other, hint=0):
+    near = trade(cut_near(member, other, far, hint), 1)
     frames = own.shape[0]
     return pl.pallas_call(
         gather_kernel,
@@ -971,13 +952,13 @@
     )(member, own, far, near)
 
 
-def forward(member, frame_images, frame_stats, styles, biases, w_one, w_two, w_down, w_up, count):
+def forward(member, frame_images, frame_stats, styles, biases, works, count):
     frames = frame_images.shape[0]
     strip = H // count
     return pl.pallas_call(
         lambda *refs: forward_kernel(count, *refs),
-        in_specs=[in_smem()] + [in_vmem()] * 8,
-        out_specs=[in_vmem()] * (count + 7),
+        in_specs=[in_smem()] + [in_vmem()] * 7,
+        out_specs=[in_vmem()] * (count + 11),
         out_shape=[shape((frames, strip, W * C), bf16)] * count
         + [
             shape((frames,) + WINDOWS, bf16),
@@ -987,12 +968,14 @@
             shape((frames,) + TILES, f32),
             shape((frames,) + COARSE, f32),
             shape((frames,) + SMALL, f32),
-        ],
-        scratch_shapes=[pltpu.VMEM((frames,) + IMAGE, f32), pltpu.VMEM((frames,) + TILES, f32)],
+        ]
+        + [shape(dims, bf16) for dims in OPERANDS[4:]],
+        scratch_shapes=[pltpu.VMEM((frames,) + IMAGE, f32), pltpu.VMEM((frames,) + TILES, f32)]
+        + [pltpu.VMEM(dims, bf16) for dims in OPERANDS[:4]],
         compiler_params=params(),
         cost_estimate=cost(1 << 10, 1 << 10),
         name="forward",
-    )(member, frame_images, frame_stats, styles, biases, w_one, w_two, w_down, w_up)
+    )(member, frame_images, frame_stats, styles, biases, *works)
 
 
 def backward(member, cot, frame_images, styles, stats, middle, down, w_up, w_down, w_two, w_one, count):
@@ -1056,33 +1039,39 @@
         far_kernel,
         in_specs=[in_smem(), in_place(pltpu.HBM)],
         out_specs=[in_vmem()] * 3,
-        out_shape=[shape(half, array.dtype), shape(share, array.dtype), shape(share, array.dtype)],
+        out_shape=[pltpu.VMEM(dims, array.dtype) for dims in (half, share, share)],
         scratch_shapes=[pltpu.SemaphoreType.DMA((3,))],
         compiler_params=params(),
         name="far",
     )(member, array)
 
 
-def cut_near(member, other, far, hints):
-    other = pltpu.with_memory_space_constraint(other, pltpu.VMEM)
+def cut_near(member, other, far, hint):
     shared = pl.pallas_call(
         share_kernel,
         in_specs=[in_smem(), in_vmem()],
         out_specs=in_vmem(),
         out_shape=shape(other.shape, other.dtype),
         compiler_params=params(),
-        cost_estimate=cost(BLOCK * KEYS * 2 * LANES * hints[0], 1 << 20),
         name="shared",
     )(member, far)
+    mark = pl.pallas_call(
+        mark_kernel,
+        in_specs=[in_vmem()],
+        out_specs=in_vmem(),
+        out_shape=shape(SMALL, f32),
+        compiler_params=params(),
+        cost_estimate=cost(BLOCK * KEYS * 2 * LANES * hint, 1 << 20),
+        name="mark",
+    )(far)
     return pl.pallas_call(
         near_kernel,
-        in_specs=[in_vmem()] * 2,
+        in_specs=[in_vmem()] * 3,
         out_specs=in_vmem(),
         out_shape=shape(far.shape, other.dtype),
         compiler_params=params(),
-        cost_estimate=cost(BLOCK * KEYS * 2 * LANES * hints[1], 1 << 20),
         name="near",
-    )(other, shared)
+    )(other, shared, mark)
 
 
 def pack(ids, kernels, ada_one, ada_two, act_table, noise_table, biases):
@@ -1113,16 +1102,13 @@
 
 
 def prepare(where, ids, packed, mine, other, count, rows, cells, frames):
-    return pl.pallas_call(
+    found = pl.pallas_call(
         lambda *refs: prepare_kernel(count, rows, cells, *refs),
         in_specs=[in_smem()] * 4 + [in_vmem()] * 3,
-        out_specs=[in_vmem()] * 11,
-        out_shape=[shape(d, bf16) for d in OPERANDS]
-        + [shape((frames,) + SMALL, f32), shape(SMALL, f32), shape((count * frames, LANES), f32)],
+        out_specs=[in_vmem()] * 6,
+        out_shape=[shape((frames,) + SMALL, f32), shape(SMALL, f32), shape((count // 2,) + SMALL, f32)]
+        + [shape((n * C, LANES), f32) for n in (9, 18, 9)],
         scratch_shapes=[
-            pltpu.VMEM((9 * C, LANES), f32),
-            pltpu.VMEM((18 * C, LANES), f32),
-            pltpu.VMEM((9 * C, LANES), f32),
             pltpu.VMEM((count * cells, LANES), f32),
             pltpu.VMEM((count * cells, LANES), f32),
             pltpu.VMEM((count * cells // LANES, TABLE_ROWS, LANES), f32),
@@ -1130,22 +1116,28 @@
         compiler_params=params(),
         name="prepare",
     )(where, *ids, packed, mine, other)
-
-
-def weight_messages(where, wins, tiles, pieces, bias_sums, count, rows):
+    return found[0], found[1], found[2], found[3:]
+
+
+def weight_messages(where, wins, tiles, pieces, bias_sums, ids, count, rows):
     frames = pieces.shape[0]
     size = count // 2 * 3 * rows
     return pl.pallas_call(
         lambda *refs: message_kernel(count, rows, *refs),
-        in_specs=[in_smem()] + [in_vmem()] * 10,
-        out_specs=[in_vmem()] * 3,
-        out_shape=[shape((size, LANES), f32), shape((PARTS, LANES), f32), shape((size, LANES), bf16)],
+        in_specs=[in_smem()] + [in_vmem()] * 11,
+        out_specs=[in_vmem()] * 4,
+        out_shape=[
+            shape((size, LANES), f32),
+            shape((PARTS, LANES), f32),
+            shape((size, LANES), bf16),
+            shape((count * frames, LANES), f32),
+        ],
         scratch_shapes=sum_scratch()
         + [pltpu.VMEM((9 * C, LANES), f32), pltpu.VMEM((18 * C, LANES), f32), pltpu.VMEM((9 * C, LANES), f32)],
         compiler_params=params(),
         cost_estimate=cost(frames * BLOCK * KEYS * 2 * LANES * 5, frames * (6 << 20)),
         name="weights",
-    )(where, *wins, *tiles, pieces, bias_sums)
+    )(where, *wins, *tiles, pieces, bias_sums, ids)
 
 
 def join_messages(where, kept, small, theirs, half, rows, frames):
@@ -1165,7 +1157,7 @@
         lambda *refs: reduce_kernel(half, rows, cells, frames, *refs),
         in_specs=[in_smem()] + [in_vmem()] * (half + 6),
         out_specs=in_vmem(),
-        out_shape=shape((3 * rows + 2 * cells, LANES), f32),
+        out_shape=shape((3 * rows + 2 * cells, LANES), bf16),
         scratch_shapes=[
             pltpu.VMEM((half * frames, LANES), f32),
             pltpu.VMEM((half * frames, LANES), f32),
@@ -1178,10 +1170,10 @@
     )(where, own, *messages, hots, act_table, noise_table, ada_one, ada_two)
 
 
-def finish(first, second, rows, cells, width):
+def finish(parts, rows, cells, width):
     act_grad, noise_grad, one, two, *rest = pl.pallas_call(
-        lambda *refs: finish_kernel(rows, cells, *refs),
-        in_specs=[in_vmem()] * 2,
+        lambda *refs: finish_kernel(rows, cells, len(parts), *refs),
+        in_specs=[in_vmem()] * len(parts),
         out_specs=[in_vmem()] * 12,
         out_shape=[
             shape((NACT, cells), f32),
@@ -1196,7 +1188,7 @@
         + [shape((width,), f32)] * 4,
         compiler_params=params(),
         name="finish",
-    )(first, second)
+    )(*parts)
     return (act_grad, noise_grad, one, two, *[grad.T for grad in rest[:4]], *rest[4:])
 
 
@@ -1253,11 +1245,10 @@
     return lax.ppermute(value, ("seq", "rows"), pairs)
 
 
-def layers(member_box, frame_images, frame_stats, cot_fetched, styles, bias_rows, operands):
-    f_one, f_two, f_down, f_up, b_one, b_two, b_down, b_up = operands
+def layers(member_box, frame_images, frame_stats, cot_fetched, styles, bias_rows, works):
     count = lax.axis_size("rows")
-    *out, win_one, win_two, win_level, win_coarse, middle, down, stats = forward(
-        member_box, frame_images, frame_stats, styles, bias_rows, f_one, f_two, f_down, f_up, count
+    *out, win_one, win_two, win_level, win_coarse, middle, down, stats, b_one, b_two, b_down, b_up = forward(
+        member_box, frame_images, frame_stats, styles, bias_rows, works, count
     )
     out = trade_strips(out)
     down, cot_fetched = lax.optimization_barrier((down, cot_fetched))
@@ -1306,27 +1297,23 @@
     mine = jnp.concatenate([half_trade(packed, at) for at in range(half)], axis=0)
     other = trade(mine, 1)
     cot_fetched = fetch_far(member_box, cotangent)
-    frame_images, frame_stats = gather_frames(member_box, *fetched, FAR_HINTS)
-    *operands, styles, bias_rows, hots = prepare(where, ids, packed, mine, other, count, rows, cells, share)
+    frame_images, frame_stats = gather_frames(member_box, *fetched, FAR_HINT)
+    styles, bias_rows, group_ids, works = prepare(where, ids, packed, mine, other, count, rows, cells, share)
     out, grad_strips, wins, tiles, pieces, bias_sums = layers(
-        member_box, frame_images, frame_stats, cot_fetched, styles, bias_rows, operands
+        member_box, frame_images, frame_stats, cot_fetched, styles, bias_rows, works
     )
-    kept, small, theirs = weight_messages(where, wins, tiles, pieces, bias_sums, count, rows)
+    kept, small, theirs, hots = weight_messages(where, wins, tiles, pieces, bias_sums, group_ids, count, rows)
     theirs, out = lax.optimization_barrier((theirs, out))
     own, *messages = join_messages(where, kept, small, trade(theirs, 1), half, rows, share)
     received = [half_trade(message, at) for at, message in enumerate(messages)]
-    received, grad_strips = lax.optimization_barrier((received, grad_strips))
+    result = collect_strips(member_box, out, bf16)
+    frames_grad = collect_strips(member_box, grad_strips, f32)
+    received, result, frames_grad = lax.optimization_barrier((received, result, frames_grad))
     sums = reduce_messages(
         where, own, received, hots, act_table, noise_table, ada_one, ada_two, rows, cells, 2 * share
     )
-    offset = 1
-    while 2 * offset < lax.axis_size("rows"):
-        sums = sums + trade(sums, offset)
-        offset *= 2
-    result = collect_strips(member_box, out, bf16)
-    frames_grad = collect_strips(member_box, grad_strips, f32)
-    sums = sums.astype(bf16)
-    return (result, frames_grad, *finish(sums, trade(sums, offset), rows, cells, width))
+    parts = [trade(sums, offset) for offset in range(lax.axis_size("rows"))]
+    return (result, frames_grad, *finish(parts, rows, cells, width))
 
 
 def local_general(
@@ -1361,7 +1348,12 @@
     noise_full = gathered(noise_table, 1)
     ada_full = gathered(jnp.concatenate([ada_one, ada_two], axis=1), 0).astype(f32)
     biases = gathered(jnp.stack([bias_one, bias_two, bias_down, bias_up]), 1).astype(f32)
-    operands = expand(gathered(conv_one, 0), gathered(conv_two, 0), gathered(down_kernel, 0), gathered(up_kernel, 0))
+    wide = lambda kernel: gathered(kernel, 0).astype(f32)
+    works = (
+        jnp.concatenate([wide(conv_one), wide(conv_two)], axis=1),
+        twice(wide(up_kernel)),
+        twice(wide(down_kernel)),
+    )
 
     own = lambda ids: lax.dynamic_slice_in_dim(ids, member * share, share)
     own_actions, own_noise, own_valid = own(actions), own(noise_ids), own(valid)
@@ -1383,7 +1375,7 @@
     )
     bias_rows = pad_small([twice(biases[k]) for k in range(4)])
     out, grad_strips, wins, tiles, pieces, bias_sums = layers(
-        member_box, frame_images, frame_stats, cot_fetched, styles, bias_rows, operands
+        member_box, frame_images, frame_stats, cot_fetched, styles, bias_rows, works
     )
     g_one, g_two, g_down, g_up = weight_grads(wins, tiles)
     result = collect_strips(member_box, out, bf16)

time: 73.7 us -> 71.1 us (0.965)
  waiting for transfers between devices: 13.6 us -> 10 us
  starting transfers between devices: 22.2 us -> 23.4 us
  Pallas kernels: 36.4 us -> 35.5 us
    ppermute x8, waiting for transfers between devices: 7.48 us -> 3.09 us  [half_trade(): return lax.ppermute(value, ('seq', 'rows'), pairs)]
    ppermute x14 -> x15, starting transfers between devices: 10.1 us -> 11.4 us  [trade(): return lax.ppermute(value, 'rows', [(i, i ^ offset) for i in range(count)])]
    ppermute x14 -> x15, waiting for transfers between devices: 6.15 us -> 6.95 us  [trade(): return lax.ppermute(value, 'rows', [(i, i ^ offset) for i in range(count)])]
    pallas_call x3 -> x5, Pallas kernels: 1.68 us -> 0.89 us  [the longest x1 0.82 us: finish(): pl.pallas_call(lambda *refs: finish_kernel(rows, cells, len(parts), *refs...]
  transfers between devices with their start and end apart: 22 -> 23, of which waited for: 8 -> 7; matrix products, arithmetic and copies ran while one was open for 0% -> 0% of each run, Pallas kernels for 45% -> 45%
where the time goes in v6:
time: 71.1 us; the launch traced here: 70.8 us
  Pallas kernels  35.5 us (50%)
  starting transfers between devices  23.4 us (33%)
  waiting for transfers between devices  10 us (14%)
  between operations  1.06 us (1%)
  local copies, waits for them, and re-layouts  0.73 us (1%)
    ppermute x8, starting transfers between devices, half_trade(): return lax.ppermute(value, ('seq', 'rows'), pairs)  12 us
    ppermute x15, starting transfers between devices, trade(): return lax.ppermute(value, 'rows', [(i, i ^ offset) for i in range(count)])  11.4 us
    pallas_call x1, Pallas kernels, backward(): pl.pallas_call(lambda *refs: backward_kernel(count, *refs), in_specs=[in_...  8.65 us
    pallas_call x1, Pallas kernels, forward(): pl.pallas_call(lambda *refs: forward_kernel(count, *refs), in_specs=[in_s...  7.52 us
    pallas_call x1, Pallas kernels, weight_messages(): pl.pallas_call(lambda *refs: message_kernel(count, rows, *refs), in_specs...  6.99 us
    ppermute x15, waiting for transfers between devices, trade(): return lax.ppermute(value, 'rows', [(i, i ^ offset) for i in range(count)])  6.95 us
    pallas_call x2, Pallas kernels, cut_far(): pl.pallas_call(far_kernel, in_specs=[in_smem(), in_place(pltpu.HBM)], out...  3.24 us
    ppermute x8, waiting for transfers between devices, half_trade(): return lax.ppermute(value, ('seq', 'rows'), pairs)  3.09 us
  transfers between devices with their start and end apart: 23, of which 7 were waited for; matrix products, arithmetic and copies ran while one was open for 0% of the time, Pallas kernels for 45%

profile of v6, /device:TPU:0, one launch (start us, length us, event | category | flops | bytes accessed | tf_op | source)
XLA Modules:
  0.0 70.8 jit_solution(11553895776468011217)
XLA Ops:
  0.7 1.2 %far.2 = (bf16[4,16,4096]{2,1,0:T(8,128)(2,1)S(1)}, bf16[2,16,4096]{2,1,0:T(8,128)(2,1)S(1)}, bf16[2,16,4096]{2,1,0:T(8,128)(2,1)S(1)}) custom-call(s32[1]{0:T(128)} %bitcast.1.member_ref.refs_0_, bf16[8,16,4096]{2,1,0:T(8,128)(2,1)} %array.2), custom_call_target="tpu_custom_call" | custom-call | tf_op jit(solution)/shard_map/far/pallas_call | solution.py:1038
  1.9 3.0 %collective-permute-start = (bf16[4,16,4096]{2,1,0:T(8,128)(2,1)S(1)}, bf16[4,16,4096]{2,1,0:T(8,128)(2,1)S(1)}, u32[]{:S(2)}, u32[]{:S(2)}) collective-permute-start(bf16[4,16,4096]{2,1,0:T(8,128)(2,1)S(1)} %get-tuple-element.92), channel_id=1, source_target_pairs={{0,2},{1,3},{2,0},{3,1},{4,6},{5,7},{6,4},{7,5},{8,10},{9,11},{10,... | collective-permute-start | bytes 1572872 | tf_op jit(solution)/shard_map/ppermute | solution.py:1234
  4.9 1.8 %pack.1.refs_4_ = bf16[288,128]{1,0:T(8,128)(2,1)} custom-call(s32[8]{0:T(128)} %refs_1_.3, s32[8]{0:T(128)} %refs_2_.3, s32[8]{0:T(128)} %refs_3_.1, bf16[64,72]{1,0:T(8,128)(2,1)} %bitcast.19, bf16[64,72]{1,0:T(8,128)(2,1)} %bitcast.20, bf16[64,72]{1,0:T(8,128)(2,1)} %bitcast.21, bf16[64,144]{1,0:T(8,128)(2,1)} %bitcast.15, bf16[32,128]{1,0:T(8,128)(2,1)} %refs_9_.3, ...), custom_call_target="tpu_custom_call" | custom-call | flops 16106127360 | bytes 1048576 | tf_op jit(solution)/shard_map/pack/pallas_call | solution.py:1080
  6.7 3.6 %collective-permute-start.2 = (bf16[288,128]{1,0:T(8,128)(2,1)}, bf16[288,128]{1,0:T(8,128)(2,1)S(1)}, u32[]{:S(2)}, u32[]{:S(2)}) collective-permute-start(bf16[288,128]{1,0:T(8,128)(2,1)} %pack.1.refs_4_), channel_id=1, source_target_pairs={{0,24},{1,29},{2,26},{3,31},{4,28},{5,25},{6,30},{7,27},{8,16},{9,... | collective-permute-start | bytes 221192 | tf_op jit(solution)/shard_map/ppermute | solution.py:1245
  10.3 0.7 collective-permute-start.5
  11.0 0.5 collective-permute-start.4
  11.5 1.2 %collective-permute-start.3 = (bf16[288,128]{1,0:T(8,128)(2,1)}, bf16[288,128]{1,0:T(8,128)(2,1)S(1)}, u32[]{:S(2)}, u32[]{:S(2)}) collective-permute-start(bf16[288,128]{1,0:T(8,128)(2,1)} %pack.1.refs_4_), channel_id=1, source_target_pairs={{0,20},{1,17},{2,22},{3,19},{4,16},{5,21},{6,18},{7,23},{8,28},{9,... | collective-permute-start | bytes 221192 | tf_op jit(solution)/shard_map/ppermute | solution.py:1245
  12.7 2.0 %far.3 = (bf16[4,16,4096]{2,1,0:T(8,128)(2,1)}, bf16[2,16,4096]{2,1,0:T(8,128)(2,1)S(1)}, bf16[2,16,4096]{2,1,0:T(8,128)(2,1)S(1)}) custom-call(s32[1]{0:T(128)} %bitcast.1.member_ref.refs_0_, bf16[8,16,4096]{2,1,0:T(8,128)(2,1)} %array.3), custom_call_target="tpu_custom_call" | custom-call | tf_op jit(solution)/shard_map/far/pallas_call | solution.py:1038
  14.7 0.0 collective-permute-done.2
  14.8 0.4 collective-permute-start.7
  15.1 1.7 %collective-permute-done.far = bf16[4,16,4096]{2,1,0:T(8,128)(2,1)S(1)} collective-permute-done((bf16[4,16,4096]{2,1,0:T(8,128)(2,1)S(1)}, bf16[4,16,4096]{2,1,0:T(8,128)(2,1)S(1)}, u32[]{:S(2)}, u32[]{:S(2)}) %collective-permute-start) | collective-permute-done | bytes 524320 | tf_op jit(solution)/shard_map/ppermute | solution.py:1234
  16.9 0.1 collective-permute-start.1
  17.0 1.5 %collective-permute-done.3 = bf16[288,128]{1,0:T(8,128)(2,1)S(1)} collective-permute-done((bf16[288,128]{1,0:T(8,128)(2,1)}, bf16[288,128]{1,0:T(8,128)(2,1)S(1)}, u32[]{:S(2)}, u32[]{:S(2)}) %collective-permute-start.3) | collective-permute-done | bytes 73760 | tf_op jit(solution)/shard_map/ppermute | solution.py:1245
  18.5 0.0 collective-permute-done.4
  18.5 0.0 collective-permute-done.5
  18.6 0.9 %collective-permute-start.6 = (bf16[1152,128]{1,0:T(8,128)(2,1)S(1)}, bf16[1152,128]{1,0:T(8,128)(2,1)S(1)}, u32[]{:S(2)}, u32[]{:S(2)}) collective-permute-start(bf16[1152,128]{1,0:T(8,128)(2,1)S(1)} %constant_dynamic-update-slice_fusion.refs_5_), channel_id=1, source_target_pairs={{0,1},{1,0},{2,3},{3,2},{4,5},{5,4},{6,7},{7,6},{8,9},{9,8},{10,11... | collective-permute-start | bytes 884744 | tf_op jit(solution)/shard_map/ppermute | solution.py:1234
  19.5 0.1 pad_add_fusion.refs_0_
  19.6 1.1 %collective-permute-done.6.refs_6_ = bf16[1152,128]{1,0:T(8,128)(2,1)S(1)} collective-permute-done((bf16[1152,128]{1,0:T(8,128)(2,1)S(1)}, bf16[1152,128]{1,0:T(8,128)(2,1)S(1)}, u32[]{:S(2)}, u32[]{:S(2)}) %collective-permute-start.6) | collective-permute-done | bytes 294944 | tf_op jit(solution)/shard_map/ppermute | solution.py:1234
  20.7 0.0 copy-done
  20.7 0.0 copy-done.5
  20.7 0.6 copy-done.7
  21.4 1.0 %prepare.1 = (f32[2,8,128]{2,1,0:T(8,128)S(1)}, f32[8,128]{1,0:T(8,128)S(1)}, f32[4,8,128]{2,1,0:T(8,128)S(1)}, f32[576,128]{1,0:T(8,128)S(1)}, f32[1152,128]{1,0:T(8,128)S(1)}, /*index=5*/f32[576,128]{1,0:T(8,128)S(1)}) custom-call(s32[2]{0:T(128)S(1)} %pad_add_fusion.refs_0_, s32[8]{0:T(128)S(1)} %copy-done.5, s32[8]{0:T(128)S(1)} %copy-done.6, ...), custom_call_target="tpu_custom_call" | custom-call | tf_op jit(solution)/shard_map/prepare/pallas_call | solution.py:1105
  22.4 0.0 collective-permute-done.1.near
  22.4 0.5 frames.2
  22.9 7.5 %forward.1 = (bf16[2,16,4096]{2,1,0:T(8,128)(2,1)S(1)}, bf16[2,16,4096]{2,1,0:T(8,128)(2,1)S(1)}, bf16[2,16,4096]{2,1,0:T(8,128)(2,1)S(1)}, bf16[2,16,4096]{2,1,...) custom-call(s32[1]{0:T(128)} %bitcast.1.member_ref.refs_0_, ...), custom_call_target="tpu_custom_call" | custom-call | flops 2048 | bytes 1024 | tf_op jit(solution)/shard_map/forward/pallas_call | solution.py:958
  30.5 0.0 collective-permute-done.7.far
  30.6 0.4 collective-permute-start.8
  31.0 0.1 collective-permute-start.9
  31.1 0.5 collective-permute-start.10
  31.7 1.2 %collective-permute-start.11 = (bf16[2,16,4096]{2,1,0:T(8,128)(2,1)S(1)}, bf16[2,16,4096]{2,1,0:T(8,128)(2,1)S(1)}, u32[]{:S(2)}, u32[]{:S(2)}) collective-permute-start(bf16[2,16,4096]{2,1,0:T(8,128)(2,1)S(1)} %get-tuple-element.134), channel_id=1, source_target_pairs={{0,3},{1,2},{2,1},{3,0},{4,7},{5,6},{6,5},{7,4},{8,11},{9,10},{10,... | collective-permute-start | bytes 786440 | tf_op jit(solution)/shard_map/ppermute | solution.py:1234
  32.9 0.0 collective-permute-done.8.near
  32.9 0.5 frames.3
  33.4 8.6 %backward.1 = (bf16[2,16,4096]{2,1,0:T(8,128)(2,1)S(1)}, bf16[2,16,4096]{2,1,0:T(8,128)(2,1)S(1)}, bf16[2,16,4096]{2,1,0:T(8,128)(2,1)S(1)}, bf16[2,16,4096]{2,1...) custom-call(s32[1]{0:T(128)} %bitcast.1.member_ref.refs_0_, ...), custom_call_target="tpu_custom_call" | custom-call | flops 5368709120 | bytes 20971520 | tf_op jit(solution)/shard_map/backward/pallas_call | solution.py:984
  42.0 0.5 collective-permute-start.17
  42.5 0.5 collective-permute-start.18
  43.0 7.0 %weights.1 = (f32[864,128]{1,0:T(8,128)S(1)}, f32[16,128]{1,0:T(8,128)S(1)}, bf16[864,128]{1,0:T(8,128)(2,1)S(1)}, f32[16,128]{1,0:T(8,128)S(1)}) custom-call(s32[2]{0:T(128)S(1)} %pad_add_fusion.refs_0_, bf16[2,4,33,32,128]{4,3,2,1,0:T(8,128)(2,1)S(1)} %get-tuple-element.101.refs_1_, bf16[2,4,33,32,128]{4,3,2,1,0:T(8,128)(2,1)S(1)} %get-tuple-element.102.refs_2_, ...), custom_call_target="tpu_custom_call" | custom-call | flops 5368709120 | bytes 12582912 | tf_op jit(solution)/shard_map/weights/pallas_call | solution.py:1125
  50.0 0.0 collective-permute-done.9.refs_1_
  50.0 0.0 collective-permute-done.10.refs_2_
  50.0 0.0 collective-permute-done.11.refs_3_
  50.1 0.1 collective-permute-start.12
  50.1 1.6 %collective-permute-start.19 = (bf16[2,16,4096]{2,1,0:T(8,128)(2,1)S(1)}, bf16[2,16,4096]{2,1,0:T(8,128)(2,1)S(1)}, u32[]{:S(2)}, u32[]{:S(2)}) collective-permute-start(bf16[2,16,4096]{2,1,0:T(8,128)(2,1)S(1)} %get-tuple-element.147), channel_id=1, source_target_pairs={{0,3},{1,2},{2,1},{3,0},{4,7},{5,6},{6,5},{7,4},{8,11},{9,10},{10,... | collective-permute-start | bytes 786440 | tf_op jit(solution)/shard_map/ppermute | solution.py:1234
  51.8 0.0 collective-permute-done.12.refs_3_
  51.8 0.6 join.1
  52.4 3.5 %collective-permute-start.13 = (bf16[216,128]{1,0:T(8,128)(2,1)S(1)}, bf16[216,128]{1,0:T(8,128)(2,1)S(1)}, u32[]{:S(2)}, u32[]{:S(2)}) collective-permute-start(bf16[216,128]{1,0:T(8,128)(2,1)S(1)} %get-tuple-element.136), channel_id=1, source_target_pairs={{0,24},{1,29},{2,26},{3,31},{4,28},{5,25},{6,30},{7,27},{8,16},{9,... | collective-permute-start | bytes 165896 | tf_op jit(solution)/shard_map/ppermute | solution.py:1245
  55.9 0.4 collective-permute-start.14
  56.3 0.0 collective-permute-done.17.refs_1_
  56.3 1.5 %collective-permute-start.15 = (bf16[216,128]{1,0:T(8,128)(2,1)S(1)}, bf16[216,128]{1,0:T(8,128)(2,1)S(1)}, u32[]{:S(2)}, u32[]{:S(2)}) collective-permute-start(bf16[216,128]{1,0:T(8,128)(2,1)S(1)} %get-tuple-element.138), channel_id=1, source_target_pairs={{0,12},{1,9},{2,14},{3,11},{4,8},{5,13},{6,10},{7,15},{8,4},{9,1},... | collective-permute-start | bytes 165896 | tf_op jit(solution)/shard_map/ppermute | solution.py:1245
  57.7 0.0 collective-permute-done.18.refs_2_
  57.7 0.7 collective-permute-start.16
  58.4 1.0 %collect.2 = bf16[4,2,16,4096]{3,2,1,0:T(8,128)(2,1)} custom-call(s32[1]{0:T(128)} %bitcast.1.member_ref.refs_0_, bf16[2,16,4096]{2,1,0:T(8,128)(2,1)S(1)} %get-tuple-element.140.refs_0_, bf16[2,16,4096]{2,1,0:T(8,128)(2,1)S(1)} %collective-permute-done.9.refs_1_, bf16[2,16,4096]{2,1,0:T(8,128)(2,1)S(1)} %collective-permute-done.10.refs_2_, ...), custom_call_target="tpu_custom_call" | custom-call | tf_op jit(solution)/shard_map/collect/pallas_call | solution.py:1208
  59.5 0.0 collective-permute-done.19.refs_3_
  59.5 1.4 %collect.3 = f32[4,2,16,4096]{3,2,1,0:T(8,128)} custom-call(s32[1]{0:T(128)} %bitcast.1.member_ref.refs_0_, bf16[2,16,4096]{2,1,0:T(8,128)(2,1)S(1)} %get-tuple-element.144.refs_0_, bf16[2,16,4096]{2,1,0:T(8,128)(2,1)S(1)} %collective-permute-done.17.refs_1_, bf16[2,16,4096]{2,1,0:T(8,128)(2,1)S(1)} %collective-permute-done.18.refs_2_, ...), custom_call_target="tpu_custom_call" | custom-call | tf_op jit(solution)/shard_map/collect/pallas_call | solution.py:1208
  60.9 0.0 collective-permute-done.13.refs_2_
  60.9 1.3 %collective-permute-done.14.refs_3_ = bf16[216,128]{1,0:T(8,128)(2,1)S(1)} collective-permute-done((bf16[216,128]{1,0:T(8,128)(2,1)S(1)}, bf16[216,128]{1,0:T(8,128)(2,1)S(1)}, u32[]{:S(2)}, u32[]{:S(2)}) %collective-permute-start.14) | collective-permute-done | bytes 55328 | tf_op jit(solution)/shard_map/ppermute | solution.py:1245
  62.2 0.3 collective-permute-done.15.refs_4_
  62.5 0.0 collective-permute-done.16.refs_5_
  62.5 1.3 %reduce.1.refs_0_ = bf16[280,128]{1,0:T(8,128)(2,1)S(1)} custom-call(s32[2]{0:T(128)S(1)} %pad_add_fusion.refs_0_, f32[216,128]{1,0:T(8,128)S(1)} %get-tuple-element.150.refs_1_, bf16[216,128]{1,0:T(8,128)(2,1)S(1)} %collective-permute-done.13.refs_2_, bf16[216,128]{1,0:T(8,128)(2,1)S(1)} %collective-permute-done.14.refs_3_, ...), custom_call_target="tpu_custom_call" | custom-call | tf_op jit(solution)/shard_map/reduce/pallas_call | solution.py:1156
  63.8 1.1 %collective-permute-start.22 = (bf16[280,128]{1,0:T(8,128)(2,1)S(1)}, bf16[280,128]{1,0:T(8,128)(2,1)S(1)}, u32[]{:S(2)}, u32[]{:S(2)}) collective-permute-start(bf16[280,128]{1,0:T(8,128)(2,1)S(1)} %reduce.1.refs_0_), channel_id=1, source_target_pairs={{0,3},{1,2},{2,1},{3,0},{4,7},{5,6},{6,5},{7,4},{8,11},{9,10},{10,... | collective-permute-start | bytes 215048 | tf_op jit(solution)/shard_map/ppermute | solution.py:1234
  64.9 0.9 %collective-permute-start.21 = (bf16[280,128]{1,0:T(8,128)(2,1)S(1)}, bf16[280,128]{1,0:T(8,128)(2,1)S(1)}, u32[]{:S(2)}, u32[]{:S(2)}) collective-permute-start(bf16[280,128]{1,0:T(8,128)(2,1)S(1)} %reduce.1.refs_0_), channel_id=1, source_target_pairs={{0,2},{1,3},{2,0},{3,1},{4,6},{5,7},{6,4},{7,5},{8,10},{9,11},{10,... | collective-permute-start | bytes 215048 | tf_op jit(solution)/shard_map/ppermute | solution.py:1234
  65.8 0.0 collective-permute-start.20
  65.8 2.1 %collective-permute-done.22.refs_3_ = bf16[280,128]{1,0:T(8,128)(2,1)S(1)} collective-permute-done((bf16[280,128]{1,0:T(8,128)(2,1)S(1)}, bf16[280,128]{1,0:T(8,128)(2,1)S(1)}, u32[]{:S(2)}, u32[]{:S(2)}) %collective-permute-start.22) | collective-permute-done | bytes 71712 | tf_op jit(solution)/shard_map/ppermute | solution.py:1234
  67.9 2.0 %collective-permute-done.21.refs_2_ = bf16[280,128]{1,0:T(8,128)(2,1)S(1)} collective-permute-done((bf16[280,128]{1,0:T(8,128)(2,1)S(1)}, bf16[280,128]{1,0:T(8,128)(2,1)S(1)}, u32[]{:S(2)}, u32[]{:S(2)}) %collective-permute-start.21) | collective-permute-done | bytes 71712 | tf_op jit(solution)/shard_map/ppermute | solution.py:1234
  69.9 0.0 collective-permute-done.20.refs_1_
  69.9 0.8 %finish.1 = (f32[18,32]{1,0:T(8,128)}, f32[32,32]{1,0:T(8,128)}, f32[32,128]{1,0:T(8,128)}, f32[32,128]{1,0:T(8,128)}, f32[64,72]{1,0:T(8,128)}, /*index=5*/f32[...) custom-call(bf16[280,128]{1,0:T(8,128)(2,1)S(1)} %reduce.1.refs_0_, ...), custom_call_target="tpu_custom_call" | custom-call | tf_op jit(solution)/shard_map/finish/pallas_call | solution.py:1174
  (23 shorter events, 0.2 us)
Async XLA Ops:
  1.9 15.0 %collective-permute-start = (bf16[4,16,4096]{2,1,0:T(8,128)(2,1)S(1)}, bf16[4,16,4096]{2,1,0:T(8,128)(2,1)S(1)}, u32[]{:S(2)}, u32[]{:S(2)}) collective-permute-start(bf16[4,16,4096]{2,1,0:T(8,128)(2,1)S(1)} %get-tuple-element.92), channel_id=1, source_target_pairs={{0,2},{1,3},{2,0},{3,1},{4,6},{5,7},{6,4},{7,5},{8,10},{9,11},{10,... | collective-permute-start | bytes 1572872 | tf_op jit(solution)/shard_map/ppermute | solution.py:1234
  6.7 8.0 %collective-permute-start.2 = (bf16[288,128]{1,0:T(8,128)(2,1)}, bf16[288,128]{1,0:T(8,128)(2,1)S(1)}, u32[]{:S(2)}, u32[]{:S(2)}) collective-permute-start(bf16[288,128]{1,0:T(8,128)(2,1)} %pack.1.refs_4_), channel_id=1, source_target_pairs={{0,24},{1,29},{2,26},{3,31},{4,28},{5,25},{6,30},{7,27},{8,16},{9,... | collective-permute-start | bytes 221192 | tf_op jit(solution)/shard_map/ppermute | solution.py:1245
  10.3 8.2 %collective-permute-start.5 = (bf16[288,128]{1,0:T(8,128)(2,1)}, bf16[288,128]{1,0:T(8,128)(2,1)S(1)}, u32[]{:S(2)}, u32[]{:S(2)}) collective-permute-start(bf16[288,128]{1,0:T(8,128)(2,1)} %pack.1.refs_4_), channel_id=1, source_target_pairs={{1,5},{3,7},{5,1},{7,3},{9,13},{11,15},{13,9},{15,11},{17,21},{19,... | collective-permute-start | bytes 221192 | tf_op jit(solution)/shard_map/ppermute | solution.py:1245
  11.0 7.5 %collective-permute-start.4 = (bf16[288,128]{1,0:T(8,128)(2,1)}, bf16[288,128]{1,0:T(8,128)(2,1)S(1)}, u32[]{:S(2)}, u32[]{:S(2)}) collective-permute-start(bf16[288,128]{1,0:T(8,128)(2,1)} %pack.1.refs_4_), channel_id=1, source_target_pairs={{0,12},{1,9},{2,14},{3,11},{4,8},{5,13},{6,10},{7,15},{8,4},{9,1},... | collective-permute-start | bytes 221192 | tf_op jit(solution)/shard_map/ppermute | solution.py:1245
  11.5 7.0 %collective-permute-start.3 = (bf16[288,128]{1,0:T(8,128)(2,1)}, bf16[288,128]{1,0:T(8,128)(2,1)S(1)}, u32[]{:S(2)}, u32[]{:S(2)}) collective-permute-start(bf16[288,128]{1,0:T(8,128)(2,1)} %pack.1.refs_4_), channel_id=1, source_target_pairs={{0,20},{1,17},{2,22},{3,19},{4,16},{5,21},{6,18},{7,23},{8,28},{9,... | collective-permute-start | bytes 221192 | tf_op jit(solution)/shard_map/ppermute | solution.py:1245
  14.8 15.7 %collective-permute-start.7 = (bf16[4,16,4096]{2,1,0:T(8,128)(2,1)}, bf16[4,16,4096]{2,1,0:T(8,128)(2,1)S(1)}, u32[]{:S(2)}, u32[]{:S(2)}) collective-permute-start(bf16[4,16,4096]{2,1,0:T(8,128)(2,1)} %get-tuple-element.106), channel_id=1, source_target_pairs={{0,2},{1,3},{2,0},{3,1},{4,6},{5,7},{6,4},{7,5},{8,10},{9,11},{10,... | collective-permute-start | bytes 1572872 | tf_op jit(solution)/shard_map/ppermute | solution.py:1234
  16.8 3.9 %copy-start = (bf16[288,128]{1,0:T(8,128)(2,1)S(1)}, bf16[288,128]{1,0:T(8,128)(2,1)}, u32[]{:S(2)}) copy-start(bf16[288,128]{1,0:T(8,128)(2,1)} %pack.1.refs_4_) | copy-start | bytes 221188
  16.8 3.9 %copy-start.5 = (s32[8]{0:T(128)S(1)}, s32[8]{0:T(128)}, u32[]{:S(2)}) copy-start(s32[8]{0:T(128)} %refs_1_.3) | copy-start | bytes 100
  16.8 3.9 %copy-start.6 = (s32[8]{0:T(128)S(1)}, s32[8]{0:T(128)}, u32[]{:S(2)}) copy-start(s32[8]{0:T(128)} %refs_2_.3) | copy-start | bytes 100
  16.9 5.5 %collective-permute-start.1 = (bf16[4,16,4096]{2,1,0:T(8,128)(2,1)S(1)}, bf16[4,16,4096]{2,1,0:T(8,128)(2,1)S(1)}, u32[]{:S(2)}, u32[]{:S(2)}) collective-permute-start(bf16[4,16,4096]{2,1,0:T(8,128)(2,1)S(1)} %near.2), channel_id=1, source_target_pairs={{0,1},{1,0},{2,3},{3,2},{4,5},{5,4},{6,7},{7,6},{8,9},{9,8},{10,11... | collective-permute-start | bytes 1572872 | tf_op jit(solution)/shard_map/ppermute | solution.py:1234
  18.6 2.1 %collective-permute-start.6 = (bf16[1152,128]{1,0:T(8,128)(2,1)S(1)}, bf16[1152,128]{1,0:T(8,128)(2,1)S(1)}, u32[]{:S(2)}, u32[]{:S(2)}) collective-permute-start(bf16[1152,128]{1,0:T(8,128)(2,1)S(1)} %constant_dynamic-update-slice_fusion.refs_5_), channel_id=1, source_target_pairs={{0,1},{1,0},{2,3},{3,2},{4,5},{5,4},{6,7},{7,6},{8,9},{9,8},{10,11... | collective-permute-start | bytes 884744 | tf_op jit(solution)/shard_map/ppermute | solution.py:1234
  20.7 0.7 copy-start.7
  30.6 2.3 %collective-permute-start.8 = (bf16[4,16,4096]{2,1,0:T(8,128)(2,1)S(1)}, bf16[4,16,4096]{2,1,0:T(8,128)(2,1)S(1)}, u32[]{:S(2)}, u32[]{:S(2)}) collective-permute-start(bf16[4,16,4096]{2,1,0:T(8,128)(2,1)S(1)} %near.3), channel_id=1, source_target_pairs={{0,1},{1,0},{2,3},{3,2},{4,5},{5,4},{6,7},{7,6},{8,9},{9,8},{10,11... | collective-permute-start | bytes 1572872 | tf_op jit(solution)/shard_map/ppermute | solution.py:1234
  31.0 19.0 %collective-permute-start.9 = (bf16[2,16,4096]{2,1,0:T(8,128)(2,1)S(1)}, bf16[2,16,4096]{2,1,0:T(8,128)(2,1)S(1)}, u32[]{:S(2)}, u32[]{:S(2)}) collective-permute-start(bf16[2,16,4096]{2,1,0:T(8,128)(2,1)S(1)} %get-tuple-element.132), channel_id=1, source_target_pairs={{0,1},{1,0},{2,3},{3,2},{4,5},{5,4},{6,7},{7,6},{8,9},{9,8},{10,11... | collective-permute-start | bytes 786440 | tf_op jit(solution)/shard_map/ppermute | solution.py:1234
  31.1 18.9 %collective-permute-start.10 = (bf16[2,16,4096]{2,1,0:T(8,128)(2,1)S(1)}, bf16[2,16,4096]{2,1,0:T(8,128)(2,1)S(1)}, u32[]{:S(2)}, u32[]{:S(2)}) collective-permute-start(bf16[2,16,4096]{2,1,0:T(8,128)(2,1)S(1)} %get-tuple-element.133), channel_id=1, source_target_pairs={{0,2},{1,3},{2,0},{3,1},{4,6},{5,7},{6,4},{7,5},{8,10},{9,11},{10,... | collective-permute-start | bytes 786440 | tf_op jit(solution)/shard_map/ppermute | solution.py:1234
  31.7 18.4 %collective-permute-start.11 = (bf16[2,16,4096]{2,1,0:T(8,128)(2,1)S(1)}, bf16[2,16,4096]{2,1,0:T(8,128)(2,1)S(1)}, u32[]{:S(2)}, u32[]{:S(2)}) collective-permute-start(bf16[2,16,4096]{2,1,0:T(8,128)(2,1)S(1)} %get-tuple-element.134), channel_id=1, source_target_pairs={{0,3},{1,2},{2,1},{3,0},{4,7},{5,6},{6,5},{7,4},{8,11},{9,10},{10,... | collective-permute-start | bytes 786440 | tf_op jit(solution)/shard_map/ppermute | solution.py:1234
  42.0 14.2 %collective-permute-start.17 = (bf16[2,16,4096]{2,1,0:T(8,128)(2,1)S(1)}, bf16[2,16,4096]{2,1,0:T(8,128)(2,1)S(1)}, u32[]{:S(2)}, u32[]{:S(2)}) collective-permute-start(bf16[2,16,4096]{2,1,0:T(8,128)(2,1)S(1)} %get-tuple-element.145), channel_id=1, source_target_pairs={{0,1},{1,0},{2,3},{3,2},{4,5},{5,4},{6,7},{7,6},{8,9},{9,8},{10,11... | collective-permute-start | bytes 786440 | tf_op jit(solution)/shard_map/ppermute | solution.py:1234
  42.5 15.2 %collective-permute-start.18 = (bf16[2,16,4096]{2,1,0:T(8,128)(2,1)S(1)}, bf16[2,16,4096]{2,1,0:T(8,128)(2,1)S(1)}, u32[]{:S(2)}, u32[]{:S(2)}) collective-permute-start(bf16[2,16,4096]{2,1,0:T(8,128)(2,1)S(1)} %get-tuple-element.146), channel_id=1, source_target_pairs={{0,2},{1,3},{2,0},{3,1},{4,6},{5,7},{6,4},{7,5},{8,10},{9,11},{10,... | collective-permute-start | bytes 786440 | tf_op jit(solution)/shard_map/ppermute | solution.py:1234
  50.1 1.7 %collective-permute-start.12 = (bf16[864,128]{1,0:T(8,128)(2,1)S(1)}, bf16[864,128]{1,0:T(8,128)(2,1)S(1)}, u32[]{:S(2)}, u32[]{:S(2)}) collective-permute-start(bf16[864,128]{1,0:T(8,128)(2,1)S(1)} %get-tuple-element.135), channel_id=1, source_target_pairs={{0,1},{1,0},{2,3},{3,2},{4,5},{5,4},{6,7},{7,6},{8,9},{9,8},{10,11... | collective-permute-start | bytes 663560 | tf_op jit(solution)/shard_map/ppermute | solution.py:1234
  50.1 9.3 %collective-permute-start.19 = (bf16[2,16,4096]{2,1,0:T(8,128)(2,1)S(1)}, bf16[2,16,4096]{2,1,0:T(8,128)(2,1)S(1)}, u32[]{:S(2)}, u32[]{:S(2)}) collective-permute-start(bf16[2,16,4096]{2,1,0:T(8,128)(2,1)S(1)} %get-tuple-element.147), channel_id=1, source_target_pairs={{0,3},{1,2},{2,1},{3,0},{4,7},{5,6},{6,5},{7,4},{8,11},{9,10},{10,... | collective-permute-start | bytes 786440 | tf_op jit(solution)/shard_map/ppermute | solution.py:1234
  52.4 8.5 %collective-permute-start.13 = (bf16[216,128]{1,0:T(8,128)(2,1)S(1)}, bf16[216,128]{1,0:T(8,128)(2,1)S(1)}, u32[]{:S(2)}, u32[]{:S(2)}) collective-permute-start(bf16[216,128]{1,0:T(8,128)(2,1)S(1)} %get-tuple-element.136), channel_id=1, source_target_pairs={{0,24},{1,29},{2,26},{3,31},{4,28},{5,25},{6,30},{7,27},{8,16},{9,... | collective-permute-start | bytes 165896 | tf_op jit(solution)/shard_map/ppermute | solution.py:1245
  55.9 6.3 %collective-permute-start.14 = (bf16[216,128]{1,0:T(8,128)(2,1)S(1)}, bf16[216,128]{1,0:T(8,128)(2,1)S(1)}, u32[]{:S(2)}, u32[]{:S(2)}) collective-permute-start(bf16[216,128]{1,0:T(8,128)(2,1)S(1)} %get-tuple-element.137), channel_id=1, source_target_pairs={{0,20},{1,17},{2,22},{3,19},{4,16},{5,21},{6,18},{7,23},{8,28},{9,... | collective-permute-start | bytes 165896 | tf_op jit(solution)/shard_map/ppermute | solution.py:1245
  56.3 6.2 %collective-permute-start.15 = (bf16[216,128]{1,0:T(8,128)(2,1)S(1)}, bf16[216,128]{1,0:T(8,128)(2,1)S(1)}, u32[]{:S(2)}, u32[]{:S(2)}) collective-permute-start(bf16[216,128]{1,0:T(8,128)(2,1)S(1)} %get-tuple-element.138), channel_id=1, source_target_pairs={{0,12},{1,9},{2,14},{3,11},{4,8},{5,13},{6,10},{7,15},{8,4},{9,1},... | collective-permute-start | bytes 165896 | tf_op jit(solution)/shard_map/ppermute | solution.py:1245
  57.7 4.7 %collective-permute-start.16 = (bf16[216,128]{1,0:T(8,128)(2,1)S(1)}, bf16[216,128]{1,0:T(8,128)(2,1)S(1)}, u32[]{:S(2)}, u32[]{:S(2)}) collective-permute-start(bf16[216,128]{1,0:T(8,128)(2,1)S(1)} %get-tuple-element.139), channel_id=1, source_target_pairs={{1,5},{3,7},{5,1},{7,3},{9,13},{11,15},{13,9},{15,11},{17,21},{19,... | collective-permute-start | bytes 165896 | tf_op jit(solution)/shard_map/ppermute | solution.py:1245
  59.4 3.1 %copy-start.1 = (bf16[32,128]{1,0:T(8,128)(2,1)S(1)}, bf16[32,128]{1,0:T(8,128)(2,1)}, u32[]{:S(2)}) copy-start(bf16[32,128]{1,0:T(8,128)(2,1)} %refs_9_.3) | copy-start | bytes 24580
  59.4 3.1 %copy-start.2 = (bf16[32,128]{1,0:T(8,128)(2,1)S(1)}, bf16[32,128]{1,0:T(8,128)(2,1)}, u32[]{:S(2)}) copy-start(bf16[32,128]{1,0:T(8,128)(2,1)} %refs_10_.3) | copy-start | bytes 24580
  59.4 3.1 %copy-start.3 = (bf16[32,32]{1,0:T(8,128)(2,1)S(1)}, bf16[32,32]{1,0:T(8,128)(2,1)}, u32[]{:S(2)}) copy-start(bf16[32,32]{1,0:T(8,128)(2,1)} %refs_8_.3) | copy-start | bytes 6148
  59.4 3.1 %copy-start.4 = (bf16[18,32]{1,0:T(8,128)(2,1)S(1)}, bf16[18,32]{1,0:T(8,128)(2,1)}, u32[]{:S(2)}) copy-start(bf16[18,32]{1,0:T(8,128)(2,1)} %refs_7_.3) | copy-start | bytes 3460
  63.8 4.1 %collective-permute-start.22 = (bf16[280,128]{1,0:T(8,128)(2,1)S(1)}, bf16[280,128]{1,0:T(8,128)(2,1)S(1)}, u32[]{:S(2)}, u32[]{:S(2)}) collective-permute-start(bf16[280,128]{1,0:T(8,128)(2,1)S(1)} %reduce.1.refs_0_), channel_id=1, source_target_pairs={{0,3},{1,2},{2,1},{3,0},{4,7},{5,6},{6,5},{7,4},{8,11},{9,10},{10,... | collective-permute-start | bytes 215048 | tf_op jit(solution)/shard_map/ppermute | solution.py:1234
  64.9 5.0 %collective-permute-start.21 = (bf16[280,128]{1,0:T(8,128)(2,1)S(1)}, bf16[280,128]{1,0:T(8,128)(2,1)S(1)}, u32[]{:S(2)}, u32[]{:S(2)}) collective-permute-start(bf16[280,128]{1,0:T(8,128)(2,1)S(1)} %reduce.1.refs_0_), channel_id=1, source_target_pairs={{0,2},{1,3},{2,0},{3,1},{4,6},{5,7},{6,4},{7,5},{8,10},{9,11},{10,... | collective-permute-start | bytes 215048 | tf_op jit(solution)/shard_map/ppermute | solution.py:1234
  65.8 4.1 %collective-permute-start.20 = (bf16[280,128]{1,0:T(8,128)(2,1)S(1)}, bf16[280,128]{1,0:T(8,128)(2,1)S(1)}, u32[]{:S(2)}, u32[]{:S(2)}) collective-permute-start(bf16[280,128]{1,0:T(8,128)(2,1)S(1)} %reduce.1.refs_0_), channel_id=1, source_target_pairs={{0,1},{1,0},{2,3},{3,2},{4,5},{5,4},{6,7},{7,6},{8,9},{9,8},{10,11... | collective-permute-start | bytes 215048 | tf_op jit(solution)/shard_map/ppermute | solution.py:1234

commit v7 on v6

--- a/solution.py
+++ b/solution.py
@@ -103,7 +103,7 @@
 def norm_stats(sums, squares):
     average = group_sum(both_parities(sums)) / MEMBERS
     variance = group_sum(both_parities(squares)) / MEMBERS - average * average
-    return average, lax.rsqrt(variance + EPS)
+    return average, lax.rsqrt(jnp.maximum(variance, 0.0) + EPS)
 
 
 def strip_start(member, offset, strip):
@@ -320,7 +320,7 @@
             g = pre_grad[0, j]
             g = g + swap_halves(g)
             h = down[j] * 0.5
-            d = 0.5 * g * slope_twice(h)
+            d = g * slope_twice(h)
             pair = jnp.where(low_lanes, d, after)
             coarse_pairs[j] = pair.astype(bf16)
             coarse_below[j] = row_after(pair).astype(bf16)
@@ -357,7 +357,7 @@
             shift_sum = jnp.zeros((1, LANES), f32)
             for a in range(2):
                 v = value(a)
-                g = 0.5 * y[:, a * LANES : (a + 1) * LANES] * slope_twice(v * half_gain + half_shift)
+                g = y[:, a * LANES : (a + 1) * LANES] * slope_twice(v * half_gain + half_shift)
                 pre_grad[a] = tiles_of(g)
                 shift_sum = shift_sum + total(g)
                 scale_sum = scale_sum + total(g * ((v - average) * inverse))
@@ -413,7 +413,7 @@
     return lax.dot_general(left, right, (((0,), (0,)), ((), ())), preferred_element_type=f32)
 
 
-def accumulate(wins, tiles, sums):
+def accumulate(wins, tiles, sums, folds):
     win_one, win_two, win_level, win_coarse = wins
     tile_out, tile_level, tile_mid, coarse_pairs = tiles
     sum_one, sum_two, sum_down, sum_up = sums
@@ -434,7 +434,14 @@
     sum_up[: 16 * C, :] = outer(operand(win_level, range(4)), out_blocks)
     sum_down[...] = outer(operand(win_level, range(3)), coarse_pairs[...].reshape(cells, LANES))
     sum_two[...] = outer(operand(win_two, range(4)), blocks(tile_level))
+    folds[0]()
     sum_one[...] = outer(operand(win_one, range(4)), blocks(tile_mid))
+    folds[1]()
+    folds[2]()
+
+
+def taps():
+    return [(p, q, (3 * p + q) * C) for p in range(3) for q in range(3)]
 
 
 def fold(sums, p, q):
@@ -457,16 +464,23 @@
     wins, tiles, grads, sums = refs[:4], refs[4:8], refs[8:12], refs[12:]
     g_one, g_two, g_down, g_up = grads
     sum_one, sum_two, sum_down, sum_up = sums
-    accumulate(wins, tiles, sums)
-    for p in range(3):
-        for q in range(3):
-            at = (3 * p + q) * C
-            g_one[at : at + C, :] = fold(sum_one, p, q)[:, :C]
-            g_two[at : at + C, :] = fold(sum_two, p, q)[:, :C]
+
+    def fold_up():
+        for p, q, at in taps():
             g_up[2 * at : 2 * at + C, :] = fold_coarse(sum_up, p, q)[:, :C]
             g_up[2 * at + C : 2 * at + 2 * C, :] = fold(sum_up, p, q)[:, :C]
             place = (p * 4 + q) * C
             g_down[at : at + C, :] = sum_down[place : place + C, :C]
+
+    def fold_two():
+        for p, q, at in taps():
+            g_two[at : at + C, :] = fold(sum_two, p, q)[:, :C]
+
+    def fold_one():
+        for p, q, at in taps():
+            g_one[at : at + C, :] = fold(sum_one, p, q)[:, :C]
+
+    accumulate(wins, tiles, sums, (fold_up, fold_two, fold_one))
 
 
 PARTS = 16
@@ -496,18 +510,24 @@
     taken = 2 * pieces.shape[0]
     for at in range(ids.shape[0]):
         write_hots(hots, at * taken, where_ref[1] // 2 * taken, taken, ids[at])
-    accumulate(wins, tiles, sums)
     low_lanes = lane_ids((C, LANES)) < C
-    for p in range(3):
-        for q in range(3):
-            at = (3 * p + q) * C
-            g_pair[at : at + C, :] = jnp.where(
-                low_lanes, fold(sum_one, p, q), swap_halves(fold(sum_two, p, q))
-            )
+
+    def fold_up():
+        for p, q, at in taps():
             g_up[2 * at : 2 * at + C, :] = fold_coarse(sum_up, p, q)
             g_up[2 * at + C : 2 * at + 2 * C, :] = fold(sum_up, p, q)
             place = (p * 4 + q) * C
             g_down[at : at + C, :] = sum_down[place : place + C, :]
+
+    def fold_two():
+        for p, q, at in taps():
+            g_pair[at : at + C, :] = swap_halves(fold(sum_two, p, q))
+
+    def fold_one():
+        for p, q, at in taps():
+            g_pair[at : at + C, :] = jnp.where(low_lanes, fold(sum_one, p, q), g_pair[at : at + C, :])
+
+    accumulate(wins, tiles, sums, (fold_up, fold_two, fold_one))
     frames = pieces.shape[0]
     small[...] = jnp.zeros_like(small)
     total_bias = bias_sums[0, 0:4, :]
@@ -603,7 +623,9 @@
     for ref, ada in ((high_one, ada_one), (high_two, ada_two)):
         ref[...] = jnp.zeros_like(ref)
         ref[C : C + cells, :] = ada[...].astype(f32)
-    embed_grad = exact(one, high_one[...], ((1,), (1,))) + exact(two, high_two[...], ((1,), (1,)))
+    pieces = jnp.concatenate([one, two], axis=1)
+    embed_grad = exact(pieces, jnp.concatenate([high_one[...], high_two[...]], axis=1), ((1,), (1,)))
+    ada_grads = exact(embed, pieces, ((0,), (0,)))
     width = C // (2 * half)
     bias = pltpu.roll(jnp.concatenate([bias, bias], axis=0), (LANES - place * width) % LANES, axis=1)
     extra = below(jnp.concatenate([exact(hot, embed_grad, ((0,), (0,))), bias], axis=0), rows)
@@ -611,8 +633,8 @@
     blocks = (
         sums[:at],
         jnp.where(lane_ids((rows, LANES)) < C, sums[at:], extra),
-        exact(embed, one, ((0,), (0,))),
-        exact(embed, two, ((0,), (0,))),
+        ada_grads[:, :LANES],
+        ada_grads[:, LANES:],
     )
     out[...] = jnp.concatenate(blocks, axis=0).astype(out.dtype)
 
@@ -683,7 +705,7 @@
 def write_backward_operands(turned_pairs, b_one, b_two, b_down, b_up):
     low_lanes = lane_ids((C, LANES)) < C
     zero = jnp.zeros((C, LANES), f32)
-    def taps(pairs, base, step):
+    def taps(pairs, base, step, scale=1.0):
         found = {}
         for p in range(3):
             for q in range(3):
@@ -691,7 +713,7 @@
                 pair = pairs[at // LANES]
                 other = swap_halves(pair)
                 low, high = (pair, other) if at % LANES == 0 else (other, pair)
-                found[p, q] = jnp.where(low_lanes, low, high)
+                found[p, q] = jnp.where(low_lanes, low, high) * scale
         return found
 
     def write(ref, lane, found):
@@ -708,12 +730,12 @@
                         ref[at : at + C, lane + a * LANES : lane + (a + 1) * LANES] = zero.astype(bf16)
 
     one, two = turned_pairs("one"), turned_pairs("two")
-    write(b_one, 0, taps(one, 0, C))
+    write(b_one, 0, taps(one, 0, C, 0.5))
     yield
-    write(b_two, 0, taps(two, 0, C))
+    write(b_two, 0, taps(two, 0, C, 0.5))
     yield
     pairs = turned_pairs("up")
-    write(b_up, 0, taps(pairs, 0, 2 * C))
+    write(b_up, 0, taps(pairs, 0, 2 * C, 0.5))
     yield
     write(b_up, 2 * LANES, taps(pairs, C, 2 * C))
     yield
@@ -743,19 +765,35 @@
     return jnp.concatenate([wide, jnp.zeros((C, LANES), f32)], axis=0).T[: values.shape[1]]
 
 
-def far_kernel(member_ref, array, out, own, other, sent):
-    half, share = out.shape[0], own.shape[0]
-    member = member_ref[0]
-    copies = [
-        pltpu.make_async_copy(array.at[pl.ds(first, ref.shape[0])], ref, sent.at[k])
-        for k, (first, ref) in enumerate(
-            (((1 - member // 2) * half, out), (member * share, own), ((member ^ 1) * share, other))
-        )
-    ]
+def copy_all(pairs, sent):
+    copies = [pltpu.make_async_copy(source, target, sent.at[k]) for k, (source, target) in enumerate(pairs)]
     for copy in copies:
         copy.start()
     for copy in copies:
         copy.wait()
+
+
+def far_part(member, array, out):
+    half = out.shape[0]
+    return array.at[pl.ds((1 - member // 2) * half, half)], out
+
+
+def strip_parts(member, array, own, other):
+    share = own.shape[0]
+    return [
+        (array.at[pl.ds(member * share, share)], own),
+        (array.at[pl.ds((member ^ 1) * share, share)], other),
+    ]
+
+
+def far_kernel(member_ref, array, out, sent):
+    copy_all([far_part(member_ref[0], array, out)], sent)
+
+
+def cut_kernel(member_ref, frames, cotangent, own, other, far, cot_own, cot_other, sent):
+    member = member_ref[0]
+    pairs = strip_parts(member, frames, own, other) + strip_parts(member, cotangent, cot_own, cot_other)
+    copy_all([far_part(member, cotangent, far)] + pairs, sent)
 
 
 def share_kernel(member_ref, far, out):
@@ -832,8 +870,8 @@
 
 
 def prepare_kernel(count, rows, cells, *refs):
-    where_ref, actions, noise_ids, valid, packed, mine, other = refs[:7]
-    styles, biases, ids, work_pair, work_up, work_down, work_one, work_two, work_table = refs[7:]
+    where_ref, packed, mine, other = refs[:4]
+    styles, biases, ids, work_pair, work_up, work_down, work_one, work_two, work_table, hots = refs[4:]
     place, member, frames = where_ref[0], where_ref[1], styles.shape[0]
     style_at, _, size = pack_sizes(rows, cells)
     bias_rows = jnp.zeros(SMALL, f32)
@@ -871,16 +909,12 @@
             ids[at] = extra[ID_ROW : ID_ROW + 8]
     biases[...] = bias_rows + swap_halves(bias_rows)
 
-    lanes = lane_ids((8, LANES))
-    row_at = lax.broadcasted_iota(jnp.int32, (8, LANES), 0)
-    hot = jnp.zeros((8, LANES), f32)
-    for f in range(frames):
-        at = member * frames + f
-        here = jnp.where(lanes == actions[at] + ACT_ROW, valid[at], 0) + jnp.where(lanes == noise_ids[at] + NOISE_ROW, 1, 0)
-        hot = jnp.where(row_at == f, here.astype(f32), hot)
-    hot = hot[:, :TABLE_ROWS].astype(bf16)
+    at = 2 * rows + ID_ROW
+    hots[...] = jnp.zeros_like(hots)
+    write_hots(hots, 0, member * frames, frames, packed[at : at + 8, :].astype(f32))
+    hot = hots[:, :TABLE_ROWS].astype(bf16)
     embed = jnp.concatenate([matmul(hot, work_table[k].astype(bf16)) for k in range(work_table.shape[0])], axis=1)
-    low_lanes = lanes < C
+    low_lanes = lane_ids(SMALL) < C
     for k, work in enumerate((work_one, work_two)):
         style = jnp.dot(embed, work[...], precision=precise, preferred_element_type=f32)
         other = swap_halves(style)
@@ -932,11 +966,6 @@
 
 def cost(macs, moved):
     return pl.CostEstimate(flops=2 * macs, bytes_accessed=moved, transcendentals=0)
-
-
-def fetch_far(member, array):
-    far, own, other = cut_far(member, array, lax.axis_size("rows"))
-    return trade(far, 2), own, other
 
 
 def gather_frames(member, far, own, other, hint=0):
@@ -1032,18 +1061,31 @@
     return pl.BlockSpec(memory_space=space)
 
 
-def cut_far(member, array, count):
-    half, share = ((array.shape[0] // n,) + array.shape[1:] for n in (2, count))
+def cut_far(member, array):
     array = pltpu.with_memory_space_constraint(array, pltpu.HBM)
     return pl.pallas_call(
         far_kernel,
         in_specs=[in_smem(), in_place(pltpu.HBM)],
-        out_specs=[in_vmem()] * 3,
-        out_shape=[pltpu.VMEM(dims, array.dtype) for dims in (half, share, share)],
-        scratch_shapes=[pltpu.SemaphoreType.DMA((3,))],
+        out_specs=in_vmem(),
+        out_shape=pltpu.VMEM((array.shape[0] // 2,) + array.shape[1:], array.dtype),
+        scratch_shapes=[pltpu.SemaphoreType.DMA((1,))],
         compiler_params=params(),
         name="far",
     )(member, array)
+
+
+def cut_others(member, frames, cotangent, count):
+    half, share = ((frames.shape[0] // n,) + frames.shape[1:] for n in (2, count))
+    frames, cotangent = (pltpu.with_memory_space_constraint(array, pltpu.HBM) for array in (frames, cotangent))
+    return pl.pallas_call(
+        cut_kernel,
+        in_specs=[in_smem()] + [in_place(pltpu.HBM)] * 2,
+        out_specs=[in_vmem()] * 5,
+        out_shape=[pltpu.VMEM(dims, frames.dtype) for dims in (share, share, half, share, share)],
+        scratch_shapes=[pltpu.SemaphoreType.DMA((5,))],
+        compiler_params=params(),
+        name="cut",
+    )(member, frames, cotangent)
 
 
 def cut_near(member, other, far, hint):
@@ -1101,10 +1143,10 @@
 )
 
 
-def prepare(where, ids, packed, mine, other, count, rows, cells, frames):
+def prepare(where, packed, mine, other, count, rows, cells, frames):
     found = pl.pallas_call(
         lambda *refs: prepare_kernel(count, rows, cells, *refs),
-        in_specs=[in_smem()] * 4 + [in_vmem()] * 3,
+        in_specs=[in_smem()] + [in_vmem()] * 3,
         out_specs=[in_vmem()] * 6,
         out_shape=[shape((frames,) + SMALL, f32), shape(SMALL, f32), shape((count // 2,) + SMALL, f32)]
         + [shape((n * C, LANES), f32) for n in (9, 18, 9)],
@@ -1112,10 +1154,11 @@
             pltpu.VMEM((count * cells, LANES), f32),
             pltpu.VMEM((count * cells, LANES), f32),
             pltpu.VMEM((count * cells // LANES, TABLE_ROWS, LANES), f32),
+            pltpu.VMEM(SMALL, f32),
         ],
         compiler_params=params(),
         name="prepare",
-    )(where, *ids, packed, mine, other)
+    )(where, packed, mine, other)
     return found[0], found[1], found[2], found[3:]
 
 
@@ -1292,13 +1335,14 @@
     ids = (actions, noise_ids, valid)
     kernels = (conv_one, conv_two, down_kernel, up_kernel)
     biases = (bias_one, bias_two, bias_down, bias_up)
-    fetched = fetch_far(member_box, frames)
+    far = trade(cut_far(member_box, frames), 2)
     packed = pack(ids, kernels, ada_one, ada_two, act_table, noise_table, biases)
     mine = jnp.concatenate([half_trade(packed, at) for at in range(half)], axis=0)
     other = trade(mine, 1)
-    cot_fetched = fetch_far(member_box, cotangent)
-    frame_images, frame_stats = gather_frames(member_box, *fetched, FAR_HINT)
-    styles, bias_rows, group_ids, works = prepare(where, ids, packed, mine, other, count, rows, cells, share)
+    own, near, cot_far, *cot_rest = cut_others(member_box, frames, cotangent, lax.axis_size("rows"))
+    cot_fetched = (trade(cot_far, 2), *cot_rest)
+    frame_images, frame_stats = gather_frames(member_box, far, own, near, FAR_HINT)
+    styles, bias_rows, group_ids, works = prepare(where, packed, mine, other, count, rows, cells, share)
     out, grad_strips, wins, tiles, pieces, bias_sums = layers(
         member_box, frame_images, frame_stats, cot_fetched, styles, bias_rows, works
     )
@@ -1312,7 +1356,8 @@
     sums = reduce_messages(
         where, own, received, hots, act_table, noise_table, ada_one, ada_two, rows, cells, 2 * share
     )
-    parts = [trade(sums, offset) for offset in range(lax.axis_size("rows"))]
+    pair = (sums.astype(f32) + trade(sums, 1).astype(f32)).astype(bf16)
+    parts = [pair, trade(pair, 2)]
     return (result, frames_grad, *finish(parts, rows, cells, width))
 
 
@@ -1342,8 +1387,10 @@
     def gathered(value, axis):
         return lax.all_gather(value, "seq", axis=axis, tiled=True)
 
-    cot_fetched = fetch_far(member_box, cotangent)
-    frame_images, frame_stats = gather_frames(member_box, *fetch_far(member_box, frames))
+    far = trade(cut_far(member_box, frames), 2)
+    own, near, cot_far, *cot_rest = cut_others(member_box, frames, cotangent, lax.axis_size("rows"))
+    cot_fetched = (trade(cot_far, 2), *cot_rest)
+    frame_images, frame_stats = gather_frames(member_box, far, own, near)
     act_full = gathered(act_table, 1)
     noise_full = gathered(noise_table, 1)
     ada_full = gathered(jnp.concatenate([ada_one, ada_two], axis=1), 0).astype(f32)

time: 71.1 us -> 68.9 us (0.969)
  Pallas kernels: 35.5 us -> 34.5 us
    pallas_call x2 -> x1, Pallas kernels: 3.24 us -> 1.06 us  [cut_far(): pl.pallas_call(far_kernel, in_specs=[in_smem(), in_place(pltpu.HBM)], out...]
    pallas_call x0 -> x1, Pallas kernels: none -> 2.18 us  [cut_others(): pl.pallas_call(cut_kernel, in_specs=[in_smem()] + [in_place(pltpu.HBM)] *...]
    ppermute x15 -> x14, starting transfers between devices: 11.4 us -> 11.2 us  [trade(): return lax.ppermute(value, 'rows', [(i, i ^ offset) for i in range(count)])]
    ppermute x15 -> x14, waiting for transfers between devices: 6.95 us -> 6.79 us  [trade(): return lax.ppermute(value, 'rows', [(i, i ^ offset) for i in range(count)])]
  transfers between devices with their start and end apart: 23 -> 22, of which waited for: 7 -> 7; matrix products, arithmetic and copies ran while one was open for 0% -> 0% of each run, Pallas kernels for 45% -> 46%
where the time goes in v7:
time: 68.9 us; the launch traced here: 68.7 us
  Pallas kernels  34.5 us (50%)
  starting transfers between devices  23.2 us (34%)
  waiting for transfers between devices  9.71 us (14%)
  between operations  1.05 us (2%)
    ppermute x8, starting transfers between devices, half_trade(): return lax.ppermute(value, ('seq', 'rows'), pairs)  12 us
    ppermute x14, starting transfers between devices, trade(): return lax.ppermute(value, 'rows', [(i, i ^ offset) for i in range(count)])  11.2 us
    pallas_call x1, Pallas kernels, backward(): pl.pallas_call(lambda *refs: backward_kernel(count, *refs), in_specs=[in_...  8.48 us
    pallas_call x1, Pallas kernels, forward(): pl.pallas_call(lambda *refs: forward_kernel(count, *refs), in_specs=[in_s...  7.43 us
    ppermute x14, waiting for transfers between devices, trade(): return lax.ppermute(value, 'rows', [(i, i ^ offset) for i in range(count)])  6.79 us
    pallas_call x1, Pallas kernels, weight_messages(): pl.pallas_call(lambda *refs: message_kernel(count, rows, *refs), in_specs...  6.43 us
    ppermute x8, waiting for transfers between devices, half_trade(): return lax.ppermute(value, ('seq', 'rows'), pairs)  2.92 us
    pallas_call x2, Pallas kernels, collect_strips(): pl.pallas_call(collect_kernel, grid=(frames,), in_specs=[in_smem()] + [pl...  2.46 us
  transfers between devices with their start and end apart: 22, of which 7 were waited for; matrix products, arithmetic and copies ran while one was open for 0% of the time, Pallas kernels for 46%

profile of v7, /device:TPU:0, one launch (start us, length us, event | category | flops | bytes accessed | tf_op | source)
XLA Modules:
  0.0 68.7 jit_solution(11538264592096281400)
XLA Ops:
  0.6 1.1 %far.1 = bf16[4,16,4096]{2,1,0:T(8,128)(2,1)S(1)} custom-call(s32[1]{0:T(128)} %bitcast.1.member_ref.refs_0_, bf16[8,16,4096]{2,1,0:T(8,128)(2,1)} %array.1), custom_call_target="tpu_custom_call" | custom-call | tf_op jit(solution)/shard_map/far/pallas_call | solution.py:1066
  1.7 3.0 %collective-permute-start = (bf16[4,16,4096]{2,1,0:T(8,128)(2,1)S(1)}, bf16[4,16,4096]{2,1,0:T(8,128)(2,1)S(1)}, u32[]{:S(2)}, u32[]{:S(2)}) collective-permute-start(bf16[4,16,4096]{2,1,0:T(8,128)(2,1)S(1)} %far.1), channel_id=1, source_target_pairs={{0,2},{1,3},{2,0},{3,1},{4,6},{5,7},{6,4},{7,5},{8,10},{9,11},{10,... | collective-permute-start | bytes 1572872 | tf_op jit(solution)/shard_map/ppermute | solution.py:1277
  4.7 1.8 %pack.1.refs_1_ = bf16[288,128]{1,0:T(8,128)(2,1)} custom-call(s32[8]{0:T(128)} %refs_0_.1, s32[8]{0:T(128)} %refs_1_.1, s32[8]{0:T(128)} %refs_2_.1, bf16[64,72]{1,0:T(8,128)(2,1)} %bitcast.19, bf16[64,72]{1,0:T(8,128)(2,1)} %bitcast.20, bf16[64,72]{1,0:T(8,128)(2,1)} %bitcast.21, bf16[64,144]{1,0:T(8,128)(2,1)} %bitcast.15, bf16[32,128]{1,0:T(8,128)(2,1)} %refs_9_.3, ...), custom_call_target="tpu_custom_call" | custom-call | flops 16106127360 | bytes 1048576 | tf_op jit(solution)/shard_map/pack/pallas_call | solution.py:1122
  6.5 3.6 %collective-permute-start.2 = (bf16[288,128]{1,0:T(8,128)(2,1)}, bf16[288,128]{1,0:T(8,128)(2,1)S(1)}, u32[]{:S(2)}, u32[]{:S(2)}) collective-permute-start(bf16[288,128]{1,0:T(8,128)(2,1)} %pack.1.refs_1_), channel_id=1, source_target_pairs={{0,24},{1,29},{2,26},{3,31},{4,28},{5,25},{6,30},{7,27},{8,16},{9,... | collective-permute-start | bytes 221192 | tf_op jit(solution)/shard_map/ppermute | solution.py:1288
  10.1 0.7 collective-permute-start.5
  10.8 0.5 collective-permute-start.4
  11.3 1.2 %collective-permute-start.3 = (bf16[288,128]{1,0:T(8,128)(2,1)}, bf16[288,128]{1,0:T(8,128)(2,1)S(1)}, u32[]{:S(2)}, u32[]{:S(2)}) collective-permute-start(bf16[288,128]{1,0:T(8,128)(2,1)} %pack.1.refs_1_), channel_id=1, source_target_pairs={{0,20},{1,17},{2,22},{3,19},{4,16},{5,21},{6,18},{7,23},{8,28},{9,... | collective-permute-start | bytes 221192 | tf_op jit(solution)/shard_map/ppermute | solution.py:1288
  12.5 2.2 %cut.1 = (bf16[2,16,4096]{2,1,0:T(8,128)(2,1)S(1)}, bf16[2,16,4096]{2,1,0:T(8,128)(2,1)S(1)}, bf16[4,16,4096]{2,1,0:T(8,128)(2,1)}, bf16[2,16,4096]{2,1,0:T(8,128)(2,1)S(1)}, bf16[2,16,4096]{2,1,0:T(8,128)(2,1)S(1)}) custom-call(s32[1]{0:T(128)} %bitcast.1.member_ref.refs_0_, bf16[8,16,4096]{2,1,0:T(8,128)(2,1)} %array.1, bf16[8,16,4096]{2,1,0:T(8,128)(2,1)} %cotangent.1), custom_call_target="tpu_custom_call" | custom-call | tf_op jit(solution)/shard_map/cut/pallas_call | solution.py:1080
  14.7 0.0 collective-permute-done.2
  14.7 0.4 collective-permute-start.7
  15.1 1.6 %collective-permute-done.far = bf16[4,16,4096]{2,1,0:T(8,128)(2,1)S(1)} collective-permute-done((bf16[4,16,4096]{2,1,0:T(8,128)(2,1)S(1)}, bf16[4,16,4096]{2,1,0:T(8,128)(2,1)S(1)}, u32[]{:S(2)}, u32[]{:S(2)}) %collective-permute-start) | collective-permute-done | bytes 524320 | tf_op jit(solution)/shard_map/ppermute | solution.py:1277
  16.7 0.1 collective-permute-start.1
  16.8 1.5 %collective-permute-done.3 = bf16[288,128]{1,0:T(8,128)(2,1)S(1)} collective-permute-done((bf16[288,128]{1,0:T(8,128)(2,1)}, bf16[288,128]{1,0:T(8,128)(2,1)S(1)}, u32[]{:S(2)}, u32[]{:S(2)}) %collective-permute-start.3) | collective-permute-done | bytes 73760 | tf_op jit(solution)/shard_map/ppermute | solution.py:1288
  18.3 0.0 collective-permute-done.4
  18.4 0.0 collective-permute-done.5
  18.4 0.9 %collective-permute-start.6 = (bf16[1152,128]{1,0:T(8,128)(2,1)S(1)}, bf16[1152,128]{1,0:T(8,128)(2,1)S(1)}, u32[]{:S(2)}, u32[]{:S(2)}) collective-permute-start(bf16[1152,128]{1,0:T(8,128)(2,1)S(1)} %constant_dynamic-update-slice_fusion.refs_2_), channel_id=1, source_target_pairs={{0,1},{1,0},{2,3},{3,2},{4,5},{5,4},{6,7},{7,6},{8,9},{9,8},{10,11... | collective-permute-start | bytes 884744 | tf_op jit(solution)/shard_map/ppermute | solution.py:1277
  19.3 0.1 pad_add_fusion.refs_0_
  19.4 1.1 %collective-permute-done.6.refs_3_ = bf16[1152,128]{1,0:T(8,128)(2,1)S(1)} collective-permute-done((bf16[1152,128]{1,0:T(8,128)(2,1)S(1)}, bf16[1152,128]{1,0:T(8,128)(2,1)S(1)}, u32[]{:S(2)}, u32[]{:S(2)}) %collective-permute-start.6) | collective-permute-done | bytes 294944 | tf_op jit(solution)/shard_map/ppermute | solution.py:1277
  20.5 0.0 copy-done
  20.5 1.0 %prepare.1 = (f32[2,8,128]{2,1,0:T(8,128)S(1)}, f32[8,128]{1,0:T(8,128)S(1)}, f32[4,8,128]{2,1,0:T(8,128)S(1)}, f32[576,128]{1,0:T(8,128)S(1)}, f32[1152,128]{1,0:T(8,128)S(1)}, /*index=5*/f32[576,128]{1,0:T(8,128)S(1)}) custom-call(s32[2]{0:T(128)S(1)} %pad_add_fusion.refs_0_, bf16[288,128]{1,0:T(8,128)(2,1)S(1)} %copy-done, ...), custom_call_target="tpu_custom_call" | custom-call | tf_op jit(solution)/shard_map/prepare/pallas_call | solution.py:1147
  21.6 0.0 collective-permute-done.1.near
  21.6 0.5 frames.4
  22.1 7.4 %forward.1 = (bf16[2,16,4096]{2,1,0:T(8,128)(2,1)S(1)}, bf16[2,16,4096]{2,1,0:T(8,128)(2,1)S(1)}, bf16[2,16,4096]{2,1,0:T(8,128)(2,1)S(1)}, bf16[2,16,4096]{2,1,...) custom-call(s32[1]{0:T(128)} %bitcast.1.member_ref.refs_0_, ...), custom_call_target="tpu_custom_call" | custom-call | flops 2048 | bytes 1024 | tf_op jit(solution)/shard_map/forward/pallas_call | solution.py:987
  29.5 0.0 collective-permute-done.7.far
  29.6 0.4 collective-permute-start.8
  30.1 0.1 collective-permute-start.9
  30.2 0.5 collective-permute-start.10
  30.7 1.2 %collective-permute-start.11 = (bf16[2,16,4096]{2,1,0:T(8,128)(2,1)S(1)}, bf16[2,16,4096]{2,1,0:T(8,128)(2,1)S(1)}, u32[]{:S(2)}, u32[]{:S(2)}) collective-permute-start(bf16[2,16,4096]{2,1,0:T(8,128)(2,1)S(1)} %get-tuple-element.132), channel_id=1, source_target_pairs={{0,3},{1,2},{2,1},{3,0},{4,7},{5,6},{6,5},{7,4},{8,11},{9,10},{10,... | collective-permute-start | bytes 786440 | tf_op jit(solution)/shard_map/ppermute | solution.py:1277
  31.9 0.0 collective-permute-done.8.near
  31.9 0.5 frames.5
  32.5 8.5 %backward.1 = (bf16[2,16,4096]{2,1,0:T(8,128)(2,1)S(1)}, bf16[2,16,4096]{2,1,0:T(8,128)(2,1)S(1)}, bf16[2,16,4096]{2,1,0:T(8,128)(2,1)S(1)}, bf16[2,16,4096]{2,1...) custom-call(s32[1]{0:T(128)} %bitcast.1.member_ref.refs_0_, ...), custom_call_target="tpu_custom_call" | custom-call | flops 5368709120 | bytes 20971520 | tf_op jit(solution)/shard_map/backward/pallas_call | solution.py:1013
  40.9 0.5 collective-permute-start.17
  41.4 0.5 collective-permute-start.18
  41.9 6.4 %weights.1 = (f32[864,128]{1,0:T(8,128)S(1)}, f32[16,128]{1,0:T(8,128)S(1)}, bf16[864,128]{1,0:T(8,128)(2,1)S(1)}, f32[16,128]{1,0:T(8,128)S(1)}) custom-call(s32[2]{0:T(128)S(1)} %pad_add_fusion.refs_0_, bf16[2,4,33,32,128]{4,3,2,1,0:T(8,128)(2,1)S(1)} %get-tuple-element.99.refs_1_, bf16[2,4,33,32,128]{4,3,2,1,0:T(8,128)(2,1)S(1)} %get-tuple-element.100.refs_2_, ...), custom_call_target="tpu_custom_call" | custom-call | flops 5368709120 | bytes 12582912 | tf_op jit(solution)/shard_map/weights/pallas_call | solution.py:1168
  48.4 0.0 collective-permute-done.9.refs_1_
  48.4 0.0 collective-permute-done.10.refs_2_
  48.4 0.0 collective-permute-done.11.refs_3_
  48.4 0.1 collective-permute-start.12
  48.5 1.6 %collective-permute-start.19 = (bf16[2,16,4096]{2,1,0:T(8,128)(2,1)S(1)}, bf16[2,16,4096]{2,1,0:T(8,128)(2,1)S(1)}, u32[]{:S(2)}, u32[]{:S(2)}) collective-permute-start(bf16[2,16,4096]{2,1,0:T(8,128)(2,1)S(1)} %get-tuple-element.145), channel_id=1, source_target_pairs={{0,3},{1,2},{2,1},{3,0},{4,7},{5,6},{6,5},{7,4},{8,11},{9,10},{10,... | collective-permute-start | bytes 786440 | tf_op jit(solution)/shard_map/ppermute | solution.py:1277
  50.1 0.0 collective-permute-done.12.refs_3_
  50.1 0.6 join.1
  50.7 3.3 %collective-permute-start.13 = (bf16[216,128]{1,0:T(8,128)(2,1)S(1)}, bf16[216,128]{1,0:T(8,128)(2,1)S(1)}, u32[]{:S(2)}, u32[]{:S(2)}) collective-permute-start(bf16[216,128]{1,0:T(8,128)(2,1)S(1)} %get-tuple-element.134), channel_id=1, source_target_pairs={{0,24},{1,29},{2,26},{3,31},{4,28},{5,25},{6,30},{7,27},{8,16},{9,... | collective-permute-start | bytes 165896 | tf_op jit(solution)/shard_map/ppermute | solution.py:1288
  54.0 0.4 collective-permute-start.14
  54.4 0.0 collective-permute-done.17.refs_1_
  54.4 1.6 %collective-permute-start.15 = (bf16[216,128]{1,0:T(8,128)(2,1)S(1)}, bf16[216,128]{1,0:T(8,128)(2,1)S(1)}, u32[]{:S(2)}, u32[]{:S(2)}) collective-permute-start(bf16[216,128]{1,0:T(8,128)(2,1)S(1)} %get-tuple-element.136), channel_id=1, source_target_pairs={{0,12},{1,9},{2,14},{3,11},{4,8},{5,13},{6,10},{7,15},{8,4},{9,1},... | collective-permute-start | bytes 165896 | tf_op jit(solution)/shard_map/ppermute | solution.py:1288
  56.1 0.0 collective-permute-done.18.refs_2_
  56.1 0.7 collective-permute-start.16
  56.7 1.0 %collect.2 = bf16[4,2,16,4096]{3,2,1,0:T(8,128)(2,1)} custom-call(s32[1]{0:T(128)} %bitcast.1.member_ref.refs_0_, bf16[2,16,4096]{2,1,0:T(8,128)(2,1)S(1)} %get-tuple-element.138.refs_0_, bf16[2,16,4096]{2,1,0:T(8,128)(2,1)S(1)} %collective-permute-done.9.refs_1_, bf16[2,16,4096]{2,1,0:T(8,128)(2,1)S(1)} %collective-permute-done.10.refs_2_, ...), custom_call_target="tpu_custom_call" | custom-call | tf_op jit(solution)/shard_map/collect/pallas_call | solution.py:1251
  57.8 0.0 collective-permute-done.19.refs_3_
  57.8 1.4 %collect.3 = f32[4,2,16,4096]{3,2,1,0:T(8,128)} custom-call(s32[1]{0:T(128)} %bitcast.1.member_ref.refs_0_, bf16[2,16,4096]{2,1,0:T(8,128)(2,1)S(1)} %get-tuple-element.142.refs_0_, bf16[2,16,4096]{2,1,0:T(8,128)(2,1)S(1)} %collective-permute-done.17.refs_1_, bf16[2,16,4096]{2,1,0:T(8,128)(2,1)S(1)} %collective-permute-done.18.refs_2_, ...), custom_call_target="tpu_custom_call" | custom-call | tf_op jit(solution)/shard_map/collect/pallas_call | solution.py:1251
  59.2 0.0 collective-permute-done.13.refs_2_
  59.2 1.1 %collective-permute-done.14.refs_3_ = bf16[216,128]{1,0:T(8,128)(2,1)S(1)} collective-permute-done((bf16[216,128]{1,0:T(8,128)(2,1)S(1)}, bf16[216,128]{1,0:T(8,128)(2,1)S(1)}, u32[]{:S(2)}, u32[]{:S(2)}) %collective-permute-start.14) | collective-permute-done | bytes 55328 | tf_op jit(solution)/shard_map/ppermute | solution.py:1288
  60.3 0.3 collective-permute-done.15.refs_4_
  60.6 0.0 collective-permute-done.16.refs_5_
  60.6 0.0 copy-done.1
  60.6 0.0 copy-done.2
  60.6 0.0 copy-done.3
  60.7 0.0 copy-done.4
  60.7 1.1 %reduce.1 = bf16[280,128]{1,0:T(8,128)(2,1)S(1)} custom-call(s32[2]{0:T(128)S(1)} %pad_add_fusion.refs_0_, f32[216,128]{1,0:T(8,128)S(1)} %get-tuple-element.148.refs_1_, bf16[216,128]{1,0:T(8,128)(2,1)S(1)} %collective-permute-done.13.refs_2_, bf16[216,128]{1,0:T(8,128)(2,1)S(1)} %collective-permute-done.14.refs_3_, ...), custom_call_target="tpu_custom_call" | custom-call | tf_op jit(solution)/shard_map/reduce/pallas_call | solution.py:1199
  61.8 0.5 collective-permute-start.20
  62.2 0.9 %collective-permute-done.20 = bf16[280,128]{1,0:T(8,128)(2,1)S(1)} collective-permute-done((bf16[280,128]{1,0:T(8,128)(2,1)S(1)}, bf16[280,128]{1,0:T(8,128)(2,1)S(1)}, u32[]{:S(2)}, u32[]{:S(2)}) %collective-permute-start.20) | collective-permute-done | bytes 71712 | tf_op jit(solution)/shard_map/ppermute | solution.py:1277
  63.1 1.4 %collective-permute-start.21 = (bf16[280,128]{1,0:T(8,128)(2,1)S(1)}, bf16[280,128]{1,0:T(8,128)(2,1)S(1)}, u32[]{:S(2)}, u32[]{:S(2)}) collective-permute-start(bf16[280,128]{1,0:T(8,128)(2,1)S(1)} %add_convert_fusion.refs_0_), channel_id=1, source_target_pairs={{0,2},{1,3},{2,0},{3,1},{4,6},{5,7},{6,4},{7,5},{8,10},{9,11},{10,... | collective-permute-start | bytes 215048 | tf_op jit(solution)/shard_map/ppermute | solution.py:1277
  64.5 3.2 %collective-permute-done.21.refs_1_ = bf16[280,128]{1,0:T(8,128)(2,1)S(1)} collective-permute-done((bf16[280,128]{1,0:T(8,128)(2,1)S(1)}, bf16[280,128]{1,0:T(8,128)(2,1)S(1)}, u32[]{:S(2)}, u32[]{:S(2)}) %collective-permute-start.21) | collective-permute-done | bytes 71712 | tf_op jit(solution)/shard_map/ppermute | solution.py:1277
  67.7 0.8 %finish.1 = (f32[18,32]{1,0:T(8,128)}, f32[32,32]{1,0:T(8,128)}, f32[32,128]{1,0:T(8,128)}, f32[32,128]{1,0:T(8,128)}, f32[64,72]{1,0:T(8,128)}, /*index=5*/f32[...) custom-call(bf16[280,128]{1,0:T(8,128)(2,1)S(1)} %add_convert_fusion, ...), custom_call_target="tpu_custom_call" | custom-call | tf_op jit(solution)/shard_map/finish/pallas_call | solution.py:1217
  (16 shorter events, 0.2 us)
Async XLA Ops:
  1.7 15.0 %collective-permute-start = (bf16[4,16,4096]{2,1,0:T(8,128)(2,1)S(1)}, bf16[4,16,4096]{2,1,0:T(8,128)(2,1)S(1)}, u32[]{:S(2)}, u32[]{:S(2)}) collective-permute-start(bf16[4,16,4096]{2,1,0:T(8,128)(2,1)S(1)} %far.1), channel_id=1, source_target_pairs={{0,2},{1,3},{2,0},{3,1},{4,6},{5,7},{6,4},{7,5},{8,10},{9,11},{10,... | collective-permute-start | bytes 1572872 | tf_op jit(solution)/shard_map/ppermute | solution.py:1277
  6.5 8.2 %collective-permute-start.2 = (bf16[288,128]{1,0:T(8,128)(2,1)}, bf16[288,128]{1,0:T(8,128)(2,1)S(1)}, u32[]{:S(2)}, u32[]{:S(2)}) collective-permute-start(bf16[288,128]{1,0:T(8,128)(2,1)} %pack.1.refs_1_), channel_id=1, source_target_pairs={{0,24},{1,29},{2,26},{3,31},{4,28},{5,25},{6,30},{7,27},{8,16},{9,... | collective-permute-start | bytes 221192 | tf_op jit(solution)/shard_map/ppermute | solution.py:1288
  10.1 8.2 %collective-permute-start.5 = (bf16[288,128]{1,0:T(8,128)(2,1)}, bf16[288,128]{1,0:T(8,128)(2,1)S(1)}, u32[]{:S(2)}, u32[]{:S(2)}) collective-permute-start(bf16[288,128]{1,0:T(8,128)(2,1)} %pack.1.refs_1_), channel_id=1, source_target_pairs={{1,5},{3,7},{5,1},{7,3},{9,13},{11,15},{13,9},{15,11},{17,21},{19,... | collective-permute-start | bytes 221192 | tf_op jit(solution)/shard_map/ppermute | solution.py:1288
  10.8 7.5 %collective-permute-start.4 = (bf16[288,128]{1,0:T(8,128)(2,1)}, bf16[288,128]{1,0:T(8,128)(2,1)S(1)}, u32[]{:S(2)}, u32[]{:S(2)}) collective-permute-start(bf16[288,128]{1,0:T(8,128)(2,1)} %pack.1.refs_1_), channel_id=1, source_target_pairs={{0,12},{1,9},{2,14},{3,11},{4,8},{5,13},{6,10},{7,15},{8,4},{9,1},... | collective-permute-start | bytes 221192 | tf_op jit(solution)/shard_map/ppermute | solution.py:1288
  11.3 7.0 %collective-permute-start.3 = (bf16[288,128]{1,0:T(8,128)(2,1)}, bf16[288,128]{1,0:T(8,128)(2,1)S(1)}, u32[]{:S(2)}, u32[]{:S(2)}) collective-permute-start(bf16[288,128]{1,0:T(8,128)(2,1)} %pack.1.refs_1_), channel_id=1, source_target_pairs={{0,20},{1,17},{2,22},{3,19},{4,16},{5,21},{6,18},{7,23},{8,28},{9,... | collective-permute-start | bytes 221192 | tf_op jit(solution)/shard_map/ppermute | solution.py:1288
  14.7 14.8 %collective-permute-start.7 = (bf16[4,16,4096]{2,1,0:T(8,128)(2,1)}, bf16[4,16,4096]{2,1,0:T(8,128)(2,1)S(1)}, u32[]{:S(2)}, u32[]{:S(2)}) collective-permute-start(bf16[4,16,4096]{2,1,0:T(8,128)(2,1)} %get-tuple-element.104), channel_id=1, source_target_pairs={{0,2},{1,3},{2,0},{3,1},{4,6},{5,7},{6,4},{7,5},{8,10},{9,11},{10,... | collective-permute-start | bytes 1572872 | tf_op jit(solution)/shard_map/ppermute | solution.py:1277
  16.7 3.9 %copy-start = (bf16[288,128]{1,0:T(8,128)(2,1)S(1)}, bf16[288,128]{1,0:T(8,128)(2,1)}, u32[]{:S(2)}) copy-start(bf16[288,128]{1,0:T(8,128)(2,1)} %pack.1.refs_1_) | copy-start | bytes 221188
  16.7 4.8 %collective-permute-start.1 = (bf16[4,16,4096]{2,1,0:T(8,128)(2,1)S(1)}, bf16[4,16,4096]{2,1,0:T(8,128)(2,1)S(1)}, u32[]{:S(2)}, u32[]{:S(2)}) collective-permute-start(bf16[4,16,4096]{2,1,0:T(8,128)(2,1)S(1)} %near.2), channel_id=1, source_target_pairs={{0,1},{1,0},{2,3},{3,2},{4,5},{5,4},{6,7},{7,6},{8,9},{9,8},{10,11... | collective-permute-start | bytes 1572872 | tf_op jit(solution)/shard_map/ppermute | solution.py:1277
  18.4 2.1 %collective-permute-start.6 = (bf16[1152,128]{1,0:T(8,128)(2,1)S(1)}, bf16[1152,128]{1,0:T(8,128)(2,1)S(1)}, u32[]{:S(2)}, u32[]{:S(2)}) collective-permute-start(bf16[1152,128]{1,0:T(8,128)(2,1)S(1)} %constant_dynamic-update-slice_fusion.refs_2_), channel_id=1, source_target_pairs={{0,1},{1,0},{2,3},{3,2},{4,5},{5,4},{6,7},{7,6},{8,9},{9,8},{10,11... | collective-permute-start | bytes 884744 | tf_op jit(solution)/shard_map/ppermute | solution.py:1277
  29.6 2.3 %collective-permute-start.8 = (bf16[4,16,4096]{2,1,0:T(8,128)(2,1)S(1)}, bf16[4,16,4096]{2,1,0:T(8,128)(2,1)S(1)}, u32[]{:S(2)}, u32[]{:S(2)}) collective-permute-start(bf16[4,16,4096]{2,1,0:T(8,128)(2,1)S(1)} %near.3), channel_id=1, source_target_pairs={{0,1},{1,0},{2,3},{3,2},{4,5},{5,4},{6,7},{7,6},{8,9},{9,8},{10,11... | collective-permute-start | bytes 1572872 | tf_op jit(solution)/shard_map/ppermute | solution.py:1277
  30.1 18.3 %collective-permute-start.9 = (bf16[2,16,4096]{2,1,0:T(8,128)(2,1)S(1)}, bf16[2,16,4096]{2,1,0:T(8,128)(2,1)S(1)}, u32[]{:S(2)}, u32[]{:S(2)}) collective-permute-start(bf16[2,16,4096]{2,1,0:T(8,128)(2,1)S(1)} %get-tuple-element.130), channel_id=1, source_target_pairs={{0,1},{1,0},{2,3},{3,2},{4,5},{5,4},{6,7},{7,6},{8,9},{9,8},{10,11... | collective-permute-start | bytes 786440 | tf_op jit(solution)/shard_map/ppermute | solution.py:1277
  30.2 18.2 %collective-permute-start.10 = (bf16[2,16,4096]{2,1,0:T(8,128)(2,1)S(1)}, bf16[2,16,4096]{2,1,0:T(8,128)(2,1)S(1)}, u32[]{:S(2)}, u32[]{:S(2)}) collective-permute-start(bf16[2,16,4096]{2,1,0:T(8,128)(2,1)S(1)} %get-tuple-element.131), channel_id=1, source_target_pairs={{0,2},{1,3},{2,0},{3,1},{4,6},{5,7},{6,4},{7,5},{8,10},{9,11},{10,... | collective-permute-start | bytes 786440 | tf_op jit(solution)/shard_map/ppermute | solution.py:1277
  30.7 17.7 %collective-permute-start.11 = (bf16[2,16,4096]{2,1,0:T(8,128)(2,1)S(1)}, bf16[2,16,4096]{2,1,0:T(8,128)(2,1)S(1)}, u32[]{:S(2)}, u32[]{:S(2)}) collective-permute-start(bf16[2,16,4096]{2,1,0:T(8,128)(2,1)S(1)} %get-tuple-element.132), channel_id=1, source_target_pairs={{0,3},{1,2},{2,1},{3,0},{4,7},{5,6},{6,5},{7,4},{8,11},{9,10},{10,... | collective-permute-start | bytes 786440 | tf_op jit(solution)/shard_map/ppermute | solution.py:1277
  40.9 13.5 %collective-permute-start.17 = (bf16[2,16,4096]{2,1,0:T(8,128)(2,1)S(1)}, bf16[2,16,4096]{2,1,0:T(8,128)(2,1)S(1)}, u32[]{:S(2)}, u32[]{:S(2)}) collective-permute-start(bf16[2,16,4096]{2,1,0:T(8,128)(2,1)S(1)} %get-tuple-element.143), channel_id=1, source_target_pairs={{0,1},{1,0},{2,3},{3,2},{4,5},{5,4},{6,7},{7,6},{8,9},{9,8},{10,11... | collective-permute-start | bytes 786440 | tf_op jit(solution)/shard_map/ppermute | solution.py:1277
  41.4 14.6 %collective-permute-start.18 = (bf16[2,16,4096]{2,1,0:T(8,128)(2,1)S(1)}, bf16[2,16,4096]{2,1,0:T(8,128)(2,1)S(1)}, u32[]{:S(2)}, u32[]{:S(2)}) collective-permute-start(bf16[2,16,4096]{2,1,0:T(8,128)(2,1)S(1)} %get-tuple-element.144), channel_id=1, source_target_pairs={{0,2},{1,3},{2,0},{3,1},{4,6},{5,7},{6,4},{7,5},{8,10},{9,11},{10,... | collective-permute-start | bytes 786440 | tf_op jit(solution)/shard_map/ppermute | solution.py:1277
  48.4 1.7 %collective-permute-start.12 = (bf16[864,128]{1,0:T(8,128)(2,1)S(1)}, bf16[864,128]{1,0:T(8,128)(2,1)S(1)}, u32[]{:S(2)}, u32[]{:S(2)}) collective-permute-start(bf16[864,128]{1,0:T(8,128)(2,1)S(1)} %get-tuple-element.133), channel_id=1, source_target_pairs={{0,1},{1,0},{2,3},{3,2},{4,5},{5,4},{6,7},{7,6},{8,9},{9,8},{10,11... | collective-permute-start | bytes 663560 | tf_op jit(solution)/shard_map/ppermute | solution.py:1277
  48.5 9.3 %collective-permute-start.19 = (bf16[2,16,4096]{2,1,0:T(8,128)(2,1)S(1)}, bf16[2,16,4096]{2,1,0:T(8,128)(2,1)S(1)}, u32[]{:S(2)}, u32[]{:S(2)}) collective-permute-start(bf16[2,16,4096]{2,1,0:T(8,128)(2,1)S(1)} %get-tuple-element.145), channel_id=1, source_target_pairs={{0,3},{1,2},{2,1},{3,0},{4,7},{5,6},{6,5},{7,4},{8,11},{9,10},{10,... | collective-permute-start | bytes 786440 | tf_op jit(solution)/shard_map/ppermute | solution.py:1277
  50.7 8.5 %collective-permute-start.13 = (bf16[216,128]{1,0:T(8,128)(2,1)S(1)}, bf16[216,128]{1,0:T(8,128)(2,1)S(1)}, u32[]{:S(2)}, u32[]{:S(2)}) collective-permute-start(bf16[216,128]{1,0:T(8,128)(2,1)S(1)} %get-tuple-element.134), channel_id=1, source_target_pairs={{0,24},{1,29},{2,26},{3,31},{4,28},{5,25},{6,30},{7,27},{8,16},{9,... | collective-permute-start | bytes 165896 | tf_op jit(solution)/shard_map/ppermute | solution.py:1288
  54.0 6.3 %collective-permute-start.14 = (bf16[216,128]{1,0:T(8,128)(2,1)S(1)}, bf16[216,128]{1,0:T(8,128)(2,1)S(1)}, u32[]{:S(2)}, u32[]{:S(2)}) collective-permute-start(bf16[216,128]{1,0:T(8,128)(2,1)S(1)} %get-tuple-element.135), channel_id=1, source_target_pairs={{0,20},{1,17},{2,22},{3,19},{4,16},{5,21},{6,18},{7,23},{8,28},{9,... | collective-permute-start | bytes 165896 | tf_op jit(solution)/shard_map/ppermute | solution.py:1288
  54.4 6.2 %collective-permute-start.15 = (bf16[216,128]{1,0:T(8,128)(2,1)S(1)}, bf16[216,128]{1,0:T(8,128)(2,1)S(1)}, u32[]{:S(2)}, u32[]{:S(2)}) collective-permute-start(bf16[216,128]{1,0:T(8,128)(2,1)S(1)} %get-tuple-element.136), channel_id=1, source_target_pairs={{0,12},{1,9},{2,14},{3,11},{4,8},{5,13},{6,10},{7,15},{8,4},{9,1},... | collective-permute-start | bytes 165896 | tf_op jit(solution)/shard_map/ppermute | solution.py:1288
  56.1 4.6 %collective-permute-start.16 = (bf16[216,128]{1,0:T(8,128)(2,1)S(1)}, bf16[216,128]{1,0:T(8,128)(2,1)S(1)}, u32[]{:S(2)}, u32[]{:S(2)}) collective-permute-start(bf16[216,128]{1,0:T(8,128)(2,1)S(1)} %get-tuple-element.137), channel_id=1, source_target_pairs={{1,5},{3,7},{5,1},{7,3},{9,13},{11,15},{13,9},{15,11},{17,21},{19,... | collective-permute-start | bytes 165896 | tf_op jit(solution)/shard_map/ppermute | solution.py:1288
  57.8 2.9 %copy-start.1 = (bf16[32,128]{1,0:T(8,128)(2,1)S(1)}, bf16[32,128]{1,0:T(8,128)(2,1)}, u32[]{:S(2)}) copy-start(bf16[32,128]{1,0:T(8,128)(2,1)} %refs_9_.3) | copy-start | bytes 24580
  57.8 2.9 %copy-start.2 = (bf16[32,128]{1,0:T(8,128)(2,1)S(1)}, bf16[32,128]{1,0:T(8,128)(2,1)}, u32[]{:S(2)}) copy-start(bf16[32,128]{1,0:T(8,128)(2,1)} %refs_10_.3) | copy-start | bytes 24580
  57.8 2.9 %copy-start.3 = (bf16[32,32]{1,0:T(8,128)(2,1)S(1)}, bf16[32,32]{1,0:T(8,128)(2,1)}, u32[]{:S(2)}) copy-start(bf16[32,32]{1,0:T(8,128)(2,1)} %refs_8_.3) | copy-start | bytes 6148
  57.8 2.9 %copy-start.4 = (bf16[18,32]{1,0:T(8,128)(2,1)S(1)}, bf16[18,32]{1,0:T(8,128)(2,1)}, u32[]{:S(2)}) copy-start(bf16[18,32]{1,0:T(8,128)(2,1)} %refs_7_.3) | copy-start | bytes 3460
  61.8 1.4 %collective-permute-start.20 = (bf16[280,128]{1,0:T(8,128)(2,1)S(1)}, bf16[280,128]{1,0:T(8,128)(2,1)S(1)}, u32[]{:S(2)}, u32[]{:S(2)}) collective-permute-start(bf16[280,128]{1,0:T(8,128)(2,1)S(1)} %reduce.1), channel_id=1, source_target_pairs={{0,1},{1,0},{2,3},{3,2},{4,5},{5,4},{6,7},{7,6},{8,9},{9,8},{10,11... | collective-permute-start | bytes 215048 | tf_op jit(solution)/shard_map/ppermute | solution.py:1277
  63.1 4.5 %collective-permute-start.21 = (bf16[280,128]{1,0:T(8,128)(2,1)S(1)}, bf16[280,128]{1,0:T(8,128)(2,1)S(1)}, u32[]{:S(2)}, u32[]{:S(2)}) collective-permute-start(bf16[280,128]{1,0:T(8,128)(2,1)S(1)} %add_convert_fusion.refs_0_), channel_id=1, source_target_pairs={{0,2},{1,3},{2,0},{3,1},{4,6},{5,7},{6,4},{7,5},{8,10},{9,11},{10,... | collective-permute-start | bytes 215048 | tf_op jit(solution)/shard_map/ppermute | solution.py:1277

commit v8 on v7

--- a/solution.py
+++ b/solution.py
@@ -118,11 +118,11 @@
             image[j, pl.ds(start, rows), :] = strip[:, j * LANES : (j + 1) * LANES].astype(f32)
 
 
-def store_strips(member, image, f, strips):
+def store_strips(member, image, f, strips, pairs=range(PAIRS)):
     for offset, strip in enumerate(strips):
         rows = strip.shape[1]
         start = strip_start(member, offset, rows)
-        for j in range(PAIRS):
+        for j in pairs:
             strip[f, :, j * LANES : (j + 1) * LANES] = image[j, pl.ds(start, rows), :].astype(strip.dtype)
 
 
@@ -395,10 +395,10 @@
                 x = parity_rows(frame_image, parity, j)
                 g = pre_grad[parity, j] * gain_one + (constant_one - x * slope_one) + level_grad[parity, j]
                 image[j, pl.ds(parity, HALF, stride=2), :] = g
+            store_strips(member, image, f, out, (j,))
             return carry
 
         over_pairs(frame_body, 0)
-        store_strips(member, image, f, out)
         for k, value in enumerate((scale_one, shift_one, scale_two, shift_two)):
             pieces[k : k + 1, :] = value[0:1]
         pieces[4:8, :] = jnp.zeros((4, LANES), f32)

time: 68.9 us -> 68.8 us (level)
  no operation moved by 1% of the time
where the time goes in v8:
time: 68.8 us; the launch traced here: 68.5 us
  Pallas kernels  34.3 us (50%)
  starting transfers between devices  23.2 us (34%)
  waiting for transfers between devices  9.79 us (14%)
  between operations  1.05 us (2%)
    ppermute x8, starting transfers between devices, half_trade(): return lax.ppermute(value, ('seq', 'rows'), pairs)  12 us
    ppermute x14, starting transfers between devices, trade(): return lax.ppermute(value, 'rows', [(i, i ^ offset) for i in range(count)])  11.2 us
    pallas_call x1, Pallas kernels, backward(): pl.pallas_call(lambda *refs: backward_kernel(count, *refs), in_specs=[in_...  8.28 us
    pallas_call x1, Pallas kernels, forward(): pl.pallas_call(lambda *refs: forward_kernel(count, *refs), in_specs=[in_s...  7.43 us
    ppermute x14, waiting for transfers between devices, trade(): return lax.ppermute(value, 'rows', [(i, i ^ offset) for i in range(count)])  6.82 us
    pallas_call x1, Pallas kernels, weight_messages(): pl.pallas_call(lambda *refs: message_kernel(count, rows, *refs), in_specs...  6.43 us
    ppermute x8, waiting for transfers between devices, half_trade(): return lax.ppermute(value, ('seq', 'rows'), pairs)  2.96 us
    pallas_call x2, Pallas kernels, collect_strips(): pl.pallas_call(collect_kernel, grid=(frames,), in_specs=[in_smem()] + [pl...  2.46 us
  transfers between devices with their start and end apart: 22, of which 7 were waited for; matrix products, arithmetic and copies ran while one was open for 0% of the time, Pallas kernels for 46%

profile of v8, /device:TPU:0, one launch (start us, length us, event | category | flops | bytes accessed | tf_op | source)
XLA Modules:
  0.0 68.5 jit_solution(16810135883368086755)
XLA Ops:
  0.6 1.1 %far.1 = bf16[4,16,4096]{2,1,0:T(8,128)(2,1)S(1)} custom-call(s32[1]{0:T(128)} %bitcast.1.member_ref.refs_0_, bf16[8,16,4096]{2,1,0:T(8,128)(2,1)} %array.1), custom_call_target="tpu_custom_call" | custom-call | tf_op jit(solution)/shard_map/far/pallas_call | solution.py:1066
  1.7 3.0 %collective-permute-start = (bf16[4,16,4096]{2,1,0:T(8,128)(2,1)S(1)}, bf16[4,16,4096]{2,1,0:T(8,128)(2,1)S(1)}, u32[]{:S(2)}, u32[]{:S(2)}) collective-permute-start(bf16[4,16,4096]{2,1,0:T(8,128)(2,1)S(1)} %far.1), channel_id=1, source_target_pairs={{0,2},{1,3},{2,0},{3,1},{4,6},{5,7},{6,4},{7,5},{8,10},{9,11},{10,... | collective-permute-start | bytes 1572872 | tf_op jit(solution)/shard_map/ppermute | solution.py:1277
  4.7 1.8 %pack.1.refs_1_ = bf16[288,128]{1,0:T(8,128)(2,1)} custom-call(s32[8]{0:T(128)} %refs_0_.1, s32[8]{0:T(128)} %refs_1_.1, s32[8]{0:T(128)} %refs_2_.1, bf16[64,72]{1,0:T(8,128)(2,1)} %bitcast.19, bf16[64,72]{1,0:T(8,128)(2,1)} %bitcast.20, bf16[64,72]{1,0:T(8,128)(2,1)} %bitcast.21, bf16[64,144]{1,0:T(8,128)(2,1)} %bitcast.15, bf16[32,128]{1,0:T(8,128)(2,1)} %refs_9_.3, ...), custom_call_target="tpu_custom_call" | custom-call | flops 16106127360 | bytes 1048576 | tf_op jit(solution)/shard_map/pack/pallas_call | solution.py:1122
  6.5 3.6 %collective-permute-start.2 = (bf16[288,128]{1,0:T(8,128)(2,1)}, bf16[288,128]{1,0:T(8,128)(2,1)S(1)}, u32[]{:S(2)}, u32[]{:S(2)}) collective-permute-start(bf16[288,128]{1,0:T(8,128)(2,1)} %pack.1.refs_1_), channel_id=1, source_target_pairs={{0,24},{1,29},{2,26},{3,31},{4,28},{5,25},{6,30},{7,27},{8,16},{9,... | collective-permute-start | bytes 221192 | tf_op jit(solution)/shard_map/ppermute | solution.py:1288
  10.1 0.7 collective-permute-start.5
  10.8 0.5 collective-permute-start.4
  11.3 1.2 %collective-permute-start.3 = (bf16[288,128]{1,0:T(8,128)(2,1)}, bf16[288,128]{1,0:T(8,128)(2,1)S(1)}, u32[]{:S(2)}, u32[]{:S(2)}) collective-permute-start(bf16[288,128]{1,0:T(8,128)(2,1)} %pack.1.refs_1_), channel_id=1, source_target_pairs={{0,20},{1,17},{2,22},{3,19},{4,16},{5,21},{6,18},{7,23},{8,28},{9,... | collective-permute-start | bytes 221192 | tf_op jit(solution)/shard_map/ppermute | solution.py:1288
  12.5 2.2 %cut.1 = (bf16[2,16,4096]{2,1,0:T(8,128)(2,1)S(1)}, bf16[2,16,4096]{2,1,0:T(8,128)(2,1)S(1)}, bf16[4,16,4096]{2,1,0:T(8,128)(2,1)}, bf16[2,16,4096]{2,1,0:T(8,128)(2,1)S(1)}, bf16[2,16,4096]{2,1,0:T(8,128)(2,1)S(1)}) custom-call(s32[1]{0:T(128)} %bitcast.1.member_ref.refs_0_, bf16[8,16,4096]{2,1,0:T(8,128)(2,1)} %array.1, bf16[8,16,4096]{2,1,0:T(8,128)(2,1)} %cotangent.1), custom_call_target="tpu_custom_call" | custom-call | tf_op jit(solution)/shard_map/cut/pallas_call | solution.py:1080
  14.7 0.0 collective-permute-done.2
  14.7 0.4 collective-permute-start.7
  15.1 1.6 %collective-permute-done.far = bf16[4,16,4096]{2,1,0:T(8,128)(2,1)S(1)} collective-permute-done((bf16[4,16,4096]{2,1,0:T(8,128)(2,1)S(1)}, bf16[4,16,4096]{2,1,0:T(8,128)(2,1)S(1)}, u32[]{:S(2)}, u32[]{:S(2)}) %collective-permute-start) | collective-permute-done | bytes 524320 | tf_op jit(solution)/shard_map/ppermute | solution.py:1277
  16.7 0.1 collective-permute-start.1
  16.8 1.5 %collective-permute-done.3 = bf16[288,128]{1,0:T(8,128)(2,1)S(1)} collective-permute-done((bf16[288,128]{1,0:T(8,128)(2,1)}, bf16[288,128]{1,0:T(8,128)(2,1)S(1)}, u32[]{:S(2)}, u32[]{:S(2)}) %collective-permute-start.3) | collective-permute-done | bytes 73760 | tf_op jit(solution)/shard_map/ppermute | solution.py:1288
  18.3 0.0 collective-permute-done.4
  18.4 0.0 collective-permute-done.5
  18.4 0.9 %collective-permute-start.6 = (bf16[1152,128]{1,0:T(8,128)(2,1)S(1)}, bf16[1152,128]{1,0:T(8,128)(2,1)S(1)}, u32[]{:S(2)}, u32[]{:S(2)}) collective-permute-start(bf16[1152,128]{1,0:T(8,128)(2,1)S(1)} %constant_dynamic-update-slice_fusion.refs_2_), channel_id=1, source_target_pairs={{0,1},{1,0},{2,3},{3,2},{4,5},{5,4},{6,7},{7,6},{8,9},{9,8},{10,11... | collective-permute-start | bytes 884744 | tf_op jit(solution)/shard_map/ppermute | solution.py:1277
  19.3 0.1 pad_add_fusion.refs_0_
  19.4 1.1 %collective-permute-done.6.refs_3_ = bf16[1152,128]{1,0:T(8,128)(2,1)S(1)} collective-permute-done((bf16[1152,128]{1,0:T(8,128)(2,1)S(1)}, bf16[1152,128]{1,0:T(8,128)(2,1)S(1)}, u32[]{:S(2)}, u32[]{:S(2)}) %collective-permute-start.6) | collective-permute-done | bytes 294944 | tf_op jit(solution)/shard_map/ppermute | solution.py:1277
  20.5 0.0 copy-done
  20.5 1.0 %prepare.1 = (f32[2,8,128]{2,1,0:T(8,128)S(1)}, f32[8,128]{1,0:T(8,128)S(1)}, f32[4,8,128]{2,1,0:T(8,128)S(1)}, f32[576,128]{1,0:T(8,128)S(1)}, f32[1152,128]{1,0:T(8,128)S(1)}, /*index=5*/f32[576,128]{1,0:T(8,128)S(1)}) custom-call(s32[2]{0:T(128)S(1)} %pad_add_fusion.refs_0_, bf16[288,128]{1,0:T(8,128)(2,1)S(1)} %copy-done, ...), custom_call_target="tpu_custom_call" | custom-call | tf_op jit(solution)/shard_map/prepare/pallas_call | solution.py:1147
  21.6 0.0 collective-permute-done.1.near
  21.6 0.5 frames.4
  22.1 7.4 %forward.1 = (bf16[2,16,4096]{2,1,0:T(8,128)(2,1)S(1)}, bf16[2,16,4096]{2,1,0:T(8,128)(2,1)S(1)}, bf16[2,16,4096]{2,1,0:T(8,128)(2,1)S(1)}, bf16[2,16,4096]{2,1,...) custom-call(s32[1]{0:T(128)} %bitcast.1.member_ref.refs_0_, ...), custom_call_target="tpu_custom_call" | custom-call | flops 2048 | bytes 1024 | tf_op jit(solution)/shard_map/forward/pallas_call | solution.py:987
  29.5 0.0 collective-permute-done.7.far
  29.6 0.4 collective-permute-start.8
  30.1 0.1 collective-permute-start.9
  30.2 0.5 collective-permute-start.10
  30.7 1.2 %collective-permute-start.11 = (bf16[2,16,4096]{2,1,0:T(8,128)(2,1)S(1)}, bf16[2,16,4096]{2,1,0:T(8,128)(2,1)S(1)}, u32[]{:S(2)}, u32[]{:S(2)}) collective-permute-start(bf16[2,16,4096]{2,1,0:T(8,128)(2,1)S(1)} %get-tuple-element.132), channel_id=1, source_target_pairs={{0,3},{1,2},{2,1},{3,0},{4,7},{5,6},{6,5},{7,4},{8,11},{9,10},{10,... | collective-permute-start | bytes 786440 | tf_op jit(solution)/shard_map/ppermute | solution.py:1277
  31.9 0.0 collective-permute-done.8.near
  31.9 0.5 frames.5
  32.5 8.3 %backward.1 = (bf16[2,16,4096]{2,1,0:T(8,128)(2,1)S(1)}, bf16[2,16,4096]{2,1,0:T(8,128)(2,1)S(1)}, bf16[2,16,4096]{2,1,0:T(8,128)(2,1)S(1)}, bf16[2,16,4096]{2,1...) custom-call(s32[1]{0:T(128)} %bitcast.1.member_ref.refs_0_, ...), custom_call_target="tpu_custom_call" | custom-call | flops 5368709120 | bytes 20971520 | tf_op jit(solution)/shard_map/backward/pallas_call | solution.py:1013
  40.7 0.5 collective-permute-start.17
  41.2 0.5 collective-permute-start.18
  41.8 6.4 %weights.1 = (f32[864,128]{1,0:T(8,128)S(1)}, f32[16,128]{1,0:T(8,128)S(1)}, bf16[864,128]{1,0:T(8,128)(2,1)S(1)}, f32[16,128]{1,0:T(8,128)S(1)}) custom-call(s32[2]{0:T(128)S(1)} %pad_add_fusion.refs_0_, bf16[2,4,33,32,128]{4,3,2,1,0:T(8,128)(2,1)S(1)} %get-tuple-element.99.refs_1_, bf16[2,4,33,32,128]{4,3,2,1,0:T(8,128)(2,1)S(1)} %get-tuple-element.100.refs_2_, ...), custom_call_target="tpu_custom_call" | custom-call | flops 5368709120 | bytes 12582912 | tf_op jit(solution)/shard_map/weights/pallas_call | solution.py:1168
  48.2 0.0 collective-permute-done.9.refs_1_
  48.2 0.0 collective-permute-done.10.refs_2_
  48.2 0.0 collective-permute-done.11.refs_3_
  48.3 0.1 collective-permute-start.12
  48.3 1.6 %collective-permute-start.19 = (bf16[2,16,4096]{2,1,0:T(8,128)(2,1)S(1)}, bf16[2,16,4096]{2,1,0:T(8,128)(2,1)S(1)}, u32[]{:S(2)}, u32[]{:S(2)}) collective-permute-start(bf16[2,16,4096]{2,1,0:T(8,128)(2,1)S(1)} %get-tuple-element.145), channel_id=1, source_target_pairs={{0,3},{1,2},{2,1},{3,0},{4,7},{5,6},{6,5},{7,4},{8,11},{9,10},{10,... | collective-permute-start | bytes 786440 | tf_op jit(solution)/shard_map/ppermute | solution.py:1277
  49.9 0.0 collective-permute-done.12.refs_3_
  49.9 0.6 join.1
  50.5 3.4 %collective-permute-start.13 = (bf16[216,128]{1,0:T(8,128)(2,1)S(1)}, bf16[216,128]{1,0:T(8,128)(2,1)S(1)}, u32[]{:S(2)}, u32[]{:S(2)}) collective-permute-start(bf16[216,128]{1,0:T(8,128)(2,1)S(1)} %get-tuple-element.134), channel_id=1, source_target_pairs={{0,24},{1,29},{2,26},{3,31},{4,28},{5,25},{6,30},{7,27},{8,16},{9,... | collective-permute-start | bytes 165896 | tf_op jit(solution)/shard_map/ppermute | solution.py:1288
  53.9 0.4 collective-permute-start.14
  54.3 0.0 collective-permute-done.17.refs_1_
  54.3 1.6 %collective-permute-start.15 = (bf16[216,128]{1,0:T(8,128)(2,1)S(1)}, bf16[216,128]{1,0:T(8,128)(2,1)S(1)}, u32[]{:S(2)}, u32[]{:S(2)}) collective-permute-start(bf16[216,128]{1,0:T(8,128)(2,1)S(1)} %get-tuple-element.136), channel_id=1, source_target_pairs={{0,12},{1,9},{2,14},{3,11},{4,8},{5,13},{6,10},{7,15},{8,4},{9,1},... | collective-permute-start | bytes 165896 | tf_op jit(solution)/shard_map/ppermute | solution.py:1288
  55.9 0.0 collective-permute-done.18.refs_2_
  55.9 0.7 collective-permute-start.16
  56.6 1.0 %collect.2 = bf16[4,2,16,4096]{3,2,1,0:T(8,128)(2,1)} custom-call(s32[1]{0:T(128)} %bitcast.1.member_ref.refs_0_, bf16[2,16,4096]{2,1,0:T(8,128)(2,1)S(1)} %get-tuple-element.138.refs_0_, bf16[2,16,4096]{2,1,0:T(8,128)(2,1)S(1)} %collective-permute-done.9.refs_1_, bf16[2,16,4096]{2,1,0:T(8,128)(2,1)S(1)} %collective-permute-done.10.refs_2_, ...), custom_call_target="tpu_custom_call" | custom-call | tf_op jit(solution)/shard_map/collect/pallas_call | solution.py:1251
  57.6 0.0 collective-permute-done.19.refs_3_
  57.6 1.4 %collect.3 = f32[4,2,16,4096]{3,2,1,0:T(8,128)} custom-call(s32[1]{0:T(128)} %bitcast.1.member_ref.refs_0_, bf16[2,16,4096]{2,1,0:T(8,128)(2,1)S(1)} %get-tuple-element.142.refs_0_, bf16[2,16,4096]{2,1,0:T(8,128)(2,1)S(1)} %collective-permute-done.17.refs_1_, bf16[2,16,4096]{2,1,0:T(8,128)(2,1)S(1)} %collective-permute-done.18.refs_2_, ...), custom_call_target="tpu_custom_call" | custom-call | tf_op jit(solution)/shard_map/collect/pallas_call | solution.py:1251
  59.0 0.0 collective-permute-done.13.refs_2_
  59.0 1.1 %collective-permute-done.14.refs_3_ = bf16[216,128]{1,0:T(8,128)(2,1)S(1)} collective-permute-done((bf16[216,128]{1,0:T(8,128)(2,1)S(1)}, bf16[216,128]{1,0:T(8,128)(2,1)S(1)}, u32[]{:S(2)}, u32[]{:S(2)}) %collective-permute-start.14) | collective-permute-done | bytes 55328 | tf_op jit(solution)/shard_map/ppermute | solution.py:1288
  60.2 0.3 collective-permute-done.15.refs_4_
  60.5 0.0 collective-permute-done.16.refs_5_
  60.5 0.0 copy-done.1
  60.5 0.0 copy-done.2
  60.5 0.0 copy-done.3
  60.5 0.0 copy-done.4
  60.5 1.1 %reduce.1 = bf16[280,128]{1,0:T(8,128)(2,1)S(1)} custom-call(s32[2]{0:T(128)S(1)} %pad_add_fusion.refs_0_, f32[216,128]{1,0:T(8,128)S(1)} %get-tuple-element.148.refs_1_, bf16[216,128]{1,0:T(8,128)(2,1)S(1)} %collective-permute-done.13.refs_2_, bf16[216,128]{1,0:T(8,128)(2,1)S(1)} %collective-permute-done.14.refs_3_, ...), custom_call_target="tpu_custom_call" | custom-call | tf_op jit(solution)/shard_map/reduce/pallas_call | solution.py:1199
  61.6 0.5 collective-permute-start.20
  62.1 0.9 %collective-permute-done.20 = bf16[280,128]{1,0:T(8,128)(2,1)S(1)} collective-permute-done((bf16[280,128]{1,0:T(8,128)(2,1)S(1)}, bf16[280,128]{1,0:T(8,128)(2,1)S(1)}, u32[]{:S(2)}, u32[]{:S(2)}) %collective-permute-start.20) | collective-permute-done | bytes 71712 | tf_op jit(solution)/shard_map/ppermute | solution.py:1277
  63.0 1.4 %collective-permute-start.21 = (bf16[280,128]{1,0:T(8,128)(2,1)S(1)}, bf16[280,128]{1,0:T(8,128)(2,1)S(1)}, u32[]{:S(2)}, u32[]{:S(2)}) collective-permute-start(bf16[280,128]{1,0:T(8,128)(2,1)S(1)} %add_convert_fusion.refs_0_), channel_id=1, source_target_pairs={{0,2},{1,3},{2,0},{3,1},{4,6},{5,7},{6,4},{7,5},{8,10},{9,11},{10,... | collective-permute-start | bytes 215048 | tf_op jit(solution)/shard_map/ppermute | solution.py:1277
  64.4 3.2 %collective-permute-done.21.refs_1_ = bf16[280,128]{1,0:T(8,128)(2,1)S(1)} collective-permute-done((bf16[280,128]{1,0:T(8,128)(2,1)S(1)}, bf16[280,128]{1,0:T(8,128)(2,1)S(1)}, u32[]{:S(2)}, u32[]{:S(2)}) %collective-permute-start.21) | collective-permute-done | bytes 71712 | tf_op jit(solution)/shard_map/ppermute | solution.py:1277
  67.5 0.8 %finish.1 = (f32[18,32]{1,0:T(8,128)}, f32[32,32]{1,0:T(8,128)}, f32[32,128]{1,0:T(8,128)}, f32[32,128]{1,0:T(8,128)}, f32[64,72]{1,0:T(8,128)}, /*index=5*/f32[...) custom-call(bf16[280,128]{1,0:T(8,128)(2,1)S(1)} %add_convert_fusion, ...), custom_call_target="tpu_custom_call" | custom-call | tf_op jit(solution)/shard_map/finish/pallas_call | solution.py:1217
  (16 shorter events, 0.2 us)
Async XLA Ops:
  1.7 15.0 %collective-permute-start = (bf16[4,16,4096]{2,1,0:T(8,128)(2,1)S(1)}, bf16[4,16,4096]{2,1,0:T(8,128)(2,1)S(1)}, u32[]{:S(2)}, u32[]{:S(2)}) collective-permute-start(bf16[4,16,4096]{2,1,0:T(8,128)(2,1)S(1)} %far.1), channel_id=1, source_target_pairs={{0,2},{1,3},{2,0},{3,1},{4,6},{5,7},{6,4},{7,5},{8,10},{9,11},{10,... | collective-permute-start | bytes 1572872 | tf_op jit(solution)/shard_map/ppermute | solution.py:1277
  6.5 8.2 %collective-permute-start.2 = (bf16[288,128]{1,0:T(8,128)(2,1)}, bf16[288,128]{1,0:T(8,128)(2,1)S(1)}, u32[]{:S(2)}, u32[]{:S(2)}) collective-permute-start(bf16[288,128]{1,0:T(8,128)(2,1)} %pack.1.refs_1_), channel_id=1, source_target_pairs={{0,24},{1,29},{2,26},{3,31},{4,28},{5,25},{6,30},{7,27},{8,16},{9,... | collective-permute-start | bytes 221192 | tf_op jit(solution)/shard_map/ppermute | solution.py:1288
  10.1 8.2 %collective-permute-start.5 = (bf16[288,128]{1,0:T(8,128)(2,1)}, bf16[288,128]{1,0:T(8,128)(2,1)S(1)}, u32[]{:S(2)}, u32[]{:S(2)}) collective-permute-start(bf16[288,128]{1,0:T(8,128)(2,1)} %pack.1.refs_1_), channel_id=1, source_target_pairs={{1,5},{3,7},{5,1},{7,3},{9,13},{11,15},{13,9},{15,11},{17,21},{19,... | collective-permute-start | bytes 221192 | tf_op jit(solution)/shard_map/ppermute | solution.py:1288
  10.8 7.5 %collective-permute-start.4 = (bf16[288,128]{1,0:T(8,128)(2,1)}, bf16[288,128]{1,0:T(8,128)(2,1)S(1)}, u32[]{:S(2)}, u32[]{:S(2)}) collective-permute-start(bf16[288,128]{1,0:T(8,128)(2,1)} %pack.1.refs_1_), channel_id=1, source_target_pairs={{0,12},{1,9},{2,14},{3,11},{4,8},{5,13},{6,10},{7,15},{8,4},{9,1},... | collective-permute-start | bytes 221192 | tf_op jit(solution)/shard_map/ppermute | solution.py:1288
  11.3 7.0 %collective-permute-start.3 = (bf16[288,128]{1,0:T(8,128)(2,1)}, bf16[288,128]{1,0:T(8,128)(2,1)S(1)}, u32[]{:S(2)}, u32[]{:S(2)}) collective-permute-start(bf16[288,128]{1,0:T(8,128)(2,1)} %pack.1.refs_1_), channel_id=1, source_target_pairs={{0,20},{1,17},{2,22},{3,19},{4,16},{5,21},{6,18},{7,23},{8,28},{9,... | collective-permute-start | bytes 221192 | tf_op jit(solution)/shard_map/ppermute | solution.py:1288
  14.7 14.8 %collective-permute-start.7 = (bf16[4,16,4096]{2,1,0:T(8,128)(2,1)}, bf16[4,16,4096]{2,1,0:T(8,128)(2,1)S(1)}, u32[]{:S(2)}, u32[]{:S(2)}) collective-permute-start(bf16[4,16,4096]{2,1,0:T(8,128)(2,1)} %get-tuple-element.104), channel_id=1, source_target_pairs={{0,2},{1,3},{2,0},{3,1},{4,6},{5,7},{6,4},{7,5},{8,10},{9,11},{10,... | collective-permute-start | bytes 1572872 | tf_op jit(solution)/shard_map/ppermute | solution.py:1277
  16.7 3.9 %copy-start = (bf16[288,128]{1,0:T(8,128)(2,1)S(1)}, bf16[288,128]{1,0:T(8,128)(2,1)}, u32[]{:S(2)}) copy-start(bf16[288,128]{1,0:T(8,128)(2,1)} %pack.1.refs_1_) | copy-start | bytes 221188
  16.7 4.8 %collective-permute-start.1 = (bf16[4,16,4096]{2,1,0:T(8,128)(2,1)S(1)}, bf16[4,16,4096]{2,1,0:T(8,128)(2,1)S(1)}, u32[]{:S(2)}, u32[]{:S(2)}) collective-permute-start(bf16[4,16,4096]{2,1,0:T(8,128)(2,1)S(1)} %near.2), channel_id=1, source_target_pairs={{0,1},{1,0},{2,3},{3,2},{4,5},{5,4},{6,7},{7,6},{8,9},{9,8},{10,11... | collective-permute-start | bytes 1572872 | tf_op jit(solution)/shard_map/ppermute | solution.py:1277
  18.4 2.1 %collective-permute-start.6 = (bf16[1152,128]{1,0:T(8,128)(2,1)S(1)}, bf16[1152,128]{1,0:T(8,128)(2,1)S(1)}, u32[]{:S(2)}, u32[]{:S(2)}) collective-permute-start(bf16[1152,128]{1,0:T(8,128)(2,1)S(1)} %constant_dynamic-update-slice_fusion.refs_2_), channel_id=1, source_target_pairs={{0,1},{1,0},{2,3},{3,2},{4,5},{5,4},{6,7},{7,6},{8,9},{9,8},{10,11... | collective-permute-start | bytes 884744 | tf_op jit(solution)/shard_map/ppermute | solution.py:1277
  29.6 2.3 %collective-permute-start.8 = (bf16[4,16,4096]{2,1,0:T(8,128)(2,1)S(1)}, bf16[4,16,4096]{2,1,0:T(8,128)(2,1)S(1)}, u32[]{:S(2)}, u32[]{:S(2)}) collective-permute-start(bf16[4,16,4096]{2,1,0:T(8,128)(2,1)S(1)} %near.3), channel_id=1, source_target_pairs={{0,1},{1,0},{2,3},{3,2},{4,5},{5,4},{6,7},{7,6},{8,9},{9,8},{10,11... | collective-permute-start | bytes 1572872 | tf_op jit(solution)/shard_map/ppermute | solution.py:1277
  30.1 18.2 %collective-permute-start.9 = (bf16[2,16,4096]{2,1,0:T(8,128)(2,1)S(1)}, bf16[2,16,4096]{2,1,0:T(8,128)(2,1)S(1)}, u32[]{:S(2)}, u32[]{:S(2)}) collective-permute-start(bf16[2,16,4096]{2,1,0:T(8,128)(2,1)S(1)} %get-tuple-element.130), channel_id=1, source_target_pairs={{0,1},{1,0},{2,3},{3,2},{4,5},{5,4},{6,7},{7,6},{8,9},{9,8},{10,11... | collective-permute-start | bytes 786440 | tf_op jit(solution)/shard_map/ppermute | solution.py:1277
  30.2 18.0 %collective-permute-start.10 = (bf16[2,16,4096]{2,1,0:T(8,128)(2,1)S(1)}, bf16[2,16,4096]{2,1,0:T(8,128)(2,1)S(1)}, u32[]{:S(2)}, u32[]{:S(2)}) collective-permute-start(bf16[2,16,4096]{2,1,0:T(8,128)(2,1)S(1)} %get-tuple-element.131), channel_id=1, source_target_pairs={{0,2},{1,3},{2,0},{3,1},{4,6},{5,7},{6,4},{7,5},{8,10},{9,11},{10,... | collective-permute-start | bytes 786440 | tf_op jit(solution)/shard_map/ppermute | solution.py:1277
  30.7 17.5 %collective-permute-start.11 = (bf16[2,16,4096]{2,1,0:T(8,128)(2,1)S(1)}, bf16[2,16,4096]{2,1,0:T(8,128)(2,1)S(1)}, u32[]{:S(2)}, u32[]{:S(2)}) collective-permute-start(bf16[2,16,4096]{2,1,0:T(8,128)(2,1)S(1)} %get-tuple-element.132), channel_id=1, source_target_pairs={{0,3},{1,2},{2,1},{3,0},{4,7},{5,6},{6,5},{7,4},{8,11},{9,10},{10,... | collective-permute-start | bytes 786440 | tf_op jit(solution)/shard_map/ppermute | solution.py:1277
  40.7 13.6 %collective-permute-start.17 = (bf16[2,16,4096]{2,1,0:T(8,128)(2,1)S(1)}, bf16[2,16,4096]{2,1,0:T(8,128)(2,1)S(1)}, u32[]{:S(2)}, u32[]{:S(2)}) collective-permute-start(bf16[2,16,4096]{2,1,0:T(8,128)(2,1)S(1)} %get-tuple-element.143), channel_id=1, source_target_pairs={{0,1},{1,0},{2,3},{3,2},{4,5},{5,4},{6,7},{7,6},{8,9},{9,8},{10,11... | collective-permute-start | bytes 786440 | tf_op jit(solution)/shard_map/ppermute | solution.py:1277
  41.2 14.6 %collective-permute-start.18 = (bf16[2,16,4096]{2,1,0:T(8,128)(2,1)S(1)}, bf16[2,16,4096]{2,1,0:T(8,128)(2,1)S(1)}, u32[]{:S(2)}, u32[]{:S(2)}) collective-permute-start(bf16[2,16,4096]{2,1,0:T(8,128)(2,1)S(1)} %get-tuple-element.144), channel_id=1, source_target_pairs={{0,2},{1,3},{2,0},{3,1},{4,6},{5,7},{6,4},{7,5},{8,10},{9,11},{10,... | collective-permute-start | bytes 786440 | tf_op jit(solution)/shard_map/ppermute | solution.py:1277
  48.3 1.7 %collective-permute-start.12 = (bf16[864,128]{1,0:T(8,128)(2,1)S(1)}, bf16[864,128]{1,0:T(8,128)(2,1)S(1)}, u32[]{:S(2)}, u32[]{:S(2)}) collective-permute-start(bf16[864,128]{1,0:T(8,128)(2,1)S(1)} %get-tuple-element.133), channel_id=1, source_target_pairs={{0,1},{1,0},{2,3},{3,2},{4,5},{5,4},{6,7},{7,6},{8,9},{9,8},{10,11... | collective-permute-start | bytes 663560 | tf_op jit(solution)/shard_map/ppermute | solution.py:1277
  48.3 9.3 %collective-permute-start.19 = (bf16[2,16,4096]{2,1,0:T(8,128)(2,1)S(1)}, bf16[2,16,4096]{2,1,0:T(8,128)(2,1)S(1)}, u32[]{:S(2)}, u32[]{:S(2)}) collective-permute-start(bf16[2,16,4096]{2,1,0:T(8,128)(2,1)S(1)} %get-tuple-element.145), channel_id=1, source_target_pairs={{0,3},{1,2},{2,1},{3,0},{4,7},{5,6},{6,5},{7,4},{8,11},{9,10},{10,... | collective-permute-start | bytes 786440 | tf_op jit(solution)/shard_map/ppermute | solution.py:1277
  50.5 8.5 %collective-permute-start.13 = (bf16[216,128]{1,0:T(8,128)(2,1)S(1)}, bf16[216,128]{1,0:T(8,128)(2,1)S(1)}, u32[]{:S(2)}, u32[]{:S(2)}) collective-permute-start(bf16[216,128]{1,0:T(8,128)(2,1)S(1)} %get-tuple-element.134), channel_id=1, source_target_pairs={{0,24},{1,29},{2,26},{3,31},{4,28},{5,25},{6,30},{7,27},{8,16},{9,... | collective-permute-start | bytes 165896 | tf_op jit(solution)/shard_map/ppermute | solution.py:1288
  53.9 6.3 %collective-permute-start.14 = (bf16[216,128]{1,0:T(8,128)(2,1)S(1)}, bf16[216,128]{1,0:T(8,128)(2,1)S(1)}, u32[]{:S(2)}, u32[]{:S(2)}) collective-permute-start(bf16[216,128]{1,0:T(8,128)(2,1)S(1)} %get-tuple-element.135), channel_id=1, source_target_pairs={{0,20},{1,17},{2,22},{3,19},{4,16},{5,21},{6,18},{7,23},{8,28},{9,... | collective-permute-start | bytes 165896 | tf_op jit(solution)/shard_map/ppermute | solution.py:1288
  54.3 6.2 %collective-permute-start.15 = (bf16[216,128]{1,0:T(8,128)(2,1)S(1)}, bf16[216,128]{1,0:T(8,128)(2,1)S(1)}, u32[]{:S(2)}, u32[]{:S(2)}) collective-permute-start(bf16[216,128]{1,0:T(8,128)(2,1)S(1)} %get-tuple-element.136), channel_id=1, source_target_pairs={{0,12},{1,9},{2,14},{3,11},{4,8},{5,13},{6,10},{7,15},{8,4},{9,1},... | collective-permute-start | bytes 165896 | tf_op jit(solution)/shard_map/ppermute | solution.py:1288
  55.9 4.6 %collective-permute-start.16 = (bf16[216,128]{1,0:T(8,128)(2,1)S(1)}, bf16[216,128]{1,0:T(8,128)(2,1)S(1)}, u32[]{:S(2)}, u32[]{:S(2)}) collective-permute-start(bf16[216,128]{1,0:T(8,128)(2,1)S(1)} %get-tuple-element.137), channel_id=1, source_target_pairs={{1,5},{3,7},{5,1},{7,3},{9,13},{11,15},{13,9},{15,11},{17,21},{19,... | collective-permute-start | bytes 165896 | tf_op jit(solution)/shard_map/ppermute | solution.py:1288
  57.6 2.9 %copy-start.1 = (bf16[32,128]{1,0:T(8,128)(2,1)S(1)}, bf16[32,128]{1,0:T(8,128)(2,1)}, u32[]{:S(2)}) copy-start(bf16[32,128]{1,0:T(8,128)(2,1)} %refs_9_.3) | copy-start | bytes 24580
  57.6 2.9 %copy-start.2 = (bf16[32,128]{1,0:T(8,128)(2,1)S(1)}, bf16[32,128]{1,0:T(8,128)(2,1)}, u32[]{:S(2)}) copy-start(bf16[32,128]{1,0:T(8,128)(2,1)} %refs_10_.3) | copy-start | bytes 24580
  57.6 2.9 %copy-start.3 = (bf16[32,32]{1,0:T(8,128)(2,1)S(1)}, bf16[32,32]{1,0:T(8,128)(2,1)}, u32[]{:S(2)}) copy-start(bf16[32,32]{1,0:T(8,128)(2,1)} %refs_8_.3) | copy-start | bytes 6148
  57.6 2.9 %copy-start.4 = (bf16[18,32]{1,0:T(8,128)(2,1)S(1)}, bf16[18,32]{1,0:T(8,128)(2,1)}, u32[]{:S(2)}) copy-start(bf16[18,32]{1,0:T(8,128)(2,1)} %refs_7_.3) | copy-start | bytes 3460
  61.6 1.4 %collective-permute-start.20 = (bf16[280,128]{1,0:T(8,128)(2,1)S(1)}, bf16[280,128]{1,0:T(8,128)(2,1)S(1)}, u32[]{:S(2)}, u32[]{:S(2)}) collective-permute-start(bf16[280,128]{1,0:T(8,128)(2,1)S(1)} %reduce.1), channel_id=1, source_target_pairs={{0,1},{1,0},{2,3},{3,2},{4,5},{5,4},{6,7},{7,6},{8,9},{9,8},{10,11... | collective-permute-start | bytes 215048 | tf_op jit(solution)/shard_map/ppermute | solution.py:1277
  63.0 4.5 %collective-permute-start.21 = (bf16[280,128]{1,0:T(8,128)(2,1)S(1)}, bf16[280,128]{1,0:T(8,128)(2,1)S(1)}, u32[]{:S(2)}, u32[]{:S(2)}) collective-permute-start(bf16[280,128]{1,0:T(8,128)(2,1)S(1)} %add_convert_fusion.refs_0_), channel_id=1, source_target_pairs={{0,2},{1,3},{2,0},{3,1},{4,6},{5,7},{6,4},{7,5},{8,10},{9,11},{10,... | collective-permute-start | bytes 215048 | tf_op jit(solution)/shard_map/ppermute | solution.py:1277

commit v9 on v8

--- a/solution.py
+++ b/solution.py
@@ -352,16 +352,16 @@
             average, inverse = stats[2 * k : 2 * k + 1, :], stats[2 * k + 1 : 2 * k + 2, :]
             gain = inverse * style[2 * k : 2 * k + 1, :]
             half_gain = 0.5 * gain
-            half_shift = 0.5 * (style[2 * k + 1 : 2 * k + 2, :] - average * gain)
+            half_shift = 0.5 * style[2 * k + 1 : 2 * k + 2, :]
             scale_sum = jnp.zeros((1, LANES), f32)
             shift_sum = jnp.zeros((1, LANES), f32)
             for a in range(2):
-                v = value(a)
+                v = value(a) - average
                 g = y[:, a * LANES : (a + 1) * LANES] * slope_twice(v * half_gain + half_shift)
                 pre_grad[a] = tiles_of(g)
                 shift_sum = shift_sum + total(g)
-                scale_sum = scale_sum + total(g * ((v - average) * inverse))
-            scale_sum, shift_sum = both_parities(scale_sum), both_parities(shift_sum)
+                scale_sum = scale_sum + total(g * v)
+            scale_sum, shift_sum = both_parities(scale_sum * inverse), both_parities(shift_sum)
             factor = style[2 * k : 2 * k + 1, :]
             center = group_sum(factor * shift_sum) / MEMBERS
             tilt = group_sum(factor * scale_sum) / MEMBERS

time: 68.8 us -> 68.7 us (level)
  no operation moved by 1% of the time
where the time goes in v9:
time: 68.7 us; the launch traced here: 68.4 us
  Pallas kernels  34.2 us (50%)
  starting transfers between devices  23.2 us (34%)
  waiting for transfers between devices  9.79 us (14%)
  between operations  1.05 us (2%)
    ppermute x8, starting transfers between devices, half_trade(): return lax.ppermute(value, ('seq', 'rows'), pairs)  12 us
    ppermute x14, starting transfers between devices, trade(): return lax.ppermute(value, 'rows', [(i, i ^ offset) for i in range(count)])  11.2 us
    pallas_call x1, Pallas kernels, backward(): pl.pallas_call(lambda *refs: backward_kernel(count, *refs), in_specs=[in_...  8.13 us
    pallas_call x1, Pallas kernels, forward(): pl.pallas_call(lambda *refs: forward_kernel(count, *refs), in_specs=[in_s...  7.43 us
    ppermute x14, waiting for transfers between devices, trade(): return lax.ppermute(value, 'rows', [(i, i ^ offset) for i in range(count)])  6.83 us
    pallas_call x1, Pallas kernels, weight_messages(): pl.pallas_call(lambda *refs: message_kernel(count, rows, *refs), in_specs...  6.43 us
    ppermute x8, waiting for transfers between devices, half_trade(): return lax.ppermute(value, ('seq', 'rows'), pairs)  2.97 us
    pallas_call x2, Pallas kernels, collect_strips(): pl.pallas_call(collect_kernel, grid=(frames,), in_specs=[in_smem()] + [pl...  2.46 us
  transfers between devices with their start and end apart: 22, of which 7 were waited for; matrix products, arithmetic and copies ran while one was open for 0% of the time, Pallas kernels for 46%

profile of v9, /device:TPU:0, one launch (start us, length us, event | category | flops | bytes accessed | tf_op | source)
XLA Modules:
  0.0 68.4 jit_solution(2392992757518143328)
XLA Ops:
  0.6 1.1 %far.1 = bf16[4,16,4096]{2,1,0:T(8,128)(2,1)S(1)} custom-call(s32[1]{0:T(128)} %bitcast.1.member_ref.refs_0_, bf16[8,16,4096]{2,1,0:T(8,128)(2,1)} %array.1), custom_call_target="tpu_custom_call" | custom-call | tf_op jit(solution)/shard_map/far/pallas_call | solution.py:1066
  1.7 3.0 %collective-permute-start = (bf16[4,16,4096]{2,1,0:T(8,128)(2,1)S(1)}, bf16[4,16,4096]{2,1,0:T(8,128)(2,1)S(1)}, u32[]{:S(2)}, u32[]{:S(2)}) collective-permute-start(bf16[4,16,4096]{2,1,0:T(8,128)(2,1)S(1)} %far.1), channel_id=1, source_target_pairs={{0,2},{1,3},{2,0},{3,1},{4,6},{5,7},{6,4},{7,5},{8,10},{9,11},{10,... | collective-permute-start | bytes 1572872 | tf_op jit(solution)/shard_map/ppermute | solution.py:1277
  4.7 1.8 %pack.1.refs_1_ = bf16[288,128]{1,0:T(8,128)(2,1)} custom-call(s32[8]{0:T(128)} %refs_0_.1, s32[8]{0:T(128)} %refs_1_.1, s32[8]{0:T(128)} %refs_2_.1, bf16[64,72]{1,0:T(8,128)(2,1)} %bitcast.19, bf16[64,72]{1,0:T(8,128)(2,1)} %bitcast.20, bf16[64,72]{1,0:T(8,128)(2,1)} %bitcast.21, bf16[64,144]{1,0:T(8,128)(2,1)} %bitcast.15, bf16[32,128]{1,0:T(8,128)(2,1)} %refs_9_.3, ...), custom_call_target="tpu_custom_call" | custom-call | flops 16106127360 | bytes 1048576 | tf_op jit(solution)/shard_map/pack/pallas_call | solution.py:1122
  6.5 3.6 %collective-permute-start.2 = (bf16[288,128]{1,0:T(8,128)(2,1)}, bf16[288,128]{1,0:T(8,128)(2,1)S(1)}, u32[]{:S(2)}, u32[]{:S(2)}) collective-permute-start(bf16[288,128]{1,0:T(8,128)(2,1)} %pack.1.refs_1_), channel_id=1, source_target_pairs={{0,24},{1,29},{2,26},{3,31},{4,28},{5,25},{6,30},{7,27},{8,16},{9,... | collective-permute-start | bytes 221192 | tf_op jit(solution)/shard_map/ppermute | solution.py:1288
  10.1 0.7 collective-permute-start.5
  10.8 0.5 collective-permute-start.4
  11.3 1.2 %collective-permute-start.3 = (bf16[288,128]{1,0:T(8,128)(2,1)}, bf16[288,128]{1,0:T(8,128)(2,1)S(1)}, u32[]{:S(2)}, u32[]{:S(2)}) collective-permute-start(bf16[288,128]{1,0:T(8,128)(2,1)} %pack.1.refs_1_), channel_id=1, source_target_pairs={{0,20},{1,17},{2,22},{3,19},{4,16},{5,21},{6,18},{7,23},{8,28},{9,... | collective-permute-start | bytes 221192 | tf_op jit(solution)/shard_map/ppermute | solution.py:1288
  12.5 2.2 %cut.1 = (bf16[2,16,4096]{2,1,0:T(8,128)(2,1)S(1)}, bf16[2,16,4096]{2,1,0:T(8,128)(2,1)S(1)}, bf16[4,16,4096]{2,1,0:T(8,128)(2,1)}, bf16[2,16,4096]{2,1,0:T(8,128)(2,1)S(1)}, bf16[2,16,4096]{2,1,0:T(8,128)(2,1)S(1)}) custom-call(s32[1]{0:T(128)} %bitcast.1.member_ref.refs_0_, bf16[8,16,4096]{2,1,0:T(8,128)(2,1)} %array.1, bf16[8,16,4096]{2,1,0:T(8,128)(2,1)} %cotangent.1), custom_call_target="tpu_custom_call" | custom-call | tf_op jit(solution)/shard_map/cut/pallas_call | solution.py:1080
  14.7 0.0 collective-permute-done.2
  14.7 0.4 collective-permute-start.7
  15.1 1.6 %collective-permute-done.far = bf16[4,16,4096]{2,1,0:T(8,128)(2,1)S(1)} collective-permute-done((bf16[4,16,4096]{2,1,0:T(8,128)(2,1)S(1)}, bf16[4,16,4096]{2,1,0:T(8,128)(2,1)S(1)}, u32[]{:S(2)}, u32[]{:S(2)}) %collective-permute-start) | collective-permute-done | bytes 524320 | tf_op jit(solution)/shard_map/ppermute | solution.py:1277
  16.7 0.1 collective-permute-start.1
  16.8 1.5 %collective-permute-done.3 = bf16[288,128]{1,0:T(8,128)(2,1)S(1)} collective-permute-done((bf16[288,128]{1,0:T(8,128)(2,1)}, bf16[288,128]{1,0:T(8,128)(2,1)S(1)}, u32[]{:S(2)}, u32[]{:S(2)}) %collective-permute-start.3) | collective-permute-done | bytes 73760 | tf_op jit(solution)/shard_map/ppermute | solution.py:1288
  18.3 0.0 collective-permute-done.4
  18.4 0.0 collective-permute-done.5
  18.4 0.9 %collective-permute-start.6 = (bf16[1152,128]{1,0:T(8,128)(2,1)S(1)}, bf16[1152,128]{1,0:T(8,128)(2,1)S(1)}, u32[]{:S(2)}, u32[]{:S(2)}) collective-permute-start(bf16[1152,128]{1,0:T(8,128)(2,1)S(1)} %constant_dynamic-update-slice_fusion.refs_2_), channel_id=1, source_target_pairs={{0,1},{1,0},{2,3},{3,2},{4,5},{5,4},{6,7},{7,6},{8,9},{9,8},{10,11... | collective-permute-start | bytes 884744 | tf_op jit(solution)/shard_map/ppermute | solution.py:1277
  19.3 0.1 pad_add_fusion.refs_0_
  19.4 1.1 %collective-permute-done.6.refs_3_ = bf16[1152,128]{1,0:T(8,128)(2,1)S(1)} collective-permute-done((bf16[1152,128]{1,0:T(8,128)(2,1)S(1)}, bf16[1152,128]{1,0:T(8,128)(2,1)S(1)}, u32[]{:S(2)}, u32[]{:S(2)}) %collective-permute-start.6) | collective-permute-done | bytes 294944 | tf_op jit(solution)/shard_map/ppermute | solution.py:1277
  20.5 0.0 copy-done
  20.5 1.0 %prepare.1 = (f32[2,8,128]{2,1,0:T(8,128)S(1)}, f32[8,128]{1,0:T(8,128)S(1)}, f32[4,8,128]{2,1,0:T(8,128)S(1)}, f32[576,128]{1,0:T(8,128)S(1)}, f32[1152,128]{1,0:T(8,128)S(1)}, /*index=5*/f32[576,128]{1,0:T(8,128)S(1)}) custom-call(s32[2]{0:T(128)S(1)} %pad_add_fusion.refs_0_, bf16[288,128]{1,0:T(8,128)(2,1)S(1)} %copy-done, ...), custom_call_target="tpu_custom_call" | custom-call | tf_op jit(solution)/shard_map/prepare/pallas_call | solution.py:1147
  21.6 0.0 collective-permute-done.1.near
  21.6 0.5 frames.4
  22.1 7.4 %forward.1 = (bf16[2,16,4096]{2,1,0:T(8,128)(2,1)S(1)}, bf16[2,16,4096]{2,1,0:T(8,128)(2,1)S(1)}, bf16[2,16,4096]{2,1,0:T(8,128)(2,1)S(1)}, bf16[2,16,4096]{2,1,...) custom-call(s32[1]{0:T(128)} %bitcast.1.member_ref.refs_0_, ...), custom_call_target="tpu_custom_call" | custom-call | flops 2048 | bytes 1024 | tf_op jit(solution)/shard_map/forward/pallas_call | solution.py:987
  29.5 0.0 collective-permute-done.7.far
  29.6 0.4 collective-permute-start.8
  30.1 0.1 collective-permute-start.9
  30.2 0.5 collective-permute-start.10
  30.7 1.2 %collective-permute-start.11 = (bf16[2,16,4096]{2,1,0:T(8,128)(2,1)S(1)}, bf16[2,16,4096]{2,1,0:T(8,128)(2,1)S(1)}, u32[]{:S(2)}, u32[]{:S(2)}) collective-permute-start(bf16[2,16,4096]{2,1,0:T(8,128)(2,1)S(1)} %get-tuple-element.132), channel_id=1, source_target_pairs={{0,3},{1,2},{2,1},{3,0},{4,7},{5,6},{6,5},{7,4},{8,11},{9,10},{10,... | collective-permute-start | bytes 786440 | tf_op jit(solution)/shard_map/ppermute | solution.py:1277
  31.9 0.0 collective-permute-done.8.near
  31.9 0.5 frames.5
  32.5 8.1 %backward.1 = (bf16[2,16,4096]{2,1,0:T(8,128)(2,1)S(1)}, bf16[2,16,4096]{2,1,0:T(8,128)(2,1)S(1)}, bf16[2,16,4096]{2,1,0:T(8,128)(2,1)S(1)}, bf16[2,16,4096]{2,1...) custom-call(s32[1]{0:T(128)} %bitcast.1.member_ref.refs_0_, ...), custom_call_target="tpu_custom_call" | custom-call | flops 5368709120 | bytes 20971520 | tf_op jit(solution)/shard_map/backward/pallas_call | solution.py:1013
  40.6 0.5 collective-permute-start.17
  41.1 0.5 collective-permute-start.18
  41.7 6.4 %weights.1 = (f32[864,128]{1,0:T(8,128)S(1)}, f32[16,128]{1,0:T(8,128)S(1)}, bf16[864,128]{1,0:T(8,128)(2,1)S(1)}, f32[16,128]{1,0:T(8,128)S(1)}) custom-call(s32[2]{0:T(128)S(1)} %pad_add_fusion.refs_0_, bf16[2,4,33,32,128]{4,3,2,1,0:T(8,128)(2,1)S(1)} %get-tuple-element.99.refs_1_, bf16[2,4,33,32,128]{4,3,2,1,0:T(8,128)(2,1)S(1)} %get-tuple-element.100.refs_2_, ...), custom_call_target="tpu_custom_call" | custom-call | flops 5368709120 | bytes 12582912 | tf_op jit(solution)/shard_map/weights/pallas_call | solution.py:1168
  48.1 0.0 collective-permute-done.9.refs_1_
  48.1 0.0 collective-permute-done.10.refs_2_
  48.1 0.0 collective-permute-done.11.refs_3_
  48.1 0.1 collective-permute-start.12
  48.2 1.6 %collective-permute-start.19 = (bf16[2,16,4096]{2,1,0:T(8,128)(2,1)S(1)}, bf16[2,16,4096]{2,1,0:T(8,128)(2,1)S(1)}, u32[]{:S(2)}, u32[]{:S(2)}) collective-permute-start(bf16[2,16,4096]{2,1,0:T(8,128)(2,1)S(1)} %get-tuple-element.145), channel_id=1, source_target_pairs={{0,3},{1,2},{2,1},{3,0},{4,7},{5,6},{6,5},{7,4},{8,11},{9,10},{10,... | collective-permute-start | bytes 786440 | tf_op jit(solution)/shard_map/ppermute | solution.py:1277
  49.8 0.0 collective-permute-done.12.refs_3_
  49.8 0.6 join.1
  50.4 3.4 %collective-permute-start.13 = (bf16[216,128]{1,0:T(8,128)(2,1)S(1)}, bf16[216,128]{1,0:T(8,128)(2,1)S(1)}, u32[]{:S(2)}, u32[]{:S(2)}) collective-permute-start(bf16[216,128]{1,0:T(8,128)(2,1)S(1)} %get-tuple-element.134), channel_id=1, source_target_pairs={{0,24},{1,29},{2,26},{3,31},{4,28},{5,25},{6,30},{7,27},{8,16},{9,... | collective-permute-start | bytes 165896 | tf_op jit(solution)/shard_map/ppermute | solution.py:1288
  53.8 0.4 collective-permute-start.14
  54.2 0.0 collective-permute-done.17.refs_1_
  54.2 1.6 %collective-permute-start.15 = (bf16[216,128]{1,0:T(8,128)(2,1)S(1)}, bf16[216,128]{1,0:T(8,128)(2,1)S(1)}, u32[]{:S(2)}, u32[]{:S(2)}) collective-permute-start(bf16[216,128]{1,0:T(8,128)(2,1)S(1)} %get-tuple-element.136), channel_id=1, source_target_pairs={{0,12},{1,9},{2,14},{3,11},{4,8},{5,13},{6,10},{7,15},{8,4},{9,1},... | collective-permute-start | bytes 165896 | tf_op jit(solution)/shard_map/ppermute | solution.py:1288
  55.8 0.0 collective-permute-done.18.refs_2_
  55.8 0.7 collective-permute-start.16
  56.4 1.0 %collect.2 = bf16[4,2,16,4096]{3,2,1,0:T(8,128)(2,1)} custom-call(s32[1]{0:T(128)} %bitcast.1.member_ref.refs_0_, bf16[2,16,4096]{2,1,0:T(8,128)(2,1)S(1)} %get-tuple-element.138.refs_0_, bf16[2,16,4096]{2,1,0:T(8,128)(2,1)S(1)} %collective-permute-done.9.refs_1_, bf16[2,16,4096]{2,1,0:T(8,128)(2,1)S(1)} %collective-permute-done.10.refs_2_, ...), custom_call_target="tpu_custom_call" | custom-call | tf_op jit(solution)/shard_map/collect/pallas_call | solution.py:1251
  57.5 0.0 collective-permute-done.19.refs_3_
  57.5 1.4 %collect.3 = f32[4,2,16,4096]{3,2,1,0:T(8,128)} custom-call(s32[1]{0:T(128)} %bitcast.1.member_ref.refs_0_, bf16[2,16,4096]{2,1,0:T(8,128)(2,1)S(1)} %get-tuple-element.142.refs_0_, bf16[2,16,4096]{2,1,0:T(8,128)(2,1)S(1)} %collective-permute-done.17.refs_1_, bf16[2,16,4096]{2,1,0:T(8,128)(2,1)S(1)} %collective-permute-done.18.refs_2_, ...), custom_call_target="tpu_custom_call" | custom-call | tf_op jit(solution)/shard_map/collect/pallas_call | solution.py:1251
  58.9 0.0 collective-permute-done.13.refs_2_
  58.9 1.1 %collective-permute-done.14.refs_3_ = bf16[216,128]{1,0:T(8,128)(2,1)S(1)} collective-permute-done((bf16[216,128]{1,0:T(8,128)(2,1)S(1)}, bf16[216,128]{1,0:T(8,128)(2,1)S(1)}, u32[]{:S(2)}, u32[]{:S(2)}) %collective-permute-start.14) | collective-permute-done | bytes 55328 | tf_op jit(solution)/shard_map/ppermute | solution.py:1288
  60.0 0.3 collective-permute-done.15.refs_4_
  60.4 0.0 collective-permute-done.16.refs_5_
  60.4 0.0 copy-done.1
  60.4 0.0 copy-done.2
  60.4 0.0 copy-done.3
  60.4 0.0 copy-done.4
  60.4 1.1 %reduce.1 = bf16[280,128]{1,0:T(8,128)(2,1)S(1)} custom-call(s32[2]{0:T(128)S(1)} %pad_add_fusion.refs_0_, f32[216,128]{1,0:T(8,128)S(1)} %get-tuple-element.148.refs_1_, bf16[216,128]{1,0:T(8,128)(2,1)S(1)} %collective-permute-done.13.refs_2_, bf16[216,128]{1,0:T(8,128)(2,1)S(1)} %collective-permute-done.14.refs_3_, ...), custom_call_target="tpu_custom_call" | custom-call | tf_op jit(solution)/shard_map/reduce/pallas_call | solution.py:1199
  61.5 0.5 collective-permute-start.20
  61.9 0.9 %collective-permute-done.20 = bf16[280,128]{1,0:T(8,128)(2,1)S(1)} collective-permute-done((bf16[280,128]{1,0:T(8,128)(2,1)S(1)}, bf16[280,128]{1,0:T(8,128)(2,1)S(1)}, u32[]{:S(2)}, u32[]{:S(2)}) %collective-permute-start.20) | collective-permute-done | bytes 71712 | tf_op jit(solution)/shard_map/ppermute | solution.py:1277
  62.9 1.4 %collective-permute-start.21 = (bf16[280,128]{1,0:T(8,128)(2,1)S(1)}, bf16[280,128]{1,0:T(8,128)(2,1)S(1)}, u32[]{:S(2)}, u32[]{:S(2)}) collective-permute-start(bf16[280,128]{1,0:T(8,128)(2,1)S(1)} %add_convert_fusion.refs_0_), channel_id=1, source_target_pairs={{0,2},{1,3},{2,0},{3,1},{4,6},{5,7},{6,4},{7,5},{8,10},{9,11},{10,... | collective-permute-start | bytes 215048 | tf_op jit(solution)/shard_map/ppermute | solution.py:1277
  64.2 3.2 %collective-permute-done.21.refs_1_ = bf16[280,128]{1,0:T(8,128)(2,1)S(1)} collective-permute-done((bf16[280,128]{1,0:T(8,128)(2,1)S(1)}, bf16[280,128]{1,0:T(8,128)(2,1)S(1)}, u32[]{:S(2)}, u32[]{:S(2)}) %collective-permute-start.21) | collective-permute-done | bytes 71712 | tf_op jit(solution)/shard_map/ppermute | solution.py:1277
  67.4 0.8 %finish.1 = (f32[18,32]{1,0:T(8,128)}, f32[32,32]{1,0:T(8,128)}, f32[32,128]{1,0:T(8,128)}, f32[32,128]{1,0:T(8,128)}, f32[64,72]{1,0:T(8,128)}, /*index=5*/f32[...) custom-call(bf16[280,128]{1,0:T(8,128)(2,1)S(1)} %add_convert_fusion, ...), custom_call_target="tpu_custom_call" | custom-call | tf_op jit(solution)/shard_map/finish/pallas_call | solution.py:1217
  (16 shorter events, 0.2 us)
Async XLA Ops:
  1.7 15.0 %collective-permute-start = (bf16[4,16,4096]{2,1,0:T(8,128)(2,1)S(1)}, bf16[4,16,4096]{2,1,0:T(8,128)(2,1)S(1)}, u32[]{:S(2)}, u32[]{:S(2)}) collective-permute-start(bf16[4,16,4096]{2,1,0:T(8,128)(2,1)S(1)} %far.1), channel_id=1, source_target_pairs={{0,2},{1,3},{2,0},{3,1},{4,6},{5,7},{6,4},{7,5},{8,10},{9,11},{10,... | collective-permute-start | bytes 1572872 | tf_op jit(solution)/shard_map/ppermute | solution.py:1277
  6.5 8.2 %collective-permute-start.2 = (bf16[288,128]{1,0:T(8,128)(2,1)}, bf16[288,128]{1,0:T(8,128)(2,1)S(1)}, u32[]{:S(2)}, u32[]{:S(2)}) collective-permute-start(bf16[288,128]{1,0:T(8,128)(2,1)} %pack.1.refs_1_), channel_id=1, source_target_pairs={{0,24},{1,29},{2,26},{3,31},{4,28},{5,25},{6,30},{7,27},{8,16},{9,... | collective-permute-start | bytes 221192 | tf_op jit(solution)/shard_map/ppermute | solution.py:1288
  10.1 8.2 %collective-permute-start.5 = (bf16[288,128]{1,0:T(8,128)(2,1)}, bf16[288,128]{1,0:T(8,128)(2,1)S(1)}, u32[]{:S(2)}, u32[]{:S(2)}) collective-permute-start(bf16[288,128]{1,0:T(8,128)(2,1)} %pack.1.refs_1_), channel_id=1, source_target_pairs={{1,5},{3,7},{5,1},{7,3},{9,13},{11,15},{13,9},{15,11},{17,21},{19,... | collective-permute-start | bytes 221192 | tf_op jit(solution)/shard_map/ppermute | solution.py:1288
  10.8 7.5 %collective-permute-start.4 = (bf16[288,128]{1,0:T(8,128)(2,1)}, bf16[288,128]{1,0:T(8,128)(2,1)S(1)}, u32[]{:S(2)}, u32[]{:S(2)}) collective-permute-start(bf16[288,128]{1,0:T(8,128)(2,1)} %pack.1.refs_1_), channel_id=1, source_target_pairs={{0,12},{1,9},{2,14},{3,11},{4,8},{5,13},{6,10},{7,15},{8,4},{9,1},... | collective-permute-start | bytes 221192 | tf_op jit(solution)/shard_map/ppermute | solution.py:1288
  11.3 7.0 %collective-permute-start.3 = (bf16[288,128]{1,0:T(8,128)(2,1)}, bf16[288,128]{1,0:T(8,128)(2,1)S(1)}, u32[]{:S(2)}, u32[]{:S(2)}) collective-permute-start(bf16[288,128]{1,0:T(8,128)(2,1)} %pack.1.refs_1_), channel_id=1, source_target_pairs={{0,20},{1,17},{2,22},{3,19},{4,16},{5,21},{6,18},{7,23},{8,28},{9,... | collective-permute-start | bytes 221192 | tf_op jit(solution)/shard_map/ppermute | solution.py:1288
  14.7 14.8 %collective-permute-start.7 = (bf16[4,16,4096]{2,1,0:T(8,128)(2,1)}, bf16[4,16,4096]{2,1,0:T(8,128)(2,1)S(1)}, u32[]{:S(2)}, u32[]{:S(2)}) collective-permute-start(bf16[4,16,4096]{2,1,0:T(8,128)(2,1)} %get-tuple-element.104), channel_id=1, source_target_pairs={{0,2},{1,3},{2,0},{3,1},{4,6},{5,7},{6,4},{7,5},{8,10},{9,11},{10,... | collective-permute-start | bytes 1572872 | tf_op jit(solution)/shard_map/ppermute | solution.py:1277
  16.7 3.9 %copy-start = (bf16[288,128]{1,0:T(8,128)(2,1)S(1)}, bf16[288,128]{1,0:T(8,128)(2,1)}, u32[]{:S(2)}) copy-start(bf16[288,128]{1,0:T(8,128)(2,1)} %pack.1.refs_1_) | copy-start | bytes 221188
  16.7 4.8 %collective-permute-start.1 = (bf16[4,16,4096]{2,1,0:T(8,128)(2,1)S(1)}, bf16[4,16,4096]{2,1,0:T(8,128)(2,1)S(1)}, u32[]{:S(2)}, u32[]{:S(2)}) collective-permute-start(bf16[4,16,4096]{2,1,0:T(8,128)(2,1)S(1)} %near.2), channel_id=1, source_target_pairs={{0,1},{1,0},{2,3},{3,2},{4,5},{5,4},{6,7},{7,6},{8,9},{9,8},{10,11... | collective-permute-start | bytes 1572872 | tf_op jit(solution)/shard_map/ppermute | solution.py:1277
  18.4 2.1 %collective-permute-start.6 = (bf16[1152,128]{1,0:T(8,128)(2,1)S(1)}, bf16[1152,128]{1,0:T(8,128)(2,1)S(1)}, u32[]{:S(2)}, u32[]{:S(2)}) collective-permute-start(bf16[1152,128]{1,0:T(8,128)(2,1)S(1)} %constant_dynamic-update-slice_fusion.refs_2_), channel_id=1, source_target_pairs={{0,1},{1,0},{2,3},{3,2},{4,5},{5,4},{6,7},{7,6},{8,9},{9,8},{10,11... | collective-permute-start | bytes 884744 | tf_op jit(solution)/shard_map/ppermute | solution.py:1277
  29.6 2.3 %collective-permute-start.8 = (bf16[4,16,4096]{2,1,0:T(8,128)(2,1)S(1)}, bf16[4,16,4096]{2,1,0:T(8,128)(2,1)S(1)}, u32[]{:S(2)}, u32[]{:S(2)}) collective-permute-start(bf16[4,16,4096]{2,1,0:T(8,128)(2,1)S(1)} %near.3), channel_id=1, source_target_pairs={{0,1},{1,0},{2,3},{3,2},{4,5},{5,4},{6,7},{7,6},{8,9},{9,8},{10,11... | collective-permute-start | bytes 1572872 | tf_op jit(solution)/shard_map/ppermute | solution.py:1277
  30.1 18.0 %collective-permute-start.9 = (bf16[2,16,4096]{2,1,0:T(8,128)(2,1)S(1)}, bf16[2,16,4096]{2,1,0:T(8,128)(2,1)S(1)}, u32[]{:S(2)}, u32[]{:S(2)}) collective-permute-start(bf16[2,16,4096]{2,1,0:T(8,128)(2,1)S(1)} %get-tuple-element.130), channel_id=1, source_target_pairs={{0,1},{1,0},{2,3},{3,2},{4,5},{5,4},{6,7},{7,6},{8,9},{9,8},{10,11... | collective-permute-start | bytes 786440 | tf_op jit(solution)/shard_map/ppermute | solution.py:1277
  30.2 17.9 %collective-permute-start.10 = (bf16[2,16,4096]{2,1,0:T(8,128)(2,1)S(1)}, bf16[2,16,4096]{2,1,0:T(8,128)(2,1)S(1)}, u32[]{:S(2)}, u32[]{:S(2)}) collective-permute-start(bf16[2,16,4096]{2,1,0:T(8,128)(2,1)S(1)} %get-tuple-element.131), channel_id=1, source_target_pairs={{0,2},{1,3},{2,0},{3,1},{4,6},{5,7},{6,4},{7,5},{8,10},{9,11},{10,... | collective-permute-start | bytes 786440 | tf_op jit(solution)/shard_map/ppermute | solution.py:1277
  30.7 17.4 %collective-permute-start.11 = (bf16[2,16,4096]{2,1,0:T(8,128)(2,1)S(1)}, bf16[2,16,4096]{2,1,0:T(8,128)(2,1)S(1)}, u32[]{:S(2)}, u32[]{:S(2)}) collective-permute-start(bf16[2,16,4096]{2,1,0:T(8,128)(2,1)S(1)} %get-tuple-element.132), channel_id=1, source_target_pairs={{0,3},{1,2},{2,1},{3,0},{4,7},{5,6},{6,5},{7,4},{8,11},{9,10},{10,... | collective-permute-start | bytes 786440 | tf_op jit(solution)/shard_map/ppermute | solution.py:1277
  40.6 13.6 %collective-permute-start.17 = (bf16[2,16,4096]{2,1,0:T(8,128)(2,1)S(1)}, bf16[2,16,4096]{2,1,0:T(8,128)(2,1)S(1)}, u32[]{:S(2)}, u32[]{:S(2)}) collective-permute-start(bf16[2,16,4096]{2,1,0:T(8,128)(2,1)S(1)} %get-tuple-element.143), channel_id=1, source_target_pairs={{0,1},{1,0},{2,3},{3,2},{4,5},{5,4},{6,7},{7,6},{8,9},{9,8},{10,11... | collective-permute-start | bytes 786440 | tf_op jit(solution)/shard_map/ppermute | solution.py:1277
  41.1 14.6 %collective-permute-start.18 = (bf16[2,16,4096]{2,1,0:T(8,128)(2,1)S(1)}, bf16[2,16,4096]{2,1,0:T(8,128)(2,1)S(1)}, u32[]{:S(2)}, u32[]{:S(2)}) collective-permute-start(bf16[2,16,4096]{2,1,0:T(8,128)(2,1)S(1)} %get-tuple-element.144), channel_id=1, source_target_pairs={{0,2},{1,3},{2,0},{3,1},{4,6},{5,7},{6,4},{7,5},{8,10},{9,11},{10,... | collective-permute-start | bytes 786440 | tf_op jit(solution)/shard_map/ppermute | solution.py:1277
  48.1 1.7 %collective-permute-start.12 = (bf16[864,128]{1,0:T(8,128)(2,1)S(1)}, bf16[864,128]{1,0:T(8,128)(2,1)S(1)}, u32[]{:S(2)}, u32[]{:S(2)}) collective-permute-start(bf16[864,128]{1,0:T(8,128)(2,1)S(1)} %get-tuple-element.133), channel_id=1, source_target_pairs={{0,1},{1,0},{2,3},{3,2},{4,5},{5,4},{6,7},{7,6},{8,9},{9,8},{10,11... | collective-permute-start | bytes 663560 | tf_op jit(solution)/shard_map/ppermute | solution.py:1277
  48.2 9.3 %collective-permute-start.19 = (bf16[2,16,4096]{2,1,0:T(8,128)(2,1)S(1)}, bf16[2,16,4096]{2,1,0:T(8,128)(2,1)S(1)}, u32[]{:S(2)}, u32[]{:S(2)}) collective-permute-start(bf16[2,16,4096]{2,1,0:T(8,128)(2,1)S(1)} %get-tuple-element.145), channel_id=1, source_target_pairs={{0,3},{1,2},{2,1},{3,0},{4,7},{5,6},{6,5},{7,4},{8,11},{9,10},{10,... | collective-permute-start | bytes 786440 | tf_op jit(solution)/shard_map/ppermute | solution.py:1277
  50.4 8.5 %collective-permute-start.13 = (bf16[216,128]{1,0:T(8,128)(2,1)S(1)}, bf16[216,128]{1,0:T(8,128)(2,1)S(1)}, u32[]{:S(2)}, u32[]{:S(2)}) collective-permute-start(bf16[216,128]{1,0:T(8,128)(2,1)S(1)} %get-tuple-element.134), channel_id=1, source_target_pairs={{0,24},{1,29},{2,26},{3,31},{4,28},{5,25},{6,30},{7,27},{8,16},{9,... | collective-permute-start | bytes 165896 | tf_op jit(solution)/shard_map/ppermute | solution.py:1288
  53.8 6.3 %collective-permute-start.14 = (bf16[216,128]{1,0:T(8,128)(2,1)S(1)}, bf16[216,128]{1,0:T(8,128)(2,1)S(1)}, u32[]{:S(2)}, u32[]{:S(2)}) collective-permute-start(bf16[216,128]{1,0:T(8,128)(2,1)S(1)} %get-tuple-element.135), channel_id=1, source_target_pairs={{0,20},{1,17},{2,22},{3,19},{4,16},{5,21},{6,18},{7,23},{8,28},{9,... | collective-permute-start | bytes 165896 | tf_op jit(solution)/shard_map/ppermute | solution.py:1288
  54.2 6.2 %collective-permute-start.15 = (bf16[216,128]{1,0:T(8,128)(2,1)S(1)}, bf16[216,128]{1,0:T(8,128)(2,1)S(1)}, u32[]{:S(2)}, u32[]{:S(2)}) collective-permute-start(bf16[216,128]{1,0:T(8,128)(2,1)S(1)} %get-tuple-element.136), channel_id=1, source_target_pairs={{0,12},{1,9},{2,14},{3,11},{4,8},{5,13},{6,10},{7,15},{8,4},{9,1},... | collective-permute-start | bytes 165896 | tf_op jit(solution)/shard_map/ppermute | solution.py:1288
  55.8 4.6 %collective-permute-start.16 = (bf16[216,128]{1,0:T(8,128)(2,1)S(1)}, bf16[216,128]{1,0:T(8,128)(2,1)S(1)}, u32[]{:S(2)}, u32[]{:S(2)}) collective-permute-start(bf16[216,128]{1,0:T(8,128)(2,1)S(1)} %get-tuple-element.137), channel_id=1, source_target_pairs={{1,5},{3,7},{5,1},{7,3},{9,13},{11,15},{13,9},{15,11},{17,21},{19,... | collective-permute-start | bytes 165896 | tf_op jit(solution)/shard_map/ppermute | solution.py:1288
  57.5 2.9 %copy-start.1 = (bf16[32,128]{1,0:T(8,128)(2,1)S(1)}, bf16[32,128]{1,0:T(8,128)(2,1)}, u32[]{:S(2)}) copy-start(bf16[32,128]{1,0:T(8,128)(2,1)} %refs_9_.3) | copy-start | bytes 24580
  57.5 2.9 %copy-start.2 = (bf16[32,128]{1,0:T(8,128)(2,1)S(1)}, bf16[32,128]{1,0:T(8,128)(2,1)}, u32[]{:S(2)}) copy-start(bf16[32,128]{1,0:T(8,128)(2,1)} %refs_10_.3) | copy-start | bytes 24580
  57.5 2.9 %copy-start.3 = (bf16[32,32]{1,0:T(8,128)(2,1)S(1)}, bf16[32,32]{1,0:T(8,128)(2,1)}, u32[]{:S(2)}) copy-start(bf16[32,32]{1,0:T(8,128)(2,1)} %refs_8_.3) | copy-start | bytes 6148
  57.5 2.9 %copy-start.4 = (bf16[18,32]{1,0:T(8,128)(2,1)S(1)}, bf16[18,32]{1,0:T(8,128)(2,1)}, u32[]{:S(2)}) copy-start(bf16[18,32]{1,0:T(8,128)(2,1)} %refs_7_.3) | copy-start | bytes 3460
  61.5 1.4 %collective-permute-start.20 = (bf16[280,128]{1,0:T(8,128)(2,1)S(1)}, bf16[280,128]{1,0:T(8,128)(2,1)S(1)}, u32[]{:S(2)}, u32[]{:S(2)}) collective-permute-start(bf16[280,128]{1,0:T(8,128)(2,1)S(1)} %reduce.1), channel_id=1, source_target_pairs={{0,1},{1,0},{2,3},{3,2},{4,5},{5,4},{6,7},{7,6},{8,9},{9,8},{10,11... | collective-permute-start | bytes 215048 | tf_op jit(solution)/shard_map/ppermute | solution.py:1277
  62.9 4.5 %collective-permute-start.21 = (bf16[280,128]{1,0:T(8,128)(2,1)S(1)}, bf16[280,128]{1,0:T(8,128)(2,1)S(1)}, u32[]{:S(2)}, u32[]{:S(2)}) collective-permute-start(bf16[280,128]{1,0:T(8,128)(2,1)S(1)} %add_convert_fusion.refs_0_), channel_id=1, source_target_pairs={{0,2},{1,3},{2,0},{3,1},{4,6},{5,7},{6,4},{7,5},{8,10},{9,11},{10,... | collective-permute-start | bytes 215048 | tf_op jit(solution)/shard_map/ppermute | solution.py:1277
